TPU v7x, 32 devices: a whole 2x2x4 slice. The times are simulated.
32 devices in a mesh: comp: 4 (over x, core), feat: 8 (over z, y).
Axes of the slice: x: 2, y: 2, z: 4, core: 2. Of those that a mesh axis runs over, the one named last changes fastest.
Arguments:
- samples: float32 [1, 192, 28672], P(None, None, 'feat'), may hold values from -20 to 20, as said below
- start_vectors: float32 [256, 28672], P('comp', 'feat'), may hold values from -8 to 8
Outputs:
- vectors: float32 [256, 28672], P('comp', 'feat')
Inputs may be any that keep to these rules, and one draw needn't show every extreme that they name: `samples`: activation rows with feature scales that differ over a factor of ten.
All inputs are finite; a program needn't handle non-finite values.
Results may differ from a plain program's by a relative error of at most 0.0001.
Values sent between devices are 32-bit elements; how exact they have to be, the bound alone decides.
No kernel may reach another device: no remote copies, remote signals or barrier semaphores. Data moves between devices by JAX's collectives and lax.ppermute only.
A program may use at most 64 MiB of HBM per device.

v0:
```python
import math

import jax
import jax.numpy as jnp
from jax import lax
from jax.sharding import PartitionSpec as P

step_rate = 0.1
epsilon = 1e-06
highest = lax.Precision.HIGHEST


def project(sample, vectors, root_width):
    return jnp.einsum("rd,kd->rk", sample, vectors, precision=highest) / root_width


def normalize(updated, features):
    summed = lax.psum(jnp.sum(updated * updated, axis=1), "feat")
    return updated * lax.rsqrt(summed / features + epsilon)[:, None]


def couplings(every_images, own_images, earlier):
    intersection = (
        jnp.einsum("rj,ri->ji", every_images, own_images, precision=highest) / own_images.shape[0]
    )
    return jnp.where(earlier, intersection, jnp.float32(0.0))


def add_parent(coupling, pieces):
    return jnp.einsum("ji,jd->id", coupling, pieces, precision=highest)


def shards(samples, start_vectors):
    per_group = start_vectors.shape[0]
    features = samples.shape[2] * lax.axis_size("feat")
    total_rows = per_group * lax.axis_size("comp")
    root_width = math.sqrt(features)
    group_index = lax.axis_index("comp")
    own_columns = group_index * per_group + jnp.arange(per_group, dtype=jnp.int32)
    earlier = jnp.arange(total_rows, dtype=jnp.int32)[:, None] < own_columns[None, :]
    current = normalize(start_vectors, features)
    sample = samples[0]
    vector = current
    own_images = lax.psum(project(sample, vector, root_width), "feat")
    every_images = lax.all_gather(own_images, "comp", axis=1, tiled=True)
    coupling = couplings(every_images, own_images, earlier)
    penalty = add_parent(coupling, lax.all_gather(vector, "comp", axis=0, tiled=True))
    gradient = (
        root_width
        * jnp.einsum("rk,rd->kd", own_images, sample, precision=highest)
        / sample.shape[0]
        - penalty
    )
    current = vector + step_rate * gradient
    current = normalize(current, features)
    return current


def solution(mesh):
    in_specs = (P(None, None, "feat"), P("comp", "feat"))
    out_specs = P("comp", "feat")
    return jax.shard_map(shards, mesh=mesh, in_specs=in_specs, out_specs=out_specs, check_vma=False)
```

profile of v0, /device:TPU:0, one launch (start us, length us, event | category | flops | bytes accessed | tf_op | source)
XLA Modules:
  0.0 112.6 jit_solution(119580499015229046)
XLA Ops:
  6.5 0.0 copy-start
  6.5 0.0 all-gather.2.cloned.1.call-start
  6.5 1.5 %multiply_reduce_fusion.1 = f32[64]{0:T(128)S(1)} fusion(f32[64,3584]{1,0:T(8,128)} %param.3), kind=kLoop, calls=%fused_computation.12 | loop fusion | flops 458688 | bytes 917760 | tf_op jit(solution)/shard_map/reduce_sum | solution.py:18
  8.0 23.1 %psum.21 = f32[64]{0:T(128)S(1)} all-reduce(f32[64]{0:T(128)S(1)} %multiply_reduce_fusion.1), channel_id=1, replica_groups=mesh['comp'=4,'feat'=8] {'feat'}, use_global_device_ids=true, to_apply=%region_1.0 | all-reduce | flops 64 | bytes 512 | tf_op jit(solution)/shard_map/psum | solution.py:18
  31.2 2.2 %broadcast_multiply_fusion.1 = f32[64,3584]{1,0:T(8,128)} fusion(f32[64,3584]{1,0:T(8,128)} %param.3, f32[64]{0:T(128)S(1)} %add_rsqrt_fusion.1), kind=kLoop, calls=%fused_computation.14 | loop fusion | flops 229376 | bytes 1835264 | tf_op jit(solution)/shard_map/mul | solution.py:19
  33.4 0.0 all-gather.2.cloned.1.call-update
  33.4 0.0 copy-done
  33.4 3.9 %fusion.10 = f32[192,64]{0,1:T(8,128)S(1)} fusion(f32[64,3584]{1,0:T(8,128)} %broadcast_multiply_fusion.1, f32[1,192,3584]{2,1,0:T(8,128)S(1)} %copy-done), kind=kOutput, calls=%fused_computation.10 | convolution fusion | flops 528494592 | bytes 3719168 | tf_op jit(solution)/shard_map/rd,kd->rk/dot_general | solution.py:14
  37.4 33.4 %psum.22 = f32[192,64]{0,1:T(8,128)S(1)} all-reduce(f32[192,64]{0,1:T(8,128)S(1)} %fusion.10), channel_id=1, replica_groups=mesh['comp'=4,'feat'=8] {'feat'}, use_global_device_ids=true, to_apply=%region_2.0 | all-reduce | flops 12288 | bytes 98304 | tf_op jit(solution)/shard_map/psum | solution.py:44
  70.7 5.8 %all_gather.6 = f32[192,256]{0,1:T(8,128)S(1)} all-gather(f32[192,64]{0,1:T(8,128)S(1)} %psum.22), channel_id=1, replica_groups=mesh['comp'=4,'feat'=8] {'comp'}, dimensions={1}, use_global_device_ids=true | all-gather | bytes 245760 | tf_op jit(solution)/shard_map/all_gather | solution.py:45
  76.5 0.4 fusion.6
  76.9 0.0 all-gather.2.cloned.1.call-done
  76.9 0.0 copy-start.1
  77.0 4.4 %fusion.13 = f32[64,3584]{1,0:T(8,128)S(1)} fusion(f32[256,64]{1,0:T(8,128)S(1)} %fusion.6, f32[256,3584]{1,0:T(8,128)} %all-gather.2.cloned.1.call-done), kind=kOutput, calls=%fused_computation.19 | convolution fusion | flops 704643072 | bytes 4653056 | tf_op jit(solution)/shard_map/ji,jd->id/dot_general | solution.py:30
  81.4 0.0 copy-done.1
  81.4 2.9 %multiply_reduce_fusion = (f32[64]{0:T(128)S(1)}, f32[64,3584]{1,0:T(8,128)}) fusion(f32[64,3584]{1,0:T(8,128)S(1)} %copy-done.1, f32[64,3584]{1,0:T(8,128)S(1)} %fusion.13, f32[192,64]{0,1:T(8,128)S(1)} %psum.22, f32[1,192,3584]{2,1,0:T(8,128)S(1)} %copy-done), kind=kOutput, calls=%fused_computation.11 | convolution fusion | flops 529858496 | bytes 5554432 | tf_op jit(solution)/shard_map/rk,rd->kd/dot_general | solution.py:50
  84.3 19.2 %psum.23 = f32[64]{0:T(128)S(1)} all-reduce(f32[64]{0:T(128)S(1)} %get-tuple-element.5), channel_id=1, replica_groups=mesh['comp'=4,'feat'=8] {'feat'}, use_global_device_ids=true, to_apply=%region_4.5 | all-reduce | flops 64 | bytes 512 | tf_op jit(solution)/shard_map/psum | solution.py:18
  103.5 2.2 %broadcast_multiply_fusion = f32[64,3584]{1,0:T(8,128)} fusion(f32[64,3584]{1,0:T(8,128)} %get-tuple-element.6, f32[64]{0:T(128)S(1)} %add_rsqrt_fusion), kind=kLoop, calls=%fused_computation.13 | loop fusion | flops 229376 | bytes 1835264 | tf_op jit(solution)/shard_map/mul | solution.py:19
  (3 shorter events, 0.0 us)
Async XLA Ops:
  6.5 26.9 %copy-start = (f32[1,192,3584]{2,1,0:T(8,128)S(1)}, f32[1,192,3584]{2,1,0:T(8,128)}, u32[]{:S(2)}) copy-start(f32[1,192,3584]{2,1,0:T(8,128)} %param.2) | copy-start | bytes 8257540
  6.5 70.4 %all-gather.2.cloned.1.call-start = ((), (), s32[]{:S(2)}) async-start(), calls=%async_computation | async-start | bytes 4587520 | tf_op jit(solution)/shard_map/all_gather | solution.py:47
  76.9 4.5 %copy-start.1 = (f32[64,3584]{1,0:T(8,128)S(1)}, f32[64,3584]{1,0:T(8,128)}, u32[]{:S(2)}) copy-start(f32[64,3584]{1,0:T(8,128)} %broadcast_multiply_fusion.1) | copy-start | bytes 2752516
Sparse Core Ops, SparseCore 0:
  33.5 28.7 all-gather.1
where the time goes:
time: 113 us
  blocking collectives  81.4 us (72%)
  between operations  13.4 us (12%)
  matrix products  11.7 us (10%)
  other arithmetic  5.98 us (5%)
    psum x2, blocking collectives, normalize(): summed = lax.psum(jnp.sum(updated * updated, axis=1), 'feat')  42.3 us
    psum x1, blocking collectives, shards(): own_images = lax.psum(project(sample, vector, root_width), 'feat')  33.4 us
    all_gather x1, blocking collectives, shards(): every_images = lax.all_gather(own_images, 'comp', axis=1, tiled=True)  5.79 us
    mul x2, other arithmetic, normalize(): return updated * lax.rsqrt(summed / features + epsilon)[:, None]  4.47 us
    dot_general x1, matrix products, add_parent(): return jnp.einsum('ji,jd->id', coupling, pieces, precision=highest)  4.44 us
    dot_general x1, matrix products, project(): jnp.einsum('rd,kd->rk', sample, vectors, precision=highest) / root_width  3.94 us
    dot_general x1, matrix products, shards(): jnp.einsum('rk,rd->kd', own_images, sample, precision=highest)  2.91 us
  transfers between devices with their start and end apart: 1, of which 0 were waited for; matrix products, arithmetic and copies ran while one was open for 4% of the time, Pallas kernels for 0%

commit v1 on v0

v1 whole, which is shorter than its diff:
```python
import math

import jax
import jax.numpy as jnp
from jax import lax
from jax.sharding import PartitionSpec as P

step_rate = 0.1
epsilon = 1e-06
high = lax.Precision.HIGH


def earlier_blocks(own, comp):
    cores = 2 if comp % 2 == 0 else 1
    chips = comp // cores
    group = lax.axis_index("comp")
    blocks = [(own, group)]
    if cores == 2:
        swap = [(i, i ^ 1) for i in range(comp)]
    travelling = own
    for step in range(chips):
        if step > 0:
            travelling = lax.ppermute(travelling, "comp", [(i, i + cores) for i in range(comp - cores)])
            blocks.append((travelling, group - step * cores))
        if cores == 2:
            other = lax.ppermute(travelling, "comp", swap)
            blocks.append((other, (group ^ 1) - step * cores))
    return blocks


def shards(samples, start_vectors):
    comp = lax.axis_size("comp")
    feat = lax.axis_size("feat")
    per_group = start_vectors.shape[0]
    sample = samples[0]
    rows = sample.shape[0]
    features = sample.shape[1] * feat
    total = per_group * comp
    root_width = math.sqrt(features)
    group = lax.axis_index("comp")

    blocks = earlier_blocks(start_vectors, comp)

    raw = jnp.einsum("kd,rd->kr", start_vectors, sample, precision=high)
    squares = jnp.sum(start_vectors * start_vectors, axis=1, keepdims=True)
    partial = jnp.concatenate([raw, squares], axis=1)
    share = -(-per_group // feat)
    partial = jnp.pad(partial, ((0, share * feat - per_group), (0, 0)))
    pieces = lax.all_to_all(partial, "feat", split_axis=0, concat_axis=0, tiled=True)
    summed = jnp.sum(pieces.reshape(feat, share, rows + 1), axis=0)
    everything = lax.all_gather(summed, ("comp", "feat"), axis=0, tiled=True)
    everything = everything.reshape(comp, share * feat, rows + 1)[:, :per_group].reshape(total, rows + 1)

    scale = lax.rsqrt(everything[:, rows:] / features + epsilon)
    images = everything[:, :rows] * (scale / root_width)
    own_images = lax.dynamic_slice_in_dim(images, group * per_group, per_group, 0)
    own_scale = lax.dynamic_slice_in_dim(scale, group * per_group, per_group, 0)
    intersection = jnp.einsum("ir,jr->ij", own_images, images, precision=lax.Precision.HIGHEST) / rows
    own_rows = group * per_group + jnp.arange(per_group, dtype=jnp.int32)
    coupling = jnp.where(
        jnp.arange(total, dtype=jnp.int32)[None, :] < own_rows[:, None], intersection * scale[:, 0][None, :], 0.0
    )

    updated = own_scale * start_vectors + (step_rate * root_width / rows) * jnp.einsum(
        "kr,rd->kd", own_images, sample, precision=high
    )
    for block, owner in blocks:
        part = lax.dynamic_slice_in_dim(coupling, jnp.maximum(owner, 0) * per_group, per_group, 1)
        part = jnp.where(owner >= 0, part, 0.0)
        updated = updated - step_rate * jnp.einsum("ij,jd->id", part, block, precision=high)

    norms = jnp.broadcast_to(jnp.sum(updated * updated, axis=1), (feat, per_group))
    sums = lax.all_to_all(norms, "feat", split_axis=0, concat_axis=0, tiled=True)
    return updated * lax.rsqrt(jnp.sum(sums, axis=0) / features + epsilon)[:, None]


def solution(mesh):
    in_specs = (P(None, None, "feat"), P("comp", "feat"))
    out_specs = P("comp", "feat")
    return jax.shard_map(shards, mesh=mesh, in_specs=in_specs, out_specs=out_specs, check_vma=False)
```

time: 113 us -> 110 us (0.973)
  between operations: 13.4 us -> 0.16 us
  starting transfers between devices: 0.01 us -> 11.9 us
  waiting for transfers between devices: 0.04 us -> 6.88 us
  blocking collectives: 81.4 us -> 74.6 us
  other arithmetic: 5.98 us -> 4.65 us
    psum x3 -> x0, blocking collectives: 75.6 us -> none  [the longest x2 42.3 us: normalize(): summed = lax.psum(jnp.sum(updated * updated, axis=1), 'feat')]
    all_gather x1, blocking collectives: 5.79 us -> 65.1 us  [shards(): everything = lax.all_gather(summed, ('comp', 'feat'), axis=0, tiled=True)]
    all_to_all x0 -> x1, blocking collectives: none -> 9.46 us  [shards(): lax.all_to_all(norms, 'feat', split_axis=0, concat_axis=0, tiled=True)]
    all_to_all x0 -> x1, waiting for transfers between devices: none -> 6.87 us  [shards(): lax.all_to_all(partial, 'feat', split_axis=0, concat_axis=0, tiled=True)]
    ppermute x0 -> x3, starting transfers between devices: none -> 6.11 us  [the longest x1 6.03 us: earlier_blocks(): lax.ppermute(travelling, 'comp', [(i, i + cores) for i in range(comp - co...]
    all_to_all x0 -> x1, starting transfers between devices: none -> 5.83 us  [shards(): lax.all_to_all(partial, 'feat', split_axis=0, concat_axis=0, tiled=True)]
    mul x2 -> x3, other arithmetic: 4.47 us -> 2.56 us  [the longest x1 2.23 us: shards(): updated * lax.rsqrt(jnp.sum(sums, axis=0) / features + epsilon)[:, None]]
    dot_general x4 -> x7, matrix products: 11.7 us -> 11.2 us  [the longest x4 5.91 us: shards(): jnp.einsum('ij,jd->id', part, block, precision=high)]
  transfers between devices with their start and end apart: 1 -> 4, of which waited for: 0 -> 1; matrix products, arithmetic and copies ran while one was open for 4% -> 11% of each run, Pallas kernels for 0% -> 0%
where the time goes in v1:
time: 110 us
  blocking collectives  74.6 us (68%)
  starting transfers between devices  11.9 us (11%)
  matrix products  11.2 us (10%)
  waiting for transfers between devices  6.88 us (6%)
  other arithmetic  4.65 us (4%)
    all_gather x1, blocking collectives, shards(): everything = lax.all_gather(summed, ('comp', 'feat'), axis=0, tiled=True)  65.1 us
    all_to_all x1, blocking collectives, shards(): lax.all_to_all(norms, 'feat', split_axis=0, concat_axis=0, tiled=True)  9.46 us
    all_to_all x1, waiting for transfers between devices, shards(): lax.all_to_all(partial, 'feat', split_axis=0, concat_axis=0, tiled=True)  6.87 us
    ppermute x1, starting transfers between devices, earlier_blocks(): lax.ppermute(travelling, 'comp', [(i, i + cores) for i in range(comp - co...  6.03 us
    dot_general x4, matrix products, shards(): jnp.einsum('ij,jd->id', part, block, precision=high)  5.91 us
    all_to_all x1, starting transfers between devices, shards(): lax.all_to_all(partial, 'feat', split_axis=0, concat_axis=0, tiled=True)  5.83 us
    dot_general x1, matrix products, shards(): raw = jnp.einsum('kd,rd->kr', start_vectors, sample, precision=high)  2.62 us
    dot_general x1, matrix products, shards(): jnp.einsum('kr,rd->kd', own_images, sample, precision=high)  2.25 us
  transfers between devices with their start and end apart: 4, of which 1 were waited for; matrix products, arithmetic and copies ran while one was open for 11% of the time, Pallas kernels for 0%

profile of v1, /device:TPU:0, one launch (start us, length us, event | category | flops | bytes accessed | tf_op | source)
XLA Modules:
  0.0 109.6 jit_solution(16329780231581143045)
XLA Ops:
  0.0 0.0 copy-start
  0.0 6.0 %collective-permute-start.1 = (f32[64,3584]{1,0:T(8,128)}, f32[64,3584]{1,0:T(8,128)}, u32[]{:S(2)}, u32[]{:S(2)}) collective-permute-start(f32[64,3584]{1,0:T(8,128)} %param.3), channel_id=1, source_target_pairs={{0,16},{8,24},{1,17},{9,25},{2,18},{10,26},{3,19},{11,27},{4,20},{... | collective-permute-start | bytes 2752520 | tf_op jit(solution)/shard_map/ppermute | solution.py:23
  6.0 0.0 collective-permute-start
  6.0 1.3 %multiply_reduce_fusion.1 = f32[64]{0:T(128)S(1)} fusion(f32[64,3584]{1,0:T(8,128)} %param.3), kind=kLoop, calls=%fused_computation.17 | loop fusion | flops 458688 | bytes 917760 | tf_op jit(solution)/shard_map/reduce_sum | solution.py:45
  7.4 0.1 concatenate.8
  7.5 0.0 copy-done
  7.5 2.6 %fusion.5 = f32[8,8,192]{2,1,0:T(8,128)S(1)} fusion(f32[1,192,3584]{2,1,0:T(8,128)S(1)} %copy-done, f32[64,3584]{1,0:T(8,128)} %param.3), kind=kOutput, calls=%fused_computation.10 | convolution fusion | flops 264241152 | bytes 3719168 | tf_op jit(solution)/shard_map/kd,rd->kr/dot_general | solution.py:44
  10.2 0.7 pad_maximum_fusion
  10.9 5.8 %all-to-all-start = ((f32[8,8,193]{2,1,0:T(8,128)}), f32[8,8,193]{2,1,0:T(8,128)S(1)}, u32[]{:S(2)}, u32[]{:S(2)}) async-start(f32[8,8,193]{2,1,0:T(8,128)} %pad_maximum_fusion), calls=%async_computation | async-start | bytes 131072 | tf_op jit(solution)/shard_map/all_to_all | solution.py:49
  16.7 6.9 %all-to-all-done = f32[8,8,193]{2,1,0:T(8,128)S(1)} async-done(((f32[8,8,193]{2,1,0:T(8,128)}), f32[8,8,193]{2,1,0:T(8,128)S(1)}, u32[]{:S(2)}, u32[]{:S(2)}) %all-to-all-start) | async-done | bytes 49440 | tf_op jit(solution)/shard_map/all_to_all | solution.py:49
  23.6 65.1 %all_gather.3 = f32[256,193]{1,0:T(8,128)S(1)} all-gather(f32[8,193]{1,0:T(8,128)S(1)} %reduce_sum.37), channel_id=1, replica_groups=mesh['comp'=4,'feat'=8] {'comp','feat'}, dimensions={0}, use_global_device_ids=true | all-gather | bytes 203808 | tf_op jit(solution)/shard_map/all_gather | solution.py:51
  88.7 0.2 multiply_reduce_fusion.2
  89.0 0.1 dynamic-slice_reduce_fusion
  89.1 0.0 copy-start.1
  89.1 0.1 slice_multiply_fusion
  89.2 2.3 %fusion.4 = f32[64,3584]{1,0:T(8,128)S(1)} fusion(f32[1,192,3584]{2,1,0:T(8,128)S(1)} %copy-done, f32[64,3584]{1,0:T(8,128)} %param.3, f32[64]{0:T(128)S(1)} %dynamic-slice_reduce_fusion, f32[256,192]{1,0:T(8,128)S(1)} %slice_multiply_fusion, s32[]{:T(128)S(6)} %select_n.46), kind=kOutput, calls=%fused_computation.9 | convolution fusion | flops 264929280 | bytes 4653572 | tf_op jit(solution)/shard_map/kr,rd->kd/dot_general | solution.py:64
  91.4 0.0 collective-permute-done.1
  91.5 0.1 collective-permute-start.2
  91.5 0.4 fusion.8
  91.9 0.0 copy-done.1
  91.9 0.7 fusion.3
  92.6 1.8 %convolution_multiply_fusion.1 = f32[64,3584]{1,0:T(8,128)S(1)} fusion(f32[64,3584]{1,0:T(8,128)} %collective-permute-done.1, f32[64,256]{1,0:T(8,128)S(1)} %fusion.8, s32[]{:T(128)S(6)} %select_n.55, pred[]{:T(512)S(6)} %ge.14), kind=kOutput, calls=%fused_computation.2 | convolution fusion | flops 88313856 | bytes 1867781 | tf_op jit(solution)/shard_map/ij,jd->id/dot_general | solution.py:70
  94.3 0.0 collective-permute-done
  94.4 1.8 %fusion.2 = f32[64,3584]{1,0:T(8,128)S(1)} fusion(f32[64,3584]{1,0:T(8,128)S(1)} %convolution_multiply_fusion.1, f32[64,3584]{1,0:T(8,128)S(1)} %fusion.3, f32[64,3584]{1,0:T(8,128)} %collective-permute-done, f32[64,256]{1,0:T(8,128)S(1)} %fusion.8, s32[]{:T(128)S(6)} %select_n.52, pred[]{:T(512)S(6)} %ge.13), kind=kOutput, calls=%fused_computation.5 | convolution fusion | flops 88772608 | bytes 3702789 | tf_op jit(solution)/shard_map/ij,jd->id/dot_general | solution.py:70
  96.2 0.0 collective-permute-done.2
  96.2 1.7 %multiply_reduce_fusion = (f32[64]{0:T(128)S(1)}, f32[64,3584]{1,0:T(8,128)}) fusion(f32[64,3584]{1,0:T(8,128)S(1)} %fusion.2, f32[64,3584]{1,0:T(8,128)S(1)} %collective-permute-done.2, f32[64,256]{1,0:T(8,128)S(1)} %fusion.8, s32[]{:T(128)S(6)} %select_n.58, pred[]{:T(512)S(6)} %ge.15), kind=kOutput, calls=%fused_computation.16 | convolution fusion | flops 89001920 | bytes 2785541 | tf_op jit(solution)/shard_map/ij,jd->id/dot_general | solution.py:70
  97.9 9.5 %all_to_all.12 = f32[8,1,64]{2,1,0:T(1,128)S(1)} all-to-all(f32[8,1,64]{2,1,0:T(1,128)S(1)} %broadcast_in_dim.20), channel_id=1, replica_groups=mesh['comp'=4,'feat'=8] {'feat'}, dimensions={0} | all-to-all | bytes 4096 | tf_op jit(solution)/shard_map/all_to_all | solution.py:73
  107.4 2.2 %broadcast_multiply_fusion = f32[64,3584]{1,0:T(8,128)} fusion(f32[64,3584]{1,0:T(8,128)} %get-tuple-element.9, f32[64]{0:T(128)S(1)} %add_rsqrt_fusion), kind=kLoop, calls=%fused_computation.18 | loop fusion | flops 229376 | bytes 1835264 | tf_op jit(solution)/shard_map/mul | solution.py:74
  (5 shorter events, 0.0 us)
Async XLA Ops:
  0.0 7.5 %copy-start = (f32[1,192,3584]{2,1,0:T(8,128)S(1)}, f32[1,192,3584]{2,1,0:T(8,128)}, u32[]{:S(2)}) copy-start(f32[1,192,3584]{2,1,0:T(8,128)} %param.2) | copy-start | bytes 8257540
  0.0 91.4 %collective-permute-start.1 = (f32[64,3584]{1,0:T(8,128)}, f32[64,3584]{1,0:T(8,128)}, u32[]{:S(2)}, u32[]{:S(2)}) collective-permute-start(f32[64,3584]{1,0:T(8,128)} %param.3), channel_id=1, source_target_pairs={{0,16},{8,24},{1,17},{9,25},{2,18},{10,26},{3,19},{11,27},{4,20},{... | collective-permute-start | bytes 2752520 | tf_op jit(solution)/shard_map/ppermute | solution.py:23
  6.0 88.3 %collective-permute-start = (f32[64,3584]{1,0:T(8,128)}, f32[64,3584]{1,0:T(8,128)}, u32[]{:S(2)}, u32[]{:S(2)}) collective-permute-start(f32[64,3584]{1,0:T(8,128)} %param.3), channel_id=1, source_target_pairs={{0,8},{8,0},{16,24},{24,16},{1,9},{9,1},{17,25},{25,17},{2,10},{10... | collective-permute-start | bytes 2752520 | tf_op jit(solution)/shard_map/ppermute | solution.py:26
  10.9 12.7 %all-to-all-start = ((f32[8,8,193]{2,1,0:T(8,128)}), f32[8,8,193]{2,1,0:T(8,128)S(1)}, u32[]{:S(2)}, u32[]{:S(2)}) async-start(f32[8,8,193]{2,1,0:T(8,128)} %pad_maximum_fusion), calls=%async_computation | async-start | bytes 131072 | tf_op jit(solution)/shard_map/all_to_all | solution.py:49
  89.1 2.8 %copy-start.1 = (f32[64,3584]{1,0:T(8,128)S(1)}, f32[64,3584]{1,0:T(8,128)}, u32[]{:S(2)}) copy-start(f32[64,3584]{1,0:T(8,128)} %param.3) | copy-start | bytes 2752516
  91.5 4.7 %collective-permute-start.2 = (f32[64,3584]{1,0:T(8,128)}, f32[64,3584]{1,0:T(8,128)S(1)}, u32[]{:S(2)}, u32[]{:S(2)}) collective-permute-start(f32[64,3584]{1,0:T(8,128)} %collective-permute-done.1), channel_id=1, source_target_pairs={{0,8},{8,0},{16,24},{24,16},{1,9},{9,1},{17,25},{25,17},{2,10},{10... | collective-permute-start | bytes 2752520 | tf_op jit(solution)/shard_map/ppermute | solution.py:26

commit v2 on v1

v2 whole, which is shorter than its diff:
```python
import math

import jax
import jax.numpy as jnp
from jax import lax
from jax.sharding import PartitionSpec as P

step_rate = 0.1
epsilon = 1e-06
high = lax.Precision.HIGH


def partner(index, step, size):
    if size & (size - 1) == 0:
        return index ^ step
    return (index + step) % size


def source(index, step, size):
    if size & (size - 1) == 0:
        return index ^ step
    return (index - step) % size


def swap_all(pieces, axis):
    size = lax.axis_size(axis)
    return [pieces[0]] + [
        lax.ppermute(pieces[step], axis, [(i, partner(i, step, size)) for i in range(size)]) for step in range(1, size)
    ]


def earlier_blocks(own, comp):
    cores = 2 if comp % 2 == 0 else 1
    chips = comp // cores
    group = lax.axis_index("comp")
    blocks = [(own, group)]
    if cores == 2:
        swap = [(i, i ^ 1) for i in range(comp)]
    travelling = own
    for step in range(chips):
        if step > 0:
            travelling = lax.ppermute(travelling, "comp", [(i, i + cores) for i in range(comp - cores)])
            blocks.append((travelling, group - step * cores))
        if cores == 2:
            other = lax.ppermute(travelling, "comp", swap)
            blocks.append((other, (group ^ 1) - step * cores))
    return blocks


def shards(samples, start_vectors):
    comp = lax.axis_size("comp")
    feat = lax.axis_size("feat")
    per_group = start_vectors.shape[0]
    sample = samples[0]
    rows = sample.shape[0]
    features = sample.shape[1] * feat
    root_width = math.sqrt(features)
    group = lax.axis_index("comp")
    place = lax.axis_index("feat")

    blocks = earlier_blocks(start_vectors, comp)

    raw = jnp.einsum("kd,rd->kr", start_vectors, sample, precision=high)
    squares = jnp.sum(start_vectors * start_vectors, axis=1, keepdims=True)
    partial = jnp.concatenate([raw, squares], axis=1)
    share = -(-per_group // feat)
    partial = jnp.pad(partial, ((0, share * feat - per_group), (0, 0)))
    pieces = [
        lax.dynamic_slice_in_dim(partial, partner(place, step, feat) * share, share, 0) for step in range(feat)
    ]
    summed = sum(swap_all(pieces, "feat"))
    gathered = jnp.zeros((share * feat, rows + 1), jnp.float32)
    for step, piece in enumerate(swap_all([summed] * feat, "feat")):
        gathered = lax.dynamic_update_slice_in_dim(gathered, piece, source(place, step, feat) * share, 0)
    gathered = gathered[:per_group]

    def scaled(block):
        scale = lax.rsqrt(block[:, rows:] / features + epsilon)
        return block[:, :rows] * (scale / root_width), scale

    own_images, own_scale = scaled(gathered)
    updated = own_scale * start_vectors + (step_rate * root_width / rows) * jnp.einsum(
        "kr,rd->kd", own_images, sample, precision=high
    )
    own_rows = jnp.arange(per_group, dtype=jnp.int32)[:, None]
    other_rows = jnp.arange(per_group, dtype=jnp.int32)[None, :]
    for (projected, owner), (block, _) in zip(earlier_blocks(gathered, comp), blocks):
        images, scale = scaled(projected)
        intersection = jnp.einsum("ir,jr->ij", own_images, images, precision=lax.Precision.HIGHEST) / rows
        earlier = (owner >= 0) & (owner * per_group + other_rows < group * per_group + own_rows)
        coupling = jnp.where(earlier, intersection * scale[:, 0][None, :], 0.0)
        updated = updated - step_rate * jnp.einsum("ij,jd->id", coupling, block, precision=high)

    sums = swap_all([jnp.sum(updated * updated, axis=1)] * feat, "feat")
    return updated * lax.rsqrt(sum(sums) / features + epsilon)[:, None]


def solution(mesh):
    in_specs = (P(None, None, "feat"), P("comp", "feat"))
    out_specs = P("comp", "feat")
    return jax.shard_map(shards, mesh=mesh, in_specs=in_specs, out_specs=out_specs, check_vma=False)
```

time: 110 us -> 77.3 us (0.70)
  blocking collectives: 74.6 us -> 0 us
  starting transfers between devices: 11.9 us -> 40 us
  waiting for transfers between devices: 6.88 us -> 15.4 us
  local copies, waits for them, and re-layouts: 0.26 us -> 7.48 us
  other arithmetic: 4.65 us -> 2.86 us
    all_gather x1 -> x0, blocking collectives: 65.1 us -> none  [shards(): everything = lax.all_gather(summed, ('comp', 'feat'), axis=0, tiled=True)]
    ppermute x0 -> x21, starting transfers between devices: none -> 33 us  [swap_all(): lax.ppermute(pieces[step], axis, [(i, partner(i, step, size)) for i in ra...]
    all_to_all x1 -> x0, blocking collectives: 9.46 us -> none  [shards(): lax.all_to_all(norms, 'feat', split_axis=0, concat_axis=0, tiled=True)]
    ppermute x0 -> x21, waiting for transfers between devices: none -> 9.31 us  [swap_all(): lax.ppermute(pieces[step], axis, [(i, partner(i, step, size)) for i in ra...]
    all_to_all x1 -> x0, waiting for transfers between devices: 6.87 us -> none  [shards(): lax.all_to_all(partial, 'feat', split_axis=0, concat_axis=0, tiled=True)]
    ppermute x1 -> x2, waiting for transfers between devices: 0.01 us -> 6.09 us  [earlier_blocks(): lax.ppermute(travelling, 'comp', [(i, i + cores) for i in range(comp - co...]
    dynamic_update_slice x0 -> x8, local copies, waits for them, and re-layouts: none -> 6.06 us  [shards(): lax.dynamic_update_slice_in_dim(gathered, piece, source(place, step, feat...]
    all_to_all x1 -> x0, starting transfers between devices: 5.83 us -> none  [shards(): lax.all_to_all(partial, 'feat', split_axis=0, concat_axis=0, tiled=True)]
  transfers between devices with their start and end apart: 4 -> 27, of which waited for: 1 -> 7; matrix products, arithmetic and copies ran while one was open for 11% -> 19% of each run, Pallas kernels for 0% -> 0%
where the time goes in v2:
time: 77.3 us; the launch traced here: 77 us
  starting transfers between devices  40 us (52%)
  waiting for transfers between devices  15.4 us (20%)
  matrix products  10.9 us (14%)
  local copies, waits for them, and re-layouts  7.48 us (10%)
  other arithmetic  2.86 us (4%)
    ppermute x21, starting transfers between devices, swap_all(): lax.ppermute(pieces[step], axis, [(i, partner(i, step, size)) for i in ra...  33 us
    ppermute x21, waiting for transfers between devices, swap_all(): lax.ppermute(pieces[step], axis, [(i, partner(i, step, size)) for i in ra...  9.31 us
    ppermute x2, waiting for transfers between devices, earlier_blocks(): lax.ppermute(travelling, 'comp', [(i, i + cores) for i in range(comp - co...  6.09 us
    dynamic_update_slice x8, local copies, waits for them, and re-layouts, shards(): lax.dynamic_update_slice_in_dim(gathered, piece, source(place, step, feat...  6.06 us
    ppermute x2, starting transfers between devices, earlier_blocks(): lax.ppermute(travelling, 'comp', [(i, i + cores) for i in range(comp - co...  5.77 us
    dot_general x4, matrix products, shards(): jnp.einsum('ij,jd->id', coupling, block, precision=high)  4.63 us
    dot_general x1, matrix products, shards(): raw = jnp.einsum('kd,rd->kr', start_vectors, sample, precision=high)  2.62 us
    dot_general x1, matrix products, shards(): jnp.einsum('kr,rd->kd', own_images, sample, precision=high)  2.23 us
  transfers between devices with their start and end apart: 27, of which 7 were waited for; matrix products, arithmetic and copies ran while one was open for 19% of the time, Pallas kernels for 0%

profile of v2, /device:TPU:0, one launch (start us, length us, event | category | flops | bytes accessed | tf_op | source)
XLA Modules:
  0.0 77.0 jit_solution(10926509936303478809)
XLA Ops:
  0.0 1.5 %multiply_reduce_fusion.1 = f32[64]{0:T(128)S(1)} fusion(f32[64,3584]{1,0:T(8,128)} %param.3), kind=kLoop, calls=%fused_computation.22 | loop fusion | flops 458688 | bytes 917760 | tf_op jit(solution)/shard_map/reduce_sum | solution.py:64
  1.6 0.5 copy-done
  2.1 2.6 %fusion.6 = f32[64,192]{1,0:T(8,128)S(1)} fusion(f32[64,3584]{1,0:T(8,128)} %param.3, f32[1,192,3584]{2,1,0:T(8,128)S(1)} %copy-done), kind=kOutput, calls=%fused_computation.11 | convolution fusion | flops 264241152 | bytes 3719168 | tf_op jit(solution)/shard_map/kd,rd->kr/dot_general | solution.py:63
  4.8 6.0 %collective-permute-start.6 = (f32[8,193]{1,0:T(8,128)S(1)}, f32[8,193]{1,0:T(8,128)S(1)}, u32[]{:S(2)}, u32[]{:S(2)}) collective-permute-start(f32[8,193]{1,0:T(8,128)S(1)} %fusion.20), channel_id=1, source_target_pairs={{0,7},{1,6},{2,5},{3,4},{4,3},{5,2},{6,1},{7,0},{8,15},{9,14},{10,... | collective-permute-start | bytes 18536 | tf_op jit(solution)/shard_map/ppermute | solution.py:28
  10.9 0.5 collective-permute-start
  11.4 3.0 %collective-permute-start.2 = (f32[8,193]{1,0:T(8,128)S(1)}, f32[8,193]{1,0:T(8,128)S(1)}, u32[]{:S(2)}, u32[]{:S(2)}) collective-permute-start(f32[8,193]{1,0:T(8,128)S(1)} %get-tuple-element.15), channel_id=1, source_target_pairs={{0,3},{1,2},{2,1},{3,0},{4,7},{5,6},{6,5},{7,4},{8,11},{9,10},{10,... | collective-permute-start | bytes 18536 | tf_op jit(solution)/shard_map/ppermute | solution.py:28
  14.4 2.9 %collective-permute-start.4 = (f32[8,193]{1,0:T(8,128)S(1)}, f32[8,193]{1,0:T(8,128)S(1)}, u32[]{:S(2)}, u32[]{:S(2)}) collective-permute-start(f32[8,193]{1,0:T(8,128)S(1)} %get-tuple-element.17), channel_id=1, source_target_pairs={{0,5},{1,4},{2,7},{3,6},{4,1},{5,0},{6,3},{7,2},{8,13},{9,12},{10,... | collective-permute-start | bytes 18536 | tf_op jit(solution)/shard_map/ppermute | solution.py:28
  17.3 0.1 collective-permute-start.5
  17.4 1.6 %collective-permute-done.3 = f32[8,193]{1,0:T(8,128)S(1)} collective-permute-done((f32[8,193]{1,0:T(8,128)S(1)}, f32[8,193]{1,0:T(8,128)S(1)}, u32[]{:S(2)}, u32[]{:S(2)}) %collective-permute-start.3) | collective-permute-done | bytes 6208 | tf_op jit(solution)/shard_map/ppermute | solution.py:28
  18.9 0.9 %collective-permute-done.4 = f32[8,193]{1,0:T(8,128)S(1)} collective-permute-done((f32[8,193]{1,0:T(8,128)S(1)}, f32[8,193]{1,0:T(8,128)S(1)}, u32[]{:S(2)}, u32[]{:S(2)}) %collective-permute-start.4) | collective-permute-done | bytes 6208 | tf_op jit(solution)/shard_map/ppermute | solution.py:28
  19.8 2.9 %collective-permute-done.5 = f32[8,193]{1,0:T(8,128)S(1)} collective-permute-done((f32[8,193]{1,0:T(8,128)S(1)}, f32[8,193]{1,0:T(8,128)S(1)}, u32[]{:S(2)}, u32[]{:S(2)}) %collective-permute-start.5) | collective-permute-done | bytes 6208 | tf_op jit(solution)/shard_map/ppermute | solution.py:28
  22.8 1.6 %collective-permute-start.7 = (f32[8,193]{1,0:T(8,128)S(1)}, f32[8,193]{1,0:T(8,128)S(1)}, u32[]{:S(2)}, u32[]{:S(2)}) collective-permute-start(f32[8,193]{1,0:T(8,128)S(1)} %fusion.28), channel_id=1, source_target_pairs={{0,1},{1,0},{2,3},{3,2},{4,5},{5,4},{6,7},{7,6},{8,9},{9,8},{10,11... | collective-permute-start | bytes 18536 | tf_op jit(solution)/shard_map/ppermute | solution.py:28
  24.4 1.4 %collective-permute-start.13 = (f32[8,193]{1,0:T(8,128)S(1)}, f32[8,193]{1,0:T(8,128)S(1)}, u32[]{:S(2)}, u32[]{:S(2)}) collective-permute-start(f32[8,193]{1,0:T(8,128)S(1)} %fusion.28), channel_id=1, source_target_pairs={{0,7},{1,6},{2,5},{3,4},{4,3},{5,2},{6,1},{7,0},{8,15},{9,14},{10,... | collective-permute-start | bytes 18536 | tf_op jit(solution)/shard_map/ppermute | solution.py:28
  25.8 2.4 %collective-permute-start.12 = (f32[8,193]{1,0:T(8,128)S(1)}, f32[8,193]{1,0:T(8,128)S(1)}, u32[]{:S(2)}, u32[]{:S(2)}) collective-permute-start(f32[8,193]{1,0:T(8,128)S(1)} %fusion.28), channel_id=1, source_target_pairs={{0,6},{1,7},{2,4},{3,5},{4,2},{5,3},{6,0},{7,1},{8,14},{9,15},{10,... | collective-permute-start | bytes 18536 | tf_op jit(solution)/shard_map/ppermute | solution.py:28
  28.2 0.5 collective-permute-start.11
  28.7 3.3 %collective-permute-start.10 = (f32[8,193]{1,0:T(8,128)S(1)}, f32[8,193]{1,0:T(8,128)S(1)}, u32[]{:S(2)}, u32[]{:S(2)}) collective-permute-start(f32[8,193]{1,0:T(8,128)S(1)} %fusion.28), channel_id=1, source_target_pairs={{0,4},{1,5},{2,6},{3,7},{4,0},{5,1},{6,2},{7,3},{8,12},{9,13},{10,... | collective-permute-start | bytes 18536 | tf_op jit(solution)/shard_map/ppermute | solution.py:28
  32.3 0.6 dynamic_update_slice.24
  32.9 0.1 copy.5
  33.0 0.8 %dynamic_update_slice.25 = f32[64,193]{0,1:T(8,128)S(1)} dynamic-update-slice(f32[64,193]{0,1:T(8,128)S(1)} %dynamic_update_slice.24, f32[8,193]{0,1:T(8,128)S(1)} %copy.5, s32[]{:T(128)S(6)} %select_n.46, s32[]{:T(128)} %constant.18.clone.1) | dynamic-update-slice | bytes 12356 | tf_op jit(solution)/shard_map/dynamic_update_slice | solution.py:74
  33.9 0.8 %dynamic_update_slice.26 = f32[64,193]{0,1:T(8,128)S(1)} dynamic-update-slice(f32[64,193]{0,1:T(8,128)S(1)} %dynamic_update_slice.25, f32[8,193]{0,1:T(8,128)S(1)} %copy.6, s32[]{:T(128)S(6)} %select_n.47, s32[]{:T(128)} %constant.18.clone.1) | dynamic-update-slice | bytes 12356 | tf_op jit(solution)/shard_map/dynamic_update_slice | solution.py:74
  34.7 1.9 %collective-permute-done.9 = f32[8,193]{1,0:T(8,128)S(1)} collective-permute-done((f32[8,193]{1,0:T(8,128)S(1)}, f32[8,193]{1,0:T(8,128)S(1)}, u32[]{:S(2)}, u32[]{:S(2)}) %collective-permute-start.9) | collective-permute-done | bytes 6208 | tf_op jit(solution)/shard_map/ppermute | solution.py:28
  36.6 4.3 %collective-permute-start.17 = (f32[64,3584]{1,0:T(8,128)}, f32[64,3584]{1,0:T(8,128)}, u32[]{:S(2)}, u32[]{:S(2)}) collective-permute-start(f32[64,3584]{1,0:T(8,128)} %param.3), channel_id=1, source_target_pairs={{0,16},{8,24},{1,17},{9,25},{2,18},{10,26},{3,19},{11,27},{4,20},{... | collective-permute-start | bytes 2752520 | tf_op jit(solution)/shard_map/ppermute | solution.py:42
  41.1 0.8 %dynamic_update_slice.27 = f32[64,193]{0,1:T(8,128)S(1)} dynamic-update-slice(f32[64,193]{0,1:T(8,128)S(1)} %dynamic_update_slice.26, f32[8,193]{0,1:T(8,128)S(1)} %copy.7, s32[]{:T(128)S(6)} %select_n.48, s32[]{:T(128)} %constant.18.clone.1) | dynamic-update-slice | bytes 12356 | tf_op jit(solution)/shard_map/dynamic_update_slice | solution.py:74
  42.1 0.8 %dynamic_update_slice.28 = f32[64,193]{0,1:T(8,128)S(1)} dynamic-update-slice(f32[64,193]{0,1:T(8,128)S(1)} %dynamic_update_slice.27, f32[8,193]{0,1:T(8,128)S(1)} %copy.8, s32[]{:T(128)S(6)} %select_n.49, s32[]{:T(128)} %constant.18.clone.1) | dynamic-update-slice | bytes 12356 | tf_op jit(solution)/shard_map/dynamic_update_slice | solution.py:74
  43.0 0.8 %dynamic_update_slice.29 = f32[64,193]{0,1:T(8,128)S(1)} dynamic-update-slice(f32[64,193]{0,1:T(8,128)S(1)} %dynamic_update_slice.28, f32[8,193]{0,1:T(8,128)S(1)} %copy.9, s32[]{:T(128)S(6)} %select_n.50, s32[]{:T(128)} %constant.18.clone.1) | dynamic-update-slice | bytes 12356 | tf_op jit(solution)/shard_map/dynamic_update_slice | solution.py:74
  43.9 0.8 %dynamic_update_slice.30 = f32[64,193]{0,1:T(8,128)S(1)} dynamic-update-slice(f32[64,193]{0,1:T(8,128)S(1)} %dynamic_update_slice.29, f32[8,193]{0,1:T(8,128)S(1)} %copy.10, s32[]{:T(128)S(6)} %select_n.51, s32[]{:T(128)} %constant.18.clone.1) | dynamic-update-slice | bytes 12356 | tf_op jit(solution)/shard_map/dynamic_update_slice | solution.py:74
  44.8 0.8 %dynamic_update_slice.31 = f32[64,193]{0,1:T(8,128)S(1)} dynamic-update-slice(f32[64,193]{0,1:T(8,128)S(1)} %dynamic_update_slice.30, f32[8,193]{0,1:T(8,128)S(1)} %copy.11, s32[]{:T(128)S(6)} %select_n.52, s32[]{:T(128)} %constant.18.clone.1) | dynamic-update-slice | bytes 12356 | tf_op jit(solution)/shard_map/dynamic_update_slice | solution.py:74
  45.6 1.4 %collective-permute-start.16 = (f32[64,193]{0,1:T(8,128)S(1)}, f32[64,193]{0,1:T(8,128)S(1)}, u32[]{:S(2)}, u32[]{:S(2)}) collective-permute-start(f32[64,193]{0,1:T(8,128)S(1)} %dynamic_update_slice.31), channel_id=1, source_target_pairs={{0,16},{8,24},{1,17},{9,25},{2,18},{10,26},{3,19},{11,27},{4,20},{... | collective-permute-start | bytes 148232 | tf_op jit(solution)/shard_map/ppermute | solution.py:42
  47.1 0.6 collective-permute-start.14
  47.6 2.2 %fusion.4 = f32[64,3584]{1,0:T(8,128)S(1)} fusion(f32[1,192,3584]{2,1,0:T(8,128)S(1)} %copy-done, f32[64,3584]{1,0:T(8,128)} %param.3, f32[64]{0:T(128)S(1)} %bitcast.32, f32[64,193]{0,1:T(8,128)S(1)} %dynamic_update_slice.31, f32[64]{0:T(128)S(1)} %multiply_bitcast_fusion.6), kind=kOutput, calls=%fused_computation.9 | convolution fusion | flops 264941568 | bytes 4686848 | tf_op jit(solution)/shard_map/kr,rd->kd/dot_general | solution.py:82
  49.9 0.4 fusion.11
  50.2 0.6 fusion.3
  50.8 6.1 %collective-permute-done.16 = f32[64,193]{0,1:T(8,128)S(1)} collective-permute-done((f32[64,193]{0,1:T(8,128)S(1)}, f32[64,193]{0,1:T(8,128)S(1)}, u32[]{:S(2)}, u32[]{:S(2)}) %collective-permute-start.16) | collective-permute-done | bytes 49440 | tf_op jit(solution)/shard_map/ppermute | solution.py:42
  56.9 0.4 fusion.9
  57.3 0.4 fusion.10
  57.6 0.6 collective-permute-start.19
  58.2 0.4 fusion.8
  58.6 1.7 %convolution_multiply_fusion.1 = f32[64,3584]{1,0:T(8,128)S(1)} fusion(f32[64,64]{1,0:T(8,128)S(1)} %fusion.9, f32[64,3584]{1,0:T(8,128)} %collective-permute-done.17), kind=kOutput, calls=%fused_computation.2 | convolution fusion | flops 88309760 | bytes 1851392 | tf_op jit(solution)/shard_map/ij,jd->id/dot_general | solution.py:92
  60.3 1.7 %fusion.2 = f32[64,3584]{1,0:T(8,128)S(1)} fusion(f32[64,3584]{1,0:T(8,128)S(1)} %convolution_multiply_fusion.1, f32[64,3584]{1,0:T(8,128)S(1)} %fusion.3, f32[64,64]{1,0:T(8,128)S(1)} %fusion.10, f32[64,3584]{1,0:T(8,128)} %collective-permute-done.15), kind=kOutput, calls=%fused_computation.5 | convolution fusion | flops 88768512 | bytes 3686400 | tf_op jit(solution)/shard_map/ij,jd->id/dot_general | solution.py:92
  62.0 0.7 multiply_reduce_fusion
  62.7 1.6 %collective-permute-start.26 = (f32[64]{0:T(128)S(1)}, f32[64]{0:T(128)S(1)}, u32[]{:S(2)}, u32[]{:S(2)}) collective-permute-start(f32[64]{0:T(128)S(1)} %get-tuple-element.19), channel_id=1, source_target_pairs={{0,7},{1,6},{2,5},{3,4},{4,3},{5,2},{6,1},{7,0},{8,15},{9,14},{10,... | collective-permute-start | bytes 776 | tf_op jit(solution)/shard_map/ppermute | solution.py:28
  64.3 2.3 %collective-permute-start.25 = (f32[64]{0:T(128)S(1)}, f32[64]{0:T(128)S(1)}, u32[]{:S(2)}, u32[]{:S(2)}) collective-permute-start(f32[64]{0:T(128)S(1)} %get-tuple-element.19), channel_id=1, source_target_pairs={{0,6},{1,7},{2,4},{3,5},{4,2},{5,3},{6,0},{7,1},{8,14},{9,15},{10,... | collective-permute-start | bytes 776 | tf_op jit(solution)/shard_map/ppermute | solution.py:28
  66.5 3.9 %collective-permute-start.23 = (f32[64]{0:T(128)S(1)}, f32[64]{0:T(128)S(1)}, u32[]{:S(2)}, u32[]{:S(2)}) collective-permute-start(f32[64]{0:T(128)S(1)} %get-tuple-element.19), channel_id=1, source_target_pairs={{0,4},{1,5},{2,6},{3,7},{4,0},{5,1},{6,2},{7,3},{8,12},{9,13},{10,... | collective-permute-start | bytes 776 | tf_op jit(solution)/shard_map/ppermute | solution.py:28
  70.4 2.0 %collective-permute-start.21 = (f32[64]{0:T(128)S(1)}, f32[64]{0:T(128)S(1)}, u32[]{:S(2)}, u32[]{:S(2)}) collective-permute-start(f32[64]{0:T(128)S(1)} %get-tuple-element.19), channel_id=1, source_target_pairs={{0,2},{1,3},{2,0},{3,1},{4,6},{5,7},{6,4},{7,5},{8,10},{9,11},{10,... | collective-permute-start | bytes 776 | tf_op jit(solution)/shard_map/ppermute | solution.py:28
  72.4 1.5 %collective-permute-start.20 = (f32[64]{0:T(128)S(1)}, f32[64]{0:T(128)S(1)}, u32[]{:S(2)}, u32[]{:S(2)}) collective-permute-start(f32[64]{0:T(128)S(1)} %get-tuple-element.19), channel_id=1, source_target_pairs={{0,1},{1,0},{2,3},{3,2},{4,5},{5,4},{6,7},{7,6},{8,9},{9,8},{10,11... | collective-permute-start | bytes 776 | tf_op jit(solution)/shard_map/ppermute | solution.py:28
  73.9 0.9 %collective-permute-done.22 = f32[64]{0:T(128)S(1)} collective-permute-done((f32[64]{0:T(128)S(1)}, f32[64]{0:T(128)S(1)}, u32[]{:S(2)}, u32[]{:S(2)}) %collective-permute-start.22) | collective-permute-done | bytes 288 | tf_op jit(solution)/shard_map/ppermute | solution.py:28
  74.8 1.1 %collective-permute-done.20 = f32[64]{0:T(128)S(1)} collective-permute-done((f32[64]{0:T(128)S(1)}, f32[64]{0:T(128)S(1)}, u32[]{:S(2)}, u32[]{:S(2)}) %collective-permute-start.20) | collective-permute-done | bytes 288 | tf_op jit(solution)/shard_map/ppermute | solution.py:28
  75.9 1.1 %broadcast_multiply_fusion = f32[64,3584]{1,0:T(8,128)} fusion(f32[64,3584]{1,0:T(8,128)S(1)} %get-tuple-element.20, f32[64]{0:T(128)S(1)} %add_rsqrt_fusion), kind=kLoop, calls=%fused_computation.23 | loop fusion | flops 229376 | bytes 1835264 | tf_op jit(solution)/shard_map/mul | solution.py:95
  (52 shorter events, 1.4 us)
Async XLA Ops:
  0.0 2.1 %copy-start = (f32[1,192,3584]{2,1,0:T(8,128)S(1)}, f32[1,192,3584]{2,1,0:T(8,128)}, u32[]{:S(2)}) copy-start(f32[1,192,3584]{2,1,0:T(8,128)} %param.2) | copy-start | bytes 8257540
  4.8 9.6 %collective-permute-start.6 = (f32[8,193]{1,0:T(8,128)S(1)}, f32[8,193]{1,0:T(8,128)S(1)}, u32[]{:S(2)}, u32[]{:S(2)}) collective-permute-start(f32[8,193]{1,0:T(8,128)S(1)} %fusion.20), channel_id=1, source_target_pairs={{0,7},{1,6},{2,5},{3,4},{4,3},{5,2},{6,1},{7,0},{8,15},{9,14},{10,... | collective-permute-start | bytes 18536 | tf_op jit(solution)/shard_map/ppermute | solution.py:28
  10.9 6.4 %collective-permute-start = (f32[8,193]{1,0:T(8,128)S(1)}, f32[8,193]{1,0:T(8,128)S(1)}, u32[]{:S(2)}, u32[]{:S(2)}) collective-permute-start(f32[8,193]{1,0:T(8,128)S(1)} %get-tuple-element.13), channel_id=1, source_target_pairs={{0,1},{1,0},{2,3},{3,2},{4,5},{5,4},{6,7},{7,6},{8,9},{9,8},{10,11... | collective-permute-start | bytes 18536 | tf_op jit(solution)/shard_map/ppermute | solution.py:28
  11.4 6.0 %collective-permute-start.1 = (f32[8,193]{1,0:T(8,128)S(1)}, f32[8,193]{1,0:T(8,128)S(1)}, u32[]{:S(2)}, u32[]{:S(2)}) collective-permute-start(f32[8,193]{1,0:T(8,128)S(1)} %get-tuple-element.14), channel_id=1, source_target_pairs={{0,2},{1,3},{2,0},{3,1},{4,6},{5,7},{6,4},{7,5},{8,10},{9,11},{10,... | collective-permute-start | bytes 18536 | tf_op jit(solution)/shard_map/ppermute | solution.py:28
  11.4 6.0 %collective-permute-start.2 = (f32[8,193]{1,0:T(8,128)S(1)}, f32[8,193]{1,0:T(8,128)S(1)}, u32[]{:S(2)}, u32[]{:S(2)}) collective-permute-start(f32[8,193]{1,0:T(8,128)S(1)} %get-tuple-element.15), channel_id=1, source_target_pairs={{0,3},{1,2},{2,1},{3,0},{4,7},{5,6},{6,5},{7,4},{8,11},{9,10},{10,... | collective-permute-start | bytes 18536 | tf_op jit(solution)/shard_map/ppermute | solution.py:28
  14.4 4.6 %collective-permute-start.3 = (f32[8,193]{1,0:T(8,128)S(1)}, f32[8,193]{1,0:T(8,128)S(1)}, u32[]{:S(2)}, u32[]{:S(2)}) collective-permute-start(f32[8,193]{1,0:T(8,128)S(1)} %get-tuple-element.16), channel_id=1, source_target_pairs={{0,4},{1,5},{2,6},{3,7},{4,0},{5,1},{6,2},{7,3},{8,12},{9,13},{10,... | collective-permute-start | bytes 18536 | tf_op jit(solution)/shard_map/ppermute | solution.py:28
  14.4 5.5 %collective-permute-start.4 = (f32[8,193]{1,0:T(8,128)S(1)}, f32[8,193]{1,0:T(8,128)S(1)}, u32[]{:S(2)}, u32[]{:S(2)}) collective-permute-start(f32[8,193]{1,0:T(8,128)S(1)} %get-tuple-element.17), channel_id=1, source_target_pairs={{0,5},{1,4},{2,7},{3,6},{4,1},{5,0},{6,3},{7,2},{8,13},{9,12},{10,... | collective-permute-start | bytes 18536 | tf_op jit(solution)/shard_map/ppermute | solution.py:28
  17.3 5.5 %collective-permute-start.5 = (f32[8,193]{1,0:T(8,128)S(1)}, f32[8,193]{1,0:T(8,128)S(1)}, u32[]{:S(2)}, u32[]{:S(2)}) collective-permute-start(f32[8,193]{1,0:T(8,128)S(1)} %get-tuple-element.18), channel_id=1, source_target_pairs={{0,6},{1,7},{2,4},{3,5},{4,2},{5,3},{6,0},{7,1},{8,14},{9,15},{10,... | collective-permute-start | bytes 18536 | tf_op jit(solution)/shard_map/ppermute | solution.py:28
  22.8 5.9 %collective-permute-start.8 = (f32[8,193]{1,0:T(8,128)S(1)}, f32[8,193]{1,0:T(8,128)S(1)}, u32[]{:S(2)}, u32[]{:S(2)}) collective-permute-start(f32[8,193]{1,0:T(8,128)S(1)} %fusion.28), channel_id=1, source_target_pairs={{0,2},{1,3},{2,0},{3,1},{4,6},{5,7},{6,4},{7,5},{8,10},{9,11},{10,... | collective-permute-start | bytes 18536 | tf_op jit(solution)/shard_map/ppermute | solution.py:28
  22.8 9.2 %collective-permute-start.7 = (f32[8,193]{1,0:T(8,128)S(1)}, f32[8,193]{1,0:T(8,128)S(1)}, u32[]{:S(2)}, u32[]{:S(2)}) collective-permute-start(f32[8,193]{1,0:T(8,128)S(1)} %fusion.28), channel_id=1, source_target_pairs={{0,1},{1,0},{2,3},{3,2},{4,5},{5,4},{6,7},{7,6},{8,9},{9,8},{10,11... | collective-permute-start | bytes 18536 | tf_op jit(solution)/shard_map/ppermute | solution.py:28
  24.4 20.3 %collective-permute-start.13 = (f32[8,193]{1,0:T(8,128)S(1)}, f32[8,193]{1,0:T(8,128)S(1)}, u32[]{:S(2)}, u32[]{:S(2)}) collective-permute-start(f32[8,193]{1,0:T(8,128)S(1)} %fusion.28), channel_id=1, source_target_pairs={{0,7},{1,6},{2,5},{3,4},{4,3},{5,2},{6,1},{7,0},{8,15},{9,14},{10,... | collective-permute-start | bytes 18536 | tf_op jit(solution)/shard_map/ppermute | solution.py:28
  25.8 18.0 %collective-permute-start.12 = (f32[8,193]{1,0:T(8,128)S(1)}, f32[8,193]{1,0:T(8,128)S(1)}, u32[]{:S(2)}, u32[]{:S(2)}) collective-permute-start(f32[8,193]{1,0:T(8,128)S(1)} %fusion.28), channel_id=1, source_target_pairs={{0,6},{1,7},{2,4},{3,5},{4,2},{5,3},{6,0},{7,1},{8,14},{9,15},{10,... | collective-permute-start | bytes 18536 | tf_op jit(solution)/shard_map/ppermute | solution.py:28
  28.2 14.7 %collective-permute-start.11 = (f32[8,193]{1,0:T(8,128)S(1)}, f32[8,193]{1,0:T(8,128)S(1)}, u32[]{:S(2)}, u32[]{:S(2)}) collective-permute-start(f32[8,193]{1,0:T(8,128)S(1)} %fusion.28), channel_id=1, source_target_pairs={{0,5},{1,4},{2,7},{3,6},{4,1},{5,0},{6,3},{7,2},{8,13},{9,12},{10,... | collective-permute-start | bytes 18536 | tf_op jit(solution)/shard_map/ppermute | solution.py:28
  28.7 13.1 %collective-permute-start.10 = (f32[8,193]{1,0:T(8,128)S(1)}, f32[8,193]{1,0:T(8,128)S(1)}, u32[]{:S(2)}, u32[]{:S(2)}) collective-permute-start(f32[8,193]{1,0:T(8,128)S(1)} %fusion.28), channel_id=1, source_target_pairs={{0,4},{1,5},{2,6},{3,7},{4,0},{5,1},{6,2},{7,3},{8,12},{9,13},{10,... | collective-permute-start | bytes 18536 | tf_op jit(solution)/shard_map/ppermute | solution.py:28
  32.0 4.6 %collective-permute-start.9 = (f32[8,193]{1,0:T(8,128)S(1)}, f32[8,193]{1,0:T(8,128)S(1)}, u32[]{:S(2)}, u32[]{:S(2)}) collective-permute-start(f32[8,193]{1,0:T(8,128)S(1)} %fusion.28), channel_id=1, source_target_pairs={{0,3},{1,2},{2,1},{3,0},{4,7},{5,6},{6,5},{7,4},{8,11},{9,10},{10,... | collective-permute-start | bytes 18536 | tf_op jit(solution)/shard_map/ppermute | solution.py:28
  36.6 21.0 %collective-permute-start.17 = (f32[64,3584]{1,0:T(8,128)}, f32[64,3584]{1,0:T(8,128)}, u32[]{:S(2)}, u32[]{:S(2)}) collective-permute-start(f32[64,3584]{1,0:T(8,128)} %param.3), channel_id=1, source_target_pairs={{0,16},{8,24},{1,17},{9,25},{2,18},{10,26},{3,19},{11,27},{4,20},{... | collective-permute-start | bytes 2752520 | tf_op jit(solution)/shard_map/ppermute | solution.py:42
  41.9 18.4 %collective-permute-start.15 = (f32[64,3584]{1,0:T(8,128)}, f32[64,3584]{1,0:T(8,128)}, u32[]{:S(2)}, u32[]{:S(2)}) collective-permute-start(f32[64,3584]{1,0:T(8,128)} %param.3), channel_id=1, source_target_pairs={{0,8},{8,0},{16,24},{24,16},{1,9},{9,1},{17,25},{25,17},{2,10},{10... | collective-permute-start | bytes 2752520 | tf_op jit(solution)/shard_map/ppermute | solution.py:45
  45.6 4.6 %copy-start.1 = (f32[64,3584]{1,0:T(8,128)S(1)}, f32[64,3584]{1,0:T(8,128)}, u32[]{:S(2)}) copy-start(f32[64,3584]{1,0:T(8,128)} %param.3) | copy-start | bytes 2752516
  45.6 11.3 %collective-permute-start.16 = (f32[64,193]{0,1:T(8,128)S(1)}, f32[64,193]{0,1:T(8,128)S(1)}, u32[]{:S(2)}, u32[]{:S(2)}) collective-permute-start(f32[64,193]{0,1:T(8,128)S(1)} %dynamic_update_slice.31), channel_id=1, source_target_pairs={{0,16},{8,24},{1,17},{9,25},{2,18},{10,26},{3,19},{11,27},{4,20},{... | collective-permute-start | bytes 148232 | tf_op jit(solution)/shard_map/ppermute | solution.py:42
  47.1 9.8 %collective-permute-start.14 = (f32[64,193]{0,1:T(8,128)S(1)}, f32[64,193]{0,1:T(8,128)S(1)}, u32[]{:S(2)}, u32[]{:S(2)}) collective-permute-start(f32[64,193]{0,1:T(8,128)S(1)} %dynamic_update_slice.31), channel_id=1, source_target_pairs={{0,8},{8,0},{16,24},{24,16},{1,9},{9,1},{17,25},{25,17},{2,10},{10... | collective-permute-start | bytes 148232 | tf_op jit(solution)/shard_map/ppermute | solution.py:45
  56.9 1.3 %collective-permute-start.18 = (f32[64,193]{0,1:T(8,128)S(1)}, f32[64,193]{0,1:T(8,128)S(1)}, u32[]{:S(2)}, u32[]{:S(2)}) collective-permute-start(f32[64,193]{0,1:T(8,128)S(1)} %collective-permute-done.16), channel_id=1, source_target_pairs={{0,8},{8,0},{16,24},{24,16},{1,9},{9,1},{17,25},{25,17},{2,10},{10... | collective-permute-start | bytes 148232 | tf_op jit(solution)/shard_map/ppermute | solution.py:45
  57.6 4.4 %collective-permute-start.19 = (f32[64,3584]{1,0:T(8,128)}, f32[64,3584]{1,0:T(8,128)S(1)}, u32[]{:S(2)}, u32[]{:S(2)}) collective-permute-start(f32[64,3584]{1,0:T(8,128)} %collective-permute-done.17), channel_id=1, source_target_pairs={{0,8},{8,0},{16,24},{24,16},{1,9},{9,1},{17,25},{25,17},{2,10},{10... | collective-permute-start | bytes 2752520 | tf_op jit(solution)/shard_map/ppermute | solution.py:45
  62.7 7.7 %collective-permute-start.26 = (f32[64]{0:T(128)S(1)}, f32[64]{0:T(128)S(1)}, u32[]{:S(2)}, u32[]{:S(2)}) collective-permute-start(f32[64]{0:T(128)S(1)} %get-tuple-element.19), channel_id=1, source_target_pairs={{0,7},{1,6},{2,5},{3,4},{4,3},{5,2},{6,1},{7,0},{8,15},{9,14},{10,... | collective-permute-start | bytes 776 | tf_op jit(solution)/shard_map/ppermute | solution.py:28
  64.3 8.1 %collective-permute-start.25 = (f32[64]{0:T(128)S(1)}, f32[64]{0:T(128)S(1)}, u32[]{:S(2)}, u32[]{:S(2)}) collective-permute-start(f32[64]{0:T(128)S(1)} %get-tuple-element.19), channel_id=1, source_target_pairs={{0,6},{1,7},{2,4},{3,5},{4,2},{5,3},{6,0},{7,1},{8,14},{9,15},{10,... | collective-permute-start | bytes 776 | tf_op jit(solution)/shard_map/ppermute | solution.py:28
  66.5 7.4 %collective-permute-start.24 = (f32[64]{0:T(128)S(1)}, f32[64]{0:T(128)S(1)}, u32[]{:S(2)}, u32[]{:S(2)}) collective-permute-start(f32[64]{0:T(128)S(1)} %get-tuple-element.19), channel_id=1, source_target_pairs={{0,5},{1,4},{2,7},{3,6},{4,1},{5,0},{6,3},{7,2},{8,13},{9,12},{10,... | collective-permute-start | bytes 776 | tf_op jit(solution)/shard_map/ppermute | solution.py:28
  66.5 7.4 %collective-permute-start.23 = (f32[64]{0:T(128)S(1)}, f32[64]{0:T(128)S(1)}, u32[]{:S(2)}, u32[]{:S(2)}) collective-permute-start(f32[64]{0:T(128)S(1)} %get-tuple-element.19), channel_id=1, source_target_pairs={{0,4},{1,5},{2,6},{3,7},{4,0},{5,1},{6,2},{7,3},{8,12},{9,13},{10,... | collective-permute-start | bytes 776 | tf_op jit(solution)/shard_map/ppermute | solution.py:28
  70.4 4.4 %collective-permute-start.22 = (f32[64]{0:T(128)S(1)}, f32[64]{0:T(128)S(1)}, u32[]{:S(2)}, u32[]{:S(2)}) collective-permute-start(f32[64]{0:T(128)S(1)} %get-tuple-element.19), channel_id=1, source_target_pairs={{0,3},{1,2},{2,1},{3,0},{4,7},{5,6},{6,5},{7,4},{8,11},{9,10},{10,... | collective-permute-start | bytes 776 | tf_op jit(solution)/shard_map/ppermute | solution.py:28
  70.4 4.4 %collective-permute-start.21 = (f32[64]{0:T(128)S(1)}, f32[64]{0:T(128)S(1)}, u32[]{:S(2)}, u32[]{:S(2)}) collective-permute-start(f32[64]{0:T(128)S(1)} %get-tuple-element.19), channel_id=1, source_target_pairs={{0,2},{1,3},{2,0},{3,1},{4,6},{5,7},{6,4},{7,5},{8,10},{9,11},{10,... | collective-permute-start | bytes 776 | tf_op jit(solution)/shard_map/ppermute | solution.py:28
  72.4 3.5 %collective-permute-start.20 = (f32[64]{0:T(128)S(1)}, f32[64]{0:T(128)S(1)}, u32[]{:S(2)}, u32[]{:S(2)}) collective-permute-start(f32[64]{0:T(128)S(1)} %get-tuple-element.19), channel_id=1, source_target_pairs={{0,1},{1,0},{2,3},{3,2},{4,5},{5,4},{6,7},{7,6},{8,9},{9,8},{10,11... | collective-permute-start | bytes 776 | tf_op jit(solution)/shard_map/ppermute | solution.py:28

commit v3 on v0

v3 whole, which is shorter than its diff:
```python
import functools

import jax
import jax.numpy as jnp
from jax import lax
from jax.experimental import pallas as pl
from jax.experimental.pallas import tpu as pltpu
from jax.sharding import PartitionSpec as P

step_rate = 0.1
epsilon = 1e-06
lanes = 128


def tile_of(columns):
    if columns % lanes:
        return columns
    units = columns // lanes
    return lanes * max(u for u in range(1, 8) if units % u == 0)


def halves(array):
    top = array.astype(jnp.bfloat16)
    return top, (array - top.astype(jnp.float32)).astype(jnp.bfloat16)


def product(left, right, transposed=False):
    dims = (((1,), (1 if transposed else 0,)), ((), ()))
    dot = functools.partial(lax.dot_general, dimension_numbers=dims, preferred_element_type=jnp.float32)
    left_top, left_rest = halves(left)
    right_top, right_rest = halves(right)
    return dot(left_top, right_top) + (dot(left_top, right_rest) + dot(left_rest, right_top))


def project_kernel(x_ref, s_ref, out_ref):
    x, s = x_ref[...], s_ref[...]
    rows = s.shape[0]
    projected = product(x, s, transposed=True)
    squares = jnp.broadcast_to(jnp.sum(x * x, axis=1, keepdims=True), (x.shape[0], out_ref.shape[1] - rows))

    @pl.when(pl.program_id(0) == 0)
    def _():
        out_ref[:, :rows] = projected
        out_ref[:, rows:] = squares

    @pl.when(pl.program_id(0) > 0)
    def _():
        out_ref[:, :rows] += projected
        out_ref[:, rows:] += squares


def project(x, sample):
    per_group, columns = x.shape
    rows = sample.shape[0]
    width = -(-(rows + 1) // lanes) * lanes
    tile = tile_of(columns)
    return pl.pallas_call(
        project_kernel,
        grid=(columns // tile,),
        in_specs=[pl.BlockSpec((per_group, tile), lambda i: (0, i)), pl.BlockSpec((rows, tile), lambda i: (0, i))],
        out_specs=pl.BlockSpec((per_group, width), lambda i: (0, 0)),
        out_shape=jax.ShapeDtypeStruct((per_group, width), jnp.float32),
        name="project",
    )(x, sample)


def scale_of(block, rows, features):
    return lax.rsqrt(block[:, rows : rows + 1] / features + epsilon)


def own_kernel(features, p_ref, x_ref, s_ref, out_ref):
    rows = s_ref.shape[0]
    per_group = x_ref.shape[0]
    scale = scale_of(p_ref[...], rows, features)
    images = p_ref[:, :rows] * scale
    shared = product(images, images * scale, transposed=True)
    later = lax.broadcasted_iota(jnp.int32, shared.shape, 0)
    earlier = lax.broadcasted_iota(jnp.int32, shared.shape, 1)
    coupling = jnp.where(earlier < later, shared * (-step_rate / (features * rows)), 0.0)
    x = x_ref[...]
    out_ref[...] = scale * x + (product(images * (step_rate / rows), s_ref[...]) + product(coupling, x))


def own_part(projected, x, sample, features):
    per_group, columns = x.shape
    rows = sample.shape[0]
    tile = tile_of(columns)
    return pl.pallas_call(
        functools.partial(own_kernel, features),
        grid=(columns // tile,),
        in_specs=[
            pl.BlockSpec(projected.shape, lambda i: (0, 0)),
            pl.BlockSpec((per_group, tile), lambda i: (0, i)),
            pl.BlockSpec((rows, tile), lambda i: (0, i)),
        ],
        out_specs=pl.BlockSpec((per_group, tile), lambda i: (0, i)),
        out_shape=jax.ShapeDtypeStruct(x.shape, jnp.float32),
        name="own_part",
    )(projected, x, sample)


def others_kernel(features, rows, count, flags_ref, t_ref, p_ref, *refs):
    projected_refs, x_refs, out_ref, squares_ref, total = (*[refs[: count], refs[count : 2 * count]], *refs[2 * count :])
    per_group = t_ref.shape[0]
    images = p_ref[:, :rows] * (scale_of(p_ref[...], rows, features) * (-step_rate / (features * rows)))
    updated = t_ref[...]
    others = []
    for k in range(count):
        scale = scale_of(projected_refs[k][...], rows, features)
        others.append(projected_refs[k][:, :rows] * (scale * scale * flags_ref[k]))
    coupling = product(images, jnp.concatenate(others, axis=0), transposed=True)
    updated += product(coupling, jnp.concatenate([x_ref[...] for x_ref in x_refs], axis=0))
    out_ref[...] = updated
    squares = jnp.sum(updated * updated, axis=1, keepdims=True)

    @pl.when(pl.program_id(0) == 0)
    def _():
        total[...] = squares

    @pl.when(pl.program_id(0) > 0)
    def _():
        total[...] += squares

    @pl.when(pl.program_id(0) == pl.num_programs(0) - 1)
    def _():
        down = lax.broadcasted_iota(jnp.int32, (per_group, per_group), 0)
        across = lax.broadcasted_iota(jnp.int32, (per_group, per_group), 1)
        spread = jnp.broadcast_to(total[...], (per_group, per_group))
        squares_ref[...] = jnp.sum(jnp.where(down == across, spread, 0.0), axis=0, keepdims=True)


def others_part(flags, partly, projected, others, blocks, rows, features):
    per_group, columns = partly.shape
    count = len(blocks)
    tile = tile_of(columns)
    whole = pl.BlockSpec(projected.shape, lambda i: (0, 0))
    tiled = pl.BlockSpec((per_group, tile), lambda i: (0, i))
    return pl.pallas_call(
        functools.partial(others_kernel, features, rows, count),
        grid=(columns // tile,),
        in_specs=[pl.BlockSpec(memory_space=pltpu.SMEM), tiled, whole] + [whole] * count + [tiled] * count,
        out_specs=[tiled, pl.BlockSpec((1, per_group), lambda i: (0, 0))],
        out_shape=[
            jax.ShapeDtypeStruct(partly.shape, jnp.float32),
            jax.ShapeDtypeStruct((1, per_group), jnp.float32),
        ],
        scratch_shapes=[pltpu.VMEM((per_group, 1), jnp.float32)],
        name="others_part",
    )(flags, partly, projected, *others, *blocks)


def exchange(array, axis, step):
    return lax.ppermute(array, axis, [(i, i ^ step) for i in range(lax.axis_size(axis))])


def add_up(array, axis):
    size = lax.axis_size(axis)
    if size & (size - 1):
        return lax.psum(array, axis)
    step = 1
    while step < size:
        array = array + exchange(array, axis, step)
        step *= 2
    return array


def gather(own, size):
    if size & (size - 1):
        arrays = lax.all_gather(own, "comp")
        group = lax.axis_index("comp")
        return [arrays[(group + k) % size] for k in range(1, size)]
    across = [own] + [exchange(own, "comp", step) for step in range(2, size, 2)]
    beside = [exchange(array, "comp", 1) for array in across] if size > 1 else []
    return across[1:] + beside


def owners(size):
    group = lax.axis_index("comp")
    if size & (size - 1):
        return [(group + k) % size for k in range(1, size)]
    return [group ^ step for step in range(2, size, 2)] + [group ^ (step + 1) for step in range(0, size, 2)]


def shards(samples, start_vectors):
    comp = lax.axis_size("comp")
    feat = lax.axis_size("feat")
    sample = samples[0]
    rows = sample.shape[0]
    features = sample.shape[1] * feat
    group = lax.axis_index("comp")

    blocks = gather(start_vectors, comp)
    projected = add_up(project(start_vectors, sample), "feat")
    others = gather(projected, comp)
    partly = own_part(projected, start_vectors, sample, features)
    flags = (jnp.stack(owners(comp)) < group).astype(jnp.float32)
    updated, squares = others_part(flags, partly, projected, others, blocks, rows, features)
    squares = add_up(squares, "feat")[0]
    return updated * lax.rsqrt(squares / features + epsilon)[:, None]


def solution(mesh):
    in_specs = (P(None, None, "feat"), P("comp", "feat"))
    out_specs = P("comp", "feat")
    return jax.shard_map(shards, mesh=mesh, in_specs=in_specs, out_specs=out_specs, check_vma=False)
```

time: 113 us -> 76.2 us (0.67)
  blocking collectives: 81.4 us -> 0 us
  waiting for transfers between devices: 0.04 us -> 35.6 us
  starting transfers between devices: 0.01 us -> 17.9 us
  Pallas kernels: 0 us -> 15.9 us
  between operations: 13.4 us -> 0.09 us
  matrix products: 11.7 us -> 0 us
  local copies, waits for them, and re-layouts: 0.01 us -> 1.89 us
  other arithmetic: 5.98 us -> 4.36 us
    psum x3 -> x0, blocking collectives: 75.6 us -> none  [the longest x2 42.3 us: normalize(): summed = lax.psum(jnp.sum(updated * updated, axis=1), 'feat')]
    ppermute x0 -> x12, waiting for transfers between devices: none -> 35.6 us  [exchange(): lax.ppermute(array, axis, [(i, i ^ step) for i in range(lax.axis_size(axi...]
    ppermute x0 -> x12, starting transfers between devices: none -> 17.9 us  [exchange(): lax.ppermute(array, axis, [(i, i ^ step) for i in range(lax.axis_size(axi...]
    pallas_call x0 -> x3, Pallas kernels: none -> 15.9 us  [the longest x1 5.99 us: others_part(): pl.pallas_call(functools.partial(others_kernel, features, rows, count), g...]
    dot_general x4 -> x0, matrix products: 11.7 us -> none  [the longest x1 4.44 us: add_parent(): return jnp.einsum('ji,jd->id', coupling, pieces, precision=highest)]
    all_gather x1 -> x0, blocking collectives: 5.79 us -> none  [shards(): every_images = lax.all_gather(own_images, 'comp', axis=1, tiled=True)]
    mul x2 -> x1, other arithmetic: 4.47 us -> 2.23 us  [shards(): return updated * lax.rsqrt(squares / features + epsilon)[:, None]]
    unnamed x4 -> x14, local copies, waits for them, and re-layouts: 0.01 us -> 1.89 us
  transfers between devices with their start and end apart: 1 -> 12, of which waited for: 0 -> 8; matrix products, arithmetic and copies ran while one was open for 4% -> 2% of each run, Pallas kernels for 0% -> 13%
where the time goes in v3:
time: 76.2 us; the launch traced here: 75.8 us
  waiting for transfers between devices  35.6 us (47%)
  starting transfers between devices  17.9 us (23%)
  Pallas kernels  15.9 us (21%)
  other arithmetic  4.36 us (6%)
  local copies, waits for them, and re-layouts  1.89 us (2%)
    ppermute x12, waiting for transfers between devices, exchange(): lax.ppermute(array, axis, [(i, i ^ step) for i in range(lax.axis_size(axi...  35.6 us
    ppermute x12, starting transfers between devices, exchange(): lax.ppermute(array, axis, [(i, i ^ step) for i in range(lax.axis_size(axi...  17.9 us
    pallas_call x1, Pallas kernels, others_part(): pl.pallas_call(functools.partial(others_kernel, features, rows, count), g...  5.99 us
    pallas_call x1, Pallas kernels, project(): pl.pallas_call(project_kernel, grid=(columns // tile,), in_specs=[pl.Bloc...  4.97 us
    pallas_call x1, Pallas kernels, own_part(): pl.pallas_call(functools.partial(own_kernel, features), grid=(columns //...  4.94 us
    mul x1, other arithmetic, shards(): return updated * lax.rsqrt(squares / features + epsilon)[:, None]  2.23 us
    unnamed x14, local copies, waits for them, and re-layouts  1.89 us
    add x5, other arithmetic, add_up(): array = array + exchange(array, axis, step)  1.54 us
  transfers between devices with their start and end apart: 12, of which 8 were waited for; matrix products, arithmetic and copies ran while one was open for 2% of the time, Pallas kernels for 13%

profile of v3, /device:TPU:0, one launch (start us, length us, event | category | flops | bytes accessed | tf_op | source)
XLA Modules:
  0.0 75.8 jit_solution(9213431544684952184)
XLA Ops:
  0.0 2.9 %collective-permute-start.6 = (f32[64,3584]{1,0:T(8,128)}, f32[64,3584]{1,0:T(8,128)S(1)}, u32[]{:S(2)}, u32[]{:S(2)}) collective-permute-start(f32[64,3584]{1,0:T(8,128)} %x_ref.3), channel_id=1, source_target_pairs={{0,16},{8,24},{16,0},{24,8},{1,17},{9,25},{17,1},{25,9},{2,18},{10... | collective-permute-start | bytes 2752520 | tf_op jit(solution)/shard_map/ppermute | solution.py:153
  2.9 0.0 collective-permute-start.7
  2.9 20.6 %collective-permute-done.6.refs_3_ = f32[64,3584]{1,0:T(8,128)S(1)} collective-permute-done((f32[64,3584]{1,0:T(8,128)}, f32[64,3584]{1,0:T(8,128)S(1)}, u32[]{:S(2)}, u32[]{:S(2)}) %collective-permute-start.6) | collective-permute-done | bytes 917536 | tf_op jit(solution)/shard_map/ppermute | solution.py:153
  23.5 0.0 copy-start
  23.5 0.0 collective-permute-start.8
  23.5 5.0 %project.1 = f32[64,256]{1,0:T(8,128)} custom-call(f32[64,3584]{1,0:T(8,128)} %x_ref.3, f32[192,3584]{1,0:T(8,128)} %bitcast.6), custom_call_target="tpu_custom_call" | custom-call | tf_op jit(solution)/shard_map/project/pallas_call | solution.py:57
  28.5 1.8 %collective-permute-start = (f32[64,256]{1,0:T(8,128)}, f32[64,256]{1,0:T(8,128)S(1)}, u32[]{:S(2)}, u32[]{:S(2)}) collective-permute-start(f32[64,256]{1,0:T(8,128)} %project.1), channel_id=1, source_target_pairs={{0,1},{1,0},{2,3},{3,2},{4,5},{5,4},{6,7},{7,6},{8,9},{9,8},{10,11... | collective-permute-start | bytes 196616 | tf_op jit(solution)/shard_map/ppermute | solution.py:153
  30.2 2.7 %collective-permute-done = f32[64,256]{1,0:T(8,128)S(1)} collective-permute-done((f32[64,256]{1,0:T(8,128)}, f32[64,256]{1,0:T(8,128)S(1)}, u32[]{:S(2)}, u32[]{:S(2)}) %collective-permute-start) | collective-permute-done | bytes 65568 | tf_op jit(solution)/shard_map/ppermute | solution.py:153
  33.0 0.9 %add.29 = f32[64,256]{1,0:T(8,128)S(1)} add(f32[64,256]{1,0:T(8,128)} %project.1, f32[64,256]{1,0:T(8,128)S(1)} %collective-permute-done) | non-fusion elementwise | flops 16384 | bytes 196608 | tf_op jit(solution)/shard_map/add | solution.py:162
  33.8 1.9 %collective-permute-start.1 = (f32[64,256]{1,0:T(8,128)S(1)}, f32[64,256]{1,0:T(8,128)S(1)}, u32[]{:S(2)}, u32[]{:S(2)}) collective-permute-start(f32[64,256]{1,0:T(8,128)S(1)} %add.29), channel_id=1, source_target_pairs={{0,2},{1,3},{2,0},{3,1},{4,6},{5,7},{6,4},{7,5},{8,10},{9,11},{10,... | collective-permute-start | bytes 196616 | tf_op jit(solution)/shard_map/ppermute | solution.py:153
  35.7 2.4 %collective-permute-done.1 = f32[64,256]{1,0:T(8,128)S(1)} collective-permute-done((f32[64,256]{1,0:T(8,128)S(1)}, f32[64,256]{1,0:T(8,128)S(1)}, u32[]{:S(2)}, u32[]{:S(2)}) %collective-permute-start.1) | collective-permute-done | bytes 65568 | tf_op jit(solution)/shard_map/ppermute | solution.py:153
  38.1 2.9 %collective-permute-start.2 = (f32[64,256]{1,0:T(8,128)S(1)}, f32[64,256]{1,0:T(8,128)S(1)}, u32[]{:S(2)}, u32[]{:S(2)}) collective-permute-start(f32[64,256]{1,0:T(8,128)S(1)} %add.30), channel_id=1, source_target_pairs={{0,4},{1,5},{2,6},{3,7},{4,0},{5,1},{6,2},{7,3},{8,12},{9,13},{10,... | collective-permute-start | bytes 196616 | tf_op jit(solution)/shard_map/ppermute | solution.py:153
  41.1 2.3 %collective-permute-done.2 = f32[64,256]{1,0:T(8,128)S(1)} collective-permute-done((f32[64,256]{1,0:T(8,128)S(1)}, f32[64,256]{1,0:T(8,128)S(1)}, u32[]{:S(2)}, u32[]{:S(2)}) %collective-permute-start.2) | collective-permute-done | bytes 65568 | tf_op jit(solution)/shard_map/ppermute | solution.py:153
  43.4 0.0 copy-start.3
  43.4 1.8 %collective-permute-start.3 = (f32[64,256]{1,0:T(8,128)S(1)}, f32[64,256]{1,0:T(8,128)S(1)}, u32[]{:S(2)}, u32[]{:S(2)}) collective-permute-start(f32[64,256]{1,0:T(8,128)S(1)} %add.31.p_ref), channel_id=1, source_target_pairs={{0,16},{8,24},{16,0},{24,8},{1,17},{9,25},{17,1},{25,9},{2,18},{10... | collective-permute-start | bytes 196616 | tf_op jit(solution)/shard_map/ppermute | solution.py:153
  45.2 0.0 collective-permute-start.4
  45.2 2.5 %collective-permute-done.3.refs_0_ = f32[64,256]{1,0:T(8,128)S(1)} collective-permute-done((f32[64,256]{1,0:T(8,128)S(1)}, f32[64,256]{1,0:T(8,128)S(1)}, u32[]{:S(2)}, u32[]{:S(2)}) %collective-permute-start.3) | collective-permute-done | bytes 65568 | tf_op jit(solution)/shard_map/ppermute | solution.py:153
  47.7 0.0 copy-start.4
  47.7 0.0 collective-permute-start.5
  47.7 0.6 compare_convert_fusion.flags_ref
  48.3 0.0 copy-done.3
  48.3 4.9 %own_part.1.t_ref = f32[64,3584]{1,0:T(8,128)} custom-call(f32[64,256]{1,0:T(8,128)} %copy-done.3, f32[64,3584]{1,0:T(8,128)} %x_ref.3, f32[192,3584]{1,0:T(8,128)} %bitcast.7), custom_call_target="tpu_custom_call" | custom-call | tf_op jit(solution)/shard_map/own_part/pallas_call | solution.py:88
  53.3 0.0 copy-done
  53.3 0.0 collective-permute-done.4.refs_1_
  53.3 0.0 copy-start.5
  53.3 0.0 collective-permute-done.5.refs_2_
  53.3 0.0 copy-start.6
  53.3 0.0 collective-permute-done.7.refs_4_
  53.3 0.0 copy-start.1
  53.3 0.0 collective-permute-done.8.refs_5_
  53.3 0.0 copy-done.4
  53.3 0.5 copy-done.5
  53.9 0.0 copy-done.6
  53.9 0.4 copy-done.1
  54.3 0.0 copy-start.2
  54.3 0.9 %copy-done.2 = f32[64,3584]{1,0:T(8,128)} copy-done((f32[64,3584]{1,0:T(8,128)}, f32[64,3584]{1,0:T(8,128)S(1)}, u32[]{:S(2)}) %copy-start.2) | copy-done | bytes 917528
  55.2 6.0 %others_part.1 = (f32[64,3584]{1,0:T(8,128)}, f32[1,64]{1,0:T(1,128)}) custom-call(f32[3]{0:T(128)} %compare_convert_fusion.flags_ref, f32[64,3584]{1,0:T(8,128)} %own_part.1.t_ref, f32[64,256]{1,0:T(8,128)} %copy-done.3, f32[64,256]{1,0:T(8,128)} %copy-done.4, f32[64,256]{1,0:T(8,128)} %copy-done.5, f32[64,256]{1,0:T(8,128)} %copy-done.6, ...), custom_call_target="tpu_custom_call" | custom-call | tf_op jit(solution)/shard_map/others_part/pallas_call | solution.py:138
  61.2 1.8 %collective-permute-start.9 = (f32[1,64]{1,0:T(1,128)}, f32[1,64]{1,0:T(1,128)S(1)}, u32[]{:S(2)}, u32[]{:S(2)}) collective-permute-start(f32[1,64]{1,0:T(1,128)} %get-tuple-element.8), channel_id=1, source_target_pairs={{0,1},{1,0},{2,3},{3,2},{4,5},{5,4},{6,7},{7,6},{8,9},{9,8},{10,11... | collective-permute-start | bytes 776 | tf_op jit(solution)/shard_map/ppermute | solution.py:153
  63.0 1.8 %collective-permute-done.9 = f32[1,64]{1,0:T(1,128)S(1)} collective-permute-done((f32[1,64]{1,0:T(1,128)}, f32[1,64]{1,0:T(1,128)S(1)}, u32[]{:S(2)}, u32[]{:S(2)}) %collective-permute-start.9) | collective-permute-done | bytes 288 | tf_op jit(solution)/shard_map/ppermute | solution.py:153
  64.8 0.7 add.32
  65.5 1.8 %collective-permute-start.10 = (f32[1,64]{1,0:T(1,128)S(1)}, f32[1,64]{1,0:T(1,128)S(1)}, u32[]{:S(2)}, u32[]{:S(2)}) collective-permute-start(f32[1,64]{1,0:T(1,128)S(1)} %add.32), channel_id=1, source_target_pairs={{0,2},{1,3},{2,0},{3,1},{4,6},{5,7},{6,4},{7,5},{8,10},{9,11},{10,... | collective-permute-start | bytes 776 | tf_op jit(solution)/shard_map/ppermute | solution.py:153
  67.3 1.7 %collective-permute-done.10 = f32[1,64]{1,0:T(1,128)S(1)} collective-permute-done((f32[1,64]{1,0:T(1,128)S(1)}, f32[1,64]{1,0:T(1,128)S(1)}, u32[]{:S(2)}, u32[]{:S(2)}) %collective-permute-start.10) | collective-permute-done | bytes 288 | tf_op jit(solution)/shard_map/ppermute | solution.py:153
  69.1 3.0 %collective-permute-start.11 = (f32[1,64]{1,0:T(1,128)S(1)}, f32[1,64]{1,0:T(1,128)S(1)}, u32[]{:S(2)}, u32[]{:S(2)}) collective-permute-start(f32[1,64]{1,0:T(1,128)S(1)} %add.33), channel_id=1, source_target_pairs={{0,4},{1,5},{2,6},{3,7},{4,0},{5,1},{6,2},{7,3},{8,12},{9,13},{10,... | collective-permute-start | bytes 776 | tf_op jit(solution)/shard_map/ppermute | solution.py:153
  72.0 1.5 %collective-permute-done.11 = f32[1,64]{1,0:T(1,128)S(1)} collective-permute-done((f32[1,64]{1,0:T(1,128)S(1)}, f32[1,64]{1,0:T(1,128)S(1)}, u32[]{:S(2)}, u32[]{:S(2)}) %collective-permute-start.11) | collective-permute-done | bytes 288 | tf_op jit(solution)/shard_map/ppermute | solution.py:153
  73.5 2.2 %broadcast_multiply_fusion = f32[64,3584]{1,0:T(8,128)} fusion(f32[64,3584]{1,0:T(8,128)} %get-tuple-element.7, f32[64]{0:T(128)S(1)} %rsqrt_bitcast_fusion), kind=kLoop, calls=%fused_computation | loop fusion | flops 229376 | bytes 1835264 | tf_op jit(solution)/shard_map/mul | solution.py:199
  (4 shorter events, 0.0 us)
Async XLA Ops:
  0.0 23.5 %collective-permute-start.6 = (f32[64,3584]{1,0:T(8,128)}, f32[64,3584]{1,0:T(8,128)S(1)}, u32[]{:S(2)}, u32[]{:S(2)}) collective-permute-start(f32[64,3584]{1,0:T(8,128)} %x_ref.3), channel_id=1, source_target_pairs={{0,16},{8,24},{16,0},{24,8},{1,17},{9,25},{17,1},{25,9},{2,18},{10... | collective-permute-start | bytes 2752520 | tf_op jit(solution)/shard_map/ppermute | solution.py:153
  2.9 50.4 %collective-permute-start.7 = (f32[64,3584]{1,0:T(8,128)}, f32[64,3584]{1,0:T(8,128)S(1)}, u32[]{:S(2)}, u32[]{:S(2)}) collective-permute-start(f32[64,3584]{1,0:T(8,128)} %x_ref.3), channel_id=1, source_target_pairs={{0,8},{8,0},{16,24},{24,16},{1,9},{9,1},{17,25},{25,17},{2,10},{10... | collective-permute-start | bytes 2752520 | tf_op jit(solution)/shard_map/ppermute | solution.py:153
  23.5 29.8 %copy-start = (f32[64,3584]{1,0:T(8,128)}, f32[64,3584]{1,0:T(8,128)S(1)}, u32[]{:S(2)}) copy-start(f32[64,3584]{1,0:T(8,128)S(1)} %collective-permute-done.6.refs_3_) | copy-start | bytes 2752516
  23.5 29.8 %collective-permute-start.8 = (f32[64,3584]{1,0:T(8,128)S(1)}, f32[64,3584]{1,0:T(8,128)S(1)}, u32[]{:S(2)}, u32[]{:S(2)}) collective-permute-start(f32[64,3584]{1,0:T(8,128)S(1)} %collective-permute-done.6.refs_3_), channel_id=1, source_target_pairs={{0,8},{8,0},{16,24},{24,16},{1,9},{9,1},{17,25},{25,17},{2,10},{10... | collective-permute-start | bytes 2752520 | tf_op jit(solution)/shard_map/ppermute | solution.py:153
  28.5 4.5 %collective-permute-start = (f32[64,256]{1,0:T(8,128)}, f32[64,256]{1,0:T(8,128)S(1)}, u32[]{:S(2)}, u32[]{:S(2)}) collective-permute-start(f32[64,256]{1,0:T(8,128)} %project.1), channel_id=1, source_target_pairs={{0,1},{1,0},{2,3},{3,2},{4,5},{5,4},{6,7},{7,6},{8,9},{9,8},{10,11... | collective-permute-start | bytes 196616 | tf_op jit(solution)/shard_map/ppermute | solution.py:153
  33.8 4.3 %collective-permute-start.1 = (f32[64,256]{1,0:T(8,128)S(1)}, f32[64,256]{1,0:T(8,128)S(1)}, u32[]{:S(2)}, u32[]{:S(2)}) collective-permute-start(f32[64,256]{1,0:T(8,128)S(1)} %add.29), channel_id=1, source_target_pairs={{0,2},{1,3},{2,0},{3,1},{4,6},{5,7},{6,4},{7,5},{8,10},{9,11},{10,... | collective-permute-start | bytes 196616 | tf_op jit(solution)/shard_map/ppermute | solution.py:153
  38.1 5.2 %collective-permute-start.2 = (f32[64,256]{1,0:T(8,128)S(1)}, f32[64,256]{1,0:T(8,128)S(1)}, u32[]{:S(2)}, u32[]{:S(2)}) collective-permute-start(f32[64,256]{1,0:T(8,128)S(1)} %add.30), channel_id=1, source_target_pairs={{0,4},{1,5},{2,6},{3,7},{4,0},{5,1},{6,2},{7,3},{8,12},{9,13},{10,... | collective-permute-start | bytes 196616 | tf_op jit(solution)/shard_map/ppermute | solution.py:153
  43.4 4.9 %copy-start.3 = (f32[64,256]{1,0:T(8,128)}, f32[64,256]{1,0:T(8,128)S(1)}, u32[]{:S(2)}) copy-start(f32[64,256]{1,0:T(8,128)S(1)} %add.31.p_ref) | copy-start | bytes 196612
  43.4 4.3 %collective-permute-start.3 = (f32[64,256]{1,0:T(8,128)S(1)}, f32[64,256]{1,0:T(8,128)S(1)}, u32[]{:S(2)}, u32[]{:S(2)}) collective-permute-start(f32[64,256]{1,0:T(8,128)S(1)} %add.31.p_ref), channel_id=1, source_target_pairs={{0,16},{8,24},{16,0},{24,8},{1,17},{9,25},{17,1},{25,9},{2,18},{10... | collective-permute-start | bytes 196616 | tf_op jit(solution)/shard_map/ppermute | solution.py:153
  45.2 8.1 %collective-permute-start.4 = (f32[64,256]{1,0:T(8,128)S(1)}, f32[64,256]{1,0:T(8,128)S(1)}, u32[]{:S(2)}, u32[]{:S(2)}) collective-permute-start(f32[64,256]{1,0:T(8,128)S(1)} %add.31.p_ref), channel_id=1, source_target_pairs={{0,8},{8,0},{16,24},{24,16},{1,9},{9,1},{17,25},{25,17},{2,10},{10... | collective-permute-start | bytes 196616 | tf_op jit(solution)/shard_map/ppermute | solution.py:153
  47.7 5.6 %copy-start.4 = (f32[64,256]{1,0:T(8,128)}, f32[64,256]{1,0:T(8,128)S(1)}, u32[]{:S(2)}) copy-start(f32[64,256]{1,0:T(8,128)S(1)} %collective-permute-done.3.refs_0_) | copy-start | bytes 196612
  47.7 5.5 %collective-permute-start.5 = (f32[64,256]{1,0:T(8,128)S(1)}, f32[64,256]{1,0:T(8,128)S(1)}, u32[]{:S(2)}, u32[]{:S(2)}) collective-permute-start(f32[64,256]{1,0:T(8,128)S(1)} %collective-permute-done.3.refs_0_), channel_id=1, source_target_pairs={{0,8},{8,0},{16,24},{24,16},{1,9},{9,1},{17,25},{25,17},{2,10},{10... | collective-permute-start | bytes 196616 | tf_op jit(solution)/shard_map/ppermute | solution.py:153
  53.3 0.6 copy-start.5
  53.3 0.6 copy-start.6
  53.3 1.0 %copy-start.1 = (f32[64,3584]{1,0:T(8,128)}, f32[64,3584]{1,0:T(8,128)S(1)}, u32[]{:S(2)}) copy-start(f32[64,3584]{1,0:T(8,128)S(1)} %collective-permute-done.7.refs_4_) | copy-start | bytes 2752516
  54.3 0.9 %copy-start.2 = (f32[64,3584]{1,0:T(8,128)}, f32[64,3584]{1,0:T(8,128)S(1)}, u32[]{:S(2)}) copy-start(f32[64,3584]{1,0:T(8,128)S(1)} %collective-permute-done.8.refs_5_) | copy-start | bytes 2752516
  61.2 3.6 %collective-permute-start.9 = (f32[1,64]{1,0:T(1,128)}, f32[1,64]{1,0:T(1,128)S(1)}, u32[]{:S(2)}, u32[]{:S(2)}) collective-permute-start(f32[1,64]{1,0:T(1,128)} %get-tuple-element.8), channel_id=1, source_target_pairs={{0,1},{1,0},{2,3},{3,2},{4,5},{5,4},{6,7},{7,6},{8,9},{9,8},{10,11... | collective-permute-start | bytes 776 | tf_op jit(solution)/shard_map/ppermute | solution.py:153
  65.5 3.5 %collective-permute-start.10 = (f32[1,64]{1,0:T(1,128)S(1)}, f32[1,64]{1,0:T(1,128)S(1)}, u32[]{:S(2)}, u32[]{:S(2)}) collective-permute-start(f32[1,64]{1,0:T(1,128)S(1)} %add.32), channel_id=1, source_target_pairs={{0,2},{1,3},{2,0},{3,1},{4,6},{5,7},{6,4},{7,5},{8,10},{9,11},{10,... | collective-permute-start | bytes 776 | tf_op jit(solution)/shard_map/ppermute | solution.py:153
  69.1 4.5 %collective-permute-start.11 = (f32[1,64]{1,0:T(1,128)S(1)}, f32[1,64]{1,0:T(1,128)S(1)}, u32[]{:S(2)}, u32[]{:S(2)}) collective-permute-start(f32[1,64]{1,0:T(1,128)S(1)} %add.33), channel_id=1, source_target_pairs={{0,4},{1,5},{2,6},{3,7},{4,0},{5,1},{6,2},{7,3},{8,12},{9,13},{10,... | collective-permute-start | bytes 776 | tf_op jit(solution)/shard_map/ppermute | solution.py:153

commit v4 on v3

v4 whole, which is shorter than its diff:
```python
import functools

import jax
import jax.numpy as jnp
from jax import lax
from jax.experimental import pallas as pl
from jax.experimental.pallas import tpu as pltpu
from jax.sharding import PartitionSpec as P

step_rate = 0.1
epsilon = 1e-06
lanes = 128
in_vmem = pl.BlockSpec(memory_space=pltpu.VMEM)


def tile_of(columns, most):
    if columns % lanes:
        return columns
    units = columns // lanes
    return lanes * max(u for u in range(1, most + 1) if units % u == 0)


def halves(array):
    top = array.astype(jnp.bfloat16)
    return top, (array - top.astype(jnp.float32)).astype(jnp.bfloat16)


def product(left, right, transposed=False):
    dims = (((1,), (1 if transposed else 0,)), ((), ()))
    dot = functools.partial(lax.dot_general, dimension_numbers=dims, preferred_element_type=jnp.float32)
    left_top, left_rest = left if isinstance(left, tuple) else halves(left)
    right_top, right_rest = halves(right)
    rows = left_top.shape[0]
    both = dot(jnp.concatenate([left_top, left_rest], axis=0), right_top)
    return both[:rows] + (both[rows:] + dot(left_top, right_rest))


def scale_of(squares, features):
    return lax.rsqrt(squares / features + epsilon)


def loop(columns, most, body, init):
    tile = tile_of(columns, most)
    return lax.fori_loop(0, columns // tile, lambda i, c: body(pl.ds(pl.multiple_of(i * tile, tile), tile), c), init)


def project_kernel(x_ref, s_ref, out_ref):
    per_group, columns = x_ref.shape
    rows = s_ref.shape[0]

    def body(here, carry):
        x = x_ref[:, here]
        projected, squares = carry
        projected += product(x, s_ref[:, here], transposed=True)
        return projected, squares + jnp.sum(x * x, axis=1, keepdims=True)

    zeros = jnp.zeros((per_group, rows), jnp.float32), jnp.zeros((per_group, 1), jnp.float32)
    projected, squares = loop(columns, 4, body, zeros)
    out_ref[:, :rows] = projected
    out_ref[:, rows:] = jnp.broadcast_to(squares, (per_group, out_ref.shape[1] - rows))


def project(x, sample):
    per_group = x.shape[0]
    rows = sample.shape[0]
    width = -(-(rows + 1) // lanes) * lanes
    return pl.pallas_call(
        project_kernel,
        in_specs=[in_vmem, in_vmem],
        out_specs=in_vmem,
        out_shape=jax.ShapeDtypeStruct((per_group, width), jnp.float32),
        name="project",
    )(x, sample)


def own_kernel(features, p_ref, x_ref, s_ref, out_ref):
    rows = s_ref.shape[0]
    scale = scale_of(p_ref[:, rows : rows + 1], features)
    images = p_ref[:, :rows] * scale
    shared = product(images, images * scale, transposed=True)
    later = lax.broadcasted_iota(jnp.int32, shared.shape, 0)
    earlier = lax.broadcasted_iota(jnp.int32, shared.shape, 1)
    coupling = halves(jnp.where(earlier < later, shared * (-step_rate / (features * rows)), 0.0))
    images = halves(images * (step_rate / rows))

    def body(here, carry):
        x = x_ref[:, here]
        out_ref[:, here] = scale * x + (product(images, s_ref[:, here]) + product(coupling, x))
        return carry

    loop(x_ref.shape[1], 4, body, 0)


def own_part(projected, x, sample, features):
    return pl.pallas_call(
        functools.partial(own_kernel, features),
        in_specs=[in_vmem] * 3,
        out_specs=in_vmem,
        out_shape=jax.ShapeDtypeStruct(x.shape, jnp.float32),
        name="own_part",
    )(projected, x, sample)


def diagonal(count):
    down = lax.broadcasted_iota(jnp.int32, (count, count), 0)
    across = lax.broadcasted_iota(jnp.int32, (count, count), 1)
    return down == across


def others_kernel(features, rows, count, flags_ref, t_ref, p_ref, *refs):
    projected_refs, x_refs = refs[:count], refs[count : 2 * count]
    out_ref, squares_ref = refs[2 * count :]
    per_group, columns = t_ref.shape
    images = p_ref[:, :rows] * (scale_of(p_ref[:, rows : rows + 1], features) * (-step_rate / (features * rows)))
    others = []
    for k in range(count):
        scale = scale_of(projected_refs[k][:, rows : rows + 1], features)
        others.append(projected_refs[k][:, :rows] * (scale * scale * flags_ref[k]))
    coupling = halves(product(images, jnp.concatenate(others, axis=0), transposed=True))

    def body(here, squares):
        updated = t_ref[:, here] + product(coupling, jnp.concatenate([x_ref[:, here] for x_ref in x_refs], axis=0))
        out_ref[:, here] = updated
        return squares + jnp.sum(updated * updated, axis=1, keepdims=True)

    squares = loop(columns, 4, body, jnp.zeros((per_group, 1), jnp.float32))
    spread = jnp.broadcast_to(squares, (per_group, per_group))
    squares_ref[...] = jnp.sum(jnp.where(diagonal(per_group), spread, 0.0), axis=0, keepdims=True)


def others_part(flags, partly, projected, others, blocks, rows, features):
    count = len(blocks)
    return pl.pallas_call(
        functools.partial(others_kernel, features, rows, count),
        in_specs=[pl.BlockSpec(memory_space=pltpu.SMEM)] + [in_vmem] * (2 + 2 * count),
        out_specs=[in_vmem, in_vmem],
        out_shape=[
            jax.ShapeDtypeStruct(partly.shape, jnp.float32),
            jax.ShapeDtypeStruct((1, partly.shape[0]), jnp.float32),
        ],
        name="others_part",
    )(flags, partly, projected, *others, *blocks)


def finish_kernel(features, count, updated_ref, *refs):
    squares_refs, (out_ref, scaled, sems) = refs[:count], refs[count:]
    per_group, columns = updated_ref.shape
    squares = squares_refs[0][...]
    for ref in squares_refs[1:]:
        squares += ref[...]
    spread = jnp.broadcast_to(scale_of(squares, features), (per_group, per_group))
    scale = jnp.sum(jnp.where(diagonal(per_group), spread, 0.0), axis=1, keepdims=True)
    tile = tile_of(columns, 7)
    copies = []
    for i in range(columns // tile):
        here = pl.ds(i * tile, tile)
        scaled[:, here] = updated_ref[:, here] * scale
        copies.append(pltpu.make_async_copy(scaled.at[:, here], out_ref.at[:, here], sems.at[i]))
        copies[-1].start()
    for copy in copies:
        copy.wait()


def finish(updated, squares, features):
    count = len(squares)
    return pl.pallas_call(
        functools.partial(finish_kernel, features, count),
        in_specs=[in_vmem] * (1 + count),
        out_specs=pl.BlockSpec(memory_space=pl.ANY),
        out_shape=jax.ShapeDtypeStruct(updated.shape, jnp.float32),
        scratch_shapes=[
            pltpu.VMEM(updated.shape, jnp.float32),
            pltpu.SemaphoreType.DMA((updated.shape[1] // tile_of(updated.shape[1], 7),)),
        ],
        name="finish",
    )(updated, *squares)


def exchange(array, axis, step):
    return lax.ppermute(array, axis, [(i, i ^ step) for i in range(lax.axis_size(axis))])


def terms(array, axis, together):
    size = lax.axis_size(axis)
    if size & (size - 1):
        return [lax.psum(array, axis)]
    parts, step, bits = [array], 1, (size.bit_length() - 1) % together or together
    while step < size:
        array = sum(parts[1:], parts[0])
        parts = [array] + [exchange(array, axis, step * k) for k in range(1, 1 << bits)]
        step <<= bits
        bits = together
    return parts


def gather(own, size):
    if size & (size - 1):
        arrays = lax.all_gather(own, "comp")
        group = lax.axis_index("comp")
        return [arrays[(group + step) % size] for step in range(1, size)]
    return [exchange(own, "comp", step) for step in range(1, size)]


def owners(size):
    group = lax.axis_index("comp")
    steps = jnp.arange(1, size, dtype=jnp.int32)
    return (group + steps) % size if size & (size - 1) else group ^ steps


def shards(samples, start_vectors):
    comp = lax.axis_size("comp")
    feat = lax.axis_size("feat")
    sample = samples[0]
    rows = sample.shape[0]
    features = sample.shape[1] * feat
    flags = (owners(comp) < lax.axis_index("comp")).astype(jnp.float32)

    straight = {step: exchange(start_vectors, "comp", step) for step in range(1, comp) if step % 2 == 0 or step == 1}
    parts = terms(project(start_vectors, sample), "feat", 1)
    projected = sum(parts[1:], parts[0])
    others = gather(projected, comp)
    partly = own_part(projected, start_vectors, sample, features)
    blocks = []
    for step in range(1, comp):
        if step in straight:
            blocks.append(straight[step])
        else:
            arrived, partly, others = lax.optimization_barrier((straight[step - 1], partly, others))
            blocks.append(exchange(arrived, "comp", 1))
    updated, squares = others_part(flags, partly, projected, others, blocks, rows, features)
    return finish(updated, terms(squares, "feat", 2), features)


def solution(mesh):
    in_specs = (P(None, None, "feat"), P("comp", "feat"))
    out_specs = P("comp", "feat")
    return jax.shard_map(shards, mesh=mesh, in_specs=in_specs, out_specs=out_specs, check_vma=False)
```

time: 76.2 us -> 53.7 us (0.70)
  waiting for transfers between devices: 35.6 us -> 16 us
  other arithmetic: 4.36 us -> 1.99 us
  Pallas kernels: 15.9 us -> 17.2 us
  local copies, waits for them, and re-layouts: 1.89 us -> 0.6 us
    ppermute x12 -> x13, waiting for transfers between devices: 35.6 us -> 16 us  [exchange(): lax.ppermute(array, axis, [(i, i ^ step) for i in range(lax.axis_size(axi...]
    mul x1 -> x0, other arithmetic: 2.23 us -> none  [shards(): return updated * lax.rsqrt(squares / features + epsilon)[:, None]]
    pallas_call x3 -> x4, Pallas kernels: 15.9 us -> 17.2 us  [the longest x1 5.33 us: others_part(): pl.pallas_call(functools.partial(others_kernel, features, rows, count), i...]
    unnamed x14 -> x22, local copies, waits for them, and re-layouts: 1.89 us -> 0.6 us
    ppermute x12 -> x13, starting transfers between devices: 17.9 us -> 17.5 us  [exchange(): lax.ppermute(array, axis, [(i, i ^ step) for i in range(lax.axis_size(axi...]
    add x5 -> x4, other arithmetic: 1.54 us -> 1.47 us  [the longest x3 1.46 us: terms(): array = sum(parts[1:], parts[0])]
  transfers between devices with their start and end apart: 12 -> 13, of which waited for: 8 -> 7; matrix products, arithmetic and copies ran while one was open for 2% -> 3% of each run, Pallas kernels for 13% -> 18%
where the time goes in v4:
time: 53.7 us; the launch traced here: 53.5 us
  starting transfers between devices  17.5 us (33%)
  Pallas kernels  17.2 us (32%)
  waiting for transfers between devices  16 us (30%)
  other arithmetic  1.99 us (4%)
  local copies, waits for them, and re-layouts  0.6 us (1%)
    ppermute x13, starting transfers between devices, exchange(): lax.ppermute(array, axis, [(i, i ^ step) for i in range(lax.axis_size(axi...  17.5 us
    ppermute x13, waiting for transfers between devices, exchange(): lax.ppermute(array, axis, [(i, i ^ step) for i in range(lax.axis_size(axi...  16 us
    pallas_call x1, Pallas kernels, others_part(): pl.pallas_call(functools.partial(others_kernel, features, rows, count), i...  5.33 us
    pallas_call x1, Pallas kernels, own_part(): pl.pallas_call(functools.partial(own_kernel, features), in_specs=[in_vmem...  5.11 us
    pallas_call x1, Pallas kernels, project(): pl.pallas_call(project_kernel, in_specs=[in_vmem, in_vmem], out_specs=in_...  4.52 us
    pallas_call x1, Pallas kernels, finish(): pl.pallas_call(functools.partial(finish_kernel, features, count), in_spec...  2.27 us
    add x3, other arithmetic, terms(): array = sum(parts[1:], parts[0])  1.46 us
  transfers between devices with their start and end apart: 13, of which 7 were waited for; matrix products, arithmetic and copies ran while one was open for 3% of the time, Pallas kernels for 18%

profile of v4, /device:TPU:0, one launch (start us, length us, event | category | flops | bytes accessed | tf_op | source)
XLA Modules:
  0.0 53.5 jit_solution(14753599367772531024)
XLA Ops:
  0.0 2.9 %collective-permute-start = (f32[64,3584]{1,0:T(8,128)}, f32[64,3584]{1,0:T(8,128)S(1)}, u32[]{:S(2)}, u32[]{:S(2)}) collective-permute-start(f32[64,3584]{1,0:T(8,128)} %x_ref.3), channel_id=1, source_target_pairs={{0,16},{8,24},{16,0},{24,8},{1,17},{9,25},{17,1},{25,9},{2,18},{10... | collective-permute-start | bytes 2752520 | tf_op jit(solution)/shard_map/ppermute | solution.py:180
  2.9 4.5 %project.1 = f32[64,256]{1,0:T(8,128)} custom-call(f32[64,3584]{1,0:T(8,128)} %x_ref.3, f32[192,3584]{1,0:T(8,128)} %bitcast.1), custom_call_target="tpu_custom_call" | custom-call | tf_op jit(solution)/shard_map/project/pallas_call | solution.py:67
  7.5 1.5 %collective-permute-start.1 = (f32[64,256]{1,0:T(8,128)}, f32[64,256]{1,0:T(8,128)S(1)}, u32[]{:S(2)}, u32[]{:S(2)}) collective-permute-start(f32[64,256]{1,0:T(8,128)} %project.1), channel_id=1, source_target_pairs={{0,1},{1,0},{2,3},{3,2},{4,5},{5,4},{6,7},{7,6},{8,9},{9,8},{10,11... | collective-permute-start | bytes 196616 | tf_op jit(solution)/shard_map/ppermute | solution.py:180
  9.0 3.0 %collective-permute-done.1 = f32[64,256]{1,0:T(8,128)S(1)} collective-permute-done((f32[64,256]{1,0:T(8,128)}, f32[64,256]{1,0:T(8,128)S(1)}, u32[]{:S(2)}, u32[]{:S(2)}) %collective-permute-start.1) | collective-permute-done | bytes 65568 | tf_op jit(solution)/shard_map/ppermute | solution.py:180
  11.9 0.9 %add.16 = f32[64,256]{1,0:T(8,128)S(1)} add(f32[64,256]{1,0:T(8,128)} %project.1, f32[64,256]{1,0:T(8,128)S(1)} %collective-permute-done.1) | non-fusion elementwise | flops 16384 | bytes 196608 | tf_op jit(solution)/shard_map/add | solution.py:189
  12.8 1.6 %collective-permute-start.2 = (f32[64,256]{1,0:T(8,128)S(1)}, f32[64,256]{1,0:T(8,128)S(1)}, u32[]{:S(2)}, u32[]{:S(2)}) collective-permute-start(f32[64,256]{1,0:T(8,128)S(1)} %add.16), channel_id=1, source_target_pairs={{0,2},{1,3},{2,0},{3,1},{4,6},{5,7},{6,4},{7,5},{8,10},{9,11},{10,... | collective-permute-start | bytes 196616 | tf_op jit(solution)/shard_map/ppermute | solution.py:180
  14.4 2.7 %collective-permute-done.2 = f32[64,256]{1,0:T(8,128)S(1)} collective-permute-done((f32[64,256]{1,0:T(8,128)S(1)}, f32[64,256]{1,0:T(8,128)S(1)}, u32[]{:S(2)}, u32[]{:S(2)}) %collective-permute-start.2) | collective-permute-done | bytes 65568 | tf_op jit(solution)/shard_map/ppermute | solution.py:180
  17.1 2.7 %collective-permute-start.3 = (f32[64,256]{1,0:T(8,128)S(1)}, f32[64,256]{1,0:T(8,128)S(1)}, u32[]{:S(2)}, u32[]{:S(2)}) collective-permute-start(f32[64,256]{1,0:T(8,128)S(1)} %add.17), channel_id=1, source_target_pairs={{0,4},{1,5},{2,6},{3,7},{4,0},{5,1},{6,2},{7,3},{8,12},{9,13},{10,... | collective-permute-start | bytes 196616 | tf_op jit(solution)/shard_map/ppermute | solution.py:180
  19.8 2.6 %collective-permute-done.3 = f32[64,256]{1,0:T(8,128)S(1)} collective-permute-done((f32[64,256]{1,0:T(8,128)S(1)}, f32[64,256]{1,0:T(8,128)S(1)}, u32[]{:S(2)}, u32[]{:S(2)}) %collective-permute-start.3) | collective-permute-done | bytes 65568 | tf_op jit(solution)/shard_map/ppermute | solution.py:180
  22.4 0.0 copy-start.3
  22.4 0.1 collective-permute-start.6
  22.5 0.3 collective-permute-start.5
  22.7 1.6 %collective-permute-start.4 = (f32[64,256]{1,0:T(8,128)S(1)}, f32[64,256]{1,0:T(8,128)S(1)}, u32[]{:S(2)}, u32[]{:S(2)}) collective-permute-start(f32[64,256]{1,0:T(8,128)S(1)} %add.18.p_ref), channel_id=1, source_target_pairs={{0,8},{8,0},{16,24},{24,16},{1,9},{9,1},{17,25},{25,17},{2,10},{10... | collective-permute-start | bytes 196616 | tf_op jit(solution)/shard_map/ppermute | solution.py:180
  24.3 0.0 copy-done
  24.3 0.0 collective-permute-start.7
  24.3 0.0 copy-done.3
  24.3 5.1 %own_part.1.t_ref = f32[64,3584]{1,0:T(8,128)} custom-call(f32[64,256]{1,0:T(8,128)} %copy-done.3, f32[64,3584]{1,0:T(8,128)} %x_ref.3, f32[192,3584]{1,0:T(8,128)} %bitcast.2), custom_call_target="tpu_custom_call" | custom-call | tf_op jit(solution)/shard_map/own_part/pallas_call | solution.py:95
  29.4 0.0 collective-permute-done.6.refs_2_
  29.4 0.0 collective-permute-done.5.refs_1_
  29.5 0.0 copy-start.5
  29.5 0.0 collective-permute-done.4.refs_0_
  29.5 0.0 copy-start.6
  29.5 0.0 collective-permute-done.refs_4_
  29.5 0.0 copy-start.1
  29.5 0.6 %collective-permute-start.8 = (f32[64,3584]{1,0:T(8,128)S(1)}, f32[64,3584]{1,0:T(8,128)}, u32[]{:S(2)}, u32[]{:S(2)}) collective-permute-start(f32[64,3584]{1,0:T(8,128)S(1)} %collective-permute-done.refs_4_), channel_id=1, source_target_pairs={{0,8},{8,0},{16,24},{24,16},{1,9},{9,1},{17,25},{25,17},{2,10},{10... | collective-permute-start | bytes 2752520 | tf_op jit(solution)/shard_map/ppermute | solution.py:180
  30.1 0.5 compare_convert_fusion.flags_ref
  30.6 0.0 collective-permute-done.7.refs_3_
  30.6 1.7 %collective-permute-done.8.refs_5_ = f32[64,3584]{1,0:T(8,128)} collective-permute-done((f32[64,3584]{1,0:T(8,128)S(1)}, f32[64,3584]{1,0:T(8,128)}, u32[]{:S(2)}, u32[]{:S(2)}) %collective-permute-start.8) | collective-permute-done | bytes 917536 | tf_op jit(solution)/shard_map/ppermute | solution.py:180
  32.3 0.0 copy-done.4
  32.3 0.0 copy-done.5
  32.3 0.0 copy-done.6
  32.3 0.0 copy-done.1
  32.3 0.0 copy-done.2
  32.3 5.3 %others_part.1 = (f32[64,3584]{1,0:T(8,128)}, f32[1,64]{1,0:T(1,128)}) custom-call(f32[3]{0:T(128)} %compare_convert_fusion.flags_ref, f32[64,3584]{1,0:T(8,128)} %own_part.1.t_ref, f32[64,256]{1,0:T(8,128)} %copy-done.3, f32[64,256]{1,0:T(8,128)} %copy-done.6, f32[64,256]{1,0:T(8,128)} %copy-done.5, f32[64,256]{1,0:T(8,128)} %copy-done.4, ...), custom_call_target="tpu_custom_call" | custom-call | tf_op jit(solution)/shard_map/others_part/pallas_call | solution.py:133
  37.7 1.5 %collective-permute-start.9 = (f32[1,64]{1,0:T(1,128)}, f32[1,64]{1,0:T(1,128)S(1)}, u32[]{:S(2)}, u32[]{:S(2)}) collective-permute-start(f32[1,64]{1,0:T(1,128)} %get-tuple-element.18), channel_id=1, source_target_pairs={{0,1},{1,0},{2,3},{3,2},{4,5},{5,4},{6,7},{7,6},{8,9},{9,8},{10,11... | collective-permute-start | bytes 776 | tf_op jit(solution)/shard_map/ppermute | solution.py:180
  39.2 2.2 %collective-permute-done.9 = f32[1,64]{1,0:T(1,128)S(1)} collective-permute-done((f32[1,64]{1,0:T(1,128)}, f32[1,64]{1,0:T(1,128)S(1)}, u32[]{:S(2)}, u32[]{:S(2)}) %collective-permute-start.9) | collective-permute-done | bytes 288 | tf_op jit(solution)/shard_map/ppermute | solution.py:180
  41.4 0.6 %add.19.refs_0_ = f32[1,64]{1,0:T(1,128)S(1)} add(f32[1,64]{1,0:T(1,128)} %get-tuple-element.18, f32[1,64]{1,0:T(1,128)S(1)} %collective-permute-done.9) | non-fusion elementwise | flops 64 | bytes 768 | tf_op jit(solution)/shard_map/add | solution.py:189
  42.0 4.2 %collective-permute-start.12 = (f32[1,64]{1,0:T(1,128)S(1)}, f32[1,64]{1,0:T(1,128)S(1)}, u32[]{:S(2)}, u32[]{:S(2)}) collective-permute-start(f32[1,64]{1,0:T(1,128)S(1)} %add.19.refs_0_), channel_id=1, source_target_pairs={{0,6},{1,7},{2,4},{3,5},{4,2},{5,3},{6,0},{7,1},{8,14},{9,15},{10,... | collective-permute-start | bytes 776 | tf_op jit(solution)/shard_map/ppermute | solution.py:180
  46.2 0.0 collective-permute-start.11
  46.2 0.6 %collective-permute-start.10 = (f32[1,64]{1,0:T(1,128)S(1)}, f32[1,64]{1,0:T(1,128)S(1)}, u32[]{:S(2)}, u32[]{:S(2)}) collective-permute-start(f32[1,64]{1,0:T(1,128)S(1)} %add.19.refs_0_), channel_id=1, source_target_pairs={{0,2},{1,3},{2,0},{3,1},{4,6},{5,7},{6,4},{7,5},{8,10},{9,11},{10,... | collective-permute-start | bytes 776 | tf_op jit(solution)/shard_map/ppermute | solution.py:180
  46.8 0.9 %collective-permute-done.12.refs_3_ = f32[1,64]{1,0:T(1,128)S(1)} collective-permute-done((f32[1,64]{1,0:T(1,128)S(1)}, f32[1,64]{1,0:T(1,128)S(1)}, u32[]{:S(2)}, u32[]{:S(2)}) %collective-permute-start.12) | collective-permute-done | bytes 288 | tf_op jit(solution)/shard_map/ppermute | solution.py:180
  47.7 2.9 %collective-permute-done.11.refs_2_ = f32[1,64]{1,0:T(1,128)S(1)} collective-permute-done((f32[1,64]{1,0:T(1,128)S(1)}, f32[1,64]{1,0:T(1,128)S(1)}, u32[]{:S(2)}, u32[]{:S(2)}) %collective-permute-start.11) | collective-permute-done | bytes 288 | tf_op jit(solution)/shard_map/ppermute | solution.py:180
  50.7 0.0 collective-permute-done.10.refs_1_
  50.7 0.0 copy-done.7
  50.7 0.0 copy-done.8
  50.7 0.5 copy-done.9
  51.2 0.1 copy-done.10
  51.2 2.3 %finish.1 = f32[64,3584]{1,0:T(8,128)} custom-call(f32[64,3584]{1,0:T(8,128)} %get-tuple-element.17.updated_ref, f32[1,64]{1,0:T(1,128)} %copy-done.7, f32[1,64]{1,0:T(1,128)} %copy-done.10, f32[1,64]{1,0:T(1,128)} %copy-done.9, f32[1,64]{1,0:T(1,128)} %copy-done.8), custom_call_target="tpu_custom_call" | custom-call | tf_op jit(solution)/shard_map/finish/pallas_call | solution.py:166
  (9 shorter events, 0.0 us)
Async XLA Ops:
  0.0 24.3 %copy-start = (f32[64,3584]{1,0:T(8,128)S(1)}, f32[64,3584]{1,0:T(8,128)}, u32[]{:S(2)}) copy-start(f32[64,3584]{1,0:T(8,128)} %x_ref.3) | copy-start | bytes 2752516
  0.0 29.5 %collective-permute-start = (f32[64,3584]{1,0:T(8,128)}, f32[64,3584]{1,0:T(8,128)S(1)}, u32[]{:S(2)}, u32[]{:S(2)}) collective-permute-start(f32[64,3584]{1,0:T(8,128)} %x_ref.3), channel_id=1, source_target_pairs={{0,16},{8,24},{16,0},{24,8},{1,17},{9,25},{17,1},{25,9},{2,18},{10... | collective-permute-start | bytes 2752520 | tf_op jit(solution)/shard_map/ppermute | solution.py:180
  7.5 4.5 %collective-permute-start.1 = (f32[64,256]{1,0:T(8,128)}, f32[64,256]{1,0:T(8,128)S(1)}, u32[]{:S(2)}, u32[]{:S(2)}) collective-permute-start(f32[64,256]{1,0:T(8,128)} %project.1), channel_id=1, source_target_pairs={{0,1},{1,0},{2,3},{3,2},{4,5},{5,4},{6,7},{7,6},{8,9},{9,8},{10,11... | collective-permute-start | bytes 196616 | tf_op jit(solution)/shard_map/ppermute | solution.py:180
  12.8 4.3 %collective-permute-start.2 = (f32[64,256]{1,0:T(8,128)S(1)}, f32[64,256]{1,0:T(8,128)S(1)}, u32[]{:S(2)}, u32[]{:S(2)}) collective-permute-start(f32[64,256]{1,0:T(8,128)S(1)} %add.16), channel_id=1, source_target_pairs={{0,2},{1,3},{2,0},{3,1},{4,6},{5,7},{6,4},{7,5},{8,10},{9,11},{10,... | collective-permute-start | bytes 196616 | tf_op jit(solution)/shard_map/ppermute | solution.py:180
  17.1 5.2 %collective-permute-start.3 = (f32[64,256]{1,0:T(8,128)S(1)}, f32[64,256]{1,0:T(8,128)S(1)}, u32[]{:S(2)}, u32[]{:S(2)}) collective-permute-start(f32[64,256]{1,0:T(8,128)S(1)} %add.17), channel_id=1, source_target_pairs={{0,4},{1,5},{2,6},{3,7},{4,0},{5,1},{6,2},{7,3},{8,12},{9,13},{10,... | collective-permute-start | bytes 196616 | tf_op jit(solution)/shard_map/ppermute | solution.py:180
  22.4 1.9 %copy-start.3 = (f32[64,256]{1,0:T(8,128)}, f32[64,256]{1,0:T(8,128)S(1)}, u32[]{:S(2)}) copy-start(f32[64,256]{1,0:T(8,128)S(1)} %add.18.p_ref) | copy-start | bytes 196612
  22.4 7.1 %collective-permute-start.6 = (f32[64,256]{1,0:T(8,128)S(1)}, f32[64,256]{1,0:T(8,128)S(1)}, u32[]{:S(2)}, u32[]{:S(2)}) collective-permute-start(f32[64,256]{1,0:T(8,128)S(1)} %add.18.p_ref), channel_id=1, source_target_pairs={{0,24},{8,16},{16,8},{24,0},{1,25},{9,17},{17,9},{25,1},{2,26},{10... | collective-permute-start | bytes 196616 | tf_op jit(solution)/shard_map/ppermute | solution.py:180
  22.5 7.0 %collective-permute-start.5 = (f32[64,256]{1,0:T(8,128)S(1)}, f32[64,256]{1,0:T(8,128)S(1)}, u32[]{:S(2)}, u32[]{:S(2)}) collective-permute-start(f32[64,256]{1,0:T(8,128)S(1)} %add.18.p_ref), channel_id=1, source_target_pairs={{0,16},{8,24},{16,0},{24,8},{1,17},{9,25},{17,1},{25,9},{2,18},{10... | collective-permute-start | bytes 196616 | tf_op jit(solution)/shard_map/ppermute | solution.py:180
  22.7 6.7 %collective-permute-start.4 = (f32[64,256]{1,0:T(8,128)S(1)}, f32[64,256]{1,0:T(8,128)S(1)}, u32[]{:S(2)}, u32[]{:S(2)}) collective-permute-start(f32[64,256]{1,0:T(8,128)S(1)} %add.18.p_ref), channel_id=1, source_target_pairs={{0,8},{8,0},{16,24},{24,16},{1,9},{9,1},{17,25},{25,17},{2,10},{10... | collective-permute-start | bytes 196616 | tf_op jit(solution)/shard_map/ppermute | solution.py:180
  24.3 6.3 %collective-permute-start.7 = (f32[64,3584]{1,0:T(8,128)S(1)}, f32[64,3584]{1,0:T(8,128)S(1)}, u32[]{:S(2)}, u32[]{:S(2)}) collective-permute-start(f32[64,3584]{1,0:T(8,128)S(1)} %copy-done), channel_id=1, source_target_pairs={{0,8},{8,0},{16,24},{24,16},{1,9},{9,1},{17,25},{25,17},{2,10},{10... | collective-permute-start | bytes 2752520 | tf_op jit(solution)/shard_map/ppermute | solution.py:180
  29.4 2.9 %copy-start.4 = (f32[64,256]{1,0:T(8,128)}, f32[64,256]{1,0:T(8,128)S(1)}, u32[]{:S(2)}) copy-start(f32[64,256]{1,0:T(8,128)S(1)} %collective-permute-done.6.refs_2_) | copy-start | bytes 196612
  29.5 2.9 %copy-start.5 = (f32[64,256]{1,0:T(8,128)}, f32[64,256]{1,0:T(8,128)S(1)}, u32[]{:S(2)}) copy-start(f32[64,256]{1,0:T(8,128)S(1)} %collective-permute-done.5.refs_1_) | copy-start | bytes 196612
  29.5 2.8 %copy-start.6 = (f32[64,256]{1,0:T(8,128)}, f32[64,256]{1,0:T(8,128)S(1)}, u32[]{:S(2)}) copy-start(f32[64,256]{1,0:T(8,128)S(1)} %collective-permute-done.4.refs_0_) | copy-start | bytes 196612
  29.5 2.8 %copy-start.1 = (f32[64,3584]{1,0:T(8,128)}, f32[64,3584]{1,0:T(8,128)S(1)}, u32[]{:S(2)}) copy-start(f32[64,3584]{1,0:T(8,128)S(1)} %collective-permute-done.refs_4_) | copy-start | bytes 2752516
  29.5 2.8 %collective-permute-start.8 = (f32[64,3584]{1,0:T(8,128)S(1)}, f32[64,3584]{1,0:T(8,128)}, u32[]{:S(2)}, u32[]{:S(2)}) collective-permute-start(f32[64,3584]{1,0:T(8,128)S(1)} %collective-permute-done.refs_4_), channel_id=1, source_target_pairs={{0,8},{8,0},{16,24},{24,16},{1,9},{9,1},{17,25},{25,17},{2,10},{10... | collective-permute-start | bytes 2752520 | tf_op jit(solution)/shard_map/ppermute | solution.py:180
  30.6 1.7 %copy-start.2 = (f32[64,3584]{1,0:T(8,128)}, f32[64,3584]{1,0:T(8,128)S(1)}, u32[]{:S(2)}) copy-start(f32[64,3584]{1,0:T(8,128)S(1)} %collective-permute-done.7.refs_3_) | copy-start | bytes 2752516
  37.7 3.8 %collective-permute-start.9 = (f32[1,64]{1,0:T(1,128)}, f32[1,64]{1,0:T(1,128)S(1)}, u32[]{:S(2)}, u32[]{:S(2)}) collective-permute-start(f32[1,64]{1,0:T(1,128)} %get-tuple-element.18), channel_id=1, source_target_pairs={{0,1},{1,0},{2,3},{3,2},{4,5},{5,4},{6,7},{7,6},{8,9},{9,8},{10,11... | collective-permute-start | bytes 776 | tf_op jit(solution)/shard_map/ppermute | solution.py:180
  42.0 8.6 %copy-start.7 = (f32[1,64]{1,0:T(1,128)}, f32[1,64]{1,0:T(1,128)S(1)}, u32[]{:S(2)}) copy-start(f32[1,64]{1,0:T(1,128)S(1)} %add.19.refs_0_) | copy-start | bytes 772
  42.0 5.7 %collective-permute-start.12 = (f32[1,64]{1,0:T(1,128)S(1)}, f32[1,64]{1,0:T(1,128)S(1)}, u32[]{:S(2)}, u32[]{:S(2)}) collective-permute-start(f32[1,64]{1,0:T(1,128)S(1)} %add.19.refs_0_), channel_id=1, source_target_pairs={{0,6},{1,7},{2,4},{3,5},{4,2},{5,3},{6,0},{7,1},{8,14},{9,15},{10,... | collective-permute-start | bytes 776 | tf_op jit(solution)/shard_map/ppermute | solution.py:180
  46.2 4.4 %collective-permute-start.11 = (f32[1,64]{1,0:T(1,128)S(1)}, f32[1,64]{1,0:T(1,128)S(1)}, u32[]{:S(2)}, u32[]{:S(2)}) collective-permute-start(f32[1,64]{1,0:T(1,128)S(1)} %add.19.refs_0_), channel_id=1, source_target_pairs={{0,4},{1,5},{2,6},{3,7},{4,0},{5,1},{6,2},{7,3},{8,12},{9,13},{10,... | collective-permute-start | bytes 776 | tf_op jit(solution)/shard_map/ppermute | solution.py:180
  46.2 4.4 %collective-permute-start.10 = (f32[1,64]{1,0:T(1,128)S(1)}, f32[1,64]{1,0:T(1,128)S(1)}, u32[]{:S(2)}, u32[]{:S(2)}) collective-permute-start(f32[1,64]{1,0:T(1,128)S(1)} %add.19.refs_0_), channel_id=1, source_target_pairs={{0,2},{1,3},{2,0},{3,1},{4,6},{5,7},{6,4},{7,5},{8,10},{9,11},{10,... | collective-permute-start | bytes 776 | tf_op jit(solution)/shard_map/ppermute | solution.py:180
  47.7 2.9 %copy-start.8 = (f32[1,64]{1,0:T(1,128)}, f32[1,64]{1,0:T(1,128)S(1)}, u32[]{:S(2)}) copy-start(f32[1,64]{1,0:T(1,128)S(1)} %collective-permute-done.12.refs_3_) | copy-start | bytes 772
  50.7 0.5 copy-start.9
  50.7 0.6 %copy-start.10 = (f32[1,64]{1,0:T(1,128)}, f32[1,64]{1,0:T(1,128)S(1)}, u32[]{:S(2)}) copy-start(f32[1,64]{1,0:T(1,128)S(1)} %collective-permute-done.10.refs_1_) | copy-start | bytes 772

commit v5 on v4

--- a/solution.py
+++ b/solution.py
@@ -11,6 +11,7 @@
 epsilon = 1e-06
 lanes = 128
 in_vmem = pl.BlockSpec(memory_space=pltpu.VMEM)
+params = pltpu.CompilerParams(vmem_limit_bytes=16 << 20)
 
 
 def tile_of(columns, most):
@@ -69,6 +70,8 @@
         in_specs=[in_vmem, in_vmem],
         out_specs=in_vmem,
         out_shape=jax.ShapeDtypeStruct((per_group, width), jnp.float32),
+        compiler_params=params,
+        cost_estimate=pl.CostEstimate(flops=1024, bytes_accessed=1024, transcendentals=0),
         name="project",
     )(x, sample)
 
@@ -80,12 +83,12 @@
     shared = product(images, images * scale, transposed=True)
     later = lax.broadcasted_iota(jnp.int32, shared.shape, 0)
     earlier = lax.broadcasted_iota(jnp.int32, shared.shape, 1)
-    coupling = halves(jnp.where(earlier < later, shared * (-step_rate / (features * rows)), 0.0))
-    images = halves(images * (step_rate / rows))
+    coupling = jnp.where(earlier < later, shared * (-step_rate / (features * rows)), 0.0)
+    weights = halves(jnp.concatenate([images * (step_rate / rows), coupling], axis=1))
 
     def body(here, carry):
         x = x_ref[:, here]
-        out_ref[:, here] = scale * x + (product(images, s_ref[:, here]) + product(coupling, x))
+        out_ref[:, here] = scale * x + product(weights, jnp.concatenate([s_ref[:, here], x], axis=0))
         return carry
 
     loop(x_ref.shape[1], 4, body, 0)
@@ -97,6 +100,8 @@
         in_specs=[in_vmem] * 3,
         out_specs=in_vmem,
         out_shape=jax.ShapeDtypeStruct(x.shape, jnp.float32),
+        compiler_params=params,
+        cost_estimate=pl.CostEstimate(flops=1024, bytes_accessed=1024, transcendentals=0),
         name="own_part",
     )(projected, x, sample)
 
@@ -107,15 +112,21 @@
     return down == across
 
 
-def others_kernel(features, rows, count, flags_ref, t_ref, p_ref, *refs):
+def owner(group, step, size):
+    return (group + step) % size if size & (size - 1) else group ^ step
+
+
+def others_kernel(features, rows, count, t_ref, p_ref, *refs):
     projected_refs, x_refs = refs[:count], refs[count : 2 * count]
     out_ref, squares_ref = refs[2 * count :]
     per_group, columns = t_ref.shape
     images = p_ref[:, :rows] * (scale_of(p_ref[:, rows : rows + 1], features) * (-step_rate / (features * rows)))
+    group = lax.axis_index("comp")
     others = []
     for k in range(count):
+        earlier = (owner(group, k + 1, count + 1) < group).astype(jnp.float32)
         scale = scale_of(projected_refs[k][:, rows : rows + 1], features)
-        others.append(projected_refs[k][:, :rows] * (scale * scale * flags_ref[k]))
+        others.append(projected_refs[k][:, :rows] * (scale * scale * earlier))
     coupling = halves(product(images, jnp.concatenate(others, axis=0), transposed=True))
 
     def body(here, squares):
@@ -128,18 +139,20 @@
     squares_ref[...] = jnp.sum(jnp.where(diagonal(per_group), spread, 0.0), axis=0, keepdims=True)
 
 
-def others_part(flags, partly, projected, others, blocks, rows, features):
+def others_part(partly, projected, others, blocks, rows, features):
     count = len(blocks)
     return pl.pallas_call(
         functools.partial(others_kernel, features, rows, count),
-        in_specs=[pl.BlockSpec(memory_space=pltpu.SMEM)] + [in_vmem] * (2 + 2 * count),
+        in_specs=[in_vmem] * (2 + 2 * count),
         out_specs=[in_vmem, in_vmem],
         out_shape=[
             jax.ShapeDtypeStruct(partly.shape, jnp.float32),
             jax.ShapeDtypeStruct((1, partly.shape[0]), jnp.float32),
         ],
+        compiler_params=params,
+        cost_estimate=pl.CostEstimate(flops=1024, bytes_accessed=1024, transcendentals=0),
         name="others_part",
-    )(flags, partly, projected, *others, *blocks)
+    )(partly, projected, *others, *blocks)
 
 
 def finish_kernel(features, count, updated_ref, *refs):
@@ -172,6 +185,8 @@
             pltpu.VMEM(updated.shape, jnp.float32),
             pltpu.SemaphoreType.DMA((updated.shape[1] // tile_of(updated.shape[1], 7),)),
         ],
+        compiler_params=params,
+        cost_estimate=pl.CostEstimate(flops=1024, bytes_accessed=1024, transcendentals=0),
         name="finish",
     )(updated, *squares)
 
@@ -197,14 +212,8 @@
     if size & (size - 1):
         arrays = lax.all_gather(own, "comp")
         group = lax.axis_index("comp")
-        return [arrays[(group + step) % size] for step in range(1, size)]
+        return [arrays[owner(group, step, size)] for step in range(1, size)]
     return [exchange(own, "comp", step) for step in range(1, size)]
-
-
-def owners(size):
-    group = lax.axis_index("comp")
-    steps = jnp.arange(1, size, dtype=jnp.int32)
-    return (group + steps) % size if size & (size - 1) else group ^ steps
 
 
 def shards(samples, start_vectors):
@@ -213,21 +222,24 @@
     sample = samples[0]
     rows = sample.shape[0]
     features = sample.shape[1] * feat
-    flags = (owners(comp) < lax.axis_index("comp")).astype(jnp.float32)
-
-    straight = {step: exchange(start_vectors, "comp", step) for step in range(1, comp) if step % 2 == 0 or step == 1}
+    even = comp & (comp - 1) == 0
+    straight = {}
+    for step in range(1, comp):
+        if even and (step == 1 or step % 2 == 0):
+            straight[step] = exchange(start_vectors, "comp", step)
     parts = terms(project(start_vectors, sample), "feat", 1)
     projected = sum(parts[1:], parts[0])
     others = gather(projected, comp)
-    partly = own_part(projected, start_vectors, sample, features)
-    blocks = []
-    for step in range(1, comp):
+    blocks = [] if even else gather(start_vectors, comp)
+    own = projected
+    for step in range(1, comp if even else 1):
         if step in straight:
             blocks.append(straight[step])
         else:
-            arrived, partly, others = lax.optimization_barrier((straight[step - 1], partly, others))
+            arrived, others[0], own = lax.optimization_barrier((straight[step - 1], others[0], own))
             blocks.append(exchange(arrived, "comp", 1))
-    updated, squares = others_part(flags, partly, projected, others, blocks, rows, features)
+    partly = own_part(own, start_vectors, sample, features)
+    updated, squares = others_part(partly, projected, others, blocks, rows, features)
     return finish(updated, terms(squares, "feat", 2), features)
 
 

time: 53.7 us -> 44.9 us (0.84)
  Pallas kernels: 17.2 us -> 7.17 us
  local copies, waits for them, and re-layouts: 0.6 us -> 2.96 us
  other arithmetic: 1.99 us -> 0.03 us
  waiting for transfers between devices: 16 us -> 17 us
    pallas_call x1, Pallas kernels: 5.11 us -> 1.9 us  [own_part(): pl.pallas_call(functools.partial(own_kernel, features), in_specs=[in_vmem...]
    pallas_call x1, Pallas kernels: 5.33 us -> 2.35 us  [others_part(): pl.pallas_call(functools.partial(others_kernel, features, rows, count), i...]
    pallas_call x1, Pallas kernels: 4.52 us -> 1.83 us  [project(): pl.pallas_call(project_kernel, in_specs=[in_vmem, in_vmem], out_specs=in_...]
    unnamed x22 -> x4, local copies, waits for them, and re-layouts: 0.6 us -> 2.96 us
    add x3, other arithmetic: 1.46 us -> 0.02 us  [terms(): array = sum(parts[1:], parts[0])]
    pallas_call x1, Pallas kernels: 2.27 us -> 1.09 us  [finish(): pl.pallas_call(functools.partial(finish_kernel, features, count), in_spec...]
    ppermute x13, waiting for transfers between devices: 16 us -> 17 us  [exchange(): lax.ppermute(array, axis, [(i, i ^ step) for i in range(lax.axis_size(axi...]
  transfers between devices with their start and end apart: 13 -> 13, of which waited for: 7 -> 10; matrix products, arithmetic and copies ran while one was open for 3% -> 0% of each run, Pallas kernels for 18% -> 8%
where the time goes in v5:
time: 44.9 us; the launch traced here: 44.7 us
  starting transfers between devices  17.5 us (39%)
  waiting for transfers between devices  17 us (38%)
  Pallas kernels  7.17 us (16%)
  local copies, waits for them, and re-layouts  2.96 us (7%)
    ppermute x13, starting transfers between devices, exchange(): lax.ppermute(array, axis, [(i, i ^ step) for i in range(lax.axis_size(axi...  17.5 us
    ppermute x13, waiting for transfers between devices, exchange(): lax.ppermute(array, axis, [(i, i ^ step) for i in range(lax.axis_size(axi...  17 us
    unnamed x4, local copies, waits for them, and re-layouts  2.96 us
    pallas_call x1, Pallas kernels, others_part(): pl.pallas_call(functools.partial(others_kernel, features, rows, count), i...  2.35 us
    pallas_call x1, Pallas kernels, own_part(): pl.pallas_call(functools.partial(own_kernel, features), in_specs=[in_vmem...  1.9 us
    pallas_call x1, Pallas kernels, project(): pl.pallas_call(project_kernel, in_specs=[in_vmem, in_vmem], out_specs=in_...  1.83 us
    pallas_call x1, Pallas kernels, finish(): pl.pallas_call(functools.partial(finish_kernel, features, count), in_spec...  1.09 us
  transfers between devices with their start and end apart: 13, of which 10 were waited for; matrix products, arithmetic and copies ran while one was open for 0% of the time, Pallas kernels for 8%

profile of v5, /device:TPU:0, one launch (start us, length us, event | category | flops | bytes accessed | tf_op | source)
XLA Modules:
  0.0 44.7 jit_solution(6751885469027000315)
XLA Ops:
  0.0 2.9 %collective-permute-start = (f32[64,3584]{1,0:T(8,128)}, f32[64,3584]{1,0:T(8,128)S(1)}, u32[]{:S(2)}, u32[]{:S(2)}) collective-permute-start(f32[64,3584]{1,0:T(8,128)} %x_ref.3), channel_id=1, source_target_pairs={{0,16},{8,24},{16,0},{24,8},{1,17},{9,25},{17,1},{25,9},{2,18},{10... | collective-permute-start | bytes 2752520 | tf_op jit(solution)/shard_map/ppermute | solution.py:195
  2.9 0.0 copy-start
  2.9 1.8 %copy-done = f32[1,192,3584]{2,1,0:T(8,128)S(1)} copy-done((f32[1,192,3584]{2,1,0:T(8,128)S(1)}, f32[1,192,3584]{2,1,0:T(8,128)}, u32[]{:S(2)}) %copy-start) | copy-done | bytes 2752536
  4.7 0.0 copy-start.1
  4.7 1.2 %copy-done.1 = f32[64,3584]{1,0:T(8,128)S(1)} copy-done((f32[64,3584]{1,0:T(8,128)S(1)}, f32[64,3584]{1,0:T(8,128)}, u32[]{:S(2)}) %copy-start.1) | copy-done | bytes 917528
  5.9 1.8 %project.1 = f32[64,256]{1,0:T(8,128)S(1)} custom-call(f32[64,3584]{1,0:T(8,128)S(1)} %copy-done.1, f32[192,3584]{1,0:T(8,128)S(1)} %bitcast.1), custom_call_target="tpu_custom_call" | custom-call | flops 1024 | bytes 1024 | tf_op jit(solution)/shard_map/project/pallas_call | solution.py:68
  7.7 1.6 %collective-permute-start.1 = (f32[64,256]{1,0:T(8,128)S(1)}, f32[64,256]{1,0:T(8,128)S(1)}, u32[]{:S(2)}, u32[]{:S(2)}) collective-permute-start(f32[64,256]{1,0:T(8,128)S(1)} %project.1), channel_id=1, source_target_pairs={{0,1},{1,0},{2,3},{3,2},{4,5},{5,4},{6,7},{7,6},{8,9},{9,8},{10,11... | collective-permute-start | bytes 196616 | tf_op jit(solution)/shard_map/ppermute | solution.py:195
  9.3 2.7 %collective-permute-done.1 = f32[64,256]{1,0:T(8,128)S(1)} collective-permute-done((f32[64,256]{1,0:T(8,128)S(1)}, f32[64,256]{1,0:T(8,128)S(1)}, u32[]{:S(2)}, u32[]{:S(2)}) %collective-permute-start.1) | collective-permute-done | bytes 65568 | tf_op jit(solution)/shard_map/ppermute | solution.py:195
  12.1 1.6 %collective-permute-start.2 = (f32[64,256]{1,0:T(8,128)S(1)}, f32[64,256]{1,0:T(8,128)S(1)}, u32[]{:S(2)}, u32[]{:S(2)}) collective-permute-start(f32[64,256]{1,0:T(8,128)S(1)} %add.12), channel_id=1, source_target_pairs={{0,2},{1,3},{2,0},{3,1},{4,6},{5,7},{6,4},{7,5},{8,10},{9,11},{10,... | collective-permute-start | bytes 196616 | tf_op jit(solution)/shard_map/ppermute | solution.py:195
  13.7 2.7 %collective-permute-done.2 = f32[64,256]{1,0:T(8,128)S(1)} collective-permute-done((f32[64,256]{1,0:T(8,128)S(1)}, f32[64,256]{1,0:T(8,128)S(1)}, u32[]{:S(2)}, u32[]{:S(2)}) %collective-permute-start.2) | collective-permute-done | bytes 65568 | tf_op jit(solution)/shard_map/ppermute | solution.py:195
  16.4 2.6 %collective-permute-start.3 = (f32[64,256]{1,0:T(8,128)S(1)}, f32[64,256]{1,0:T(8,128)S(1)}, u32[]{:S(2)}, u32[]{:S(2)}) collective-permute-start(f32[64,256]{1,0:T(8,128)S(1)} %add.13), channel_id=1, source_target_pairs={{0,4},{1,5},{2,6},{3,7},{4,0},{5,1},{6,2},{7,3},{8,12},{9,13},{10,... | collective-permute-start | bytes 196616 | tf_op jit(solution)/shard_map/ppermute | solution.py:195
  19.1 2.6 %collective-permute-done.3 = f32[64,256]{1,0:T(8,128)S(1)} collective-permute-done((f32[64,256]{1,0:T(8,128)S(1)}, f32[64,256]{1,0:T(8,128)S(1)}, u32[]{:S(2)}, u32[]{:S(2)}) %collective-permute-start.3) | collective-permute-done | bytes 65568 | tf_op jit(solution)/shard_map/ppermute | solution.py:195
  21.7 0.1 collective-permute-start.4
  21.7 0.5 %collective-permute-start.7 = (f32[64,3584]{1,0:T(8,128)S(1)}, f32[64,3584]{1,0:T(8,128)S(1)}, u32[]{:S(2)}, u32[]{:S(2)}) collective-permute-start(f32[64,3584]{1,0:T(8,128)S(1)} %copy-done.1), channel_id=1, source_target_pairs={{0,8},{8,0},{16,24},{24,16},{1,9},{9,1},{17,25},{25,17},{2,10},{10... | collective-permute-start | bytes 2752520 | tf_op jit(solution)/shard_map/ppermute | solution.py:195
  22.2 0.7 %collective-permute-done.4.refs_0_ = f32[64,256]{1,0:T(8,128)S(1)} collective-permute-done((f32[64,256]{1,0:T(8,128)S(1)}, f32[64,256]{1,0:T(8,128)S(1)}, u32[]{:S(2)}, u32[]{:S(2)}) %collective-permute-start.4) | collective-permute-done | bytes 65568 | tf_op jit(solution)/shard_map/ppermute | solution.py:195
  23.0 0.5 %collective-permute-done.refs_4_ = f32[64,3584]{1,0:T(8,128)S(1)} collective-permute-done((f32[64,3584]{1,0:T(8,128)}, f32[64,3584]{1,0:T(8,128)S(1)}, u32[]{:S(2)}, u32[]{:S(2)}) %collective-permute-start) | collective-permute-done | bytes 917536 | tf_op jit(solution)/shard_map/ppermute | solution.py:195
  23.5 0.0 collective-permute-start.8
  23.5 1.9 %collective-permute-start.6 = (f32[64,256]{1,0:T(8,128)S(1)}, f32[64,256]{1,0:T(8,128)S(1)}, u32[]{:S(2)}, u32[]{:S(2)}) collective-permute-start(f32[64,256]{1,0:T(8,128)S(1)} %add.14.p_ref), channel_id=1, source_target_pairs={{0,24},{8,16},{16,8},{24,0},{1,25},{9,17},{17,9},{25,1},{2,26},{10... | collective-permute-start | bytes 196616 | tf_op jit(solution)/shard_map/ppermute | solution.py:195
  25.4 0.3 collective-permute-start.5
  25.6 1.9 %own_part.1.t_ref = f32[64,3584]{1,0:T(8,128)S(1)} custom-call(f32[64,256]{1,0:T(8,128)S(1)} %add.14.p_ref, f32[64,3584]{1,0:T(8,128)S(1)} %copy-done.1, f32[192,3584]{1,0:T(8,128)S(1)} %bitcast.2), custom_call_target="tpu_custom_call" | custom-call | flops 1024 | bytes 1024 | tf_op jit(solution)/shard_map/own_part/pallas_call | solution.py:98
  27.5 0.3 collective-permute-done.6.refs_2_
  27.8 1.8 %collective-permute-done.5.refs_1_ = f32[64,256]{1,0:T(8,128)S(1)} collective-permute-done((f32[64,256]{1,0:T(8,128)S(1)}, f32[64,256]{1,0:T(8,128)S(1)}, u32[]{:S(2)}, u32[]{:S(2)}) %collective-permute-start.5) | collective-permute-done | bytes 65568 | tf_op jit(solution)/shard_map/ppermute | solution.py:195
  29.6 0.0 collective-permute-done.7.refs_3_
  29.6 0.0 collective-permute-done.8.refs_5_
  29.6 2.3 %others_part.1 = (f32[64,3584]{1,0:T(8,128)S(1)}, f32[1,64]{1,0:T(1,128)S(1)}) custom-call(f32[64,3584]{1,0:T(8,128)S(1)} %own_part.1.t_ref, f32[64,256]{1,0:T(8,128)S(1)} %add.14.p_ref, f32[64,256]{1,0:T(8,128)S(1)} %collective-permute-done.4.refs_0_, f32[64,256]{1,0:T(8,128)S(1)} %collective-permute-done.5.refs_1_, ...), custom_call_target="tpu_custom_call" | custom-call | flops 1024 | bytes 1024 | tf_op jit(solution)/shard_map/others_part/pallas_call | solution.py:144
  32.0 1.6 %collective-permute-start.9 = (f32[1,64]{1,0:T(1,128)S(1)}, f32[1,64]{1,0:T(1,128)S(1)}, u32[]{:S(2)}, u32[]{:S(2)}) collective-permute-start(f32[1,64]{1,0:T(1,128)S(1)} %get-tuple-element.14), channel_id=1, source_target_pairs={{0,1},{1,0},{2,3},{3,2},{4,5},{5,4},{6,7},{7,6},{8,9},{9,8},{10,11... | collective-permute-start | bytes 776 | tf_op jit(solution)/shard_map/ppermute | solution.py:195
  33.6 2.0 %collective-permute-done.9 = f32[1,64]{1,0:T(1,128)S(1)} collective-permute-done((f32[1,64]{1,0:T(1,128)S(1)}, f32[1,64]{1,0:T(1,128)S(1)}, u32[]{:S(2)}, u32[]{:S(2)}) %collective-permute-start.9) | collective-permute-done | bytes 288 | tf_op jit(solution)/shard_map/ppermute | solution.py:195
  35.6 3.6 %collective-permute-start.12 = (f32[1,64]{1,0:T(1,128)S(1)}, f32[1,64]{1,0:T(1,128)S(1)}, u32[]{:S(2)}, u32[]{:S(2)}) collective-permute-start(f32[1,64]{1,0:T(1,128)S(1)} %add.15.refs_0_), channel_id=1, source_target_pairs={{0,6},{1,7},{2,4},{3,5},{4,2},{5,3},{6,0},{7,1},{8,14},{9,15},{10,... | collective-permute-start | bytes 776 | tf_op jit(solution)/shard_map/ppermute | solution.py:195
  39.2 0.0 collective-permute-start.11
  39.2 0.8 %collective-permute-start.10 = (f32[1,64]{1,0:T(1,128)S(1)}, f32[1,64]{1,0:T(1,128)S(1)}, u32[]{:S(2)}, u32[]{:S(2)}) collective-permute-start(f32[1,64]{1,0:T(1,128)S(1)} %add.15.refs_0_), channel_id=1, source_target_pairs={{0,2},{1,3},{2,0},{3,1},{4,6},{5,7},{6,4},{7,5},{8,10},{9,11},{10,... | collective-permute-start | bytes 776 | tf_op jit(solution)/shard_map/ppermute | solution.py:195
  40.0 0.9 %collective-permute-done.12.refs_3_ = f32[1,64]{1,0:T(1,128)S(1)} collective-permute-done((f32[1,64]{1,0:T(1,128)S(1)}, f32[1,64]{1,0:T(1,128)S(1)}, u32[]{:S(2)}, u32[]{:S(2)}) %collective-permute-start.12) | collective-permute-done | bytes 288 | tf_op jit(solution)/shard_map/ppermute | solution.py:195
  40.9 2.7 %collective-permute-done.11.refs_2_ = f32[1,64]{1,0:T(1,128)S(1)} collective-permute-done((f32[1,64]{1,0:T(1,128)S(1)}, f32[1,64]{1,0:T(1,128)S(1)}, u32[]{:S(2)}, u32[]{:S(2)}) %collective-permute-start.11) | collective-permute-done | bytes 288 | tf_op jit(solution)/shard_map/ppermute | solution.py:195
  43.6 0.0 collective-permute-done.10.refs_1_
  43.6 1.1 %finish.1 = f32[64,3584]{1,0:T(8,128)} custom-call(f32[64,3584]{1,0:T(8,128)S(1)} %get-tuple-element.13.updated_ref, f32[1,64]{1,0:T(1,128)S(1)} %add.15.refs_0_, f32[1,64]{1,0:T(1,128)S(1)} %collective-permute-done.10.refs_1_, f32[1,64]{1,0:T(1,128)S(1)} %collective-permute-done.11.refs_2_, f32[1,64]{1,0:T(1,128)S(1)} %collective-permute-done.12.refs_3_), custom_call_target="tpu_custom_call" | custom-call | flops 1024 | bytes 1024 | tf_op jit(solution)/shard_map/finish/pallas_call | solution.py:179
  (4 shorter events, 0.0 us)
Async XLA Ops:
  0.0 23.5 %collective-permute-start = (f32[64,3584]{1,0:T(8,128)}, f32[64,3584]{1,0:T(8,128)S(1)}, u32[]{:S(2)}, u32[]{:S(2)}) collective-permute-start(f32[64,3584]{1,0:T(8,128)} %x_ref.3), channel_id=1, source_target_pairs={{0,16},{8,24},{16,0},{24,8},{1,17},{9,25},{17,1},{25,9},{2,18},{10... | collective-permute-start | bytes 2752520 | tf_op jit(solution)/shard_map/ppermute | solution.py:195
  2.9 1.8 %copy-start = (f32[1,192,3584]{2,1,0:T(8,128)S(1)}, f32[1,192,3584]{2,1,0:T(8,128)}, u32[]{:S(2)}) copy-start(f32[1,192,3584]{2,1,0:T(8,128)} %param.2) | copy-start | bytes 8257540
  4.7 1.2 %copy-start.1 = (f32[64,3584]{1,0:T(8,128)S(1)}, f32[64,3584]{1,0:T(8,128)}, u32[]{:S(2)}) copy-start(f32[64,3584]{1,0:T(8,128)} %x_ref.3) | copy-start | bytes 2752516
  7.7 4.3 %collective-permute-start.1 = (f32[64,256]{1,0:T(8,128)S(1)}, f32[64,256]{1,0:T(8,128)S(1)}, u32[]{:S(2)}, u32[]{:S(2)}) collective-permute-start(f32[64,256]{1,0:T(8,128)S(1)} %project.1), channel_id=1, source_target_pairs={{0,1},{1,0},{2,3},{3,2},{4,5},{5,4},{6,7},{7,6},{8,9},{9,8},{10,11... | collective-permute-start | bytes 196616 | tf_op jit(solution)/shard_map/ppermute | solution.py:195
  12.1 4.3 %collective-permute-start.2 = (f32[64,256]{1,0:T(8,128)S(1)}, f32[64,256]{1,0:T(8,128)S(1)}, u32[]{:S(2)}, u32[]{:S(2)}) collective-permute-start(f32[64,256]{1,0:T(8,128)S(1)} %add.12), channel_id=1, source_target_pairs={{0,2},{1,3},{2,0},{3,1},{4,6},{5,7},{6,4},{7,5},{8,10},{9,11},{10,... | collective-permute-start | bytes 196616 | tf_op jit(solution)/shard_map/ppermute | solution.py:195
  16.4 5.2 %collective-permute-start.3 = (f32[64,256]{1,0:T(8,128)S(1)}, f32[64,256]{1,0:T(8,128)S(1)}, u32[]{:S(2)}, u32[]{:S(2)}) collective-permute-start(f32[64,256]{1,0:T(8,128)S(1)} %add.13), channel_id=1, source_target_pairs={{0,4},{1,5},{2,6},{3,7},{4,0},{5,1},{6,2},{7,3},{8,12},{9,13},{10,... | collective-permute-start | bytes 196616 | tf_op jit(solution)/shard_map/ppermute | solution.py:195
  21.7 1.3 %collective-permute-start.4 = (f32[64,256]{1,0:T(8,128)S(1)}, f32[64,256]{1,0:T(8,128)S(1)}, u32[]{:S(2)}, u32[]{:S(2)}) collective-permute-start(f32[64,256]{1,0:T(8,128)S(1)} %add.14.p_ref), channel_id=1, source_target_pairs={{0,8},{8,0},{16,24},{24,16},{1,9},{9,1},{17,25},{25,17},{2,10},{10... | collective-permute-start | bytes 196616 | tf_op jit(solution)/shard_map/ppermute | solution.py:195
  21.7 7.9 %collective-permute-start.7 = (f32[64,3584]{1,0:T(8,128)S(1)}, f32[64,3584]{1,0:T(8,128)S(1)}, u32[]{:S(2)}, u32[]{:S(2)}) collective-permute-start(f32[64,3584]{1,0:T(8,128)S(1)} %copy-done.1), channel_id=1, source_target_pairs={{0,8},{8,0},{16,24},{24,16},{1,9},{9,1},{17,25},{25,17},{2,10},{10... | collective-permute-start | bytes 2752520 | tf_op jit(solution)/shard_map/ppermute | solution.py:195
  23.5 6.1 %collective-permute-start.8 = (f32[64,3584]{1,0:T(8,128)S(1)}, f32[64,3584]{1,0:T(8,128)S(1)}, u32[]{:S(2)}, u32[]{:S(2)}) collective-permute-start(f32[64,3584]{1,0:T(8,128)S(1)} %collective-permute-done.refs_4_), channel_id=1, source_target_pairs={{0,8},{8,0},{16,24},{24,16},{1,9},{9,1},{17,25},{25,17},{2,10},{10... | collective-permute-start | bytes 2752520 | tf_op jit(solution)/shard_map/ppermute | solution.py:195
  23.5 4.3 %collective-permute-start.6 = (f32[64,256]{1,0:T(8,128)S(1)}, f32[64,256]{1,0:T(8,128)S(1)}, u32[]{:S(2)}, u32[]{:S(2)}) collective-permute-start(f32[64,256]{1,0:T(8,128)S(1)} %add.14.p_ref), channel_id=1, source_target_pairs={{0,24},{8,16},{16,8},{24,0},{1,25},{9,17},{17,9},{25,1},{2,26},{10... | collective-permute-start | bytes 196616 | tf_op jit(solution)/shard_map/ppermute | solution.py:195
  25.4 4.3 %collective-permute-start.5 = (f32[64,256]{1,0:T(8,128)S(1)}, f32[64,256]{1,0:T(8,128)S(1)}, u32[]{:S(2)}, u32[]{:S(2)}) collective-permute-start(f32[64,256]{1,0:T(8,128)S(1)} %add.14.p_ref), channel_id=1, source_target_pairs={{0,16},{8,24},{16,0},{24,8},{1,17},{9,25},{17,1},{25,9},{2,18},{10... | collective-permute-start | bytes 196616 | tf_op jit(solution)/shard_map/ppermute | solution.py:195
  32.0 3.6 %collective-permute-start.9 = (f32[1,64]{1,0:T(1,128)S(1)}, f32[1,64]{1,0:T(1,128)S(1)}, u32[]{:S(2)}, u32[]{:S(2)}) collective-permute-start(f32[1,64]{1,0:T(1,128)S(1)} %get-tuple-element.14), channel_id=1, source_target_pairs={{0,1},{1,0},{2,3},{3,2},{4,5},{5,4},{6,7},{7,6},{8,9},{9,8},{10,11... | collective-permute-start | bytes 776 | tf_op jit(solution)/shard_map/ppermute | solution.py:195
  35.6 5.3 %collective-permute-start.12 = (f32[1,64]{1,0:T(1,128)S(1)}, f32[1,64]{1,0:T(1,128)S(1)}, u32[]{:S(2)}, u32[]{:S(2)}) collective-permute-start(f32[1,64]{1,0:T(1,128)S(1)} %add.15.refs_0_), channel_id=1, source_target_pairs={{0,6},{1,7},{2,4},{3,5},{4,2},{5,3},{6,0},{7,1},{8,14},{9,15},{10,... | collective-permute-start | bytes 776 | tf_op jit(solution)/shard_map/ppermute | solution.py:195
  39.2 4.4 %collective-permute-start.11 = (f32[1,64]{1,0:T(1,128)S(1)}, f32[1,64]{1,0:T(1,128)S(1)}, u32[]{:S(2)}, u32[]{:S(2)}) collective-permute-start(f32[1,64]{1,0:T(1,128)S(1)} %add.15.refs_0_), channel_id=1, source_target_pairs={{0,4},{1,5},{2,6},{3,7},{4,0},{5,1},{6,2},{7,3},{8,12},{9,13},{10,... | collective-permute-start | bytes 776 | tf_op jit(solution)/shard_map/ppermute | solution.py:195
  39.2 4.4 %collective-permute-start.10 = (f32[1,64]{1,0:T(1,128)S(1)}, f32[1,64]{1,0:T(1,128)S(1)}, u32[]{:S(2)}, u32[]{:S(2)}) collective-permute-start(f32[1,64]{1,0:T(1,128)S(1)} %add.15.refs_0_), channel_id=1, source_target_pairs={{0,2},{1,3},{2,0},{3,1},{4,6},{5,7},{6,4},{7,5},{8,10},{9,11},{10,... | collective-permute-start | bytes 776 | tf_op jit(solution)/shard_map/ppermute | solution.py:195

commit v6 on v4

v6 whole, which is shorter than its diff:
```python
import functools

import jax
import jax.numpy as jnp
from jax import lax
from jax.experimental import pallas as pl
from jax.experimental.pallas import tpu as pltpu
from jax.sharding import PartitionSpec as P

step_rate = 0.1
epsilon = 1e-06
lanes = 128
in_vmem = pl.BlockSpec(memory_space=pltpu.VMEM)
anywhere = pl.BlockSpec(memory_space=pl.ANY)
params = pltpu.CompilerParams(vmem_limit_bytes=16 << 20)


def tile_of(columns, most):
    if columns % lanes:
        return columns
    units = columns // lanes
    return lanes * max(u for u in range(1, most + 1) if units % u == 0)


def halves(array):
    top = array.astype(jnp.bfloat16)
    return top, (array - top.astype(jnp.float32)).astype(jnp.bfloat16)


def product(left, right, transposed=False):
    dims = (((1,), (1 if transposed else 0,)), ((), ()))
    dot = functools.partial(lax.dot_general, dimension_numbers=dims, preferred_element_type=jnp.float32)
    left_top, left_rest = left if isinstance(left, tuple) else halves(left)
    right_top, right_rest = halves(right)
    rows = left_top.shape[0]
    both = dot(jnp.concatenate([left_top, left_rest], axis=0), right_top)
    return both[:rows] + (both[rows:] + dot(left_top, right_rest))


def scale_of(squares, features):
    return lax.rsqrt(squares / features + epsilon)


def loop(columns, most, body, init):
    tile = tile_of(columns, most)
    return lax.fori_loop(0, columns // tile, lambda i, c: body(i, pl.ds(pl.multiple_of(i * tile, tile), tile), c), init)


def place_of(cores):
    group = lax.axis_index("comp")
    return group // cores, group % cores


def diagonal(count):
    down = lax.broadcasted_iota(jnp.int32, (count, count), 0)
    across = lax.broadcasted_iota(jnp.int32, (count, count), 1)
    return down == across


def as_row(column):
    count = column.shape[0]
    return jnp.sum(jnp.where(diagonal(count), jnp.broadcast_to(column, (count, count)), 0.0), axis=0, keepdims=True)


def as_column(row):
    count = row.shape[1]
    return jnp.sum(jnp.where(diagonal(count), jnp.broadcast_to(row, (count, count)), 0.0), axis=1, keepdims=True)


def packing(per_group, rows):
    whole, rest = divmod(rows, lanes)
    folded = rest * 2 == lanes and per_group % 16 == 0
    short = per_group <= lanes
    height = whole * per_group + (per_group // 2 if folded else per_group if rest else 0) + (8 if short else per_group)
    return whole, rest, folded, short, height


def pack(projected, squares, out_ref):
    per_group, rows = projected.shape
    whole, rest, folded, short, height = packing(per_group, rows)
    for k in range(whole):
        out_ref[k * per_group : (k + 1) * per_group, :] = projected[:, k * lanes : (k + 1) * lanes]
    base, half, last = whole * per_group, per_group // 2, projected[:, whole * lanes :]
    if folded:
        out_ref[base : base + half, :] = jnp.concatenate([last[:half], last[half:]], axis=1)
        base += half
    elif rest:
        out_ref[base : base + per_group, :] = jnp.concatenate([last, jnp.zeros((per_group, lanes - rest))], axis=1)
        base += per_group
    if short:
        row = as_row(squares)
        if per_group < lanes:
            row = jnp.concatenate([row, jnp.zeros((1, lanes - per_group), jnp.float32)], axis=1)
        out_ref[base:, :] = jnp.broadcast_to(row, (8, lanes))
    else:
        out_ref[base:, :] = jnp.broadcast_to(squares, (per_group, lanes))


def unpack(p_ref, core, per_group, rows):
    whole, rest, folded, short, height = packing(per_group, rows)
    start = core * height

    def part(first, count):
        return p_ref[pl.ds(pl.multiple_of(start + first, 8), count), :]

    blocks = [part(k * per_group, per_group) for k in range(whole)]
    base, half = whole * per_group, per_group // 2
    if folded:
        last = part(base, half)
        blocks.append(jnp.concatenate([last[:, :rest], last[:, rest:]], axis=0))
        base += half
    elif rest:
        blocks.append(part(base, per_group)[:, :rest])
        base += per_group
    squares = as_column(part(base, 8)[:1, :per_group]) if short else part(base, per_group)[:, :1]
    return jnp.concatenate(blocks, axis=1), squares


def project_kernel(x_hbm, s_hbm, out_ref, x_ref, s_ref, sems):
    per_group, columns = x_ref.shape
    rows = s_ref.shape[0]

    def copies(i, here):
        return (
            pltpu.make_async_copy(x_hbm.at[:, here], x_ref.at[:, here], sems.at[0, i]),
            pltpu.make_async_copy(s_hbm.at[:, here], s_ref.at[:, here], sems.at[1, i]),
        )

    def begin(i, here, carry):
        for copy in copies(i, here):
            copy.start()
        return carry

    def body(i, here, carry):
        for copy in copies(i, here):
            copy.wait()
        x = x_ref[:, here]
        projected, squares = carry
        projected += product(x, s_ref[:, here], transposed=True)
        return projected, squares + jnp.sum(x * x, axis=1, keepdims=True)

    loop(columns, 4, begin, 0)
    zeros = jnp.zeros((per_group, rows), jnp.float32), jnp.zeros((per_group, 1), jnp.float32)
    projected, squares = loop(columns, 4, body, zeros)
    pack(projected, squares, out_ref)


def project(x, sample):
    per_group, columns = x.shape
    rows = sample.shape[0]
    height = packing(per_group, rows)[-1]
    return pl.pallas_call(
        project_kernel,
        in_specs=[anywhere] * 2,
        out_specs=[in_vmem] * 3,
        out_shape=[
            jax.ShapeDtypeStruct((height, lanes), jnp.float32),
            jax.ShapeDtypeStruct(x.shape, jnp.float32),
            jax.ShapeDtypeStruct(sample.shape, jnp.float32),
        ],
        scratch_shapes=[pltpu.SemaphoreType.DMA((2, columns // tile_of(columns, 4)))],
        compiler_params=params,
        name="project",
    )(x, sample)


def images_of(p_ref, core, rows, per_group, features):
    projected, squares = unpack(p_ref, core, per_group, rows)
    scale = scale_of(squares, features)
    return projected * scale, scale


def chip_kernel(features, cores, p_ref, s_ref, *refs):
    x_refs, out_ref = refs[:cores], refs[cores]
    rows = s_ref.shape[0]
    per_group = out_ref.shape[0]
    core = place_of(cores)[1]
    images, scale = images_of(p_ref, core, rows, per_group, features)
    shared = product(images, images * scale, transposed=True)
    later = lax.broadcasted_iota(jnp.int32, shared.shape, 0)
    earlier = lax.broadcasted_iota(jnp.int32, shared.shape, 1)
    weights = [images * (step_rate / rows), jnp.where(earlier < later, shared * (-step_rate / (features * rows)), 0.0)]
    for step in range(1, cores):
        other = (core + step) % cores
        others, others_scale = images_of(p_ref, other, rows, per_group, features)
        factor = jnp.where(other < core, -step_rate / (features * rows), 0.0)
        weights.append(product(images, others * (others_scale * factor), transposed=True))
    weights = halves(jnp.concatenate(weights, axis=1))

    def body(i, here, carry):
        x = x_refs[0][:, here]
        others = [x_ref[:, here] for x_ref in x_refs[1:]]
        out_ref[:, here] = scale * x + product(weights, jnp.concatenate([s_ref[:, here], x, *others], axis=0))
        return carry

    loop(out_ref.shape[1], 4, body, 0)


def chip_part(projected, sample, blocks, features):
    return pl.pallas_call(
        functools.partial(chip_kernel, features, len(blocks)),
        in_specs=[in_vmem] * (2 + len(blocks)),
        out_specs=in_vmem,
        out_shape=jax.ShapeDtypeStruct(blocks[0].shape, jnp.float32),
        compiler_params=params,
        name="chip_part",
    )(projected, sample, *blocks)


def others_kernel(features, rows, cores, chips, t_ref, p_ref, *refs):
    projected_refs, x_refs = refs[: chips - 1], refs[chips - 1 : (chips - 1) * (cores + 1)]
    out_ref, squares_ref = refs[(chips - 1) * (cores + 1) :]
    per_group, columns = t_ref.shape
    chip, core = place_of(cores)
    images = images_of(p_ref, core, rows, per_group, features)[0]
    others = []
    for k, projected_ref in enumerate(projected_refs):
        factor = jnp.where(partner(chip, k + 1, chips) < chip, -step_rate / (features * rows), 0.0)
        for step in range(cores):
            other, scale = images_of(projected_ref, (core + step) % cores, rows, per_group, features)
            others.append(other * (scale * factor))
    coupling = halves(product(images, jnp.concatenate(others, axis=0), transposed=True)) if others else None

    def body(i, here, squares):
        updated = t_ref[:, here]
        if others:
            updated += product(coupling, jnp.concatenate([x_ref[:, here] for x_ref in x_refs], axis=0))
        out_ref[:, here] = updated
        return squares + jnp.sum(updated * updated, axis=1, keepdims=True)

    squares = loop(columns, 4, body, jnp.zeros((per_group, 1), jnp.float32))
    squares_ref[...] = as_row(squares)


def others_part(partly, projected, others, blocks, rows, features):
    chips = len(others) + 1
    cores = len(blocks) // len(others) if others else 1
    return pl.pallas_call(
        functools.partial(others_kernel, features, rows, cores, chips),
        in_specs=[in_vmem] * (2 + len(others) + len(blocks)),
        out_specs=[in_vmem, in_vmem],
        out_shape=[
            jax.ShapeDtypeStruct(partly.shape, jnp.float32),
            jax.ShapeDtypeStruct((1, partly.shape[0]), jnp.float32),
        ],
        compiler_params=params,
        name="others_part",
    )(partly, projected, *others, *blocks)


def finish_kernel(features, cores, count, updated_ref, *refs):
    squares_refs, (out_ref, scaled, sems) = refs[:-3], refs[-3:]
    per_group, columns = updated_ref.shape
    core = place_of(cores)[1]
    squares = sum((ref[cores - 1 : cores, :] for ref in squares_refs[1:count]), squares_refs[0][cores - 1 : cores, :])
    if cores > 1:
        squares = jnp.where(core == 0, squares_refs[count][0:1, :], squares)
    scale = as_column(scale_of(squares, features))
    tile = tile_of(columns, 7)
    copies = []
    for i in range(columns // tile):
        here = pl.ds(i * tile, tile)
        scaled[:, here] = updated_ref[:, here] * scale
        copies.append(pltpu.make_async_copy(scaled.at[:, here], out_ref.at[:, here], sems.at[i]))
        copies[-1].start()
    for copy in copies:
        copy.wait()


def finish(updated, squares, count, cores, features):
    columns = updated.shape[1]
    return pl.pallas_call(
        functools.partial(finish_kernel, features, cores, count),
        in_specs=[in_vmem] * (1 + len(squares)),
        out_specs=anywhere,
        out_shape=jax.ShapeDtypeStruct(updated.shape, jnp.float32),
        scratch_shapes=[
            pltpu.VMEM(updated.shape, jnp.float32),
            pltpu.SemaphoreType.DMA((columns // tile_of(columns, 7),)),
        ],
        compiler_params=params,
        name="finish",
    )(updated, *squares)


def partner(place, step, size):
    return (place + step) % size if size & (size - 1) else place ^ step


def swap_cores(array, cores):
    return lax.ppermute(array, "comp", [(i, i ^ 1) for i in range(lax.axis_size("comp"))])


def from_chip(array, step, cores, carrying=False):
    size = lax.axis_size("comp")
    chips = size // cores
    pairs = []
    for i in range(size):
        moves = not carrying or i % cores == cores - 1
        pairs.append(((partner(i // cores, step, chips) * cores + i % cores) if moves else i, i))
    return lax.ppermute(array, "comp", pairs)


def along_feat(array, step, cores):
    comp, feat = lax.axis_size("comp"), lax.axis_size("feat")
    pairs = []
    for i in range(comp):
        for j in range(feat):
            source = partner(j, step, feat) if i % cores == cores - 1 else j
            pairs.append((i * feat + source, i * feat + j))
    return lax.ppermute(array, ("comp", "feat"), pairs)


def terms(array, cores, together):
    size = lax.axis_size("feat")
    if size & (size - 1):
        return [array] + [along_feat(array, step, cores) for step in range(1, size)]
    parts, step, bits = [array], 1, (size.bit_length() - 1) % together or together
    while step < size:
        array = sum(parts[1:], parts[0])
        parts = [array] + [along_feat(array, step * k, cores) for k in range(1, 1 << bits)]
        step <<= bits
        bits = together
    return parts


def hand_over(array, cores):
    if cores == 1:
        return array
    return jnp.where(place_of(cores)[1] == 0, swap_cores(array, cores), array)


def shards(samples, start_vectors):
    comp = lax.axis_size("comp")
    feat = lax.axis_size("feat")
    cores = 2 if comp % 2 == 0 else 1
    chips = comp // cores
    sample = samples[0]
    rows = sample.shape[0]
    features = sample.shape[1] * feat

    across = [from_chip(start_vectors, step, cores) for step in range(1, chips)]
    beside = [swap_cores(start_vectors, cores)] if cores > 1 else []

    sources = [pltpu.with_memory_space_constraint(array, pltpu.HBM) for array in (start_vectors, sample)]
    projected, vectors, sample = project(*sources)
    if cores > 1:
        projected = jnp.concatenate([swap_cores(projected, cores), projected], axis=0)
    parts = terms(projected, cores, 1)
    carried = sum(parts[1:], parts[0])
    projected = hand_over(carried, cores)
    received = [from_chip(carried, step, cores, True) for step in range(1, chips)]
    partly = chip_part(projected, sample, [vectors] + beside, features)
    blocks = []
    for k, arrived in enumerate(across):
        arrived, received[k], projected = lax.optimization_barrier((arrived, received[k], projected))
        blocks += [arrived] + ([swap_cores(arrived, cores)] if cores > 1 else [])
    others = [hand_over(array, cores) for array in received]
    updated, squares = others_part(partly, projected, others, blocks, rows, features)

    if cores > 1:
        squares = jnp.concatenate([swap_cores(squares, cores), squares], axis=0)
    squares = terms(squares, cores, 2)
    count = len(squares)
    if cores > 1:
        squares = squares + [swap_cores(sum(squares[1:], squares[0]), cores)]
    return finish(updated, squares, count, cores, features)


def solution(mesh):
    in_specs = (P(None, None, "feat"), P("comp", "feat"))
    out_specs = P("comp", "feat")
    return jax.shard_map(shards, mesh=mesh, in_specs=in_specs, out_specs=out_specs, check_vma=False)
```

time: 53.7 us -> 62.8 us (1.17)
  starting transfers between devices: 17.5 us -> 45.9 us
  waiting for transfers between devices: 16 us -> 2.68 us
  Pallas kernels: 17.2 us -> 11.4 us
  other arithmetic: 1.99 us -> 0.11 us
  local copies, waits for them, and re-layouts: 0.6 us -> 2.11 us
    ppermute x13 -> x16, starting transfers between devices: 17.5 us -> 45.9 us  [the longest x7 38.1 us: swap_cores(): lax.ppermute(array, 'comp', [(i, i ^ 1) for i in range(lax.axis_size('com...]
    ppermute x13 -> x16, waiting for transfers between devices: 16 us -> 2.68 us  [the longest x7 1.86 us: swap_cores(): lax.ppermute(array, 'comp', [(i, i ^ 1) for i in range(lax.axis_size('com...]
    pallas_call x4, Pallas kernels: 17.2 us -> 11.4 us  [the longest x1 3.6 us: chip_part(): pl.pallas_call(functools.partial(chip_kernel, features, len(blocks)), in_...]
    unnamed x22 -> x5, local copies, waits for them, and re-layouts: 0.6 us -> 2.1 us
    add x3, other arithmetic: 1.46 us -> 0.04 us  [terms(): array = sum(parts[1:], parts[0])]
  transfers between devices with their start and end apart: 13 -> 16, of which waited for: 7 -> 4; matrix products, arithmetic and copies ran while one was open for 3% -> 0% of each run, Pallas kernels for 18% -> 6%
where the time goes in v6:
time: 62.8 us; the launch traced here: 62.3 us
  starting transfers between devices  45.9 us (73%)
  Pallas kernels  11.4 us (18%)
  waiting for transfers between devices  2.68 us (4%)
  local copies, waits for them, and re-layouts  2.11 us (3%)
    ppermute x7, starting transfers between devices, swap_cores(): lax.ppermute(array, 'comp', [(i, i ^ 1) for i in range(lax.axis_size('com...  38.1 us
    ppermute x7, starting transfers between devices, along_feat(): return lax.ppermute(array, ('comp', 'feat'), pairs)  4.64 us
    pallas_call x1, Pallas kernels, chip_part(): pl.pallas_call(functools.partial(chip_kernel, features, len(blocks)), in_...  3.6 us
    pallas_call x1, Pallas kernels, others_part(): pl.pallas_call(functools.partial(others_kernel, features, rows, cores, ch...  3.53 us
    ppermute x2, starting transfers between devices, from_chip(): return lax.ppermute(array, 'comp', pairs)  3.14 us
    pallas_call x1, Pallas kernels, project(): pl.pallas_call(project_kernel, in_specs=[anywhere] * 2, out_specs=[in_vme...  3.13 us
    unnamed x5, local copies, waits for them, and re-layouts  2.1 us
    ppermute x7, waiting for transfers between devices, swap_cores(): lax.ppermute(array, 'comp', [(i, i ^ 1) for i in range(lax.axis_size('com...  1.86 us
  transfers between devices with their start and end apart: 16, of which 4 were waited for; matrix products, arithmetic and copies ran while one was open for 0% of the time, Pallas kernels for 6%

profile of v6, /device:TPU:0, one launch (start us, length us, event | category | flops | bytes accessed | tf_op | source)
XLA Modules:
  0.0 62.3 jit_solution(17970007866038427046)
XLA Ops:
  0.0 3.1 %project.1 = (f32[104,128]{1,0:T(8,128)S(1)}, f32[64,3584]{1,0:T(8,128)S(1)}, f32[192,3584]{1,0:T(8,128)S(1)}) custom-call(f32[64,3584]{1,0:T(8,128)} %x_hbm.1, f32[192,3584]{1,0:T(8,128)} %bitcast.1), custom_call_target="tpu_custom_call" | custom-call | tf_op jit(solution)/shard_map/project/pallas_call | solution.py:152
  3.1 0.0 copy-start
  3.2 0.9 %copy-done = f32[64,3584]{1,0:T(8,128)} copy-done((f32[64,3584]{1,0:T(8,128)}, f32[64,3584]{1,0:T(8,128)S(1)}, u32[]{:S(2)}) %copy-start) | copy-done | bytes 917528
  4.1 0.5 collective-permute-start
  4.5 2.5 %collective-permute-start.6 = (f32[64,3584]{1,0:T(8,128)}, f32[64,3584]{1,0:T(8,128)}, u32[]{:S(2)}, u32[]{:S(2)}) collective-permute-start(f32[64,3584]{1,0:T(8,128)} %x_hbm.1), channel_id=1, source_target_pairs={{16,0},{24,8},{0,16},{8,24},{17,1},{25,9},{1,17},{9,25},{18,2},{26... | collective-permute-start | bytes 2752520 | tf_op jit(solution)/shard_map/ppermute | solution.py:301
  7.0 0.0 collective-permute-done
  7.0 0.7 %collective-permute-start.1 = (f32[208,128]{1,0:T(8,128)S(1)}, f32[208,128]{1,0:T(8,128)S(1)}, u32[]{:S(2)}, u32[]{:S(2)}) collective-permute-start(f32[208,128]{1,0:T(8,128)S(1)} %constant_dynamic-update-slice_fusion), channel_id=1, source_target_pairs={{0,0},{1,1},{2,2},{3,3},{4,4},{5,5},{6,6},{7,7},{9,8},{8,9},{11,10... | collective-permute-start | bytes 319496 | tf_op jit(solution)/shard_map/ppermute | solution.py:311
  7.7 0.0 collective-permute-done.1
  7.8 0.7 %collective-permute-start.2 = (f32[208,128]{1,0:T(8,128)S(1)}, f32[208,128]{1,0:T(8,128)S(1)}, u32[]{:S(2)}, u32[]{:S(2)}) collective-permute-start(f32[208,128]{1,0:T(8,128)S(1)} %add.27), channel_id=1, source_target_pairs={{0,0},{1,1},{2,2},{3,3},{4,4},{5,5},{6,6},{7,7},{10,8},{11,9},{8,1... | collective-permute-start | bytes 319496 | tf_op jit(solution)/shard_map/ppermute | solution.py:311
  8.4 0.0 collective-permute-done.2
  8.5 0.7 %collective-permute-start.3 = (f32[208,128]{1,0:T(8,128)S(1)}, f32[208,128]{1,0:T(8,128)S(1)}, u32[]{:S(2)}, u32[]{:S(2)}) collective-permute-start(f32[208,128]{1,0:T(8,128)S(1)} %add.28), channel_id=1, source_target_pairs={{0,0},{1,1},{2,2},{3,3},{4,4},{5,5},{6,6},{7,7},{12,8},{13,9},{14,... | collective-permute-start | bytes 319496 | tf_op jit(solution)/shard_map/ppermute | solution.py:311
  9.1 0.0 collective-permute-done.3
  9.2 17.4 %collective-permute-start.4 = (f32[208,128]{1,0:T(8,128)S(1)}, f32[208,128]{1,0:T(8,128)S(1)}, u32[]{:S(2)}, u32[]{:S(2)}) collective-permute-start(f32[208,128]{1,0:T(8,128)S(1)} %add.29), channel_id=1, source_target_pairs={{0,8},{8,0},{16,24},{24,16},{1,9},{9,1},{17,25},{25,17},{2,10},{10... | collective-permute-start | bytes 319496 | tf_op jit(solution)/shard_map/ppermute | solution.py:291
  26.6 0.1 collective-permute-start.5
  26.7 0.7 %collective-permute-start.7 = (f32[208,128]{1,0:T(8,128)S(1)}, f32[208,128]{1,0:T(8,128)S(1)}, u32[]{:S(2)}, u32[]{:S(2)}) collective-permute-start(f32[208,128]{1,0:T(8,128)S(1)} %add.29), channel_id=1, source_target_pairs={{0,0},{24,8},{16,16},{8,24},{1,1},{25,9},{17,17},{9,25},{2,2},{26,... | collective-permute-start | bytes 319496 | tf_op jit(solution)/shard_map/ppermute | solution.py:301
  27.3 0.2 collective-permute-done.4
  27.5 0.0 collective-permute-done.7
  27.6 0.8 %collective-permute-done.6.refs_1_ = f32[64,3584]{1,0:T(8,128)} collective-permute-done((f32[64,3584]{1,0:T(8,128)}, f32[64,3584]{1,0:T(8,128)}, u32[]{:S(2)}, u32[]{:S(2)}) %collective-permute-start.6) | collective-permute-done | bytes 917536 | tf_op jit(solution)/shard_map/ppermute | solution.py:301
  28.4 4.2 %collective-permute-start.9 = (f32[64,3584]{1,0:T(8,128)}, f32[64,3584]{1,0:T(8,128)S(1)}, u32[]{:S(2)}, u32[]{:S(2)}) collective-permute-start(f32[64,3584]{1,0:T(8,128)} %collective-permute-done.6.refs_1_), channel_id=1, source_target_pairs={{0,8},{8,0},{16,24},{24,16},{1,9},{9,1},{17,25},{25,17},{2,10},{10... | collective-permute-start | bytes 2752520 | tf_op jit(solution)/shard_map/ppermute | solution.py:291
  32.5 0.0 collective-permute-start.8
  32.5 0.0 collective-permute-done.5.refs_1_
  32.5 0.0 copy-start.1
  32.5 1.2 %copy-done.1 = f32[64,3584]{1,0:T(8,128)S(1)} copy-done((f32[64,3584]{1,0:T(8,128)S(1)}, f32[64,3584]{1,0:T(8,128)}, u32[]{:S(2)}) %copy-start.1) | copy-done | bytes 917528
  33.7 3.6 %chip_part.1.t_ref = f32[64,3584]{1,0:T(8,128)S(1)} custom-call(f32[208,128]{1,0:T(8,128)S(1)} %broadcast_select_fusion.1.p_ref, f32[192,3584]{1,0:T(8,128)S(1)} %get-tuple-element.14.s_ref, f32[64,3584]{1,0:T(8,128)S(1)} %copy-done.1, f32[64,3584]{1,0:T(8,128)} %collective-permute-done.5.refs_1_), custom_call_target="tpu_custom_call" | custom-call | tf_op jit(solution)/shard_map/chip_part/pallas_call | solution.py:200
  37.3 0.0 collective-permute-done.8
  37.4 0.0 collective-permute-done.9.refs_2_
  37.4 3.5 %others_part.1 = (f32[64,3584]{1,0:T(8,128)S(1)}, f32[1,64]{1,0:T(1,128)S(1)}) custom-call(f32[64,3584]{1,0:T(8,128)S(1)} %chip_part.1.t_ref, f32[208,128]{1,0:T(8,128)S(1)} %broadcast_select_fusion.1.p_ref, f32[208,128]{1,0:T(8,128)S(1)} %broadcast_select_fusion.refs_0_, f32[64,3584]{1,0:T(8,128)} %collective-permute-done.6.refs_1_, ...), custom_call_target="tpu_custom_call" | custom-call | tf_op jit(solution)/shard_map/others_part/pallas_call | solution.py:238
  40.9 0.6 collective-permute-start.10
  41.5 0.8 %collective-permute-done.10 = f32[1,64]{1,0:T(1,128)S(1)} collective-permute-done((f32[1,64]{1,0:T(1,128)S(1)}, f32[1,64]{1,0:T(1,128)S(1)}, u32[]{:S(2)}, u32[]{:S(2)}) %collective-permute-start.10) | collective-permute-done | bytes 288 | tf_op jit(solution)/shard_map/ppermute | solution.py:291
  42.3 0.6 %collective-permute-start.11 = (f32[2,64]{1,0:T(2,128)S(1)}, f32[2,64]{1,0:T(2,128)S(1)}, u32[]{:S(2)}, u32[]{:S(2)}) collective-permute-start(f32[2,64]{1,0:T(2,128)S(1)} %pad_maximum_fusion), channel_id=1, source_target_pairs={{0,0},{1,1},{2,2},{3,3},{4,4},{5,5},{6,6},{7,7},{9,8},{8,9},{11,10... | collective-permute-start | bytes 1544 | tf_op jit(solution)/shard_map/ppermute | solution.py:311
  43.0 0.0 collective-permute-done.11
  43.0 0.7 %collective-permute-start.12 = (f32[2,64]{1,0:T(2,128)S(1)}, f32[2,64]{1,0:T(2,128)S(1)}, u32[]{:S(2)}, u32[]{:S(2)}) collective-permute-start(f32[2,64]{1,0:T(2,128)S(1)} %fusion.refs_0_), channel_id=1, source_target_pairs={{0,0},{1,1},{2,2},{3,3},{4,4},{5,5},{6,6},{7,7},{10,8},{11,9},{8,1... | collective-permute-start | bytes 1544 | tf_op jit(solution)/shard_map/ppermute | solution.py:311
  43.7 0.7 %collective-permute-start.13 = (f32[2,64]{1,0:T(2,128)S(1)}, f32[2,64]{1,0:T(2,128)S(1)}, u32[]{:S(2)}, u32[]{:S(2)}) collective-permute-start(f32[2,64]{1,0:T(2,128)S(1)} %fusion.refs_0_), channel_id=1, source_target_pairs={{0,0},{1,1},{2,2},{3,3},{4,4},{5,5},{6,6},{7,7},{12,8},{13,9},{14,... | collective-permute-start | bytes 1544 | tf_op jit(solution)/shard_map/ppermute | solution.py:311
  44.3 0.7 %collective-permute-start.14 = (f32[2,64]{1,0:T(2,128)S(1)}, f32[2,64]{1,0:T(2,128)S(1)}, u32[]{:S(2)}, u32[]{:S(2)}) collective-permute-start(f32[2,64]{1,0:T(2,128)S(1)} %fusion.refs_0_), channel_id=1, source_target_pairs={{0,0},{1,1},{2,2},{3,3},{4,4},{5,5},{6,6},{7,7},{14,8},{15,9},{12,... | collective-permute-start | bytes 1544 | tf_op jit(solution)/shard_map/ppermute | solution.py:311
  45.0 0.0 collective-permute-done.12.refs_1_
  45.0 0.0 collective-permute-done.13.refs_2_
  45.0 0.0 collective-permute-done.14.refs_3_
  45.1 15.4 %collective-permute-start.15 = (f32[2,64]{1,0:T(2,128)S(1)}, f32[2,64]{1,0:T(2,128)S(1)}, u32[]{:S(2)}, u32[]{:S(2)}) collective-permute-start(f32[2,64]{1,0:T(2,128)S(1)} %add_add_fusion), channel_id=1, source_target_pairs={{0,8},{8,0},{16,24},{24,16},{1,9},{9,1},{17,25},{25,17},{2,10},{10... | collective-permute-start | bytes 1544 | tf_op jit(solution)/shard_map/ppermute | solution.py:291
  60.4 0.8 %collective-permute-done.15.refs_4_ = f32[2,64]{1,0:T(2,128)S(1)} collective-permute-done((f32[2,64]{1,0:T(2,128)S(1)}, f32[2,64]{1,0:T(2,128)S(1)}, u32[]{:S(2)}, u32[]{:S(2)}) %collective-permute-start.15) | collective-permute-done | bytes 544 | tf_op jit(solution)/shard_map/ppermute | solution.py:291
  61.3 1.1 %finish.1 = f32[64,3584]{1,0:T(8,128)} custom-call(f32[64,3584]{1,0:T(8,128)S(1)} %get-tuple-element.19.updated_ref, f32[2,64]{1,0:T(2,128)S(1)} %fusion.refs_0_, f32[2,64]{1,0:T(2,128)S(1)} %collective-permute-done.12.refs_1_, f32[2,64]{1,0:T(2,128)S(1)} %collective-permute-done.13.refs_2_, f32[2,64]{1,0:T(2,128)S(1)} %collective-permute-done.14.refs_3_, ...), custom_call_target="tpu_custom_call" | custom-call | tf_op jit(solution)/shard_map/finish/pallas_call | solution.py:272
  (10 shorter events, 0.1 us)
Async XLA Ops:
  3.1 0.9 %copy-start = (f32[64,3584]{1,0:T(8,128)}, f32[64,3584]{1,0:T(8,128)S(1)}, u32[]{:S(2)}) copy-start(f32[64,3584]{1,0:T(8,128)S(1)} %get-tuple-element.15.refs_0_) | copy-start | bytes 2752516
  4.1 3.0 %collective-permute-start = (f32[104,128]{1,0:T(8,128)S(1)}, f32[104,128]{1,0:T(8,128)S(1)}, u32[]{:S(2)}, u32[]{:S(2)}) collective-permute-start(f32[104,128]{1,0:T(8,128)S(1)} %get-tuple-element.13), channel_id=1, source_target_pairs={{0,8},{8,0},{16,24},{24,16},{1,9},{9,1},{17,25},{25,17},{2,10},{10... | collective-permute-start | bytes 159752 | tf_op jit(solution)/shard_map/ppermute | solution.py:291
  4.5 23.8 %collective-permute-start.6 = (f32[64,3584]{1,0:T(8,128)}, f32[64,3584]{1,0:T(8,128)}, u32[]{:S(2)}, u32[]{:S(2)}) collective-permute-start(f32[64,3584]{1,0:T(8,128)} %x_hbm.1), channel_id=1, source_target_pairs={{16,0},{24,8},{0,16},{8,24},{17,1},{25,9},{1,17},{9,25},{18,2},{26... | collective-permute-start | bytes 2752520 | tf_op jit(solution)/shard_map/ppermute | solution.py:301
  7.0 0.7 %collective-permute-start.1 = (f32[208,128]{1,0:T(8,128)S(1)}, f32[208,128]{1,0:T(8,128)S(1)}, u32[]{:S(2)}, u32[]{:S(2)}) collective-permute-start(f32[208,128]{1,0:T(8,128)S(1)} %constant_dynamic-update-slice_fusion), channel_id=1, source_target_pairs={{0,0},{1,1},{2,2},{3,3},{4,4},{5,5},{6,6},{7,7},{9,8},{8,9},{11,10... | collective-permute-start | bytes 319496 | tf_op jit(solution)/shard_map/ppermute | solution.py:311
  7.8 0.7 %collective-permute-start.2 = (f32[208,128]{1,0:T(8,128)S(1)}, f32[208,128]{1,0:T(8,128)S(1)}, u32[]{:S(2)}, u32[]{:S(2)}) collective-permute-start(f32[208,128]{1,0:T(8,128)S(1)} %add.27), channel_id=1, source_target_pairs={{0,0},{1,1},{2,2},{3,3},{4,4},{5,5},{6,6},{7,7},{10,8},{11,9},{8,1... | collective-permute-start | bytes 319496 | tf_op jit(solution)/shard_map/ppermute | solution.py:311
  8.5 0.7 %collective-permute-start.3 = (f32[208,128]{1,0:T(8,128)S(1)}, f32[208,128]{1,0:T(8,128)S(1)}, u32[]{:S(2)}, u32[]{:S(2)}) collective-permute-start(f32[208,128]{1,0:T(8,128)S(1)} %add.28), channel_id=1, source_target_pairs={{0,0},{1,1},{2,2},{3,3},{4,4},{5,5},{6,6},{7,7},{12,8},{13,9},{14,... | collective-permute-start | bytes 319496 | tf_op jit(solution)/shard_map/ppermute | solution.py:311
  9.2 18.4 %collective-permute-start.4 = (f32[208,128]{1,0:T(8,128)S(1)}, f32[208,128]{1,0:T(8,128)S(1)}, u32[]{:S(2)}, u32[]{:S(2)}) collective-permute-start(f32[208,128]{1,0:T(8,128)S(1)} %add.29), channel_id=1, source_target_pairs={{0,8},{8,0},{16,24},{24,16},{1,9},{9,1},{17,25},{25,17},{2,10},{10... | collective-permute-start | bytes 319496 | tf_op jit(solution)/shard_map/ppermute | solution.py:291
  26.6 6.0 %collective-permute-start.5 = (f32[64,3584]{1,0:T(8,128)}, f32[64,3584]{1,0:T(8,128)}, u32[]{:S(2)}, u32[]{:S(2)}) collective-permute-start(f32[64,3584]{1,0:T(8,128)} %x_hbm.1), channel_id=1, source_target_pairs={{0,8},{8,0},{16,24},{24,16},{1,9},{9,1},{17,25},{25,17},{2,10},{10... | collective-permute-start | bytes 2752520 | tf_op jit(solution)/shard_map/ppermute | solution.py:291
  26.7 0.9 %collective-permute-start.7 = (f32[208,128]{1,0:T(8,128)S(1)}, f32[208,128]{1,0:T(8,128)S(1)}, u32[]{:S(2)}, u32[]{:S(2)}) collective-permute-start(f32[208,128]{1,0:T(8,128)S(1)} %add.29), channel_id=1, source_target_pairs={{0,0},{24,8},{16,16},{8,24},{1,1},{25,9},{17,17},{9,25},{2,2},{26,... | collective-permute-start | bytes 319496 | tf_op jit(solution)/shard_map/ppermute | solution.py:301
  28.4 9.0 %collective-permute-start.9 = (f32[64,3584]{1,0:T(8,128)}, f32[64,3584]{1,0:T(8,128)S(1)}, u32[]{:S(2)}, u32[]{:S(2)}) collective-permute-start(f32[64,3584]{1,0:T(8,128)} %collective-permute-done.6.refs_1_), channel_id=1, source_target_pairs={{0,8},{8,0},{16,24},{24,16},{1,9},{9,1},{17,25},{25,17},{2,10},{10... | collective-permute-start | bytes 2752520 | tf_op jit(solution)/shard_map/ppermute | solution.py:291
  32.5 4.8 %collective-permute-start.8 = (f32[208,128]{1,0:T(8,128)S(1)}, f32[208,128]{1,0:T(8,128)S(1)}, u32[]{:S(2)}, u32[]{:S(2)}) collective-permute-start(f32[208,128]{1,0:T(8,128)S(1)} %collective-permute-done.7), channel_id=1, source_target_pairs={{0,8},{8,0},{16,24},{24,16},{1,9},{9,1},{17,25},{25,17},{2,10},{10... | collective-permute-start | bytes 319496 | tf_op jit(solution)/shard_map/ppermute | solution.py:291
  32.5 1.2 %copy-start.1 = (f32[64,3584]{1,0:T(8,128)S(1)}, f32[64,3584]{1,0:T(8,128)}, u32[]{:S(2)}) copy-start(f32[64,3584]{1,0:T(8,128)} %copy-done) | copy-start | bytes 2752516
  40.9 1.4 %collective-permute-start.10 = (f32[1,64]{1,0:T(1,128)S(1)}, f32[1,64]{1,0:T(1,128)S(1)}, u32[]{:S(2)}, u32[]{:S(2)}) collective-permute-start(f32[1,64]{1,0:T(1,128)S(1)} %get-tuple-element.20), channel_id=1, source_target_pairs={{0,8},{8,0},{16,24},{24,16},{1,9},{9,1},{17,25},{25,17},{2,10},{10... | collective-permute-start | bytes 776 | tf_op jit(solution)/shard_map/ppermute | solution.py:291
  42.3 0.7 %collective-permute-start.11 = (f32[2,64]{1,0:T(2,128)S(1)}, f32[2,64]{1,0:T(2,128)S(1)}, u32[]{:S(2)}, u32[]{:S(2)}) collective-permute-start(f32[2,64]{1,0:T(2,128)S(1)} %pad_maximum_fusion), channel_id=1, source_target_pairs={{0,0},{1,1},{2,2},{3,3},{4,4},{5,5},{6,6},{7,7},{9,8},{8,9},{11,10... | collective-permute-start | bytes 1544 | tf_op jit(solution)/shard_map/ppermute | solution.py:311
  43.0 2.0 %collective-permute-start.12 = (f32[2,64]{1,0:T(2,128)S(1)}, f32[2,64]{1,0:T(2,128)S(1)}, u32[]{:S(2)}, u32[]{:S(2)}) collective-permute-start(f32[2,64]{1,0:T(2,128)S(1)} %fusion.refs_0_), channel_id=1, source_target_pairs={{0,0},{1,1},{2,2},{3,3},{4,4},{5,5},{6,6},{7,7},{10,8},{11,9},{8,1... | collective-permute-start | bytes 1544 | tf_op jit(solution)/shard_map/ppermute | solution.py:311
  43.7 1.4 %collective-permute-start.13 = (f32[2,64]{1,0:T(2,128)S(1)}, f32[2,64]{1,0:T(2,128)S(1)}, u32[]{:S(2)}, u32[]{:S(2)}) collective-permute-start(f32[2,64]{1,0:T(2,128)S(1)} %fusion.refs_0_), channel_id=1, source_target_pairs={{0,0},{1,1},{2,2},{3,3},{4,4},{5,5},{6,6},{7,7},{12,8},{13,9},{14,... | collective-permute-start | bytes 1544 | tf_op jit(solution)/shard_map/ppermute | solution.py:311
  44.3 0.7 %collective-permute-start.14 = (f32[2,64]{1,0:T(2,128)S(1)}, f32[2,64]{1,0:T(2,128)S(1)}, u32[]{:S(2)}, u32[]{:S(2)}) collective-permute-start(f32[2,64]{1,0:T(2,128)S(1)} %fusion.refs_0_), channel_id=1, source_target_pairs={{0,0},{1,1},{2,2},{3,3},{4,4},{5,5},{6,6},{7,7},{14,8},{15,9},{12,... | collective-permute-start | bytes 1544 | tf_op jit(solution)/shard_map/ppermute | solution.py:311
  45.1 16.2 %collective-permute-start.15 = (f32[2,64]{1,0:T(2,128)S(1)}, f32[2,64]{1,0:T(2,128)S(1)}, u32[]{:S(2)}, u32[]{:S(2)}) collective-permute-start(f32[2,64]{1,0:T(2,128)S(1)} %add_add_fusion), channel_id=1, source_target_pairs={{0,8},{8,0},{16,24},{24,16},{1,9},{9,1},{17,25},{25,17},{2,10},{10... | collective-permute-start | bytes 1544 | tf_op jit(solution)/shard_map/ppermute | solution.py:291

commit v7 on v4

v7 whole, which is shorter than its diff:
```python
import functools

import jax
import jax.numpy as jnp
from jax import lax
from jax.experimental import pallas as pl
from jax.experimental.pallas import tpu as pltpu
from jax.sharding import PartitionSpec as P

step_rate = 0.1
epsilon = 1e-06
lanes = 128
in_vmem = pl.BlockSpec(memory_space=pltpu.VMEM)
anywhere = pl.BlockSpec(memory_space=pl.ANY)
params = pltpu.CompilerParams(vmem_limit_bytes=16 << 20)


def tile_of(columns, most):
    if columns % lanes:
        return columns
    units = columns // lanes
    return lanes * max(u for u in range(1, most + 1) if units % u == 0)


def halves(array):
    top = array.astype(jnp.bfloat16)
    return top, (array - top.astype(jnp.float32)).astype(jnp.bfloat16)


def product(left, right, transposed=False):
    dims = (((1,), (1 if transposed else 0,)), ((), ()))
    dot = functools.partial(lax.dot_general, dimension_numbers=dims, preferred_element_type=jnp.float32)
    left_top, left_rest = left if isinstance(left, tuple) else halves(left)
    right_top, right_rest = halves(right)
    rows = left_top.shape[0]
    both = dot(jnp.concatenate([left_top, left_rest], axis=0), right_top)
    return both[:rows] + (both[rows:] + dot(left_top, right_rest))


def scale_of(squares, features):
    return lax.rsqrt(squares / features + epsilon)


def loop(columns, most, body, init):
    tile = tile_of(columns, most)
    return lax.fori_loop(0, columns // tile, lambda i, c: body(i, pl.ds(pl.multiple_of(i * tile, tile), tile), c), init)


def project_kernel(x_hbm, s_hbm, out_ref, x_ref, s_ref, sems):
    per_group, columns = x_ref.shape
    rows = s_ref.shape[0]

    def copies(i, here):
        return (
            pltpu.make_async_copy(x_hbm.at[:, here], x_ref.at[:, here], sems.at[0, i]),
            pltpu.make_async_copy(s_hbm.at[:, here], s_ref.at[:, here], sems.at[1, i]),
        )

    def begin(i, here, carry):
        for copy in copies(i, here):
            copy.start()
        return carry

    def body(i, here, carry):
        for copy in copies(i, here):
            copy.wait()
        x = x_ref[:, here]
        projected, squares = carry
        projected += product(x, s_ref[:, here], transposed=True)
        return projected, squares + jnp.sum(x * x, axis=1, keepdims=True)

    loop(columns, 4, begin, 0)
    zeros = jnp.zeros((per_group, rows), jnp.float32), jnp.zeros((per_group, 1), jnp.float32)
    projected, squares = loop(columns, 4, body, zeros)
    out_ref[:, :rows] = projected
    out_ref[:, rows:] = jnp.broadcast_to(squares, (per_group, out_ref.shape[1] - rows))


def project(x, sample):
    per_group, columns = x.shape
    rows = sample.shape[0]
    width = -(-(rows + 1) // lanes) * lanes
    return pl.pallas_call(
        project_kernel,
        in_specs=[anywhere] * 2,
        out_specs=[in_vmem] * 3,
        out_shape=[
            jax.ShapeDtypeStruct((per_group, width), jnp.float32),
            jax.ShapeDtypeStruct(x.shape, jnp.float32),
            jax.ShapeDtypeStruct(sample.shape, jnp.float32),
        ],
        scratch_shapes=[pltpu.SemaphoreType.DMA((2, columns // tile_of(columns, 4)))],
        compiler_params=params,
        name="project",
    )(x, sample)


def images_of(p_ref, rows, features):
    scale = scale_of(p_ref[:, rows : rows + 1], features)
    return p_ref[:, :rows] * scale, scale


def owner(group, step, size):
    return (group + step) % size if size & (size - 1) else group ^ step


def couplings(images, steps, projected_refs, features):
    group, size = lax.axis_index("comp"), lax.axis_size("comp")
    rows = images.shape[1]
    others = []
    for step, p_ref in zip(steps, projected_refs):
        other, scale = images_of(p_ref, rows, features)
        others.append(other * (scale * jnp.where(owner(group, step, size) < group, -step_rate / (features * rows), 0.0)))
    return product(images, jnp.concatenate(others, axis=0), transposed=True)


def first_kernel(features, steps, p_ref, s_ref, x_ref, *refs):
    count = len(steps)
    projected_refs, x_refs, out_ref = refs[:count], refs[count : 2 * count], refs[2 * count]
    rows = s_ref.shape[0]
    images, scale = images_of(p_ref, rows, features)
    shared = product(images, images * scale, transposed=True)
    later = lax.broadcasted_iota(jnp.int32, shared.shape, 0)
    earlier = lax.broadcasted_iota(jnp.int32, shared.shape, 1)
    weights = [images * (step_rate / rows), jnp.where(earlier < later, shared * (-step_rate / (features * rows)), 0.0)]
    if count:
        weights.append(couplings(images, steps, projected_refs, features))
    weights = halves(jnp.concatenate(weights, axis=1))

    def body(i, here, carry):
        x = x_ref[:, here]
        others = [ref[:, here] for ref in x_refs]
        out_ref[:, here] = scale * x + product(weights, jnp.concatenate([s_ref[:, here], x, *others], axis=0))
        return carry

    loop(x_ref.shape[1], 4, body, 0)


def first_part(projected, sample, x, steps, others, blocks, features):
    return pl.pallas_call(
        functools.partial(first_kernel, features, steps),
        in_specs=[in_vmem] * (3 + 2 * len(steps)),
        out_specs=in_vmem,
        out_shape=jax.ShapeDtypeStruct(x.shape, jnp.float32),
        compiler_params=params,
        name="first_part",
    )(projected, sample, x, *others, *blocks)


def rest_kernel(features, rows, steps, t_ref, p_ref, *refs):
    count = len(steps)
    projected_refs, x_refs, (out_ref, squares_ref) = refs[:count], refs[count : 2 * count], refs[2 * count :]
    per_group, columns = t_ref.shape
    if count:
        weights = halves(couplings(images_of(p_ref, rows, features)[0], steps, projected_refs, features))

    def body(i, here, squares):
        updated = t_ref[:, here]
        if count:
            updated += product(weights, jnp.concatenate([ref[:, here] for ref in x_refs], axis=0))
        out_ref[:, here] = updated
        return squares + jnp.sum(updated * updated, axis=1, keepdims=True)

    squares = loop(columns, 4, body, jnp.zeros((per_group, 1), jnp.float32))
    spread = jnp.broadcast_to(squares, (per_group, per_group))
    squares_ref[...] = jnp.sum(jnp.where(diagonal(per_group), spread, 0.0), axis=0, keepdims=True)


def rest_part(partly, projected, steps, others, blocks, rows, features):
    return pl.pallas_call(
        functools.partial(rest_kernel, features, rows, steps),
        in_specs=[in_vmem] * (2 + 2 * len(steps)),
        out_specs=[in_vmem, in_vmem],
        out_shape=[
            jax.ShapeDtypeStruct(partly.shape, jnp.float32),
            jax.ShapeDtypeStruct((1, partly.shape[0]), jnp.float32),
        ],
        compiler_params=params,
        name="rest_part",
    )(partly, projected, *others, *blocks)


def diagonal(count):
    down = lax.broadcasted_iota(jnp.int32, (count, count), 0)
    across = lax.broadcasted_iota(jnp.int32, (count, count), 1)
    return down == across


def finish_kernel(features, count, updated_ref, *refs):
    squares_refs, (out_ref, scaled, sems) = refs[:count], refs[count:]
    per_group, columns = updated_ref.shape
    squares = squares_refs[0][...]
    for ref in squares_refs[1:]:
        squares += ref[...]
    spread = jnp.broadcast_to(scale_of(squares, features), (per_group, per_group))
    scale = jnp.sum(jnp.where(diagonal(per_group), spread, 0.0), axis=1, keepdims=True)
    tile = tile_of(columns, 7)
    copies = []
    for i in range(columns // tile):
        here = pl.ds(i * tile, tile)
        scaled[:, here] = updated_ref[:, here] * scale
        copies.append(pltpu.make_async_copy(scaled.at[:, here], out_ref.at[:, here], sems.at[i]))
        copies[-1].start()
    for copy in copies:
        copy.wait()


def finish(updated, squares, features):
    count = len(squares)
    return pl.pallas_call(
        functools.partial(finish_kernel, features, count),
        in_specs=[in_vmem] * (1 + count),
        out_specs=anywhere,
        out_shape=jax.ShapeDtypeStruct(updated.shape, jnp.float32),
        scratch_shapes=[
            pltpu.VMEM(updated.shape, jnp.float32),
            pltpu.SemaphoreType.DMA((updated.shape[1] // tile_of(updated.shape[1], 7),)),
        ],
        compiler_params=params,
        name="finish",
    )(updated, *squares)


def exchange(array, axis, step):
    return lax.ppermute(array, axis, [(i, i ^ step) for i in range(lax.axis_size(axis))])


def terms(array, axis, together):
    size = lax.axis_size(axis)
    if size & (size - 1):
        return [lax.psum(array, axis)]
    parts, step, bits = [array], 1, (size.bit_length() - 1) % together or together
    while step < size:
        array = sum(parts[1:], parts[0])
        parts = [array] + [exchange(array, axis, step * k) for k in range(1, 1 << bits)]
        step <<= bits
        bits = together
    return parts


def gather(own):
    size = lax.axis_size("comp")
    if size & (size - 1):
        arrays, group = lax.all_gather(own, "comp"), lax.axis_index("comp")
        return {step: arrays[owner(group, step, size)] for step in range(1, size)}
    return {step: exchange(own, "comp", step) for step in range(1, size)}


def shards(samples, start_vectors):
    comp = lax.axis_size("comp")
    feat = lax.axis_size("feat")
    sample = samples[0]
    rows = sample.shape[0]
    features = sample.shape[1] * feat
    even = comp & (comp - 1) == 0

    blocks = {step: exchange(start_vectors, "comp", step) for step in range(2, comp, 2)} if even else gather(start_vectors)
    projected, vectors, sample = project(
        *(pltpu.with_memory_space_constraint(array, pltpu.HBM) for array in (start_vectors, sample))
    )
    if even and comp > 1:
        blocks[1] = exchange(vectors, "comp", 1)
    parts = terms(projected, "feat", 1)
    projected = sum(parts[1:], parts[0])
    if even:
        others = {step: exchange(projected, "comp", step) for step in range(1, comp) if step == 1 or step % 2 == 0}
    else:
        others = gather(projected)
    near = [1][: comp - 1]
    far = list(range(2, comp))

    def of(arrays, steps):
        return [arrays[step] for step in steps]

    partly = first_part(projected, sample, vectors, near, of(others, near), of(blocks, near), features)
    if even:
        for step in range(2, comp, 2):
            blocks[step], others[step], others[1] = lax.optimization_barrier((blocks[step], others[step], others[1]))
            blocks[step + 1] = exchange(blocks[step], "comp", 1)
            others[step + 1] = exchange(others[step], "comp", 1)
    updated, squares = rest_part(partly, projected, far, of(others, far), of(blocks, far), rows, features)
    return finish(updated, terms(squares, "feat", 2), features)


def solution(mesh):
    in_specs = (P(None, None, "feat"), P("comp", "feat"))
    out_specs = P("comp", "feat")
    return jax.shard_map(shards, mesh=mesh, in_specs=in_specs, out_specs=out_specs, check_vma=False)
```

time: 53.7 us -> 44.7 us (0.83)
  Pallas kernels: 17.2 us -> 8.83 us
  waiting for transfers between devices: 16 us -> 19.5 us
  other arithmetic: 1.99 us -> 0.03 us
  starting transfers between devices: 17.5 us -> 16.1 us
  local copies, waits for them, and re-layouts: 0.6 us -> 0 us
    pallas_call x3, Pallas kernels: 15 us -> 7.74 us  [the longest x1 3.06 us: project(): pl.pallas_call(project_kernel, in_specs=[anywhere] * 2, out_specs=[in_vme...]
    ppermute x13, waiting for transfers between devices: 16 us -> 19.5 us  [exchange(): lax.ppermute(array, axis, [(i, i ^ step) for i in range(lax.axis_size(axi...]
    add x3, other arithmetic: 1.46 us -> 0.02 us  [terms(): array = sum(parts[1:], parts[0])]
    ppermute x13, starting transfers between devices: 17.5 us -> 16.1 us  [exchange(): lax.ppermute(array, axis, [(i, i ^ step) for i in range(lax.axis_size(axi...]
    pallas_call x1, Pallas kernels: 2.27 us -> 1.09 us  [finish(): pl.pallas_call(functools.partial(finish_kernel, features, count), in_spec...]
    unnamed x22 -> x0, local copies, waits for them, and re-layouts: 0.6 us -> none
  transfers between devices with their start and end apart: 13 -> 13, of which waited for: 7 -> 8; matrix products, arithmetic and copies ran while one was open for 3% -> 0% of each run, Pallas kernels for 18% -> 12%
where the time goes in v7:
time: 44.7 us; the launch traced here: 44.6 us
  waiting for transfers between devices  19.5 us (44%)
  starting transfers between devices  16.1 us (36%)
  Pallas kernels  8.83 us (20%)
    ppermute x13, waiting for transfers between devices, exchange(): lax.ppermute(array, axis, [(i, i ^ step) for i in range(lax.axis_size(axi...  19.5 us
    ppermute x13, starting transfers between devices, exchange(): lax.ppermute(array, axis, [(i, i ^ step) for i in range(lax.axis_size(axi...  16.1 us
    pallas_call x1, Pallas kernels, project(): pl.pallas_call(project_kernel, in_specs=[anywhere] * 2, out_specs=[in_vme...  3.06 us
    pallas_call x1, Pallas kernels, first_part(): pl.pallas_call(functools.partial(first_kernel, features, steps), in_specs...  2.42 us
    pallas_call x1, Pallas kernels, rest_part(): pl.pallas_call(functools.partial(rest_kernel, features, rows, steps), in_...  2.27 us
    pallas_call x1, Pallas kernels, finish(): pl.pallas_call(functools.partial(finish_kernel, features, count), in_spec...  1.09 us
  transfers between devices with their start and end apart: 13, of which 8 were waited for; matrix products, arithmetic and copies ran while one was open for 0% of the time, Pallas kernels for 12%

profile of v7, /device:TPU:0, one launch (start us, length us, event | category | flops | bytes accessed | tf_op | source)
XLA Modules:
  0.0 44.6 jit_solution(15138439280193242886)
XLA Ops:
  0.0 2.9 %collective-permute-start.5 = (f32[64,3584]{1,0:T(8,128)}, f32[64,3584]{1,0:T(8,128)S(1)}, u32[]{:S(2)}, u32[]{:S(2)}) collective-permute-start(f32[64,3584]{1,0:T(8,128)} %x_hbm.1), channel_id=1, source_target_pairs={{0,16},{8,24},{16,0},{24,8},{1,17},{9,25},{17,1},{25,9},{2,18},{10... | collective-permute-start | bytes 2752520 | tf_op jit(solution)/shard_map/ppermute | solution.py:225
  2.9 3.1 %project.1 = (f32[64,256]{1,0:T(8,128)S(1)}, f32[64,3584]{1,0:T(8,128)S(1)}, f32[192,3584]{1,0:T(8,128)S(1)}) custom-call(f32[64,3584]{1,0:T(8,128)} %x_hbm.1, f32[192,3584]{1,0:T(8,128)} %bitcast.1), custom_call_target="tpu_custom_call" | custom-call | tf_op jit(solution)/shard_map/project/pallas_call | solution.py:83
  6.0 1.6 %collective-permute-start = (f32[64,256]{1,0:T(8,128)S(1)}, f32[64,256]{1,0:T(8,128)S(1)}, u32[]{:S(2)}, u32[]{:S(2)}) collective-permute-start(f32[64,256]{1,0:T(8,128)S(1)} %get-tuple-element.12), channel_id=1, source_target_pairs={{0,1},{1,0},{2,3},{3,2},{4,5},{5,4},{6,7},{7,6},{8,9},{9,8},{10,11... | collective-permute-start | bytes 196616 | tf_op jit(solution)/shard_map/ppermute | solution.py:225
  7.6 2.7 %collective-permute-done = f32[64,256]{1,0:T(8,128)S(1)} collective-permute-done((f32[64,256]{1,0:T(8,128)S(1)}, f32[64,256]{1,0:T(8,128)S(1)}, u32[]{:S(2)}, u32[]{:S(2)}) %collective-permute-start) | collective-permute-done | bytes 65568 | tf_op jit(solution)/shard_map/ppermute | solution.py:225
  10.3 1.6 %collective-permute-start.1 = (f32[64,256]{1,0:T(8,128)S(1)}, f32[64,256]{1,0:T(8,128)S(1)}, u32[]{:S(2)}, u32[]{:S(2)}) collective-permute-start(f32[64,256]{1,0:T(8,128)S(1)} %add.12), channel_id=1, source_target_pairs={{0,2},{1,3},{2,0},{3,1},{4,6},{5,7},{6,4},{7,5},{8,10},{9,11},{10,... | collective-permute-start | bytes 196616 | tf_op jit(solution)/shard_map/ppermute | solution.py:225
  12.0 2.7 %collective-permute-done.1 = f32[64,256]{1,0:T(8,128)S(1)} collective-permute-done((f32[64,256]{1,0:T(8,128)S(1)}, f32[64,256]{1,0:T(8,128)S(1)}, u32[]{:S(2)}, u32[]{:S(2)}) %collective-permute-start.1) | collective-permute-done | bytes 65568 | tf_op jit(solution)/shard_map/ppermute | solution.py:225
  14.7 2.7 %collective-permute-start.2 = (f32[64,256]{1,0:T(8,128)S(1)}, f32[64,256]{1,0:T(8,128)S(1)}, u32[]{:S(2)}, u32[]{:S(2)}) collective-permute-start(f32[64,256]{1,0:T(8,128)S(1)} %add.13), channel_id=1, source_target_pairs={{0,4},{1,5},{2,6},{3,7},{4,0},{5,1},{6,2},{7,3},{8,12},{9,13},{10,... | collective-permute-start | bytes 196616 | tf_op jit(solution)/shard_map/ppermute | solution.py:225
  17.4 2.6 %collective-permute-done.2 = f32[64,256]{1,0:T(8,128)S(1)} collective-permute-done((f32[64,256]{1,0:T(8,128)S(1)}, f32[64,256]{1,0:T(8,128)S(1)}, u32[]{:S(2)}, u32[]{:S(2)}) %collective-permute-start.2) | collective-permute-done | bytes 65568 | tf_op jit(solution)/shard_map/ppermute | solution.py:225
  19.9 0.1 collective-permute-start.3
  20.0 0.3 collective-permute-start.6
  20.3 0.2 collective-permute-start.4
  20.5 0.7 %collective-permute-done.3.refs_0_ = f32[64,256]{1,0:T(8,128)S(1)} collective-permute-done((f32[64,256]{1,0:T(8,128)S(1)}, f32[64,256]{1,0:T(8,128)S(1)}, u32[]{:S(2)}, u32[]{:S(2)}) %collective-permute-start.3) | collective-permute-done | bytes 65568 | tf_op jit(solution)/shard_map/ppermute | solution.py:225
  21.3 3.6 %collective-permute-done.6.refs_0_ = f32[64,256]{1,0:T(8,128)S(1)} collective-permute-done((f32[64,256]{1,0:T(8,128)S(1)}, f32[64,256]{1,0:T(8,128)S(1)}, u32[]{:S(2)}, u32[]{:S(2)}) %collective-permute-start.6) | collective-permute-done | bytes 65568 | tf_op jit(solution)/shard_map/ppermute | solution.py:225
  24.9 0.0 collective-permute-done.5.refs_2_
  24.9 0.0 collective-permute-start.8
  24.9 0.5 %collective-permute-start.7 = (f32[64,256]{1,0:T(8,128)S(1)}, f32[64,256]{1,0:T(8,128)S(1)}, u32[]{:S(2)}, u32[]{:S(2)}) collective-permute-start(f32[64,256]{1,0:T(8,128)S(1)} %collective-permute-done.6.refs_0_), channel_id=1, source_target_pairs={{0,8},{8,0},{16,24},{24,16},{1,9},{9,1},{17,25},{25,17},{2,10},{10... | collective-permute-start | bytes 196616 | tf_op jit(solution)/shard_map/ppermute | solution.py:225
  25.4 0.0 collective-permute-done.4.refs_1_
  25.4 2.4 %first_part.1.t_ref = f32[64,3584]{1,0:T(8,128)S(1)} custom-call(f32[64,256]{1,0:T(8,128)S(1)} %add.14.p_ref, f32[192,3584]{1,0:T(8,128)S(1)} %get-tuple-element.13.s_ref, f32[64,3584]{1,0:T(8,128)S(1)} %get-tuple-element.14.x_ref, f32[64,256]{1,0:T(8,128)S(1)} %collective-permute-done.3.refs_0_, f32[64,3584]{1,0:T(8,128)S(1)} %collective-permute-done.4.refs_1_), custom_call_target="tpu_custom_call" | custom-call | tf_op jit(solution)/shard_map/first_part/pallas_call | solution.py:140
  27.8 0.0 collective-permute-done.7.refs_1_
  27.9 0.0 collective-permute-done.8.refs_3_
  27.9 2.3 %rest_part.1 = (f32[64,3584]{1,0:T(8,128)S(1)}, f32[1,64]{1,0:T(1,128)S(1)}) custom-call(f32[64,3584]{1,0:T(8,128)S(1)} %first_part.1.t_ref, f32[64,256]{1,0:T(8,128)S(1)} %add.14.p_ref, f32[64,256]{1,0:T(8,128)S(1)} %collective-permute-done.6.refs_0_, f32[64,256]{1,0:T(8,128)S(1)} %collective-permute-done.7.refs_1_, ...), custom_call_target="tpu_custom_call" | custom-call | tf_op jit(solution)/shard_map/rest_part/pallas_call | solution.py:170
  30.1 1.8 %collective-permute-start.9 = (f32[1,64]{1,0:T(1,128)S(1)}, f32[1,64]{1,0:T(1,128)S(1)}, u32[]{:S(2)}, u32[]{:S(2)}) collective-permute-start(f32[1,64]{1,0:T(1,128)S(1)} %get-tuple-element.18), channel_id=1, source_target_pairs={{0,1},{1,0},{2,3},{3,2},{4,5},{5,4},{6,7},{7,6},{8,9},{9,8},{10,11... | collective-permute-start | bytes 776 | tf_op jit(solution)/shard_map/ppermute | solution.py:225
  32.0 1.8 %collective-permute-done.9 = f32[1,64]{1,0:T(1,128)S(1)} collective-permute-done((f32[1,64]{1,0:T(1,128)S(1)}, f32[1,64]{1,0:T(1,128)S(1)}, u32[]{:S(2)}, u32[]{:S(2)}) %collective-permute-start.9) | collective-permute-done | bytes 288 | tf_op jit(solution)/shard_map/ppermute | solution.py:225
  33.7 1.8 %collective-permute-start.10 = (f32[1,64]{1,0:T(1,128)S(1)}, f32[1,64]{1,0:T(1,128)S(1)}, u32[]{:S(2)}, u32[]{:S(2)}) collective-permute-start(f32[1,64]{1,0:T(1,128)S(1)} %add.15.refs_0_), channel_id=1, source_target_pairs={{0,2},{1,3},{2,0},{3,1},{4,6},{5,7},{6,4},{7,5},{8,10},{9,11},{10,... | collective-permute-start | bytes 776 | tf_op jit(solution)/shard_map/ppermute | solution.py:225
  35.6 2.6 %collective-permute-start.11 = (f32[1,64]{1,0:T(1,128)S(1)}, f32[1,64]{1,0:T(1,128)S(1)}, u32[]{:S(2)}, u32[]{:S(2)}) collective-permute-start(f32[1,64]{1,0:T(1,128)S(1)} %add.15.refs_0_), channel_id=1, source_target_pairs={{0,4},{1,5},{2,6},{3,7},{4,0},{5,1},{6,2},{7,3},{8,12},{9,13},{10,... | collective-permute-start | bytes 776 | tf_op jit(solution)/shard_map/ppermute | solution.py:225
  38.2 0.0 collective-permute-start.12
  38.2 0.0 collective-permute-done.10.refs_1_
  38.2 1.8 %collective-permute-done.11.refs_2_ = f32[1,64]{1,0:T(1,128)S(1)} collective-permute-done((f32[1,64]{1,0:T(1,128)S(1)}, f32[1,64]{1,0:T(1,128)S(1)}, u32[]{:S(2)}, u32[]{:S(2)}) %collective-permute-start.11) | collective-permute-done | bytes 288 | tf_op jit(solution)/shard_map/ppermute | solution.py:225
  40.0 3.5 %collective-permute-done.12.refs_3_ = f32[1,64]{1,0:T(1,128)S(1)} collective-permute-done((f32[1,64]{1,0:T(1,128)S(1)}, f32[1,64]{1,0:T(1,128)S(1)}, u32[]{:S(2)}, u32[]{:S(2)}) %collective-permute-start.12) | collective-permute-done | bytes 288 | tf_op jit(solution)/shard_map/ppermute | solution.py:225
  43.5 1.1 %finish.1 = f32[64,3584]{1,0:T(8,128)} custom-call(f32[64,3584]{1,0:T(8,128)S(1)} %get-tuple-element.17.updated_ref, f32[1,64]{1,0:T(1,128)S(1)} %add.15.refs_0_, f32[1,64]{1,0:T(1,128)S(1)} %collective-permute-done.10.refs_1_, f32[1,64]{1,0:T(1,128)S(1)} %collective-permute-done.11.refs_2_, f32[1,64]{1,0:T(1,128)S(1)} %collective-permute-done.12.refs_3_), custom_call_target="tpu_custom_call" | custom-call | tf_op jit(solution)/shard_map/finish/pallas_call | solution.py:210
  (4 shorter events, 0.0 us)
Async XLA Ops:
  0.0 24.9 %collective-permute-start.5 = (f32[64,3584]{1,0:T(8,128)}, f32[64,3584]{1,0:T(8,128)S(1)}, u32[]{:S(2)}, u32[]{:S(2)}) collective-permute-start(f32[64,3584]{1,0:T(8,128)} %x_hbm.1), channel_id=1, source_target_pairs={{0,16},{8,24},{16,0},{24,8},{1,17},{9,25},{17,1},{25,9},{2,18},{10... | collective-permute-start | bytes 2752520 | tf_op jit(solution)/shard_map/ppermute | solution.py:225
  6.0 4.3 %collective-permute-start = (f32[64,256]{1,0:T(8,128)S(1)}, f32[64,256]{1,0:T(8,128)S(1)}, u32[]{:S(2)}, u32[]{:S(2)}) collective-permute-start(f32[64,256]{1,0:T(8,128)S(1)} %get-tuple-element.12), channel_id=1, source_target_pairs={{0,1},{1,0},{2,3},{3,2},{4,5},{5,4},{6,7},{7,6},{8,9},{9,8},{10,11... | collective-permute-start | bytes 196616 | tf_op jit(solution)/shard_map/ppermute | solution.py:225
  10.3 4.3 %collective-permute-start.1 = (f32[64,256]{1,0:T(8,128)S(1)}, f32[64,256]{1,0:T(8,128)S(1)}, u32[]{:S(2)}, u32[]{:S(2)}) collective-permute-start(f32[64,256]{1,0:T(8,128)S(1)} %add.12), channel_id=1, source_target_pairs={{0,2},{1,3},{2,0},{3,1},{4,6},{5,7},{6,4},{7,5},{8,10},{9,11},{10,... | collective-permute-start | bytes 196616 | tf_op jit(solution)/shard_map/ppermute | solution.py:225
  14.7 5.2 %collective-permute-start.2 = (f32[64,256]{1,0:T(8,128)S(1)}, f32[64,256]{1,0:T(8,128)S(1)}, u32[]{:S(2)}, u32[]{:S(2)}) collective-permute-start(f32[64,256]{1,0:T(8,128)S(1)} %add.13), channel_id=1, source_target_pairs={{0,4},{1,5},{2,6},{3,7},{4,0},{5,1},{6,2},{7,3},{8,12},{9,13},{10,... | collective-permute-start | bytes 196616 | tf_op jit(solution)/shard_map/ppermute | solution.py:225
  19.9 1.3 %collective-permute-start.3 = (f32[64,256]{1,0:T(8,128)S(1)}, f32[64,256]{1,0:T(8,128)S(1)}, u32[]{:S(2)}, u32[]{:S(2)}) collective-permute-start(f32[64,256]{1,0:T(8,128)S(1)} %add.14.p_ref), channel_id=1, source_target_pairs={{0,8},{8,0},{16,24},{24,16},{1,9},{9,1},{17,25},{25,17},{2,10},{10... | collective-permute-start | bytes 196616 | tf_op jit(solution)/shard_map/ppermute | solution.py:225
  20.0 4.9 %collective-permute-start.6 = (f32[64,256]{1,0:T(8,128)S(1)}, f32[64,256]{1,0:T(8,128)S(1)}, u32[]{:S(2)}, u32[]{:S(2)}) collective-permute-start(f32[64,256]{1,0:T(8,128)S(1)} %add.14.p_ref), channel_id=1, source_target_pairs={{0,16},{8,24},{16,0},{24,8},{1,17},{9,25},{17,1},{25,9},{2,18},{10... | collective-permute-start | bytes 196616 | tf_op jit(solution)/shard_map/ppermute | solution.py:225
  20.3 5.1 %collective-permute-start.4 = (f32[64,3584]{1,0:T(8,128)S(1)}, f32[64,3584]{1,0:T(8,128)S(1)}, u32[]{:S(2)}, u32[]{:S(2)}) collective-permute-start(f32[64,3584]{1,0:T(8,128)S(1)} %get-tuple-element.14.x_ref), channel_id=1, source_target_pairs={{0,8},{8,0},{16,24},{24,16},{1,9},{9,1},{17,25},{25,17},{2,10},{10... | collective-permute-start | bytes 2752520 | tf_op jit(solution)/shard_map/ppermute | solution.py:225
  24.9 3.0 %collective-permute-start.8 = (f32[64,3584]{1,0:T(8,128)S(1)}, f32[64,3584]{1,0:T(8,128)S(1)}, u32[]{:S(2)}, u32[]{:S(2)}) collective-permute-start(f32[64,3584]{1,0:T(8,128)S(1)} %collective-permute-done.5.refs_2_), channel_id=1, source_target_pairs={{0,8},{8,0},{16,24},{24,16},{1,9},{9,1},{17,25},{25,17},{2,10},{10... | collective-permute-start | bytes 2752520 | tf_op jit(solution)/shard_map/ppermute | solution.py:225
  24.9 2.9 %collective-permute-start.7 = (f32[64,256]{1,0:T(8,128)S(1)}, f32[64,256]{1,0:T(8,128)S(1)}, u32[]{:S(2)}, u32[]{:S(2)}) collective-permute-start(f32[64,256]{1,0:T(8,128)S(1)} %collective-permute-done.6.refs_0_), channel_id=1, source_target_pairs={{0,8},{8,0},{16,24},{24,16},{1,9},{9,1},{17,25},{25,17},{2,10},{10... | collective-permute-start | bytes 196616 | tf_op jit(solution)/shard_map/ppermute | solution.py:225
  30.1 3.6 %collective-permute-start.9 = (f32[1,64]{1,0:T(1,128)S(1)}, f32[1,64]{1,0:T(1,128)S(1)}, u32[]{:S(2)}, u32[]{:S(2)}) collective-permute-start(f32[1,64]{1,0:T(1,128)S(1)} %get-tuple-element.18), channel_id=1, source_target_pairs={{0,1},{1,0},{2,3},{3,2},{4,5},{5,4},{6,7},{7,6},{8,9},{9,8},{10,11... | collective-permute-start | bytes 776 | tf_op jit(solution)/shard_map/ppermute | solution.py:225
  33.7 4.4 %collective-permute-start.10 = (f32[1,64]{1,0:T(1,128)S(1)}, f32[1,64]{1,0:T(1,128)S(1)}, u32[]{:S(2)}, u32[]{:S(2)}) collective-permute-start(f32[1,64]{1,0:T(1,128)S(1)} %add.15.refs_0_), channel_id=1, source_target_pairs={{0,2},{1,3},{2,0},{3,1},{4,6},{5,7},{6,4},{7,5},{8,10},{9,11},{10,... | collective-permute-start | bytes 776 | tf_op jit(solution)/shard_map/ppermute | solution.py:225
  35.6 4.4 %collective-permute-start.11 = (f32[1,64]{1,0:T(1,128)S(1)}, f32[1,64]{1,0:T(1,128)S(1)}, u32[]{:S(2)}, u32[]{:S(2)}) collective-permute-start(f32[1,64]{1,0:T(1,128)S(1)} %add.15.refs_0_), channel_id=1, source_target_pairs={{0,4},{1,5},{2,6},{3,7},{4,0},{5,1},{6,2},{7,3},{8,12},{9,13},{10,... | collective-permute-start | bytes 776 | tf_op jit(solution)/shard_map/ppermute | solution.py:225
  38.2 5.3 %collective-permute-start.12 = (f32[1,64]{1,0:T(1,128)S(1)}, f32[1,64]{1,0:T(1,128)S(1)}, u32[]{:S(2)}, u32[]{:S(2)}) collective-permute-start(f32[1,64]{1,0:T(1,128)S(1)} %add.15.refs_0_), channel_id=1, source_target_pairs={{0,6},{1,7},{2,4},{3,5},{4,2},{5,3},{6,0},{7,1},{8,14},{9,15},{10,... | collective-permute-start | bytes 776 | tf_op jit(solution)/shard_map/ppermute | solution.py:225

commit v8 on v7

--- a/solution.py
+++ b/solution.py
@@ -43,7 +43,7 @@
 
 def loop(columns, most, body, init):
     tile = tile_of(columns, most)
-    return lax.fori_loop(0, columns // tile, lambda i, c: body(i, pl.ds(pl.multiple_of(i * tile, tile), tile), c), init)
+    return lax.fori_loop(0, columns // tile, lambda i, c: body(i, pl.ds(pl.multiple_of(i * tile, tile), tile), c), init, unroll=True)
 
 
 def project_kernel(x_hbm, s_hbm, out_ref, x_ref, s_ref, sems):
@@ -229,12 +229,12 @@
     size = lax.axis_size(axis)
     if size & (size - 1):
         return [lax.psum(array, axis)]
-    parts, step, bits = [array], 1, (size.bit_length() - 1) % together or together
+    parts, step = [array], 1
     while step < size:
         array = sum(parts[1:], parts[0])
-        parts = [array] + [exchange(array, axis, step * k) for k in range(1, 1 << bits)]
-        step <<= bits
-        bits = together
+        width = min(1 << together, size // step)
+        parts = [array] + [exchange(array, axis, step * k) for k in range(1, width)]
+        step *= width
     return parts
 
 

time: 44.7 us -> 40.9 us (0.915)
  Pallas kernels: 8.83 us -> 6.39 us
  waiting for transfers between devices: 19.5 us -> 18.2 us
    pallas_call x1, Pallas kernels: 2.27 us -> 0.9 us  [rest_part(): pl.pallas_call(functools.partial(rest_kernel, features, rows, steps), in_...]
    ppermute x13, waiting for transfers between devices: 19.5 us -> 18.2 us  [exchange(): lax.ppermute(array, axis, [(i, i ^ step) for i in range(lax.axis_size(axi...]
    pallas_call x1, Pallas kernels: 2.42 us -> 1.47 us  [first_part(): pl.pallas_call(functools.partial(first_kernel, features, steps), in_specs...]
  transfers between devices with their start and end apart: 13 -> 13, of which waited for: 8 -> 10; matrix products, arithmetic and copies ran while one was open for 0% -> 0% of each run, Pallas kernels for 12% -> 11%
where the time goes in v8:
time: 40.9 us; the launch traced here: 40.8 us
  waiting for transfers between devices  18.2 us (44%)
  starting transfers between devices  16 us (39%)
  Pallas kernels  6.39 us (16%)
    ppermute x13, waiting for transfers between devices, exchange(): lax.ppermute(array, axis, [(i, i ^ step) for i in range(lax.axis_size(axi...  18.2 us
    ppermute x13, starting transfers between devices, exchange(): lax.ppermute(array, axis, [(i, i ^ step) for i in range(lax.axis_size(axi...  16 us
    pallas_call x1, Pallas kernels, project(): pl.pallas_call(project_kernel, in_specs=[anywhere] * 2, out_specs=[in_vme...  2.93 us
    pallas_call x1, Pallas kernels, first_part(): pl.pallas_call(functools.partial(first_kernel, features, steps), in_specs...  1.47 us
    pallas_call x1, Pallas kernels, finish(): pl.pallas_call(functools.partial(finish_kernel, features, count), in_spec...  1.08 us
    pallas_call x1, Pallas kernels, rest_part(): pl.pallas_call(functools.partial(rest_kernel, features, rows, steps), in_...  0.9 us
  transfers between devices with their start and end apart: 13, of which 10 were waited for; matrix products, arithmetic and copies ran while one was open for 0% of the time, Pallas kernels for 11%

profile of v8, /device:TPU:0, one launch (start us, length us, event | category | flops | bytes accessed | tf_op | source)
XLA Modules:
  0.0 40.8 jit_solution(5010281003231472964)
XLA Ops:
  0.0 2.9 %collective-permute-start.5 = (f32[64,3584]{1,0:T(8,128)}, f32[64,3584]{1,0:T(8,128)S(1)}, u32[]{:S(2)}, u32[]{:S(2)}) collective-permute-start(f32[64,3584]{1,0:T(8,128)} %x_hbm.1), channel_id=1, source_target_pairs={{0,16},{8,24},{16,0},{24,8},{1,17},{9,25},{17,1},{25,9},{2,18},{10... | collective-permute-start | bytes 2752520 | tf_op jit(solution)/shard_map/ppermute | solution.py:225
  2.9 2.9 %project.1 = (f32[64,256]{1,0:T(8,128)S(1)}, f32[64,3584]{1,0:T(8,128)S(1)}, f32[192,3584]{1,0:T(8,128)S(1)}) custom-call(f32[64,3584]{1,0:T(8,128)} %x_hbm.1, f32[192,3584]{1,0:T(8,128)} %bitcast.1), custom_call_target="tpu_custom_call" | custom-call | tf_op jit(solution)/shard_map/project/pallas_call | solution.py:83
  5.9 1.6 %collective-permute-start = (f32[64,256]{1,0:T(8,128)S(1)}, f32[64,256]{1,0:T(8,128)S(1)}, u32[]{:S(2)}, u32[]{:S(2)}) collective-permute-start(f32[64,256]{1,0:T(8,128)S(1)} %get-tuple-element.12), channel_id=1, source_target_pairs={{0,1},{1,0},{2,3},{3,2},{4,5},{5,4},{6,7},{7,6},{8,9},{9,8},{10,11... | collective-permute-start | bytes 196616 | tf_op jit(solution)/shard_map/ppermute | solution.py:225
  7.5 2.7 %collective-permute-done = f32[64,256]{1,0:T(8,128)S(1)} collective-permute-done((f32[64,256]{1,0:T(8,128)S(1)}, f32[64,256]{1,0:T(8,128)S(1)}, u32[]{:S(2)}, u32[]{:S(2)}) %collective-permute-start) | collective-permute-done | bytes 65568 | tf_op jit(solution)/shard_map/ppermute | solution.py:225
  10.2 1.6 %collective-permute-start.1 = (f32[64,256]{1,0:T(8,128)S(1)}, f32[64,256]{1,0:T(8,128)S(1)}, u32[]{:S(2)}, u32[]{:S(2)}) collective-permute-start(f32[64,256]{1,0:T(8,128)S(1)} %add.18), channel_id=1, source_target_pairs={{0,2},{1,3},{2,0},{3,1},{4,6},{5,7},{6,4},{7,5},{8,10},{9,11},{10,... | collective-permute-start | bytes 196616 | tf_op jit(solution)/shard_map/ppermute | solution.py:225
  11.9 2.7 %collective-permute-done.1 = f32[64,256]{1,0:T(8,128)S(1)} collective-permute-done((f32[64,256]{1,0:T(8,128)S(1)}, f32[64,256]{1,0:T(8,128)S(1)}, u32[]{:S(2)}, u32[]{:S(2)}) %collective-permute-start.1) | collective-permute-done | bytes 65568 | tf_op jit(solution)/shard_map/ppermute | solution.py:225
  14.6 2.7 %collective-permute-start.2 = (f32[64,256]{1,0:T(8,128)S(1)}, f32[64,256]{1,0:T(8,128)S(1)}, u32[]{:S(2)}, u32[]{:S(2)}) collective-permute-start(f32[64,256]{1,0:T(8,128)S(1)} %add.19), channel_id=1, source_target_pairs={{0,4},{1,5},{2,6},{3,7},{4,0},{5,1},{6,2},{7,3},{8,12},{9,13},{10,... | collective-permute-start | bytes 196616 | tf_op jit(solution)/shard_map/ppermute | solution.py:225
  17.2 2.6 %collective-permute-done.2 = f32[64,256]{1,0:T(8,128)S(1)} collective-permute-done((f32[64,256]{1,0:T(8,128)S(1)}, f32[64,256]{1,0:T(8,128)S(1)}, u32[]{:S(2)}, u32[]{:S(2)}) %collective-permute-start.2) | collective-permute-done | bytes 65568 | tf_op jit(solution)/shard_map/ppermute | solution.py:225
  19.8 0.1 collective-permute-start.3
  19.9 0.3 collective-permute-start.6
  20.2 0.2 collective-permute-start.4
  20.4 0.7 %collective-permute-done.3.refs_0_ = f32[64,256]{1,0:T(8,128)S(1)} collective-permute-done((f32[64,256]{1,0:T(8,128)S(1)}, f32[64,256]{1,0:T(8,128)S(1)}, u32[]{:S(2)}, u32[]{:S(2)}) %collective-permute-start.3) | collective-permute-done | bytes 65568 | tf_op jit(solution)/shard_map/ppermute | solution.py:225
  21.1 3.8 %collective-permute-done.6.refs_0_ = f32[64,256]{1,0:T(8,128)S(1)} collective-permute-done((f32[64,256]{1,0:T(8,128)S(1)}, f32[64,256]{1,0:T(8,128)S(1)}, u32[]{:S(2)}, u32[]{:S(2)}) %collective-permute-start.6) | collective-permute-done | bytes 65568 | tf_op jit(solution)/shard_map/ppermute | solution.py:225
  24.9 0.0 collective-permute-done.5.refs_2_
  24.9 0.0 collective-permute-start.8
  24.9 0.5 %collective-permute-start.7 = (f32[64,256]{1,0:T(8,128)S(1)}, f32[64,256]{1,0:T(8,128)S(1)}, u32[]{:S(2)}, u32[]{:S(2)}) collective-permute-start(f32[64,256]{1,0:T(8,128)S(1)} %collective-permute-done.6.refs_0_), channel_id=1, source_target_pairs={{0,8},{8,0},{16,24},{24,16},{1,9},{9,1},{17,25},{25,17},{2,10},{10... | collective-permute-start | bytes 196616 | tf_op jit(solution)/shard_map/ppermute | solution.py:225
  25.4 0.0 collective-permute-done.4.refs_1_
  25.4 1.5 %first_part.1.t_ref = f32[64,3584]{1,0:T(8,128)S(1)} custom-call(f32[64,256]{1,0:T(8,128)S(1)} %add.20.p_ref, f32[192,3584]{1,0:T(8,128)S(1)} %get-tuple-element.13.s_ref, f32[64,3584]{1,0:T(8,128)S(1)} %get-tuple-element.14.x_ref, f32[64,256]{1,0:T(8,128)S(1)} %collective-permute-done.3.refs_0_, f32[64,3584]{1,0:T(8,128)S(1)} %collective-permute-done.4.refs_1_), custom_call_target="tpu_custom_call" | custom-call | tf_op jit(solution)/shard_map/first_part/pallas_call | solution.py:140
  26.9 0.6 %collective-permute-done.7.refs_1_ = f32[64,256]{1,0:T(8,128)S(1)} collective-permute-done((f32[64,256]{1,0:T(8,128)S(1)}, f32[64,256]{1,0:T(8,128)S(1)}, u32[]{:S(2)}, u32[]{:S(2)}) %collective-permute-start.7) | collective-permute-done | bytes 65568 | tf_op jit(solution)/shard_map/ppermute | solution.py:225
  27.5 0.0 collective-permute-done.8.refs_3_
  27.5 0.9 %rest_part.1 = (f32[64,3584]{1,0:T(8,128)S(1)}, f32[1,64]{1,0:T(1,128)S(1)}) custom-call(f32[64,3584]{1,0:T(8,128)S(1)} %first_part.1.t_ref, f32[64,256]{1,0:T(8,128)S(1)} %add.20.p_ref, f32[64,256]{1,0:T(8,128)S(1)} %collective-permute-done.6.refs_0_, f32[64,256]{1,0:T(8,128)S(1)} %collective-permute-done.7.refs_1_, ...), custom_call_target="tpu_custom_call" | custom-call | tf_op jit(solution)/shard_map/rest_part/pallas_call | solution.py:170
  28.4 2.8 %collective-permute-start.11 = (f32[1,64]{1,0:T(1,128)S(1)}, f32[1,64]{1,0:T(1,128)S(1)}, u32[]{:S(2)}, u32[]{:S(2)}) collective-permute-start(f32[1,64]{1,0:T(1,128)S(1)} %get-tuple-element.18), channel_id=1, source_target_pairs={{0,3},{1,2},{2,1},{3,0},{4,7},{5,6},{6,5},{7,4},{8,11},{9,10},{10,... | collective-permute-start | bytes 776 | tf_op jit(solution)/shard_map/ppermute | solution.py:225
  31.2 0.5 %collective-permute-start.10 = (f32[1,64]{1,0:T(1,128)S(1)}, f32[1,64]{1,0:T(1,128)S(1)}, u32[]{:S(2)}, u32[]{:S(2)}) collective-permute-start(f32[1,64]{1,0:T(1,128)S(1)} %get-tuple-element.18), channel_id=1, source_target_pairs={{0,2},{1,3},{2,0},{3,1},{4,6},{5,7},{6,4},{7,5},{8,10},{9,11},{10,... | collective-permute-start | bytes 776 | tf_op jit(solution)/shard_map/ppermute | solution.py:225
  31.7 0.3 collective-permute-start.9
  31.9 0.9 %collective-permute-done.11 = f32[1,64]{1,0:T(1,128)S(1)} collective-permute-done((f32[1,64]{1,0:T(1,128)S(1)}, f32[1,64]{1,0:T(1,128)S(1)}, u32[]{:S(2)}, u32[]{:S(2)}) %collective-permute-start.11) | collective-permute-done | bytes 288 | tf_op jit(solution)/shard_map/ppermute | solution.py:225
  32.9 1.9 %collective-permute-done.10 = f32[1,64]{1,0:T(1,128)S(1)} collective-permute-done((f32[1,64]{1,0:T(1,128)S(1)}, f32[1,64]{1,0:T(1,128)S(1)}, u32[]{:S(2)}, u32[]{:S(2)}) %collective-permute-start.10) | collective-permute-done | bytes 288 | tf_op jit(solution)/shard_map/ppermute | solution.py:225
  34.8 0.5 %collective-permute-done.9 = f32[1,64]{1,0:T(1,128)S(1)} collective-permute-done((f32[1,64]{1,0:T(1,128)S(1)}, f32[1,64]{1,0:T(1,128)S(1)}, u32[]{:S(2)}, u32[]{:S(2)}) %collective-permute-start.9) | collective-permute-done | bytes 288 | tf_op jit(solution)/shard_map/ppermute | solution.py:225
  35.2 2.6 %collective-permute-start.12 = (f32[1,64]{1,0:T(1,128)S(1)}, f32[1,64]{1,0:T(1,128)S(1)}, u32[]{:S(2)}, u32[]{:S(2)}) collective-permute-start(f32[1,64]{1,0:T(1,128)S(1)} %add_add_fusion.refs_0_), channel_id=1, source_target_pairs={{0,4},{1,5},{2,6},{3,7},{4,0},{5,1},{6,2},{7,3},{8,12},{9,13},{10,... | collective-permute-start | bytes 776 | tf_op jit(solution)/shard_map/ppermute | solution.py:225
  37.8 1.9 %collective-permute-done.12.refs_1_ = f32[1,64]{1,0:T(1,128)S(1)} collective-permute-done((f32[1,64]{1,0:T(1,128)S(1)}, f32[1,64]{1,0:T(1,128)S(1)}, u32[]{:S(2)}, u32[]{:S(2)}) %collective-permute-start.12) | collective-permute-done | bytes 288 | tf_op jit(solution)/shard_map/ppermute | solution.py:225
  39.7 1.1 %finish.1 = f32[64,3584]{1,0:T(8,128)} custom-call(f32[64,3584]{1,0:T(8,128)S(1)} %get-tuple-element.17.updated_ref, f32[1,64]{1,0:T(1,128)S(1)} %add_add_fusion.refs_0_, f32[1,64]{1,0:T(1,128)S(1)} %collective-permute-done.12.refs_1_), custom_call_target="tpu_custom_call" | custom-call | tf_op jit(solution)/shard_map/finish/pallas_call | solution.py:210
  (4 shorter events, 0.0 us)
Async XLA Ops:
  0.0 24.9 %collective-permute-start.5 = (f32[64,3584]{1,0:T(8,128)}, f32[64,3584]{1,0:T(8,128)S(1)}, u32[]{:S(2)}, u32[]{:S(2)}) collective-permute-start(f32[64,3584]{1,0:T(8,128)} %x_hbm.1), channel_id=1, source_target_pairs={{0,16},{8,24},{16,0},{24,8},{1,17},{9,25},{17,1},{25,9},{2,18},{10... | collective-permute-start | bytes 2752520 | tf_op jit(solution)/shard_map/ppermute | solution.py:225
  5.9 4.3 %collective-permute-start = (f32[64,256]{1,0:T(8,128)S(1)}, f32[64,256]{1,0:T(8,128)S(1)}, u32[]{:S(2)}, u32[]{:S(2)}) collective-permute-start(f32[64,256]{1,0:T(8,128)S(1)} %get-tuple-element.12), channel_id=1, source_target_pairs={{0,1},{1,0},{2,3},{3,2},{4,5},{5,4},{6,7},{7,6},{8,9},{9,8},{10,11... | collective-permute-start | bytes 196616 | tf_op jit(solution)/shard_map/ppermute | solution.py:225
  10.2 4.3 %collective-permute-start.1 = (f32[64,256]{1,0:T(8,128)S(1)}, f32[64,256]{1,0:T(8,128)S(1)}, u32[]{:S(2)}, u32[]{:S(2)}) collective-permute-start(f32[64,256]{1,0:T(8,128)S(1)} %add.18), channel_id=1, source_target_pairs={{0,2},{1,3},{2,0},{3,1},{4,6},{5,7},{6,4},{7,5},{8,10},{9,11},{10,... | collective-permute-start | bytes 196616 | tf_op jit(solution)/shard_map/ppermute | solution.py:225
  14.6 5.2 %collective-permute-start.2 = (f32[64,256]{1,0:T(8,128)S(1)}, f32[64,256]{1,0:T(8,128)S(1)}, u32[]{:S(2)}, u32[]{:S(2)}) collective-permute-start(f32[64,256]{1,0:T(8,128)S(1)} %add.19), channel_id=1, source_target_pairs={{0,4},{1,5},{2,6},{3,7},{4,0},{5,1},{6,2},{7,3},{8,12},{9,13},{10,... | collective-permute-start | bytes 196616 | tf_op jit(solution)/shard_map/ppermute | solution.py:225
  19.8 1.3 %collective-permute-start.3 = (f32[64,256]{1,0:T(8,128)S(1)}, f32[64,256]{1,0:T(8,128)S(1)}, u32[]{:S(2)}, u32[]{:S(2)}) collective-permute-start(f32[64,256]{1,0:T(8,128)S(1)} %add.20.p_ref), channel_id=1, source_target_pairs={{0,8},{8,0},{16,24},{24,16},{1,9},{9,1},{17,25},{25,17},{2,10},{10... | collective-permute-start | bytes 196616 | tf_op jit(solution)/shard_map/ppermute | solution.py:225
  19.9 5.0 %collective-permute-start.6 = (f32[64,256]{1,0:T(8,128)S(1)}, f32[64,256]{1,0:T(8,128)S(1)}, u32[]{:S(2)}, u32[]{:S(2)}) collective-permute-start(f32[64,256]{1,0:T(8,128)S(1)} %add.20.p_ref), channel_id=1, source_target_pairs={{0,16},{8,24},{16,0},{24,8},{1,17},{9,25},{17,1},{25,9},{2,18},{10... | collective-permute-start | bytes 196616 | tf_op jit(solution)/shard_map/ppermute | solution.py:225
  20.2 5.3 %collective-permute-start.4 = (f32[64,3584]{1,0:T(8,128)S(1)}, f32[64,3584]{1,0:T(8,128)S(1)}, u32[]{:S(2)}, u32[]{:S(2)}) collective-permute-start(f32[64,3584]{1,0:T(8,128)S(1)} %get-tuple-element.14.x_ref), channel_id=1, source_target_pairs={{0,8},{8,0},{16,24},{24,16},{1,9},{9,1},{17,25},{25,17},{2,10},{10... | collective-permute-start | bytes 2752520 | tf_op jit(solution)/shard_map/ppermute | solution.py:225
  24.9 2.6 %collective-permute-start.8 = (f32[64,3584]{1,0:T(8,128)S(1)}, f32[64,3584]{1,0:T(8,128)S(1)}, u32[]{:S(2)}, u32[]{:S(2)}) collective-permute-start(f32[64,3584]{1,0:T(8,128)S(1)} %collective-permute-done.5.refs_2_), channel_id=1, source_target_pairs={{0,8},{8,0},{16,24},{24,16},{1,9},{9,1},{17,25},{25,17},{2,10},{10... | collective-permute-start | bytes 2752520 | tf_op jit(solution)/shard_map/ppermute | solution.py:225
  24.9 2.6 %collective-permute-start.7 = (f32[64,256]{1,0:T(8,128)S(1)}, f32[64,256]{1,0:T(8,128)S(1)}, u32[]{:S(2)}, u32[]{:S(2)}) collective-permute-start(f32[64,256]{1,0:T(8,128)S(1)} %collective-permute-done.6.refs_0_), channel_id=1, source_target_pairs={{0,8},{8,0},{16,24},{24,16},{1,9},{9,1},{17,25},{25,17},{2,10},{10... | collective-permute-start | bytes 196616 | tf_op jit(solution)/shard_map/ppermute | solution.py:225
  28.4 4.5 %collective-permute-start.11 = (f32[1,64]{1,0:T(1,128)S(1)}, f32[1,64]{1,0:T(1,128)S(1)}, u32[]{:S(2)}, u32[]{:S(2)}) collective-permute-start(f32[1,64]{1,0:T(1,128)S(1)} %get-tuple-element.18), channel_id=1, source_target_pairs={{0,3},{1,2},{2,1},{3,0},{4,7},{5,6},{6,5},{7,4},{8,11},{9,10},{10,... | collective-permute-start | bytes 776 | tf_op jit(solution)/shard_map/ppermute | solution.py:225
  31.2 3.5 %collective-permute-start.10 = (f32[1,64]{1,0:T(1,128)S(1)}, f32[1,64]{1,0:T(1,128)S(1)}, u32[]{:S(2)}, u32[]{:S(2)}) collective-permute-start(f32[1,64]{1,0:T(1,128)S(1)} %get-tuple-element.18), channel_id=1, source_target_pairs={{0,2},{1,3},{2,0},{3,1},{4,6},{5,7},{6,4},{7,5},{8,10},{9,11},{10,... | collective-permute-start | bytes 776 | tf_op jit(solution)/shard_map/ppermute | solution.py:225
  31.7 3.5 %collective-permute-start.9 = (f32[1,64]{1,0:T(1,128)S(1)}, f32[1,64]{1,0:T(1,128)S(1)}, u32[]{:S(2)}, u32[]{:S(2)}) collective-permute-start(f32[1,64]{1,0:T(1,128)S(1)} %get-tuple-element.18), channel_id=1, source_target_pairs={{0,1},{1,0},{2,3},{3,2},{4,5},{5,4},{6,7},{7,6},{8,9},{9,8},{10,11... | collective-permute-start | bytes 776 | tf_op jit(solution)/shard_map/ppermute | solution.py:225
  35.2 4.4 %collective-permute-start.12 = (f32[1,64]{1,0:T(1,128)S(1)}, f32[1,64]{1,0:T(1,128)S(1)}, u32[]{:S(2)}, u32[]{:S(2)}) collective-permute-start(f32[1,64]{1,0:T(1,128)S(1)} %add_add_fusion.refs_0_), channel_id=1, source_target_pairs={{0,4},{1,5},{2,6},{3,7},{4,0},{5,1},{6,2},{7,3},{8,12},{9,13},{10,... | collective-permute-start | bytes 776 | tf_op jit(solution)/shard_map/ppermute | solution.py:225

commit v9 on v8

--- a/solution.py
+++ b/solution.py
@@ -163,7 +163,8 @@
 
     squares = loop(columns, 4, body, jnp.zeros((per_group, 1), jnp.float32))
     spread = jnp.broadcast_to(squares, (per_group, per_group))
-    squares_ref[...] = jnp.sum(jnp.where(diagonal(per_group), spread, 0.0), axis=0, keepdims=True)
+    row = jnp.sum(jnp.where(diagonal(per_group), spread, 0.0), axis=0, keepdims=True)
+    squares_ref[...] = jnp.broadcast_to(row[None], squares_ref.shape)
 
 
 def rest_part(partly, projected, steps, others, blocks, rows, features):
@@ -173,7 +174,7 @@
         out_specs=[in_vmem, in_vmem],
         out_shape=[
             jax.ShapeDtypeStruct(partly.shape, jnp.float32),
-            jax.ShapeDtypeStruct((1, partly.shape[0]), jnp.float32),
+            jax.ShapeDtypeStruct((lax.axis_size("feat"), 1, partly.shape[0]), jnp.float32),
         ],
         compiler_params=params,
         name="rest_part",
@@ -189,9 +190,7 @@
 def finish_kernel(features, count, updated_ref, *refs):
     squares_refs, (out_ref, scaled, sems) = refs[:count], refs[count:]
     per_group, columns = updated_ref.shape
-    squares = squares_refs[0][...]
-    for ref in squares_refs[1:]:
-        squares += ref[...]
+    squares = jnp.sum(squares_refs[0][...], axis=0)
     spread = jnp.broadcast_to(scale_of(squares, features), (per_group, per_group))
     scale = jnp.sum(jnp.where(diagonal(per_group), spread, 0.0), axis=1, keepdims=True)
     tile = tile_of(columns, 7)
@@ -279,7 +278,7 @@
             blocks[step + 1] = exchange(blocks[step], "comp", 1)
             others[step + 1] = exchange(others[step], "comp", 1)
     updated, squares = rest_part(partly, projected, far, of(others, far), of(blocks, far), rows, features)
-    return finish(updated, terms(squares, "feat", 2), features)
+    return finish(updated, [lax.all_to_all(squares, "feat", split_axis=0, concat_axis=0, tiled=True)], features)
 
 
 def solution(mesh):

time: 40.9 us -> 42 us (1.027)
  blocking collectives: 0 us -> 12.3 us
  starting transfers between devices: 16 us -> 9.91 us
  waiting for transfers between devices: 18.2 us -> 13.1 us
    all_to_all x0 -> x1, blocking collectives: none -> 12.3 us  [shards(): lax.all_to_all(squares, 'feat', split_axis=0, concat_axis=0, tiled=True)]
    ppermute x13 -> x9, starting transfers between devices: 16 us -> 9.91 us  [exchange(): lax.ppermute(array, axis, [(i, i ^ step) for i in range(lax.axis_size(axi...]
    ppermute x13 -> x9, waiting for transfers between devices: 18.2 us -> 13.1 us  [exchange(): lax.ppermute(array, axis, [(i, i ^ step) for i in range(lax.axis_size(axi...]
  transfers between devices with their start and end apart: 13 -> 9, of which waited for: 10 -> 6; matrix products, arithmetic and copies ran while one was open for 0% -> 0% of each run, Pallas kernels for 11% -> 11%
where the time goes in v9:
time: 42 us; the launch traced here: 41.8 us
  waiting for transfers between devices  13.1 us (31%)
  blocking collectives  12.3 us (29%)
  starting transfers between devices  9.91 us (24%)
  Pallas kernels  6.39 us (15%)
    ppermute x9, waiting for transfers between devices, exchange(): lax.ppermute(array, axis, [(i, i ^ step) for i in range(lax.axis_size(axi...  13.1 us
    all_to_all x1, blocking collectives, shards(): lax.all_to_all(squares, 'feat', split_axis=0, concat_axis=0, tiled=True)  12.3 us
    ppermute x9, starting transfers between devices, exchange(): lax.ppermute(array, axis, [(i, i ^ step) for i in range(lax.axis_size(axi...  9.91 us
    pallas_call x1, Pallas kernels, project(): pl.pallas_call(project_kernel, in_specs=[anywhere] * 2, out_specs=[in_vme...  2.93 us
    pallas_call x1, Pallas kernels, first_part(): pl.pallas_call(functools.partial(first_kernel, features, steps), in_specs...  1.47 us
    pallas_call x1, Pallas kernels, finish(): pl.pallas_call(functools.partial(finish_kernel, features, count), in_spec...  1.09 us
    pallas_call x1, Pallas kernels, rest_part(): pl.pallas_call(functools.partial(rest_kernel, features, rows, steps), in_...  0.9 us
  transfers between devices with their start and end apart: 9, of which 6 were waited for; matrix products, arithmetic and copies ran while one was open for 0% of the time, Pallas kernels for 11%

profile of v9, /device:TPU:0, one launch (start us, length us, event | category | flops | bytes accessed | tf_op | source)
XLA Modules:
  0.0 41.8 jit_solution(2527440169886973901)
XLA Ops:
  0.0 2.9 %collective-permute-start.5 = (f32[64,3584]{1,0:T(8,128)}, f32[64,3584]{1,0:T(8,128)S(1)}, u32[]{:S(2)}, u32[]{:S(2)}) collective-permute-start(f32[64,3584]{1,0:T(8,128)} %x_hbm.1), channel_id=1, source_target_pairs={{0,16},{8,24},{16,0},{24,8},{1,17},{9,25},{17,1},{25,9},{2,18},{10... | collective-permute-start | bytes 2752520 | tf_op jit(solution)/shard_map/ppermute | solution.py:224
  2.9 2.9 %project.1 = (f32[64,256]{1,0:T(8,128)S(1)}, f32[64,3584]{1,0:T(8,128)S(1)}, f32[192,3584]{1,0:T(8,128)S(1)}) custom-call(f32[64,3584]{1,0:T(8,128)} %x_hbm.1, f32[192,3584]{1,0:T(8,128)} %bitcast.1), custom_call_target="tpu_custom_call" | custom-call | tf_op jit(solution)/shard_map/project/pallas_call | solution.py:83
  5.9 1.6 %collective-permute-start = (f32[64,256]{1,0:T(8,128)S(1)}, f32[64,256]{1,0:T(8,128)S(1)}, u32[]{:S(2)}, u32[]{:S(2)}) collective-permute-start(f32[64,256]{1,0:T(8,128)S(1)} %get-tuple-element.12), channel_id=1, source_target_pairs={{0,1},{1,0},{2,3},{3,2},{4,5},{5,4},{6,7},{7,6},{8,9},{9,8},{10,11... | collective-permute-start | bytes 196616 | tf_op jit(solution)/shard_map/ppermute | solution.py:224
  7.5 2.7 %collective-permute-done = f32[64,256]{1,0:T(8,128)S(1)} collective-permute-done((f32[64,256]{1,0:T(8,128)S(1)}, f32[64,256]{1,0:T(8,128)S(1)}, u32[]{:S(2)}, u32[]{:S(2)}) %collective-permute-start) | collective-permute-done | bytes 65568 | tf_op jit(solution)/shard_map/ppermute | solution.py:224
  10.2 1.6 %collective-permute-start.1 = (f32[64,256]{1,0:T(8,128)S(1)}, f32[64,256]{1,0:T(8,128)S(1)}, u32[]{:S(2)}, u32[]{:S(2)}) collective-permute-start(f32[64,256]{1,0:T(8,128)S(1)} %add.9), channel_id=1, source_target_pairs={{0,2},{1,3},{2,0},{3,1},{4,6},{5,7},{6,4},{7,5},{8,10},{9,11},{10,... | collective-permute-start | bytes 196616 | tf_op jit(solution)/shard_map/ppermute | solution.py:224
  11.9 2.7 %collective-permute-done.1 = f32[64,256]{1,0:T(8,128)S(1)} collective-permute-done((f32[64,256]{1,0:T(8,128)S(1)}, f32[64,256]{1,0:T(8,128)S(1)}, u32[]{:S(2)}, u32[]{:S(2)}) %collective-permute-start.1) | collective-permute-done | bytes 65568 | tf_op jit(solution)/shard_map/ppermute | solution.py:224
  14.6 2.7 %collective-permute-start.2 = (f32[64,256]{1,0:T(8,128)S(1)}, f32[64,256]{1,0:T(8,128)S(1)}, u32[]{:S(2)}, u32[]{:S(2)}) collective-permute-start(f32[64,256]{1,0:T(8,128)S(1)} %add.10), channel_id=1, source_target_pairs={{0,4},{1,5},{2,6},{3,7},{4,0},{5,1},{6,2},{7,3},{8,12},{9,13},{10,... | collective-permute-start | bytes 196616 | tf_op jit(solution)/shard_map/ppermute | solution.py:224
  17.2 2.6 %collective-permute-done.2 = f32[64,256]{1,0:T(8,128)S(1)} collective-permute-done((f32[64,256]{1,0:T(8,128)S(1)}, f32[64,256]{1,0:T(8,128)S(1)}, u32[]{:S(2)}, u32[]{:S(2)}) %collective-permute-start.2) | collective-permute-done | bytes 65568 | tf_op jit(solution)/shard_map/ppermute | solution.py:224
  19.8 0.1 collective-permute-start.3
  19.9 0.3 collective-permute-start.6
  20.2 0.2 collective-permute-start.4
  20.4 0.7 %collective-permute-done.3.refs_0_ = f32[64,256]{1,0:T(8,128)S(1)} collective-permute-done((f32[64,256]{1,0:T(8,128)S(1)}, f32[64,256]{1,0:T(8,128)S(1)}, u32[]{:S(2)}, u32[]{:S(2)}) %collective-permute-start.3) | collective-permute-done | bytes 65568 | tf_op jit(solution)/shard_map/ppermute | solution.py:224
  21.1 3.8 %collective-permute-done.6.refs_0_ = f32[64,256]{1,0:T(8,128)S(1)} collective-permute-done((f32[64,256]{1,0:T(8,128)S(1)}, f32[64,256]{1,0:T(8,128)S(1)}, u32[]{:S(2)}, u32[]{:S(2)}) %collective-permute-start.6) | collective-permute-done | bytes 65568 | tf_op jit(solution)/shard_map/ppermute | solution.py:224
  24.9 0.0 collective-permute-done.5.refs_2_
  24.9 0.0 collective-permute-start.8
  24.9 0.5 %collective-permute-start.7 = (f32[64,256]{1,0:T(8,128)S(1)}, f32[64,256]{1,0:T(8,128)S(1)}, u32[]{:S(2)}, u32[]{:S(2)}) collective-permute-start(f32[64,256]{1,0:T(8,128)S(1)} %collective-permute-done.6.refs_0_), channel_id=1, source_target_pairs={{0,8},{8,0},{16,24},{24,16},{1,9},{9,1},{17,25},{25,17},{2,10},{10... | collective-permute-start | bytes 196616 | tf_op jit(solution)/shard_map/ppermute | solution.py:224
  25.4 0.0 collective-permute-done.4.refs_1_
  25.4 1.5 %first_part.1.t_ref = f32[64,3584]{1,0:T(8,128)S(1)} custom-call(f32[64,256]{1,0:T(8,128)S(1)} %add.11.p_ref, f32[192,3584]{1,0:T(8,128)S(1)} %get-tuple-element.13.s_ref, f32[64,3584]{1,0:T(8,128)S(1)} %get-tuple-element.14.x_ref, f32[64,256]{1,0:T(8,128)S(1)} %collective-permute-done.3.refs_0_, f32[64,3584]{1,0:T(8,128)S(1)} %collective-permute-done.4.refs_1_), custom_call_target="tpu_custom_call" | custom-call | tf_op jit(solution)/shard_map/first_part/pallas_call | solution.py:140
  26.9 0.6 %collective-permute-done.7.refs_1_ = f32[64,256]{1,0:T(8,128)S(1)} collective-permute-done((f32[64,256]{1,0:T(8,128)S(1)}, f32[64,256]{1,0:T(8,128)S(1)}, u32[]{:S(2)}, u32[]{:S(2)}) %collective-permute-start.7) | collective-permute-done | bytes 65568 | tf_op jit(solution)/shard_map/ppermute | solution.py:224
  27.5 0.0 collective-permute-done.8.refs_3_
  27.5 0.9 %rest_part.1 = (f32[64,3584]{1,0:T(8,128)S(1)}, f32[8,1,64]{2,1,0:T(1,128)S(1)}) custom-call(f32[64,3584]{1,0:T(8,128)S(1)} %first_part.1.t_ref, f32[64,256]{1,0:T(8,128)S(1)} %add.11.p_ref, f32[64,256]{1,0:T(8,128)S(1)} %collective-permute-done.6.refs_0_, f32[64,256]{1,0:T(8,128)S(1)} %collective-permute-done.7.refs_1_, ...), custom_call_target="tpu_custom_call" | custom-call | tf_op jit(solution)/shard_map/rest_part/pallas_call | solution.py:171
  28.4 12.3 %all_to_all.5.refs_0_ = f32[8,1,64]{2,1,0:T(1,128)S(1)} all-to-all(f32[8,1,64]{2,1,0:T(1,128)S(1)} %get-tuple-element.18), channel_id=1, replica_groups=mesh['comp'=4,'feat'=8] {'feat'}, dimensions={0} | all-to-all | bytes 4096 | tf_op jit(solution)/shard_map/all_to_all | solution.py:281
  40.7 1.1 %finish.1 = f32[64,3584]{1,0:T(8,128)} custom-call(f32[64,3584]{1,0:T(8,128)S(1)} %get-tuple-element.17.updated_ref, f32[8,1,64]{2,1,0:T(1,128)S(1)} %all_to_all.5.refs_0_), custom_call_target="tpu_custom_call" | custom-call | tf_op jit(solution)/shard_map/finish/pallas_call | solution.py:209
  (3 shorter events, 0.0 us)
Async XLA Ops:
  0.0 24.9 %collective-permute-start.5 = (f32[64,3584]{1,0:T(8,128)}, f32[64,3584]{1,0:T(8,128)S(1)}, u32[]{:S(2)}, u32[]{:S(2)}) collective-permute-start(f32[64,3584]{1,0:T(8,128)} %x_hbm.1), channel_id=1, source_target_pairs={{0,16},{8,24},{16,0},{24,8},{1,17},{9,25},{17,1},{25,9},{2,18},{10... | collective-permute-start | bytes 2752520 | tf_op jit(solution)/shard_map/ppermute | solution.py:224
  5.9 4.3 %collective-permute-start = (f32[64,256]{1,0:T(8,128)S(1)}, f32[64,256]{1,0:T(8,128)S(1)}, u32[]{:S(2)}, u32[]{:S(2)}) collective-permute-start(f32[64,256]{1,0:T(8,128)S(1)} %get-tuple-element.12), channel_id=1, source_target_pairs={{0,1},{1,0},{2,3},{3,2},{4,5},{5,4},{6,7},{7,6},{8,9},{9,8},{10,11... | collective-permute-start | bytes 196616 | tf_op jit(solution)/shard_map/ppermute | solution.py:224
  10.2 4.3 %collective-permute-start.1 = (f32[64,256]{1,0:T(8,128)S(1)}, f32[64,256]{1,0:T(8,128)S(1)}, u32[]{:S(2)}, u32[]{:S(2)}) collective-permute-start(f32[64,256]{1,0:T(8,128)S(1)} %add.9), channel_id=1, source_target_pairs={{0,2},{1,3},{2,0},{3,1},{4,6},{5,7},{6,4},{7,5},{8,10},{9,11},{10,... | collective-permute-start | bytes 196616 | tf_op jit(solution)/shard_map/ppermute | solution.py:224
  14.6 5.2 %collective-permute-start.2 = (f32[64,256]{1,0:T(8,128)S(1)}, f32[64,256]{1,0:T(8,128)S(1)}, u32[]{:S(2)}, u32[]{:S(2)}) collective-permute-start(f32[64,256]{1,0:T(8,128)S(1)} %add.10), channel_id=1, source_target_pairs={{0,4},{1,5},{2,6},{3,7},{4,0},{5,1},{6,2},{7,3},{8,12},{9,13},{10,... | collective-permute-start | bytes 196616 | tf_op jit(solution)/shard_map/ppermute | solution.py:224
  19.8 1.3 %collective-permute-start.3 = (f32[64,256]{1,0:T(8,128)S(1)}, f32[64,256]{1,0:T(8,128)S(1)}, u32[]{:S(2)}, u32[]{:S(2)}) collective-permute-start(f32[64,256]{1,0:T(8,128)S(1)} %add.11.p_ref), channel_id=1, source_target_pairs={{0,8},{8,0},{16,24},{24,16},{1,9},{9,1},{17,25},{25,17},{2,10},{10... | collective-permute-start | bytes 196616 | tf_op jit(solution)/shard_map/ppermute | solution.py:224
  19.9 5.0 %collective-permute-start.6 = (f32[64,256]{1,0:T(8,128)S(1)}, f32[64,256]{1,0:T(8,128)S(1)}, u32[]{:S(2)}, u32[]{:S(2)}) collective-permute-start(f32[64,256]{1,0:T(8,128)S(1)} %add.11.p_ref), channel_id=1, source_target_pairs={{0,16},{8,24},{16,0},{24,8},{1,17},{9,25},{17,1},{25,9},{2,18},{10... | collective-permute-start | bytes 196616 | tf_op jit(solution)/shard_map/ppermute | solution.py:224
  20.2 5.3 %collective-permute-start.4 = (f32[64,3584]{1,0:T(8,128)S(1)}, f32[64,3584]{1,0:T(8,128)S(1)}, u32[]{:S(2)}, u32[]{:S(2)}) collective-permute-start(f32[64,3584]{1,0:T(8,128)S(1)} %get-tuple-element.14.x_ref), channel_id=1, source_target_pairs={{0,8},{8,0},{16,24},{24,16},{1,9},{9,1},{17,25},{25,17},{2,10},{10... | collective-permute-start | bytes 2752520 | tf_op jit(solution)/shard_map/ppermute | solution.py:224
  24.9 2.6 %collective-permute-start.8 = (f32[64,3584]{1,0:T(8,128)S(1)}, f32[64,3584]{1,0:T(8,128)S(1)}, u32[]{:S(2)}, u32[]{:S(2)}) collective-permute-start(f32[64,3584]{1,0:T(8,128)S(1)} %collective-permute-done.5.refs_2_), channel_id=1, source_target_pairs={{0,8},{8,0},{16,24},{24,16},{1,9},{9,1},{17,25},{25,17},{2,10},{10... | collective-permute-start | bytes 2752520 | tf_op jit(solution)/shard_map/ppermute | solution.py:224
  24.9 2.6 %collective-permute-start.7 = (f32[64,256]{1,0:T(8,128)S(1)}, f32[64,256]{1,0:T(8,128)S(1)}, u32[]{:S(2)}, u32[]{:S(2)}) collective-permute-start(f32[64,256]{1,0:T(8,128)S(1)} %collective-permute-done.6.refs_0_), channel_id=1, source_target_pairs={{0,8},{8,0},{16,24},{24,16},{1,9},{9,1},{17,25},{25,17},{2,10},{10... | collective-permute-start | bytes 196616 | tf_op jit(solution)/shard_map/ppermute | solution.py:224

commit v10 on v8

--- a/solution.py
+++ b/solution.py
@@ -263,7 +263,7 @@
     parts = terms(projected, "feat", 1)
     projected = sum(parts[1:], parts[0])
     if even:
-        others = {step: exchange(projected, "comp", step) for step in range(1, comp) if step == 1 or step % 2 == 0}
+        others = {step: exchange(projected, "comp", step) for step in range(1, comp, 2)}
     else:
         others = gather(projected)
     near = [1][: comp - 1]
@@ -275,9 +275,11 @@
     partly = first_part(projected, sample, vectors, near, of(others, near), of(blocks, near), features)
     if even:
         for step in range(2, comp, 2):
-            blocks[step], others[step], others[1] = lax.optimization_barrier((blocks[step], others[step], others[1]))
+            blocks[step], others[step + 1], others[1] = lax.optimization_barrier(
+                (blocks[step], others[step + 1], others[1])
+            )
             blocks[step + 1] = exchange(blocks[step], "comp", 1)
-            others[step + 1] = exchange(others[step], "comp", 1)
+            others[step] = exchange(others[step + 1], "comp", 1)
     updated, squares = rest_part(partly, projected, far, of(others, far), of(blocks, far), rows, features)
     return finish(updated, terms(squares, "feat", 2), features)
 

time: 40.9 us -> 40.4 us (0.988)
  waiting for transfers between devices: 18.2 us -> 17.7 us
    ppermute x13, waiting for transfers between devices: 18.2 us -> 17.7 us  [exchange(): lax.ppermute(array, axis, [(i, i ^ step) for i in range(lax.axis_size(axi...]
where the time goes in v10:
time: 40.4 us; the launch traced here: 40.2 us
  waiting for transfers between devices  17.7 us (44%)
  starting transfers between devices  16.1 us (40%)
  Pallas kernels  6.39 us (16%)
    ppermute x13, waiting for transfers between devices, exchange(): lax.ppermute(array, axis, [(i, i ^ step) for i in range(lax.axis_size(axi...  17.7 us
    ppermute x13, starting transfers between devices, exchange(): lax.ppermute(array, axis, [(i, i ^ step) for i in range(lax.axis_size(axi...  16.1 us
    pallas_call x1, Pallas kernels, project(): pl.pallas_call(project_kernel, in_specs=[anywhere] * 2, out_specs=[in_vme...  2.93 us
    pallas_call x1, Pallas kernels, first_part(): pl.pallas_call(functools.partial(first_kernel, features, steps), in_specs...  1.47 us
    pallas_call x1, Pallas kernels, finish(): pl.pallas_call(functools.partial(finish_kernel, features, count), in_spec...  1.08 us
    pallas_call x1, Pallas kernels, rest_part(): pl.pallas_call(functools.partial(rest_kernel, features, rows, steps), in_...  0.9 us
  transfers between devices with their start and end apart: 13, of which 10 were waited for; matrix products, arithmetic and copies ran while one was open for 0% of the time, Pallas kernels for 11%

profile of v10, /device:TPU:0, one launch (start us, length us, event | category | flops | bytes accessed | tf_op | source)
XLA Modules:
  0.0 40.2 jit_solution(1225559484868706558)
XLA Ops:
  0.0 2.9 %collective-permute-start.5 = (f32[64,3584]{1,0:T(8,128)}, f32[64,3584]{1,0:T(8,128)S(1)}, u32[]{:S(2)}, u32[]{:S(2)}) collective-permute-start(f32[64,3584]{1,0:T(8,128)} %x_hbm.1), channel_id=1, source_target_pairs={{0,16},{8,24},{16,0},{24,8},{1,17},{9,25},{17,1},{25,9},{2,18},{10... | collective-permute-start | bytes 2752520 | tf_op jit(solution)/shard_map/ppermute | solution.py:225
  2.9 2.9 %project.1 = (f32[64,256]{1,0:T(8,128)S(1)}, f32[64,3584]{1,0:T(8,128)S(1)}, f32[192,3584]{1,0:T(8,128)S(1)}) custom-call(f32[64,3584]{1,0:T(8,128)} %x_hbm.1, f32[192,3584]{1,0:T(8,128)} %bitcast.1), custom_call_target="tpu_custom_call" | custom-call | tf_op jit(solution)/shard_map/project/pallas_call | solution.py:83
  5.9 1.6 %collective-permute-start = (f32[64,256]{1,0:T(8,128)S(1)}, f32[64,256]{1,0:T(8,128)S(1)}, u32[]{:S(2)}, u32[]{:S(2)}) collective-permute-start(f32[64,256]{1,0:T(8,128)S(1)} %get-tuple-element.12), channel_id=1, source_target_pairs={{0,1},{1,0},{2,3},{3,2},{4,5},{5,4},{6,7},{7,6},{8,9},{9,8},{10,11... | collective-permute-start | bytes 196616 | tf_op jit(solution)/shard_map/ppermute | solution.py:225
  7.5 2.7 %collective-permute-done = f32[64,256]{1,0:T(8,128)S(1)} collective-permute-done((f32[64,256]{1,0:T(8,128)S(1)}, f32[64,256]{1,0:T(8,128)S(1)}, u32[]{:S(2)}, u32[]{:S(2)}) %collective-permute-start) | collective-permute-done | bytes 65568 | tf_op jit(solution)/shard_map/ppermute | solution.py:225
  10.2 1.6 %collective-permute-start.1 = (f32[64,256]{1,0:T(8,128)S(1)}, f32[64,256]{1,0:T(8,128)S(1)}, u32[]{:S(2)}, u32[]{:S(2)}) collective-permute-start(f32[64,256]{1,0:T(8,128)S(1)} %add.18), channel_id=1, source_target_pairs={{0,2},{1,3},{2,0},{3,1},{4,6},{5,7},{6,4},{7,5},{8,10},{9,11},{10,... | collective-permute-start | bytes 196616 | tf_op jit(solution)/shard_map/ppermute | solution.py:225
  11.9 2.7 %collective-permute-done.1 = f32[64,256]{1,0:T(8,128)S(1)} collective-permute-done((f32[64,256]{1,0:T(8,128)S(1)}, f32[64,256]{1,0:T(8,128)S(1)}, u32[]{:S(2)}, u32[]{:S(2)}) %collective-permute-start.1) | collective-permute-done | bytes 65568 | tf_op jit(solution)/shard_map/ppermute | solution.py:225
  14.6 2.7 %collective-permute-start.2 = (f32[64,256]{1,0:T(8,128)S(1)}, f32[64,256]{1,0:T(8,128)S(1)}, u32[]{:S(2)}, u32[]{:S(2)}) collective-permute-start(f32[64,256]{1,0:T(8,128)S(1)} %add.19), channel_id=1, source_target_pairs={{0,4},{1,5},{2,6},{3,7},{4,0},{5,1},{6,2},{7,3},{8,12},{9,13},{10,... | collective-permute-start | bytes 196616 | tf_op jit(solution)/shard_map/ppermute | solution.py:225
  17.2 2.6 %collective-permute-done.2 = f32[64,256]{1,0:T(8,128)S(1)} collective-permute-done((f32[64,256]{1,0:T(8,128)S(1)}, f32[64,256]{1,0:T(8,128)S(1)}, u32[]{:S(2)}, u32[]{:S(2)}) %collective-permute-start.2) | collective-permute-done | bytes 65568 | tf_op jit(solution)/shard_map/ppermute | solution.py:225
  19.8 0.1 collective-permute-start.3
  19.9 0.3 collective-permute-start.6
  20.2 0.2 collective-permute-start.4
  20.4 0.7 %collective-permute-done.3.refs_0_ = f32[64,256]{1,0:T(8,128)S(1)} collective-permute-done((f32[64,256]{1,0:T(8,128)S(1)}, f32[64,256]{1,0:T(8,128)S(1)}, u32[]{:S(2)}, u32[]{:S(2)}) %collective-permute-start.3) | collective-permute-done | bytes 65568 | tf_op jit(solution)/shard_map/ppermute | solution.py:225
  21.1 3.3 %collective-permute-done.6.refs_1_ = f32[64,256]{1,0:T(8,128)S(1)} collective-permute-done((f32[64,256]{1,0:T(8,128)S(1)}, f32[64,256]{1,0:T(8,128)S(1)}, u32[]{:S(2)}, u32[]{:S(2)}) %collective-permute-start.6) | collective-permute-done | bytes 65568 | tf_op jit(solution)/shard_map/ppermute | solution.py:225
  24.4 0.0 collective-permute-done.5.refs_2_
  24.4 0.3 collective-permute-start.8
  24.7 0.2 collective-permute-start.7
  24.9 0.0 collective-permute-done.4.refs_1_
  24.9 1.5 %first_part.1.t_ref = f32[64,3584]{1,0:T(8,128)S(1)} custom-call(f32[64,256]{1,0:T(8,128)S(1)} %add.20.p_ref, f32[192,3584]{1,0:T(8,128)S(1)} %get-tuple-element.13.s_ref, f32[64,3584]{1,0:T(8,128)S(1)} %get-tuple-element.14.x_ref, f32[64,256]{1,0:T(8,128)S(1)} %collective-permute-done.3.refs_0_, f32[64,3584]{1,0:T(8,128)S(1)} %collective-permute-done.4.refs_1_), custom_call_target="tpu_custom_call" | custom-call | tf_op jit(solution)/shard_map/first_part/pallas_call | solution.py:140
  26.4 0.6 %collective-permute-done.7.refs_0_ = f32[64,256]{1,0:T(8,128)S(1)} collective-permute-done((f32[64,256]{1,0:T(8,128)S(1)}, f32[64,256]{1,0:T(8,128)S(1)}, u32[]{:S(2)}, u32[]{:S(2)}) %collective-permute-start.7) | collective-permute-done | bytes 65568 | tf_op jit(solution)/shard_map/ppermute | solution.py:225
  27.0 0.0 collective-permute-done.8.refs_3_
  27.0 0.9 %rest_part.1 = (f32[64,3584]{1,0:T(8,128)S(1)}, f32[1,64]{1,0:T(1,128)S(1)}) custom-call(f32[64,3584]{1,0:T(8,128)S(1)} %first_part.1.t_ref, f32[64,256]{1,0:T(8,128)S(1)} %add.20.p_ref, f32[64,256]{1,0:T(8,128)S(1)} %collective-permute-done.7.refs_0_, f32[64,256]{1,0:T(8,128)S(1)} %collective-permute-done.6.refs_1_, ...), custom_call_target="tpu_custom_call" | custom-call | tf_op jit(solution)/shard_map/rest_part/pallas_call | solution.py:170
  27.9 2.8 %collective-permute-start.11 = (f32[1,64]{1,0:T(1,128)S(1)}, f32[1,64]{1,0:T(1,128)S(1)}, u32[]{:S(2)}, u32[]{:S(2)}) collective-permute-start(f32[1,64]{1,0:T(1,128)S(1)} %get-tuple-element.18), channel_id=1, source_target_pairs={{0,3},{1,2},{2,1},{3,0},{4,7},{5,6},{6,5},{7,4},{8,11},{9,10},{10,... | collective-permute-start | bytes 776 | tf_op jit(solution)/shard_map/ppermute | solution.py:225
  30.7 0.4 %collective-permute-start.10 = (f32[1,64]{1,0:T(1,128)S(1)}, f32[1,64]{1,0:T(1,128)S(1)}, u32[]{:S(2)}, u32[]{:S(2)}) collective-permute-start(f32[1,64]{1,0:T(1,128)S(1)} %get-tuple-element.18), channel_id=1, source_target_pairs={{0,2},{1,3},{2,0},{3,1},{4,6},{5,7},{6,4},{7,5},{8,10},{9,11},{10,... | collective-permute-start | bytes 776 | tf_op jit(solution)/shard_map/ppermute | solution.py:225
  31.1 0.3 collective-permute-start.9
  31.4 0.9 %collective-permute-done.11 = f32[1,64]{1,0:T(1,128)S(1)} collective-permute-done((f32[1,64]{1,0:T(1,128)S(1)}, f32[1,64]{1,0:T(1,128)S(1)}, u32[]{:S(2)}, u32[]{:S(2)}) %collective-permute-start.11) | collective-permute-done | bytes 288 | tf_op jit(solution)/shard_map/ppermute | solution.py:225
  32.4 1.8 %collective-permute-done.10 = f32[1,64]{1,0:T(1,128)S(1)} collective-permute-done((f32[1,64]{1,0:T(1,128)S(1)}, f32[1,64]{1,0:T(1,128)S(1)}, u32[]{:S(2)}, u32[]{:S(2)}) %collective-permute-start.10) | collective-permute-done | bytes 288 | tf_op jit(solution)/shard_map/ppermute | solution.py:225
  34.2 0.4 %collective-permute-done.9 = f32[1,64]{1,0:T(1,128)S(1)} collective-permute-done((f32[1,64]{1,0:T(1,128)S(1)}, f32[1,64]{1,0:T(1,128)S(1)}, u32[]{:S(2)}, u32[]{:S(2)}) %collective-permute-start.9) | collective-permute-done | bytes 288 | tf_op jit(solution)/shard_map/ppermute | solution.py:225
  34.7 2.6 %collective-permute-start.12 = (f32[1,64]{1,0:T(1,128)S(1)}, f32[1,64]{1,0:T(1,128)S(1)}, u32[]{:S(2)}, u32[]{:S(2)}) collective-permute-start(f32[1,64]{1,0:T(1,128)S(1)} %add_add_fusion.refs_0_), channel_id=1, source_target_pairs={{0,4},{1,5},{2,6},{3,7},{4,0},{5,1},{6,2},{7,3},{8,12},{9,13},{10,... | collective-permute-start | bytes 776 | tf_op jit(solution)/shard_map/ppermute | solution.py:225
  37.3 1.8 %collective-permute-done.12.refs_1_ = f32[1,64]{1,0:T(1,128)S(1)} collective-permute-done((f32[1,64]{1,0:T(1,128)S(1)}, f32[1,64]{1,0:T(1,128)S(1)}, u32[]{:S(2)}, u32[]{:S(2)}) %collective-permute-start.12) | collective-permute-done | bytes 288 | tf_op jit(solution)/shard_map/ppermute | solution.py:225
  39.1 1.1 %finish.1 = f32[64,3584]{1,0:T(8,128)} custom-call(f32[64,3584]{1,0:T(8,128)S(1)} %get-tuple-element.17.updated_ref, f32[1,64]{1,0:T(1,128)S(1)} %add_add_fusion.refs_0_, f32[1,64]{1,0:T(1,128)S(1)} %collective-permute-done.12.refs_1_), custom_call_target="tpu_custom_call" | custom-call | tf_op jit(solution)/shard_map/finish/pallas_call | solution.py:210
  (4 shorter events, 0.0 us)
Async XLA Ops:
  0.0 24.4 %collective-permute-start.5 = (f32[64,3584]{1,0:T(8,128)}, f32[64,3584]{1,0:T(8,128)S(1)}, u32[]{:S(2)}, u32[]{:S(2)}) collective-permute-start(f32[64,3584]{1,0:T(8,128)} %x_hbm.1), channel_id=1, source_target_pairs={{0,16},{8,24},{16,0},{24,8},{1,17},{9,25},{17,1},{25,9},{2,18},{10... | collective-permute-start | bytes 2752520 | tf_op jit(solution)/shard_map/ppermute | solution.py:225
  5.9 4.3 %collective-permute-start = (f32[64,256]{1,0:T(8,128)S(1)}, f32[64,256]{1,0:T(8,128)S(1)}, u32[]{:S(2)}, u32[]{:S(2)}) collective-permute-start(f32[64,256]{1,0:T(8,128)S(1)} %get-tuple-element.12), channel_id=1, source_target_pairs={{0,1},{1,0},{2,3},{3,2},{4,5},{5,4},{6,7},{7,6},{8,9},{9,8},{10,11... | collective-permute-start | bytes 196616 | tf_op jit(solution)/shard_map/ppermute | solution.py:225
  10.2 4.3 %collective-permute-start.1 = (f32[64,256]{1,0:T(8,128)S(1)}, f32[64,256]{1,0:T(8,128)S(1)}, u32[]{:S(2)}, u32[]{:S(2)}) collective-permute-start(f32[64,256]{1,0:T(8,128)S(1)} %add.18), channel_id=1, source_target_pairs={{0,2},{1,3},{2,0},{3,1},{4,6},{5,7},{6,4},{7,5},{8,10},{9,11},{10,... | collective-permute-start | bytes 196616 | tf_op jit(solution)/shard_map/ppermute | solution.py:225
  14.6 5.2 %collective-permute-start.2 = (f32[64,256]{1,0:T(8,128)S(1)}, f32[64,256]{1,0:T(8,128)S(1)}, u32[]{:S(2)}, u32[]{:S(2)}) collective-permute-start(f32[64,256]{1,0:T(8,128)S(1)} %add.19), channel_id=1, source_target_pairs={{0,4},{1,5},{2,6},{3,7},{4,0},{5,1},{6,2},{7,3},{8,12},{9,13},{10,... | collective-permute-start | bytes 196616 | tf_op jit(solution)/shard_map/ppermute | solution.py:225
  19.8 1.3 %collective-permute-start.3 = (f32[64,256]{1,0:T(8,128)S(1)}, f32[64,256]{1,0:T(8,128)S(1)}, u32[]{:S(2)}, u32[]{:S(2)}) collective-permute-start(f32[64,256]{1,0:T(8,128)S(1)} %add.20.p_ref), channel_id=1, source_target_pairs={{0,8},{8,0},{16,24},{24,16},{1,9},{9,1},{17,25},{25,17},{2,10},{10... | collective-permute-start | bytes 196616 | tf_op jit(solution)/shard_map/ppermute | solution.py:225
  19.9 4.5 %collective-permute-start.6 = (f32[64,256]{1,0:T(8,128)S(1)}, f32[64,256]{1,0:T(8,128)S(1)}, u32[]{:S(2)}, u32[]{:S(2)}) collective-permute-start(f32[64,256]{1,0:T(8,128)S(1)} %add.20.p_ref), channel_id=1, source_target_pairs={{0,24},{8,16},{16,8},{24,0},{1,25},{9,17},{17,9},{25,1},{2,26},{10... | collective-permute-start | bytes 196616 | tf_op jit(solution)/shard_map/ppermute | solution.py:225
  20.2 4.7 %collective-permute-start.4 = (f32[64,3584]{1,0:T(8,128)S(1)}, f32[64,3584]{1,0:T(8,128)S(1)}, u32[]{:S(2)}, u32[]{:S(2)}) collective-permute-start(f32[64,3584]{1,0:T(8,128)S(1)} %get-tuple-element.14.x_ref), channel_id=1, source_target_pairs={{0,8},{8,0},{16,24},{24,16},{1,9},{9,1},{17,25},{25,17},{2,10},{10... | collective-permute-start | bytes 2752520 | tf_op jit(solution)/shard_map/ppermute | solution.py:225
  24.4 2.6 %collective-permute-start.8 = (f32[64,3584]{1,0:T(8,128)S(1)}, f32[64,3584]{1,0:T(8,128)S(1)}, u32[]{:S(2)}, u32[]{:S(2)}) collective-permute-start(f32[64,3584]{1,0:T(8,128)S(1)} %collective-permute-done.5.refs_2_), channel_id=1, source_target_pairs={{0,8},{8,0},{16,24},{24,16},{1,9},{9,1},{17,25},{25,17},{2,10},{10... | collective-permute-start | bytes 2752520 | tf_op jit(solution)/shard_map/ppermute | solution.py:225
  24.7 2.3 %collective-permute-start.7 = (f32[64,256]{1,0:T(8,128)S(1)}, f32[64,256]{1,0:T(8,128)S(1)}, u32[]{:S(2)}, u32[]{:S(2)}) collective-permute-start(f32[64,256]{1,0:T(8,128)S(1)} %collective-permute-done.6.refs_1_), channel_id=1, source_target_pairs={{0,8},{8,0},{16,24},{24,16},{1,9},{9,1},{17,25},{25,17},{2,10},{10... | collective-permute-start | bytes 196616 | tf_op jit(solution)/shard_map/ppermute | solution.py:225
  27.9 4.5 %collective-permute-start.11 = (f32[1,64]{1,0:T(1,128)S(1)}, f32[1,64]{1,0:T(1,128)S(1)}, u32[]{:S(2)}, u32[]{:S(2)}) collective-permute-start(f32[1,64]{1,0:T(1,128)S(1)} %get-tuple-element.18), channel_id=1, source_target_pairs={{0,3},{1,2},{2,1},{3,0},{4,7},{5,6},{6,5},{7,4},{8,11},{9,10},{10,... | collective-permute-start | bytes 776 | tf_op jit(solution)/shard_map/ppermute | solution.py:225
  30.7 3.5 %collective-permute-start.10 = (f32[1,64]{1,0:T(1,128)S(1)}, f32[1,64]{1,0:T(1,128)S(1)}, u32[]{:S(2)}, u32[]{:S(2)}) collective-permute-start(f32[1,64]{1,0:T(1,128)S(1)} %get-tuple-element.18), channel_id=1, source_target_pairs={{0,2},{1,3},{2,0},{3,1},{4,6},{5,7},{6,4},{7,5},{8,10},{9,11},{10,... | collective-permute-start | bytes 776 | tf_op jit(solution)/shard_map/ppermute | solution.py:225
  31.1 3.5 %collective-permute-start.9 = (f32[1,64]{1,0:T(1,128)S(1)}, f32[1,64]{1,0:T(1,128)S(1)}, u32[]{:S(2)}, u32[]{:S(2)}) collective-permute-start(f32[1,64]{1,0:T(1,128)S(1)} %get-tuple-element.18), channel_id=1, source_target_pairs={{0,1},{1,0},{2,3},{3,2},{4,5},{5,4},{6,7},{7,6},{8,9},{9,8},{10,11... | collective-permute-start | bytes 776 | tf_op jit(solution)/shard_map/ppermute | solution.py:225
  34.7 4.4 %collective-permute-start.12 = (f32[1,64]{1,0:T(1,128)S(1)}, f32[1,64]{1,0:T(1,128)S(1)}, u32[]{:S(2)}, u32[]{:S(2)}) collective-permute-start(f32[1,64]{1,0:T(1,128)S(1)} %add_add_fusion.refs_0_), channel_id=1, source_target_pairs={{0,4},{1,5},{2,6},{3,7},{4,0},{5,1},{6,2},{7,3},{8,12},{9,13},{10,... | collective-permute-start | bytes 776 | tf_op jit(solution)/shard_map/ppermute | solution.py:225

commit v11 on v10

--- a/solution.py
+++ b/solution.py
@@ -238,6 +238,28 @@
     return parts
 
 
+def flipped_terms(array):
+    comp, feat = lax.axis_size("comp"), lax.axis_size("feat")
+    if comp % 2 or comp & (comp - 1) or feat & (feat - 1):
+        return terms(array, "feat", 2)
+    widths, step = [], 1
+    while step < feat:
+        widths.append(min(4, feat // step))
+        step *= widths[-1]
+    parts, step = [array], 1
+    for stage, width in enumerate(widths):
+        array = sum(parts[1:], parts[0])
+        flip = int(stage + 1 < len(widths) or len(widths) % 2 == 0)
+        parts = [] if flip else [array]
+        for k in range(0 if flip else 1, width):
+            pairs = [
+                (i * feat + j, (i ^ flip) * feat + (j ^ (k * step))) for i in range(comp) for j in range(feat)
+            ]
+            parts.append(lax.ppermute(array, ("comp", "feat"), pairs))
+        step *= width
+    return parts
+
+
 def gather(own):
     size = lax.axis_size("comp")
     if size & (size - 1):
@@ -281,7 +303,7 @@
             blocks[step + 1] = exchange(blocks[step], "comp", 1)
             others[step] = exchange(others[step + 1], "comp", 1)
     updated, squares = rest_part(partly, projected, far, of(others, far), of(blocks, far), rows, features)
-    return finish(updated, terms(squares, "feat", 2), features)
+    return finish(updated, flipped_terms(squares), features)
 
 
 def solution(mesh):

time: 40.4 us -> 39.4 us (0.975)
  waiting for transfers between devices: 17.7 us -> 16.7 us
    ppermute x0 -> x6, starting transfers between devices: none -> 6.23 us  [flipped_terms(): parts.append(lax.ppermute(array, ('comp', 'feat'), pairs))]
    ppermute x13 -> x9, starting transfers between devices: 16.1 us -> 9.91 us  [exchange(): lax.ppermute(array, axis, [(i, i ^ step) for i in range(lax.axis_size(axi...]
    ppermute x13 -> x9, waiting for transfers between devices: 17.7 us -> 12.6 us  [exchange(): lax.ppermute(array, axis, [(i, i ^ step) for i in range(lax.axis_size(axi...]
    ppermute x0 -> x6, waiting for transfers between devices: none -> 4.09 us  [flipped_terms(): parts.append(lax.ppermute(array, ('comp', 'feat'), pairs))]
  transfers between devices with their start and end apart: 13 -> 15, of which waited for: 10 -> 10; matrix products, arithmetic and copies ran while one was open for 0% -> 0% of each run, Pallas kernels for 11% -> 11%
where the time goes in v11:
time: 39.4 us; the launch traced here: 39.3 us
  waiting for transfers between devices  16.7 us (42%)
  starting transfers between devices  16.1 us (41%)
  Pallas kernels  6.39 us (16%)
    ppermute x9, waiting for transfers between devices, exchange(): lax.ppermute(array, axis, [(i, i ^ step) for i in range(lax.axis_size(axi...  12.6 us
    ppermute x9, starting transfers between devices, exchange(): lax.ppermute(array, axis, [(i, i ^ step) for i in range(lax.axis_size(axi...  9.91 us
    ppermute x6, starting transfers between devices, flipped_terms(): parts.append(lax.ppermute(array, ('comp', 'feat'), pairs))  6.23 us
    ppermute x6, waiting for transfers between devices, flipped_terms(): parts.append(lax.ppermute(array, ('comp', 'feat'), pairs))  4.09 us
    pallas_call x1, Pallas kernels, project(): pl.pallas_call(project_kernel, in_specs=[anywhere] * 2, out_specs=[in_vme...  2.93 us
    pallas_call x1, Pallas kernels, first_part(): pl.pallas_call(functools.partial(first_kernel, features, steps), in_specs...  1.47 us
    pallas_call x1, Pallas kernels, finish(): pl.pallas_call(functools.partial(finish_kernel, features, count), in_spec...  1.08 us
    pallas_call x1, Pallas kernels, rest_part(): pl.pallas_call(functools.partial(rest_kernel, features, rows, steps), in_...  0.9 us
  transfers between devices with their start and end apart: 15, of which 10 were waited for; matrix products, arithmetic and copies ran while one was open for 0% of the time, Pallas kernels for 11%

profile of v11, /device:TPU:0, one launch (start us, length us, event | category | flops | bytes accessed | tf_op | source)
XLA Modules:
  0.0 39.3 jit_solution(7755791290885617293)
XLA Ops:
  0.0 2.9 %collective-permute-start.5 = (f32[64,3584]{1,0:T(8,128)}, f32[64,3584]{1,0:T(8,128)S(1)}, u32[]{:S(2)}, u32[]{:S(2)}) collective-permute-start(f32[64,3584]{1,0:T(8,128)} %x_hbm.1), channel_id=1, source_target_pairs={{0,16},{8,24},{16,0},{24,8},{1,17},{9,25},{17,1},{25,9},{2,18},{10... | collective-permute-start | bytes 2752520 | tf_op jit(solution)/shard_map/ppermute | solution.py:225
  2.9 2.9 %project.1 = (f32[64,256]{1,0:T(8,128)S(1)}, f32[64,3584]{1,0:T(8,128)S(1)}, f32[192,3584]{1,0:T(8,128)S(1)}) custom-call(f32[64,3584]{1,0:T(8,128)} %x_hbm.1, f32[192,3584]{1,0:T(8,128)} %bitcast.1), custom_call_target="tpu_custom_call" | custom-call | tf_op jit(solution)/shard_map/project/pallas_call | solution.py:83
  5.9 1.6 %collective-permute-start = (f32[64,256]{1,0:T(8,128)S(1)}, f32[64,256]{1,0:T(8,128)S(1)}, u32[]{:S(2)}, u32[]{:S(2)}) collective-permute-start(f32[64,256]{1,0:T(8,128)S(1)} %get-tuple-element.12), channel_id=1, source_target_pairs={{0,1},{1,0},{2,3},{3,2},{4,5},{5,4},{6,7},{7,6},{8,9},{9,8},{10,11... | collective-permute-start | bytes 196616 | tf_op jit(solution)/shard_map/ppermute | solution.py:225
  7.5 2.7 %collective-permute-done = f32[64,256]{1,0:T(8,128)S(1)} collective-permute-done((f32[64,256]{1,0:T(8,128)S(1)}, f32[64,256]{1,0:T(8,128)S(1)}, u32[]{:S(2)}, u32[]{:S(2)}) %collective-permute-start) | collective-permute-done | bytes 65568 | tf_op jit(solution)/shard_map/ppermute | solution.py:225
  10.2 1.6 %collective-permute-start.1 = (f32[64,256]{1,0:T(8,128)S(1)}, f32[64,256]{1,0:T(8,128)S(1)}, u32[]{:S(2)}, u32[]{:S(2)}) collective-permute-start(f32[64,256]{1,0:T(8,128)S(1)} %add.18), channel_id=1, source_target_pairs={{0,2},{1,3},{2,0},{3,1},{4,6},{5,7},{6,4},{7,5},{8,10},{9,11},{10,... | collective-permute-start | bytes 196616 | tf_op jit(solution)/shard_map/ppermute | solution.py:225
  11.9 2.7 %collective-permute-done.1 = f32[64,256]{1,0:T(8,128)S(1)} collective-permute-done((f32[64,256]{1,0:T(8,128)S(1)}, f32[64,256]{1,0:T(8,128)S(1)}, u32[]{:S(2)}, u32[]{:S(2)}) %collective-permute-start.1) | collective-permute-done | bytes 65568 | tf_op jit(solution)/shard_map/ppermute | solution.py:225
  14.6 2.7 %collective-permute-start.2 = (f32[64,256]{1,0:T(8,128)S(1)}, f32[64,256]{1,0:T(8,128)S(1)}, u32[]{:S(2)}, u32[]{:S(2)}) collective-permute-start(f32[64,256]{1,0:T(8,128)S(1)} %add.19), channel_id=1, source_target_pairs={{0,4},{1,5},{2,6},{3,7},{4,0},{5,1},{6,2},{7,3},{8,12},{9,13},{10,... | collective-permute-start | bytes 196616 | tf_op jit(solution)/shard_map/ppermute | solution.py:225
  17.2 2.6 %collective-permute-done.2 = f32[64,256]{1,0:T(8,128)S(1)} collective-permute-done((f32[64,256]{1,0:T(8,128)S(1)}, f32[64,256]{1,0:T(8,128)S(1)}, u32[]{:S(2)}, u32[]{:S(2)}) %collective-permute-start.2) | collective-permute-done | bytes 65568 | tf_op jit(solution)/shard_map/ppermute | solution.py:225
  19.8 0.1 collective-permute-start.3
  19.9 0.3 collective-permute-start.6
  20.2 0.2 collective-permute-start.4
  20.4 0.7 %collective-permute-done.3.refs_0_ = f32[64,256]{1,0:T(8,128)S(1)} collective-permute-done((f32[64,256]{1,0:T(8,128)S(1)}, f32[64,256]{1,0:T(8,128)S(1)}, u32[]{:S(2)}, u32[]{:S(2)}) %collective-permute-start.3) | collective-permute-done | bytes 65568 | tf_op jit(solution)/shard_map/ppermute | solution.py:225
  21.1 3.3 %collective-permute-done.6.refs_1_ = f32[64,256]{1,0:T(8,128)S(1)} collective-permute-done((f32[64,256]{1,0:T(8,128)S(1)}, f32[64,256]{1,0:T(8,128)S(1)}, u32[]{:S(2)}, u32[]{:S(2)}) %collective-permute-start.6) | collective-permute-done | bytes 65568 | tf_op jit(solution)/shard_map/ppermute | solution.py:225
  24.4 0.0 collective-permute-done.5.refs_2_
  24.4 0.3 collective-permute-start.8
  24.7 0.2 collective-permute-start.7
  24.9 0.0 collective-permute-done.4.refs_1_
  24.9 1.5 %first_part.1.t_ref = f32[64,3584]{1,0:T(8,128)S(1)} custom-call(f32[64,256]{1,0:T(8,128)S(1)} %add.20.p_ref, f32[192,3584]{1,0:T(8,128)S(1)} %get-tuple-element.13.s_ref, f32[64,3584]{1,0:T(8,128)S(1)} %get-tuple-element.14.x_ref, f32[64,256]{1,0:T(8,128)S(1)} %collective-permute-done.3.refs_0_, f32[64,3584]{1,0:T(8,128)S(1)} %collective-permute-done.4.refs_1_), custom_call_target="tpu_custom_call" | custom-call | tf_op jit(solution)/shard_map/first_part/pallas_call | solution.py:140
  26.4 0.6 %collective-permute-done.7.refs_0_ = f32[64,256]{1,0:T(8,128)S(1)} collective-permute-done((f32[64,256]{1,0:T(8,128)S(1)}, f32[64,256]{1,0:T(8,128)S(1)}, u32[]{:S(2)}, u32[]{:S(2)}) %collective-permute-start.7) | collective-permute-done | bytes 65568 | tf_op jit(solution)/shard_map/ppermute | solution.py:225
  27.0 0.0 collective-permute-done.8.refs_3_
  27.0 0.9 %rest_part.1 = (f32[64,3584]{1,0:T(8,128)S(1)}, f32[1,64]{1,0:T(1,128)S(1)}) custom-call(f32[64,3584]{1,0:T(8,128)S(1)} %first_part.1.t_ref, f32[64,256]{1,0:T(8,128)S(1)} %add.20.p_ref, f32[64,256]{1,0:T(8,128)S(1)} %collective-permute-done.7.refs_0_, f32[64,256]{1,0:T(8,128)S(1)} %collective-permute-done.6.refs_1_, ...), custom_call_target="tpu_custom_call" | custom-call | tf_op jit(solution)/shard_map/rest_part/pallas_call | solution.py:170
  27.9 2.8 %collective-permute-start.12 = (f32[1,64]{1,0:T(1,128)S(1)}, f32[1,64]{1,0:T(1,128)S(1)}, u32[]{:S(2)}, u32[]{:S(2)}) collective-permute-start(f32[1,64]{1,0:T(1,128)S(1)} %get-tuple-element.18), channel_id=1, source_target_pairs={{0,11},{1,10},{2,9},{3,8},{4,15},{5,14},{6,13},{7,12},{8,3},{9,2},... | collective-permute-start | bytes 776 | tf_op jit(solution)/shard_map/ppermute | solution.py:258
  30.7 0.2 collective-permute-start.11
  30.9 0.4 collective-permute-start.9
  31.2 0.2 collective-permute-start.10
  31.4 0.5 %collective-permute-done.12 = f32[1,64]{1,0:T(1,128)S(1)} collective-permute-done((f32[1,64]{1,0:T(1,128)S(1)}, f32[1,64]{1,0:T(1,128)S(1)}, u32[]{:S(2)}, u32[]{:S(2)}) %collective-permute-start.12) | collective-permute-done | bytes 288 | tf_op jit(solution)/shard_map/ppermute | solution.py:258
  32.0 1.7 %collective-permute-done.11 = f32[1,64]{1,0:T(1,128)S(1)} collective-permute-done((f32[1,64]{1,0:T(1,128)S(1)}, f32[1,64]{1,0:T(1,128)S(1)}, u32[]{:S(2)}, u32[]{:S(2)}) %collective-permute-start.11) | collective-permute-done | bytes 288 | tf_op jit(solution)/shard_map/ppermute | solution.py:258
  33.6 0.0 collective-permute-done.9
  33.6 0.6 %collective-permute-done.10 = f32[1,64]{1,0:T(1,128)S(1)} collective-permute-done((f32[1,64]{1,0:T(1,128)S(1)}, f32[1,64]{1,0:T(1,128)S(1)}, u32[]{:S(2)}, u32[]{:S(2)}) %collective-permute-start.10) | collective-permute-done | bytes 288 | tf_op jit(solution)/shard_map/ppermute | solution.py:258
  34.2 0.1 collective-permute-start.13
  34.3 2.6 %collective-permute-start.14 = (f32[1,64]{1,0:T(1,128)S(1)}, f32[1,64]{1,0:T(1,128)S(1)}, u32[]{:S(2)}, u32[]{:S(2)}) collective-permute-start(f32[1,64]{1,0:T(1,128)S(1)} %add_add_fusion), channel_id=1, source_target_pairs={{0,12},{1,13},{2,14},{3,15},{4,8},{5,9},{6,10},{7,11},{8,4},{9,5},... | collective-permute-start | bytes 776 | tf_op jit(solution)/shard_map/ppermute | solution.py:258
  36.9 0.0 collective-permute-done.13.refs_0_
  36.9 1.3 %collective-permute-done.14.refs_1_ = f32[1,64]{1,0:T(1,128)S(1)} collective-permute-done((f32[1,64]{1,0:T(1,128)S(1)}, f32[1,64]{1,0:T(1,128)S(1)}, u32[]{:S(2)}, u32[]{:S(2)}) %collective-permute-start.14) | collective-permute-done | bytes 288 | tf_op jit(solution)/shard_map/ppermute | solution.py:258
  38.2 1.1 %finish.1 = f32[64,3584]{1,0:T(8,128)} custom-call(f32[64,3584]{1,0:T(8,128)S(1)} %get-tuple-element.17.updated_ref, f32[1,64]{1,0:T(1,128)S(1)} %collective-permute-done.13.refs_0_, f32[1,64]{1,0:T(1,128)S(1)} %collective-permute-done.14.refs_1_), custom_call_target="tpu_custom_call" | custom-call | tf_op jit(solution)/shard_map/finish/pallas_call | solution.py:210
  (4 shorter events, 0.0 us)
Async XLA Ops:
  0.0 24.4 %collective-permute-start.5 = (f32[64,3584]{1,0:T(8,128)}, f32[64,3584]{1,0:T(8,128)S(1)}, u32[]{:S(2)}, u32[]{:S(2)}) collective-permute-start(f32[64,3584]{1,0:T(8,128)} %x_hbm.1), channel_id=1, source_target_pairs={{0,16},{8,24},{16,0},{24,8},{1,17},{9,25},{17,1},{25,9},{2,18},{10... | collective-permute-start | bytes 2752520 | tf_op jit(solution)/shard_map/ppermute | solution.py:225
  5.9 4.3 %collective-permute-start = (f32[64,256]{1,0:T(8,128)S(1)}, f32[64,256]{1,0:T(8,128)S(1)}, u32[]{:S(2)}, u32[]{:S(2)}) collective-permute-start(f32[64,256]{1,0:T(8,128)S(1)} %get-tuple-element.12), channel_id=1, source_target_pairs={{0,1},{1,0},{2,3},{3,2},{4,5},{5,4},{6,7},{7,6},{8,9},{9,8},{10,11... | collective-permute-start | bytes 196616 | tf_op jit(solution)/shard_map/ppermute | solution.py:225
  10.2 4.3 %collective-permute-start.1 = (f32[64,256]{1,0:T(8,128)S(1)}, f32[64,256]{1,0:T(8,128)S(1)}, u32[]{:S(2)}, u32[]{:S(2)}) collective-permute-start(f32[64,256]{1,0:T(8,128)S(1)} %add.18), channel_id=1, source_target_pairs={{0,2},{1,3},{2,0},{3,1},{4,6},{5,7},{6,4},{7,5},{8,10},{9,11},{10,... | collective-permute-start | bytes 196616 | tf_op jit(solution)/shard_map/ppermute | solution.py:225
  14.6 5.2 %collective-permute-start.2 = (f32[64,256]{1,0:T(8,128)S(1)}, f32[64,256]{1,0:T(8,128)S(1)}, u32[]{:S(2)}, u32[]{:S(2)}) collective-permute-start(f32[64,256]{1,0:T(8,128)S(1)} %add.19), channel_id=1, source_target_pairs={{0,4},{1,5},{2,6},{3,7},{4,0},{5,1},{6,2},{7,3},{8,12},{9,13},{10,... | collective-permute-start | bytes 196616 | tf_op jit(solution)/shard_map/ppermute | solution.py:225
  19.8 1.3 %collective-permute-start.3 = (f32[64,256]{1,0:T(8,128)S(1)}, f32[64,256]{1,0:T(8,128)S(1)}, u32[]{:S(2)}, u32[]{:S(2)}) collective-permute-start(f32[64,256]{1,0:T(8,128)S(1)} %add.20.p_ref), channel_id=1, source_target_pairs={{0,8},{8,0},{16,24},{24,16},{1,9},{9,1},{17,25},{25,17},{2,10},{10... | collective-permute-start | bytes 196616 | tf_op jit(solution)/shard_map/ppermute | solution.py:225
  19.9 4.5 %collective-permute-start.6 = (f32[64,256]{1,0:T(8,128)S(1)}, f32[64,256]{1,0:T(8,128)S(1)}, u32[]{:S(2)}, u32[]{:S(2)}) collective-permute-start(f32[64,256]{1,0:T(8,128)S(1)} %add.20.p_ref), channel_id=1, source_target_pairs={{0,24},{8,16},{16,8},{24,0},{1,25},{9,17},{17,9},{25,1},{2,26},{10... | collective-permute-start | bytes 196616 | tf_op jit(solution)/shard_map/ppermute | solution.py:225
  20.2 4.7 %collective-permute-start.4 = (f32[64,3584]{1,0:T(8,128)S(1)}, f32[64,3584]{1,0:T(8,128)S(1)}, u32[]{:S(2)}, u32[]{:S(2)}) collective-permute-start(f32[64,3584]{1,0:T(8,128)S(1)} %get-tuple-element.14.x_ref), channel_id=1, source_target_pairs={{0,8},{8,0},{16,24},{24,16},{1,9},{9,1},{17,25},{25,17},{2,10},{10... | collective-permute-start | bytes 2752520 | tf_op jit(solution)/shard_map/ppermute | solution.py:225
  24.4 2.6 %collective-permute-start.8 = (f32[64,3584]{1,0:T(8,128)S(1)}, f32[64,3584]{1,0:T(8,128)S(1)}, u32[]{:S(2)}, u32[]{:S(2)}) collective-permute-start(f32[64,3584]{1,0:T(8,128)S(1)} %collective-permute-done.5.refs_2_), channel_id=1, source_target_pairs={{0,8},{8,0},{16,24},{24,16},{1,9},{9,1},{17,25},{25,17},{2,10},{10... | collective-permute-start | bytes 2752520 | tf_op jit(solution)/shard_map/ppermute | solution.py:225
  24.7 2.3 %collective-permute-start.7 = (f32[64,256]{1,0:T(8,128)S(1)}, f32[64,256]{1,0:T(8,128)S(1)}, u32[]{:S(2)}, u32[]{:S(2)}) collective-permute-start(f32[64,256]{1,0:T(8,128)S(1)} %collective-permute-done.6.refs_1_), channel_id=1, source_target_pairs={{0,8},{8,0},{16,24},{24,16},{1,9},{9,1},{17,25},{25,17},{2,10},{10... | collective-permute-start | bytes 196616 | tf_op jit(solution)/shard_map/ppermute | solution.py:225
  27.9 4.1 %collective-permute-start.12 = (f32[1,64]{1,0:T(1,128)S(1)}, f32[1,64]{1,0:T(1,128)S(1)}, u32[]{:S(2)}, u32[]{:S(2)}) collective-permute-start(f32[1,64]{1,0:T(1,128)S(1)} %get-tuple-element.18), channel_id=1, source_target_pairs={{0,11},{1,10},{2,9},{3,8},{4,15},{5,14},{6,13},{7,12},{8,3},{9,2},... | collective-permute-start | bytes 776 | tf_op jit(solution)/shard_map/ppermute | solution.py:258
  30.7 3.0 %collective-permute-start.11 = (f32[1,64]{1,0:T(1,128)S(1)}, f32[1,64]{1,0:T(1,128)S(1)}, u32[]{:S(2)}, u32[]{:S(2)}) collective-permute-start(f32[1,64]{1,0:T(1,128)S(1)} %get-tuple-element.18), channel_id=1, source_target_pairs={{0,10},{1,11},{2,8},{3,9},{4,14},{5,15},{6,12},{7,13},{8,2},{9,3},... | collective-permute-start | bytes 776 | tf_op jit(solution)/shard_map/ppermute | solution.py:258
  30.9 2.8 %collective-permute-start.9 = (f32[1,64]{1,0:T(1,128)S(1)}, f32[1,64]{1,0:T(1,128)S(1)}, u32[]{:S(2)}, u32[]{:S(2)}) collective-permute-start(f32[1,64]{1,0:T(1,128)S(1)} %get-tuple-element.18), channel_id=1, source_target_pairs={{0,8},{1,9},{2,10},{3,11},{4,12},{5,13},{6,14},{7,15},{8,0},{9,1},... | collective-permute-start | bytes 776 | tf_op jit(solution)/shard_map/ppermute | solution.py:258
  31.2 3.0 %collective-permute-start.10 = (f32[1,64]{1,0:T(1,128)S(1)}, f32[1,64]{1,0:T(1,128)S(1)}, u32[]{:S(2)}, u32[]{:S(2)}) collective-permute-start(f32[1,64]{1,0:T(1,128)S(1)} %get-tuple-element.18), channel_id=1, source_target_pairs={{0,9},{1,8},{2,11},{3,10},{4,13},{5,12},{6,15},{7,14},{8,1},{9,0},... | collective-permute-start | bytes 776 | tf_op jit(solution)/shard_map/ppermute | solution.py:258
  34.2 2.7 %collective-permute-start.13 = (f32[1,64]{1,0:T(1,128)S(1)}, f32[1,64]{1,0:T(1,128)S(1)}, u32[]{:S(2)}, u32[]{:S(2)}) collective-permute-start(f32[1,64]{1,0:T(1,128)S(1)} %add_add_fusion), channel_id=1, source_target_pairs={{0,8},{1,9},{2,10},{3,11},{4,12},{5,13},{6,14},{7,15},{8,0},{9,1},... | collective-permute-start | bytes 776 | tf_op jit(solution)/shard_map/ppermute | solution.py:258
  34.3 3.9 %collective-permute-start.14 = (f32[1,64]{1,0:T(1,128)S(1)}, f32[1,64]{1,0:T(1,128)S(1)}, u32[]{:S(2)}, u32[]{:S(2)}) collective-permute-start(f32[1,64]{1,0:T(1,128)S(1)} %add_add_fusion), channel_id=1, source_target_pairs={{0,12},{1,13},{2,14},{3,15},{4,8},{5,9},{6,10},{7,11},{8,4},{9,5},... | collective-permute-start | bytes 776 | tf_op jit(solution)/shard_map/ppermute | solution.py:258

commit v12 on v11

--- a/solution.py
+++ b/solution.py
@@ -43,7 +43,25 @@
 
 def loop(columns, most, body, init):
     tile = tile_of(columns, most)
-    return lax.fori_loop(0, columns // tile, lambda i, c: body(i, pl.ds(pl.multiple_of(i * tile, tile), tile), c), init, unroll=True)
+    for i in range(columns // tile):
+        init = body(i, pl.ds(i * tile, tile), init)
+    return init
+
+
+def columns_at(held, here):
+    width = held[0].shape[1]
+    wanted = range(here.start, here.start + here.size)
+    parts = []
+    for k, ref in enumerate(held):
+        first, last = max(wanted.start, k * width), min(wanted.stop, (k + 1) * width)
+        if first < last:
+            parts.append(ref[:, first - k * width : last - k * width])
+    return parts[0] if len(parts) == 1 else jnp.concatenate(parts, axis=1)
+
+
+def pieces_of(columns):
+    tile = tile_of(columns, columns // (4 * lanes) or 1)
+    return [slice(start, start + tile) for start in range(0, columns, tile)]
 
 
 def project_kernel(x_hbm, s_hbm, out_ref, x_ref, s_ref, sems):
@@ -149,15 +167,21 @@
 
 def rest_kernel(features, rows, steps, t_ref, p_ref, *refs):
     count = len(steps)
-    projected_refs, x_refs, (out_ref, squares_ref) = refs[:count], refs[count : 2 * count], refs[2 * count :]
+    projected_refs, x_refs, (out_ref, squares_ref) = refs[:count], list(refs[count:-2]), refs[-2:]
     per_group, columns = t_ref.shape
+    far = []
+    for step in steps:
+        held = [x_refs.pop(0)]
+        while sum(ref.shape[1] for ref in held) < columns:
+            held.append(x_refs.pop(0))
+        far.append(held)
     if count:
         weights = halves(couplings(images_of(p_ref, rows, features)[0], steps, projected_refs, features))
 
     def body(i, here, squares):
         updated = t_ref[:, here]
         if count:
-            updated += product(weights, jnp.concatenate([ref[:, here] for ref in x_refs], axis=0))
+            updated += product(weights, jnp.concatenate([columns_at(held, here) for held in far], axis=0))
         out_ref[:, here] = updated
         return squares + jnp.sum(updated * updated, axis=1, keepdims=True)
 
@@ -169,7 +193,7 @@
 def rest_part(partly, projected, steps, others, blocks, rows, features):
     return pl.pallas_call(
         functools.partial(rest_kernel, features, rows, steps),
-        in_specs=[in_vmem] * (2 + 2 * len(steps)),
+        in_specs=[in_vmem] * (2 + len(others) + len(blocks)),
         out_specs=[in_vmem, in_vmem],
         out_shape=[
             jax.ShapeDtypeStruct(partly.shape, jnp.float32),
@@ -285,23 +309,21 @@
     parts = terms(projected, "feat", 1)
     projected = sum(parts[1:], parts[0])
     if even:
-        others = {step: exchange(projected, "comp", step) for step in range(1, comp, 2)}
+        others = {step: exchange(projected, "comp", step) for step in range(1, comp) if step == 1 or step % 2 == 0}
     else:
         others = gather(projected)
     near = [1][: comp - 1]
     far = list(range(2, comp))
 
     def of(arrays, steps):
-        return [arrays[step] for step in steps]
+        return [piece for step in steps for piece in (arrays[step] if isinstance(arrays[step], list) else [arrays[step]])]
 
     partly = first_part(projected, sample, vectors, near, of(others, near), of(blocks, near), features)
     if even:
         for step in range(2, comp, 2):
-            blocks[step], others[step + 1], others[1] = lax.optimization_barrier(
-                (blocks[step], others[step + 1], others[1])
-            )
-            blocks[step + 1] = exchange(blocks[step], "comp", 1)
-            others[step] = exchange(others[step + 1], "comp", 1)
+            blocks[step], others[1] = lax.optimization_barrier((blocks[step], others[1]))
+            blocks[step + 1] = [exchange(blocks[step][:, here], "comp", 1) for here in pieces_of(blocks[step].shape[1])]
+            others[step + 1] = exchange(others[step], "comp", 1)
     updated, squares = rest_part(partly, projected, far, of(others, far), of(blocks, far), rows, features)
     return finish(updated, flipped_terms(squares), features)
 

time: 39.4 us -> 40.5 us (1.028)
  starting transfers between devices: 16.1 us -> 16.6 us
    ppermute x6, waiting for transfers between devices: 4.09 us -> 5.25 us  [flipped_terms(): parts.append(lax.ppermute(array, ('comp', 'feat'), pairs))]
    ppermute x9 -> x12, waiting for transfers between devices: 12.6 us -> 11.9 us  [exchange(): lax.ppermute(array, axis, [(i, i ^ step) for i in range(lax.axis_size(axi...]
    ppermute x9 -> x12, starting transfers between devices: 9.91 us -> 10.5 us  [exchange(): lax.ppermute(array, axis, [(i, i ^ step) for i in range(lax.axis_size(axi...]
  transfers between devices with their start and end apart: 15 -> 18, of which waited for: 10 -> 9; matrix products, arithmetic and copies ran while one was open for 0% -> 0% of each run, Pallas kernels for 11% -> 11%
where the time goes in v12:
time: 40.5 us; the launch traced here: 40.3 us
  waiting for transfers between devices  17.1 us (42%)
  starting transfers between devices  16.6 us (41%)
  Pallas kernels  6.41 us (16%)
    ppermute x12, waiting for transfers between devices, exchange(): lax.ppermute(array, axis, [(i, i ^ step) for i in range(lax.axis_size(axi...  11.9 us
    ppermute x12, starting transfers between devices, exchange(): lax.ppermute(array, axis, [(i, i ^ step) for i in range(lax.axis_size(axi...  10.5 us
    ppermute x6, starting transfers between devices, flipped_terms(): parts.append(lax.ppermute(array, ('comp', 'feat'), pairs))  6.09 us
    ppermute x6, waiting for transfers between devices, flipped_terms(): parts.append(lax.ppermute(array, ('comp', 'feat'), pairs))  5.25 us
    pallas_call x1, Pallas kernels, project(): pl.pallas_call(project_kernel, in_specs=[anywhere] * 2, out_specs=[in_vme...  2.93 us
    pallas_call x1, Pallas kernels, first_part(): pl.pallas_call(functools.partial(first_kernel, features, steps), in_specs...  1.49 us
    pallas_call x1, Pallas kernels, finish(): pl.pallas_call(functools.partial(finish_kernel, features, count), in_spec...  1.08 us
    pallas_call x1, Pallas kernels, rest_part(): pl.pallas_call(functools.partial(rest_kernel, features, rows, steps), in_...  0.9 us
  transfers between devices with their start and end apart: 18, of which 9 were waited for; matrix products, arithmetic and copies ran while one was open for 0% of the time, Pallas kernels for 11%

profile of v12, /device:TPU:0, one launch (start us, length us, event | category | flops | bytes accessed | tf_op | source)
XLA Modules:
  0.0 40.3 jit_solution(17466629690155927008)
XLA Ops:
  0.0 2.9 %collective-permute-start.7 = (f32[64,3584]{1,0:T(8,128)}, f32[64,3584]{1,0:T(8,128)S(1)}, u32[]{:S(2)}, u32[]{:S(2)}) collective-permute-start(f32[64,3584]{1,0:T(8,128)} %x_hbm.1), channel_id=1, source_target_pairs={{0,16},{8,24},{16,0},{24,8},{1,17},{9,25},{17,1},{25,9},{2,18},{10... | collective-permute-start | bytes 2752520 | tf_op jit(solution)/shard_map/ppermute | solution.py:249
  2.9 2.9 %project.1 = (f32[64,256]{1,0:T(8,128)S(1)}, f32[64,3584]{1,0:T(8,128)S(1)}, f32[192,3584]{1,0:T(8,128)S(1)}) custom-call(f32[64,3584]{1,0:T(8,128)} %x_hbm.1, f32[192,3584]{1,0:T(8,128)} %bitcast.1), custom_call_target="tpu_custom_call" | custom-call | tf_op jit(solution)/shard_map/project/pallas_call | solution.py:101
  5.9 0.1 collective-permute-start.4
  6.0 1.6 %collective-permute-start = (f32[64,256]{1,0:T(8,128)S(1)}, f32[64,256]{1,0:T(8,128)S(1)}, u32[]{:S(2)}, u32[]{:S(2)}) collective-permute-start(f32[64,256]{1,0:T(8,128)S(1)} %get-tuple-element.11), channel_id=1, source_target_pairs={{0,1},{1,0},{2,3},{3,2},{4,5},{5,4},{6,7},{7,6},{8,9},{9,8},{10,11... | collective-permute-start | bytes 196616 | tf_op jit(solution)/shard_map/ppermute | solution.py:249
  7.5 2.9 %collective-permute-done = f32[64,256]{1,0:T(8,128)S(1)} collective-permute-done((f32[64,256]{1,0:T(8,128)S(1)}, f32[64,256]{1,0:T(8,128)S(1)}, u32[]{:S(2)}, u32[]{:S(2)}) %collective-permute-start) | collective-permute-done | bytes 65568 | tf_op jit(solution)/shard_map/ppermute | solution.py:249
  10.5 1.6 %collective-permute-start.1 = (f32[64,256]{1,0:T(8,128)S(1)}, f32[64,256]{1,0:T(8,128)S(1)}, u32[]{:S(2)}, u32[]{:S(2)}) collective-permute-start(f32[64,256]{1,0:T(8,128)S(1)} %add.18), channel_id=1, source_target_pairs={{0,2},{1,3},{2,0},{3,1},{4,6},{5,7},{6,4},{7,5},{8,10},{9,11},{10,... | collective-permute-start | bytes 196616 | tf_op jit(solution)/shard_map/ppermute | solution.py:249
  12.1 2.7 %collective-permute-done.1 = f32[64,256]{1,0:T(8,128)S(1)} collective-permute-done((f32[64,256]{1,0:T(8,128)S(1)}, f32[64,256]{1,0:T(8,128)S(1)}, u32[]{:S(2)}, u32[]{:S(2)}) %collective-permute-start.1) | collective-permute-done | bytes 65568 | tf_op jit(solution)/shard_map/ppermute | solution.py:249
  14.8 2.7 %collective-permute-start.2 = (f32[64,256]{1,0:T(8,128)S(1)}, f32[64,256]{1,0:T(8,128)S(1)}, u32[]{:S(2)}, u32[]{:S(2)}) collective-permute-start(f32[64,256]{1,0:T(8,128)S(1)} %add.19), channel_id=1, source_target_pairs={{0,4},{1,5},{2,6},{3,7},{4,0},{5,1},{6,2},{7,3},{8,12},{9,13},{10,... | collective-permute-start | bytes 196616 | tf_op jit(solution)/shard_map/ppermute | solution.py:249
  17.5 2.6 %collective-permute-done.2 = f32[64,256]{1,0:T(8,128)S(1)} collective-permute-done((f32[64,256]{1,0:T(8,128)S(1)}, f32[64,256]{1,0:T(8,128)S(1)}, u32[]{:S(2)}, u32[]{:S(2)}) %collective-permute-start.2) | collective-permute-done | bytes 65568 | tf_op jit(solution)/shard_map/ppermute | solution.py:249
  20.1 0.1 collective-permute-start.3
  20.1 0.4 collective-permute-start.5
  20.5 0.9 %collective-permute-done.3.refs_0_ = f32[64,256]{1,0:T(8,128)S(1)} collective-permute-done((f32[64,256]{1,0:T(8,128)S(1)}, f32[64,256]{1,0:T(8,128)S(1)}, u32[]{:S(2)}, u32[]{:S(2)}) %collective-permute-start.3) | collective-permute-done | bytes 65568 | tf_op jit(solution)/shard_map/ppermute | solution.py:249
  21.4 2.3 %collective-permute-done.7.refs_2_ = f32[64,3584]{1,0:T(8,128)S(1)} collective-permute-done((f32[64,3584]{1,0:T(8,128)}, f32[64,3584]{1,0:T(8,128)S(1)}, u32[]{:S(2)}, u32[]{:S(2)}) %collective-permute-start.7) | collective-permute-done | bytes 917536 | tf_op jit(solution)/shard_map/ppermute | solution.py:249
  23.7 0.1 fusion
  23.7 0.1 collective-permute-start.10
  23.8 0.5 %collective-permute-start.11 = (f32[64,896]{1,0:T(8,128)S(1)}, f32[64,896]{1,0:T(8,128)S(1)}, u32[]{:S(2)}, u32[]{:S(2)}) collective-permute-start(f32[64,896]{1,0:T(8,128)S(1)} %get-tuple-element.17), channel_id=1, source_target_pairs={{0,8},{8,0},{16,24},{24,16},{1,9},{9,1},{17,25},{25,17},{2,10},{10... | collective-permute-start | bytes 688136 | tf_op jit(solution)/shard_map/ppermute | solution.py:249
  24.3 0.1 collective-permute-start.8
  24.4 0.5 %collective-permute-done.5.refs_0_ = f32[64,256]{1,0:T(8,128)S(1)} collective-permute-done((f32[64,256]{1,0:T(8,128)S(1)}, f32[64,256]{1,0:T(8,128)S(1)}, u32[]{:S(2)}, u32[]{:S(2)}) %collective-permute-start.5) | collective-permute-done | bytes 65568 | tf_op jit(solution)/shard_map/ppermute | solution.py:249
  24.9 0.0 collective-permute-start.9
  24.9 0.0 collective-permute-done.4.refs_1_
  24.9 0.5 %collective-permute-start.6 = (f32[64,256]{1,0:T(8,128)S(1)}, f32[64,256]{1,0:T(8,128)S(1)}, u32[]{:S(2)}, u32[]{:S(2)}) collective-permute-start(f32[64,256]{1,0:T(8,128)S(1)} %collective-permute-done.5.refs_0_), channel_id=1, source_target_pairs={{0,8},{8,0},{16,24},{24,16},{1,9},{9,1},{17,25},{25,17},{2,10},{10... | collective-permute-start | bytes 196616 | tf_op jit(solution)/shard_map/ppermute | solution.py:249
  25.4 1.5 %first_part.1.t_ref = f32[64,3584]{1,0:T(8,128)S(1)} custom-call(f32[64,256]{1,0:T(8,128)S(1)} %add.20.p_ref, f32[192,3584]{1,0:T(8,128)S(1)} %get-tuple-element.12.s_ref, f32[64,3584]{1,0:T(8,128)S(1)} %get-tuple-element.13.x_ref, f32[64,256]{1,0:T(8,128)S(1)} %collective-permute-done.3.refs_0_, f32[64,3584]{1,0:T(8,128)S(1)} %collective-permute-done.4.refs_1_), custom_call_target="tpu_custom_call" | custom-call | tf_op jit(solution)/shard_map/first_part/pallas_call | solution.py:158
  26.9 0.0 collective-permute-done.6.refs_1_
  26.9 0.0 collective-permute-done.10.refs_5_
  26.9 0.0 collective-permute-done.11.refs_6_
  26.9 0.0 collective-permute-done.8.refs_3_
  27.0 0.0 collective-permute-done.9.refs_4_
  27.0 0.9 %rest_part.1 = (f32[64,3584]{1,0:T(8,128)S(1)}, f32[1,64]{1,0:T(1,128)S(1)}) custom-call(f32[64,3584]{1,0:T(8,128)S(1)} %first_part.1.t_ref, f32[64,256]{1,0:T(8,128)S(1)} %add.20.p_ref, f32[64,256]{1,0:T(8,128)S(1)} %collective-permute-done.5.refs_0_, f32[64,256]{1,0:T(8,128)S(1)} %collective-permute-done.6.refs_1_, ...), custom_call_target="tpu_custom_call" | custom-call | tf_op jit(solution)/shard_map/rest_part/pallas_call | solution.py:194
  27.9 0.1 collective-permute-start.12
  28.0 1.9 %collective-permute-start.13 = (f32[1,64]{1,0:T(1,128)S(1)}, f32[1,64]{1,0:T(1,128)S(1)}, u32[]{:S(2)}, u32[]{:S(2)}) collective-permute-start(f32[1,64]{1,0:T(1,128)S(1)} %get-tuple-element.16), channel_id=1, source_target_pairs={{0,9},{1,8},{2,11},{3,10},{4,13},{5,12},{6,15},{7,14},{8,1},{9,0},... | collective-permute-start | bytes 776 | tf_op jit(solution)/shard_map/ppermute | solution.py:282
  29.8 1.3 %collective-permute-start.14 = (f32[1,64]{1,0:T(1,128)S(1)}, f32[1,64]{1,0:T(1,128)S(1)}, u32[]{:S(2)}, u32[]{:S(2)}) collective-permute-start(f32[1,64]{1,0:T(1,128)S(1)} %get-tuple-element.16), channel_id=1, source_target_pairs={{0,10},{1,11},{2,8},{3,9},{4,14},{5,15},{6,12},{7,13},{8,2},{9,3},... | collective-permute-start | bytes 776 | tf_op jit(solution)/shard_map/ppermute | solution.py:282
  31.2 0.1 collective-permute-start.15
  31.3 0.0 collective-permute-done.12
  31.3 0.0 collective-permute-done.13
  31.3 1.5 %collective-permute-done.14 = f32[1,64]{1,0:T(1,128)S(1)} collective-permute-done((f32[1,64]{1,0:T(1,128)S(1)}, f32[1,64]{1,0:T(1,128)S(1)}, u32[]{:S(2)}, u32[]{:S(2)}) %collective-permute-start.14) | collective-permute-done | bytes 288 | tf_op jit(solution)/shard_map/ppermute | solution.py:282
  32.8 2.2 %collective-permute-done.15 = f32[1,64]{1,0:T(1,128)S(1)} collective-permute-done((f32[1,64]{1,0:T(1,128)S(1)}, f32[1,64]{1,0:T(1,128)S(1)}, u32[]{:S(2)}, u32[]{:S(2)}) %collective-permute-start.15) | collective-permute-done | bytes 288 | tf_op jit(solution)/shard_map/ppermute | solution.py:282
  35.0 0.3 collective-permute-start.16
  35.4 2.4 %collective-permute-start.17 = (f32[1,64]{1,0:T(1,128)S(1)}, f32[1,64]{1,0:T(1,128)S(1)}, u32[]{:S(2)}, u32[]{:S(2)}) collective-permute-start(f32[1,64]{1,0:T(1,128)S(1)} %add_add_fusion), channel_id=1, source_target_pairs={{0,12},{1,13},{2,14},{3,15},{4,8},{5,9},{6,10},{7,11},{8,4},{9,5},... | collective-permute-start | bytes 776 | tf_op jit(solution)/shard_map/ppermute | solution.py:282
  37.7 0.0 collective-permute-done.16.refs_0_
  37.7 1.5 %collective-permute-done.17.refs_1_ = f32[1,64]{1,0:T(1,128)S(1)} collective-permute-done((f32[1,64]{1,0:T(1,128)S(1)}, f32[1,64]{1,0:T(1,128)S(1)}, u32[]{:S(2)}, u32[]{:S(2)}) %collective-permute-start.17) | collective-permute-done | bytes 288 | tf_op jit(solution)/shard_map/ppermute | solution.py:282
  39.2 1.1 %finish.1 = f32[64,3584]{1,0:T(8,128)} custom-call(f32[64,3584]{1,0:T(8,128)S(1)} %get-tuple-element.15.updated_ref, f32[1,64]{1,0:T(1,128)S(1)} %collective-permute-done.16.refs_0_, f32[1,64]{1,0:T(1,128)S(1)} %collective-permute-done.17.refs_1_), custom_call_target="tpu_custom_call" | custom-call | tf_op jit(solution)/shard_map/finish/pallas_call | solution.py:234
  (4 shorter events, 0.0 us)
Async XLA Ops:
  0.0 23.7 %collective-permute-start.7 = (f32[64,3584]{1,0:T(8,128)}, f32[64,3584]{1,0:T(8,128)S(1)}, u32[]{:S(2)}, u32[]{:S(2)}) collective-permute-start(f32[64,3584]{1,0:T(8,128)} %x_hbm.1), channel_id=1, source_target_pairs={{0,16},{8,24},{16,0},{24,8},{1,17},{9,25},{17,1},{25,9},{2,18},{10... | collective-permute-start | bytes 2752520 | tf_op jit(solution)/shard_map/ppermute | solution.py:249
  5.9 19.0 %collective-permute-start.4 = (f32[64,3584]{1,0:T(8,128)S(1)}, f32[64,3584]{1,0:T(8,128)S(1)}, u32[]{:S(2)}, u32[]{:S(2)}) collective-permute-start(f32[64,3584]{1,0:T(8,128)S(1)} %get-tuple-element.13.x_ref), channel_id=1, source_target_pairs={{0,8},{8,0},{16,24},{24,16},{1,9},{9,1},{17,25},{25,17},{2,10},{10... | collective-permute-start | bytes 2752520 | tf_op jit(solution)/shard_map/ppermute | solution.py:249
  6.0 4.5 %collective-permute-start = (f32[64,256]{1,0:T(8,128)S(1)}, f32[64,256]{1,0:T(8,128)S(1)}, u32[]{:S(2)}, u32[]{:S(2)}) collective-permute-start(f32[64,256]{1,0:T(8,128)S(1)} %get-tuple-element.11), channel_id=1, source_target_pairs={{0,1},{1,0},{2,3},{3,2},{4,5},{5,4},{6,7},{7,6},{8,9},{9,8},{10,11... | collective-permute-start | bytes 196616 | tf_op jit(solution)/shard_map/ppermute | solution.py:249
  10.5 4.3 %collective-permute-start.1 = (f32[64,256]{1,0:T(8,128)S(1)}, f32[64,256]{1,0:T(8,128)S(1)}, u32[]{:S(2)}, u32[]{:S(2)}) collective-permute-start(f32[64,256]{1,0:T(8,128)S(1)} %add.18), channel_id=1, source_target_pairs={{0,2},{1,3},{2,0},{3,1},{4,6},{5,7},{6,4},{7,5},{8,10},{9,11},{10,... | collective-permute-start | bytes 196616 | tf_op jit(solution)/shard_map/ppermute | solution.py:249
  14.8 5.2 %collective-permute-start.2 = (f32[64,256]{1,0:T(8,128)S(1)}, f32[64,256]{1,0:T(8,128)S(1)}, u32[]{:S(2)}, u32[]{:S(2)}) collective-permute-start(f32[64,256]{1,0:T(8,128)S(1)} %add.19), channel_id=1, source_target_pairs={{0,4},{1,5},{2,6},{3,7},{4,0},{5,1},{6,2},{7,3},{8,12},{9,13},{10,... | collective-permute-start | bytes 196616 | tf_op jit(solution)/shard_map/ppermute | solution.py:249
  20.1 1.3 %collective-permute-start.3 = (f32[64,256]{1,0:T(8,128)S(1)}, f32[64,256]{1,0:T(8,128)S(1)}, u32[]{:S(2)}, u32[]{:S(2)}) collective-permute-start(f32[64,256]{1,0:T(8,128)S(1)} %add.20.p_ref), channel_id=1, source_target_pairs={{0,8},{8,0},{16,24},{24,16},{1,9},{9,1},{17,25},{25,17},{2,10},{10... | collective-permute-start | bytes 196616 | tf_op jit(solution)/shard_map/ppermute | solution.py:249
  20.1 4.8 %collective-permute-start.5 = (f32[64,256]{1,0:T(8,128)S(1)}, f32[64,256]{1,0:T(8,128)S(1)}, u32[]{:S(2)}, u32[]{:S(2)}) collective-permute-start(f32[64,256]{1,0:T(8,128)S(1)} %add.20.p_ref), channel_id=1, source_target_pairs={{0,16},{8,24},{16,0},{24,8},{1,17},{9,25},{17,1},{25,9},{2,18},{10... | collective-permute-start | bytes 196616 | tf_op jit(solution)/shard_map/ppermute | solution.py:249
  23.7 3.2 %collective-permute-start.10 = (f32[64,896]{1,0:T(8,128)S(1)}, f32[64,896]{1,0:T(8,128)S(1)}, u32[]{:S(2)}, u32[]{:S(2)}) collective-permute-start(f32[64,896]{1,0:T(8,128)S(1)} %get-tuple-element.18), channel_id=1, source_target_pairs={{0,8},{8,0},{16,24},{24,16},{1,9},{9,1},{17,25},{25,17},{2,10},{10... | collective-permute-start | bytes 688136 | tf_op jit(solution)/shard_map/ppermute | solution.py:249
  23.8 3.1 %collective-permute-start.11 = (f32[64,896]{1,0:T(8,128)S(1)}, f32[64,896]{1,0:T(8,128)S(1)}, u32[]{:S(2)}, u32[]{:S(2)}) collective-permute-start(f32[64,896]{1,0:T(8,128)S(1)} %get-tuple-element.17), channel_id=1, source_target_pairs={{0,8},{8,0},{16,24},{24,16},{1,9},{9,1},{17,25},{25,17},{2,10},{10... | collective-permute-start | bytes 688136 | tf_op jit(solution)/shard_map/ppermute | solution.py:249
  24.3 2.6 %collective-permute-start.8 = (f32[64,896]{1,0:T(8,128)S(1)}, f32[64,896]{1,0:T(8,128)S(1)}, u32[]{:S(2)}, u32[]{:S(2)}) collective-permute-start(f32[64,896]{1,0:T(8,128)S(1)} %get-tuple-element.20), channel_id=1, source_target_pairs={{0,8},{8,0},{16,24},{24,16},{1,9},{9,1},{17,25},{25,17},{2,10},{10... | collective-permute-start | bytes 688136 | tf_op jit(solution)/shard_map/ppermute | solution.py:249
  24.9 2.1 %collective-permute-start.9 = (f32[64,896]{1,0:T(8,128)S(1)}, f32[64,896]{1,0:T(8,128)S(1)}, u32[]{:S(2)}, u32[]{:S(2)}) collective-permute-start(f32[64,896]{1,0:T(8,128)S(1)} %get-tuple-element.19), channel_id=1, source_target_pairs={{0,8},{8,0},{16,24},{24,16},{1,9},{9,1},{17,25},{25,17},{2,10},{10... | collective-permute-start | bytes 688136 | tf_op jit(solution)/shard_map/ppermute | solution.py:249
  24.9 2.0 %collective-permute-start.6 = (f32[64,256]{1,0:T(8,128)S(1)}, f32[64,256]{1,0:T(8,128)S(1)}, u32[]{:S(2)}, u32[]{:S(2)}) collective-permute-start(f32[64,256]{1,0:T(8,128)S(1)} %collective-permute-done.5.refs_0_), channel_id=1, source_target_pairs={{0,8},{8,0},{16,24},{24,16},{1,9},{9,1},{17,25},{25,17},{2,10},{10... | collective-permute-start | bytes 196616 | tf_op jit(solution)/shard_map/ppermute | solution.py:249
  27.9 3.4 %collective-permute-start.12 = (f32[1,64]{1,0:T(1,128)S(1)}, f32[1,64]{1,0:T(1,128)S(1)}, u32[]{:S(2)}, u32[]{:S(2)}) collective-permute-start(f32[1,64]{1,0:T(1,128)S(1)} %get-tuple-element.16), channel_id=1, source_target_pairs={{0,8},{1,9},{2,10},{3,11},{4,12},{5,13},{6,14},{7,15},{8,0},{9,1},... | collective-permute-start | bytes 776 | tf_op jit(solution)/shard_map/ppermute | solution.py:282
  28.0 3.3 %collective-permute-start.13 = (f32[1,64]{1,0:T(1,128)S(1)}, f32[1,64]{1,0:T(1,128)S(1)}, u32[]{:S(2)}, u32[]{:S(2)}) collective-permute-start(f32[1,64]{1,0:T(1,128)S(1)} %get-tuple-element.16), channel_id=1, source_target_pairs={{0,9},{1,8},{2,11},{3,10},{4,13},{5,12},{6,15},{7,14},{8,1},{9,0},... | collective-permute-start | bytes 776 | tf_op jit(solution)/shard_map/ppermute | solution.py:282
  29.8 3.0 %collective-permute-start.14 = (f32[1,64]{1,0:T(1,128)S(1)}, f32[1,64]{1,0:T(1,128)S(1)}, u32[]{:S(2)}, u32[]{:S(2)}) collective-permute-start(f32[1,64]{1,0:T(1,128)S(1)} %get-tuple-element.16), channel_id=1, source_target_pairs={{0,10},{1,11},{2,8},{3,9},{4,14},{5,15},{6,12},{7,13},{8,2},{9,3},... | collective-permute-start | bytes 776 | tf_op jit(solution)/shard_map/ppermute | solution.py:282
  31.2 3.9 %collective-permute-start.15 = (f32[1,64]{1,0:T(1,128)S(1)}, f32[1,64]{1,0:T(1,128)S(1)}, u32[]{:S(2)}, u32[]{:S(2)}) collective-permute-start(f32[1,64]{1,0:T(1,128)S(1)} %get-tuple-element.16), channel_id=1, source_target_pairs={{0,11},{1,10},{2,9},{3,8},{4,15},{5,14},{6,13},{7,12},{8,3},{9,2},... | collective-permute-start | bytes 776 | tf_op jit(solution)/shard_map/ppermute | solution.py:282
  35.0 2.7 %collective-permute-start.16 = (f32[1,64]{1,0:T(1,128)S(1)}, f32[1,64]{1,0:T(1,128)S(1)}, u32[]{:S(2)}, u32[]{:S(2)}) collective-permute-start(f32[1,64]{1,0:T(1,128)S(1)} %add_add_fusion), channel_id=1, source_target_pairs={{0,8},{1,9},{2,10},{3,11},{4,12},{5,13},{6,14},{7,15},{8,0},{9,1},... | collective-permute-start | bytes 776 | tf_op jit(solution)/shard_map/ppermute | solution.py:282
  35.4 3.9 %collective-permute-start.17 = (f32[1,64]{1,0:T(1,128)S(1)}, f32[1,64]{1,0:T(1,128)S(1)}, u32[]{:S(2)}, u32[]{:S(2)}) collective-permute-start(f32[1,64]{1,0:T(1,128)S(1)} %add_add_fusion), channel_id=1, source_target_pairs={{0,12},{1,13},{2,14},{3,15},{4,8},{5,9},{6,10},{7,11},{8,4},{9,5},... | collective-permute-start | bytes 776 | tf_op jit(solution)/shard_map/ppermute | solution.py:282

commit v13 on v0

v13 whole, which is shorter than its diff:
```python
import functools
import math

import jax
import jax.numpy as jnp
from jax import lax
from jax.experimental import pallas as pl
from jax.experimental.pallas import tpu as pltpu
from jax.sharding import PartitionSpec as P

step_rate = 0.1
epsilon = 1e-06
lanes = 128
in_vmem = pl.BlockSpec(memory_space=pltpu.VMEM)
anywhere = pl.BlockSpec(memory_space=pl.ANY)
params = pltpu.CompilerParams(vmem_limit_bytes=16 << 20)


def tile_of(columns, most):
    if columns % lanes:
        return columns
    units = columns // lanes
    return lanes * max(u for u in range(1, most + 1) if units % u == 0)


def halves(array):
    top = array.astype(jnp.bfloat16)
    return top, (array - top.astype(jnp.float32)).astype(jnp.bfloat16)


def product(left, right, transposed=False):
    dims = (((1,), (1 if transposed else 0,)), ((), ()))
    dot = functools.partial(lax.dot_general, dimension_numbers=dims, preferred_element_type=jnp.float32)
    left_top, left_rest = left if isinstance(left, tuple) else halves(left)
    right_top, right_rest = halves(right)
    rows = left_top.shape[0]
    both = dot(jnp.concatenate([left_top, left_rest], axis=0), right_top)
    return both[:rows] + (both[rows:] + dot(left_top, right_rest))


def scale_of(squares, features):
    return lax.rsqrt(squares / features + epsilon)


def tiles_of(columns, most):
    tile = tile_of(columns, most)
    return [pl.ds(start, tile) for start in range(0, columns, tile)]


def place_of(columns, width):
    core = lax.rem(lax.axis_index("comp"), 2)
    return core, pl.multiple_of(core * (columns - width), lanes)


def project_kernel(x_hbm, s_hbm, out_ref, s_ref, x_ref, sems):
    rows, columns = s_ref.shape
    copies = []
    for i, here in enumerate(tiles_of(columns, 4)):
        copies.append(
            (
                pltpu.make_async_copy(x_hbm.at[:, here], x_ref.at[:, here], sems.at[0, i]),
                pltpu.make_async_copy(s_hbm.at[:, here], s_ref.at[:, here], sems.at[1, i]),
            )
        )
        for copy in copies[-1]:
            copy.start()
    projected, squares = 0.0, 0.0
    for i, here in enumerate(tiles_of(columns, 4)):
        for copy in copies[i]:
            copy.wait()
        x = x_ref[:, here]
        projected += product(x, s_ref[:, here], transposed=True)
        squares += jnp.sum(x * x, axis=1, keepdims=True)
    out_ref[:, :rows] = projected
    out_ref[:, rows:] = jnp.broadcast_to(squares, (out_ref.shape[0], out_ref.shape[1] - rows))


def project(x, sample):
    per_group, columns = x.shape
    rows = sample.shape[0]
    width = -(-(rows + 1) // lanes) * lanes
    return pl.pallas_call(
        project_kernel,
        in_specs=[anywhere] * 2,
        out_specs=[in_vmem] * 2,
        out_shape=[
            jax.ShapeDtypeStruct((per_group, width), jnp.float32),
            jax.ShapeDtypeStruct(sample.shape, jnp.float32),
        ],
        scratch_shapes=[
            pltpu.VMEM(x.shape, jnp.float32),
            pltpu.SemaphoreType.DMA((2, columns // tile_of(columns, 4))),
        ],
        compiler_params=params,
        name="project",
    )(x, sample)


def images_of(p_ref, rows, features):
    scale = scale_of(p_ref[:, rows : rows + 1], features)
    return p_ref[:, :rows] * scale, scale


def chip_kernel(features, cores, p_ref, q_ref, s_ref, x_ref, y_ref, out_ref):
    rows, columns = s_ref.shape
    per_group, width = x_ref.shape
    core, start = place_of(columns, width)
    images, scales = zip(*(images_of(ref, rows, features) for ref in (p_ref, q_ref)))
    images, scale = jnp.concatenate(images, axis=0), jnp.concatenate(scales, axis=0)
    shared = product(images, images * scale, transposed=True)

    def component(axis):
        index = lax.broadcasted_iota(jnp.int32, shared.shape, axis)
        own = index < per_group
        return jnp.where(own, index + core * per_group, index - core * per_group)

    earlier = component(1) < component(0)
    coupling = jnp.where(earlier, shared * (-step_rate / (features * rows)), 0.0)
    weights = halves(jnp.concatenate([images * (step_rate / rows), coupling], axis=1))
    for here in tiles_of(width, 4):
        there = pl.ds(pl.multiple_of(start + here.start, lanes), here.size)
        vectors = jnp.concatenate([x_ref[:, here], y_ref[:, here]], axis=0)
        out_ref[:, here] = scale * vectors + product(weights, jnp.concatenate([s_ref[:, there], vectors], axis=0))


def chip_part(projected, beside, sample, mine, near, features):
    return pl.pallas_call(
        functools.partial(chip_kernel, features, 2),
        in_specs=[in_vmem] * 5,
        out_specs=in_vmem,
        out_shape=jax.ShapeDtypeStruct((2 * mine.shape[0], mine.shape[1]), jnp.float32),
        compiler_params=params,
        name="chip_part",
    )(projected, beside, sample, mine, near)


def diagonal(count):
    down = lax.broadcasted_iota(jnp.int32, (count, count), 0)
    across = lax.broadcasted_iota(jnp.int32, (count, count), 1)
    return down == across


def as_row(column):
    count = column.shape[0]
    return jnp.sum(jnp.where(diagonal(count), jnp.broadcast_to(column, (count, count)), 0.0), axis=0, keepdims=True)


def rest_kernel(features, rows, columns, steps, t_ref, p_ref, q_ref, *refs):
    count = 2 * len(steps)
    projected_refs, x_refs, (own_ref, other_ref, squares_ref) = refs[:count], refs[count : 2 * count], refs[2 * count :]
    width = t_ref.shape[1]
    per_group = t_ref.shape[0] // 2
    core = place_of(columns, width)[0]
    chip = lax.axis_index("comp") // 2
    if steps:
        images = jnp.concatenate([images_of(ref, rows, features)[0] for ref in (p_ref, q_ref)], axis=0)
        others = []
        for k, ref in enumerate(projected_refs):
            other, scale = images_of(ref, rows, features)
            factor = jnp.where(chip ^ (steps[k // 2] // 2) < chip, -step_rate / (features * rows), 0.0)
            others.append(other * (scale * factor))
        weights = halves(product(images, jnp.concatenate(others, axis=0), transposed=True))
    overlap = 2 * width - columns
    squares = 0.0
    for here in tiles_of(width, 4):
        updated = t_ref[:, here]
        if steps:
            updated += product(weights, jnp.concatenate([ref[:, here] for ref in x_refs], axis=0))
        own_ref[:, here], other_ref[:, here] = updated[:per_group], updated[per_group:]
        if here.start < overlap:
            column = here.start + lax.broadcasted_iota(jnp.int32, updated.shape, 1)
            updated = jnp.where((core == 0) | (column >= overlap), updated, 0.0)
        squares += jnp.sum(updated * updated, axis=1, keepdims=True)
    own, other = as_row(squares[:per_group]), as_row(squares[per_group:])
    squares_ref[0:1, :] = jnp.where(core == 0, own, other)
    squares_ref[1:2, :] = jnp.where(core == 0, other, own)


def rest_part(partly, projected, beside, steps, others, blocks, rows, columns, features):
    per_group, width = partly.shape[0] // 2, partly.shape[1]
    return pl.pallas_call(
        functools.partial(rest_kernel, features, rows, columns, steps),
        in_specs=[in_vmem] * (3 + len(others) + len(blocks)),
        out_specs=[in_vmem] * 3,
        out_shape=[
            jax.ShapeDtypeStruct((per_group, width), jnp.float32),
            jax.ShapeDtypeStruct((per_group, width), jnp.float32),
            jax.ShapeDtypeStruct((2, per_group), jnp.float32),
        ],
        compiler_params=params,
        name="rest_part",
    )(partly, projected, beside, *others, *blocks)


def finish_kernel(features, count, own_ref, other_ref, *refs):
    squares_refs, (out_ref, scaled, sems) = refs[:count], refs[count:]
    per_group, columns = out_ref.shape
    width = own_ref.shape[1]
    core, start = place_of(columns, width)
    squares = squares_refs[0][...]
    for ref in squares_refs[1:]:
        squares += ref[...]
    row = jnp.where(core == 0, squares[0:1], squares[1:2])
    spread = jnp.broadcast_to(scale_of(row, features), (per_group, per_group))
    scale = jnp.sum(jnp.where(diagonal(per_group), spread, 0.0), axis=1, keepdims=True)
    copies = []
    apart = 2 * width == columns
    for ref, first in ((other_ref, columns - width - start), (own_ref, start)):
        for here in tiles_of(width, 7):
            there = pl.ds(pl.multiple_of(first + here.start, lanes), here.size)
            scaled[:, there] = ref[:, here] * scale
            if apart:
                copies.append(pltpu.make_async_copy(scaled.at[:, there], out_ref.at[:, there], sems.at[len(copies)]))
                copies[-1].start()
    if not apart:
        copies.append(pltpu.make_async_copy(scaled, out_ref, sems.at[0]))
        copies[-1].start()
    for copy in copies:
        copy.wait()


def finish(own, other, squares, columns, features):
    per_group, width = own.shape
    return pl.pallas_call(
        functools.partial(finish_kernel, features, len(squares)),
        in_specs=[in_vmem] * (2 + len(squares)),
        out_specs=anywhere,
        out_shape=jax.ShapeDtypeStruct((per_group, columns), jnp.float32),
        scratch_shapes=[
            pltpu.VMEM((per_group, columns), jnp.float32),
            pltpu.SemaphoreType.DMA((2 * len(tiles_of(width, 7)),)),
        ],
        compiler_params=params,
        name="finish",
    )(own, other, *squares)


def exchange(array, axis, step):
    return lax.ppermute(array, axis, [(i, i ^ step) for i in range(lax.axis_size(axis))])


def terms(array, together, flip):
    comp, feat = lax.axis_size("comp"), lax.axis_size("feat")
    parts, step = [array], 1
    while step < feat:
        array = sum(parts[1:], parts[0])
        width = min(1 << together, feat // step)
        parts = [array]
        for k in range(1, width):
            pairs = [(i * feat + j, (i ^ flip) * feat + (j ^ (k * step))) for i in range(comp) for j in range(feat)]
            parts.append(lax.ppermute(array, ("comp", "feat"), pairs))
        step *= width
    return parts


def by_columns(samples, start_vectors):
    comp, feat = lax.axis_size("comp"), lax.axis_size("feat")
    sample = samples[0]
    rows, columns = sample.shape
    features = columns * feat
    width = -(-columns // (2 * lanes)) * lanes
    core = lax.axis_index("comp") % 2
    steps = list(range(2, comp, 2))

    mine = lax.dynamic_slice_in_dim(start_vectors, core * (columns - width), width, 1)
    theirs = lax.dynamic_slice_in_dim(start_vectors, (1 - core) * (columns - width), width, 1)
    near = exchange(theirs, "comp", 1)
    far = {step: [exchange(mine, "comp", step)] for step in steps}
    projected, sample = project(
        *(pltpu.with_memory_space_constraint(array, pltpu.HBM) for array in (start_vectors, sample))
    )
    near, projected = lax.optimization_barrier((near, projected))
    for step in steps:
        far[step].append(exchange(near, "comp", step))
    parts = terms(projected, 1, 0)
    projected = sum(parts[1:], parts[0])
    beside = exchange(projected, "comp", 1)
    others = []
    for step in steps:
        cross = exchange(projected, "comp", step + 1)
        others += [exchange(cross, "comp", 1), cross]
    partly = chip_part(projected, beside, sample, mine, near, features)
    blocks = [array for step in steps for array in far[step]]
    own, other, squares = rest_part(partly, projected, beside, steps, others, blocks, rows, columns, features)
    other = exchange(other, "comp", 1)
    squares = terms(squares + exchange(squares, "comp", 1), 2, 1)
    return finish(own, other, squares, columns, features)


def plainly(samples, start_vectors):
    per_group = start_vectors.shape[0]
    sample = samples[0]
    rows = sample.shape[0]
    features = sample.shape[1] * lax.axis_size("feat")
    root_width = math.sqrt(features)
    total = per_group * lax.axis_size("comp")
    own_columns = lax.axis_index("comp") * per_group + jnp.arange(per_group, dtype=jnp.int32)
    earlier = jnp.arange(total, dtype=jnp.int32)[:, None] < own_columns[None, :]
    einsum = functools.partial(jnp.einsum, precision=lax.Precision.HIGHEST)

    def normalize(updated):
        summed = lax.psum(jnp.sum(updated * updated, axis=1), "feat")
        return updated * scale_of(summed, features)[:, None]

    vectors = normalize(start_vectors)
    images = lax.psum(einsum("rd,kd->rk", sample, vectors) / root_width, "feat")
    every = lax.all_gather(images, "comp", axis=1, tiled=True)
    coupling = jnp.where(earlier, einsum("rj,ri->ji", every, images) / rows, 0.0)
    penalty = einsum("ji,jd->id", coupling, lax.all_gather(vectors, "comp", axis=0, tiled=True))
    gradient = root_width * einsum("rk,rd->kd", images, sample) / rows - penalty
    return normalize(vectors + step_rate * gradient)


def shards(samples, start_vectors):
    sizes = lax.axis_size("comp"), lax.axis_size("feat")
    in_pairs = sizes[0] > 1 and all(size & (size - 1) == 0 for size in sizes)
    whole_tiles = start_vectors.shape[1] % lanes == 0 and start_vectors.shape[0] % 16 == 0 and samples.shape[1] % 16 == 0
    return (by_columns if in_pairs and whole_tiles else plainly)(samples, start_vectors)


def solution(mesh):
    in_specs = (P(None, None, "feat"), P("comp", "feat"))
    out_specs = P("comp", "feat")
    return jax.shard_map(shards, mesh=mesh, in_specs=in_specs, out_specs=out_specs, check_vma=False)
```

time: 113 us -> 43 us (0.38)
  blocking collectives: 81.4 us -> 0 us
  starting transfers between devices: 0.01 us -> 19.1 us
  waiting for transfers between devices: 0.04 us -> 16.1 us
  between operations: 13.4 us -> 0.08 us
  matrix products: 11.7 us -> 0 us
  Pallas kernels: 0 us -> 6.29 us
  other arithmetic: 5.98 us -> 0.04 us
  local copies, waits for them, and re-layouts: 0.01 us -> 1.22 us
    psum x3 -> x0, blocking collectives: 75.6 us -> none  [the longest x2 42.3 us: normalize(): summed = lax.psum(jnp.sum(updated * updated, axis=1), 'feat')]
    ppermute x0 -> x15, starting transfers between devices: none -> 19.1 us  [the longest x7 13.2 us: terms(): parts.append(lax.ppermute(array, ('comp', 'feat'), pairs))]
    ppermute x0 -> x15, waiting for transfers between devices: none -> 16.1 us  [the longest x7 11.8 us: terms(): parts.append(lax.ppermute(array, ('comp', 'feat'), pairs))]
    dot_general x4 -> x0, matrix products: 11.7 us -> none  [the longest x1 4.44 us: add_parent(): return jnp.einsum('ji,jd->id', coupling, pieces, precision=highest)]
    pallas_call x0 -> x4, Pallas kernels: none -> 6.29 us  [the longest x1 2.95 us: project(): pl.pallas_call(project_kernel, in_specs=[anywhere] * 2, out_specs=[in_vme...]
    all_gather x1 -> x0, blocking collectives: 5.79 us -> none  [shards(): every_images = lax.all_gather(own_images, 'comp', axis=1, tiled=True)]
    mul x2 -> x0, other arithmetic: 4.47 us -> none  [normalize(): return updated * lax.rsqrt(summed / features + epsilon)[:, None]]
    reduce_sum x1 -> x0, other arithmetic: 1.49 us -> none  [normalize(): summed = lax.psum(jnp.sum(updated * updated, axis=1), 'feat')]
  transfers between devices with their start and end apart: 1 -> 15, of which waited for: 0 -> 8; matrix products, arithmetic and copies ran while one was open for 4% -> 0% of each run, Pallas kernels for 0% -> 10%
where the time goes in v13:
time: 43 us; the launch traced here: 42.8 us
  starting transfers between devices  19.1 us (44%)
  waiting for transfers between devices  16.1 us (37%)
  Pallas kernels  6.29 us (15%)
  local copies, waits for them, and re-layouts  1.22 us (3%)
    ppermute x7, starting transfers between devices, terms(): parts.append(lax.ppermute(array, ('comp', 'feat'), pairs))  13.2 us
    ppermute x7, waiting for transfers between devices, terms(): parts.append(lax.ppermute(array, ('comp', 'feat'), pairs))  11.8 us
    ppermute x8, starting transfers between devices, exchange(): lax.ppermute(array, axis, [(i, i ^ step) for i in range(lax.axis_size(axi...  5.85 us
    ppermute x8, waiting for transfers between devices, exchange(): lax.ppermute(array, axis, [(i, i ^ step) for i in range(lax.axis_size(axi...  4.32 us
    pallas_call x1, Pallas kernels, project(): pl.pallas_call(project_kernel, in_specs=[anywhere] * 2, out_specs=[in_vme...  2.95 us
    pallas_call x1, Pallas kernels, chip_part(): pl.pallas_call(functools.partial(chip_kernel, features, 2), in_specs=[in_...  1.31 us
    dynamic_slice x1, local copies, waits for them, and re-layouts, by_columns(): lax.dynamic_slice_in_dim(start_vectors, core * (columns - width), width, 1)  1.22 us
    pallas_call x1, Pallas kernels, finish(): pl.pallas_call(functools.partial(finish_kernel, features, len(squares)),...  1.07 us
  transfers between devices with their start and end apart: 15, of which 8 were waited for; matrix products, arithmetic and copies ran while one was open for 0% of the time, Pallas kernels for 10%

profile of v13, /device:TPU:0, one launch (start us, length us, event | category | flops | bytes accessed | tf_op | source)
XLA Modules:
  0.0 42.8 jit_solution(2768041822973074314)
XLA Ops:
  0.0 1.2 %constant_dynamic-slice_fusion = (f32[64,1792]{1,0:T(8,128)S(1)}, f32[64,1792]{1,0:T(8,128)S(1)}) fusion(f32[64,3584]{1,0:T(8,128)} %x_hbm.1, s32[]{:T(128)S(6)} %select_n.15, s32[]{:T(128)S(6)} %select_n.14), kind=kLoop, calls=%fused_computation.1 | loop fusion | bytes 1835016 | tf_op jit(solution)/shard_map/dynamic_slice | solution.py:265
  1.2 0.5 %collective-permute-start = (f32[64,1792]{1,0:T(8,128)S(1)}, f32[64,1792]{1,0:T(8,128)S(1)}, u32[]{:S(2)}, u32[]{:S(2)}) collective-permute-start(f32[64,1792]{1,0:T(8,128)S(1)} %get-tuple-element.20), channel_id=1, source_target_pairs={{0,8},{8,0},{16,24},{24,16},{1,9},{9,1},{17,25},{25,17},{2,10},{10... | collective-permute-start | bytes 1376264 | tf_op jit(solution)/shard_map/ppermute | solution.py:239
  1.7 2.6 %collective-permute-start.7 = (f32[64,1792]{1,0:T(8,128)S(1)}, f32[64,1792]{1,0:T(8,128)S(1)}, u32[]{:S(2)}, u32[]{:S(2)}) collective-permute-start(f32[64,1792]{1,0:T(8,128)S(1)} %get-tuple-element.19.x_ref), channel_id=1, source_target_pairs={{0,16},{8,24},{16,0},{24,8},{1,17},{9,25},{17,1},{25,9},{2,18},{10... | collective-permute-start | bytes 1376264 | tf_op jit(solution)/shard_map/ppermute | solution.py:239
  4.3 3.0 %project.1 = (f32[64,256]{1,0:T(8,128)S(1)}, f32[192,3584]{1,0:T(8,128)S(1)}) custom-call(f32[64,3584]{1,0:T(8,128)} %x_hbm.1, f32[192,3584]{1,0:T(8,128)} %bitcast.1), custom_call_target="tpu_custom_call" | custom-call | tf_op jit(solution)/shard_map/project/pallas_call | solution.py:82
  7.3 0.0 collective-permute-done.y_ref
  7.3 0.1 collective-permute-start.8
  7.4 2.0 %collective-permute-start.1 = (f32[64,256]{1,0:T(8,128)S(1)}, f32[64,256]{1,0:T(8,128)S(1)}, u32[]{:S(2)}, u32[]{:S(2)}) collective-permute-start(f32[64,256]{1,0:T(8,128)S(1)} %get-tuple-element.13), channel_id=1, source_target_pairs={{0,1},{1,0},{2,3},{3,2},{4,5},{5,4},{6,7},{7,6},{8,9},{9,8},{10,11... | collective-permute-start | bytes 196616 | tf_op jit(solution)/shard_map/ppermute | solution.py:251
  9.4 2.3 %collective-permute-done.1 = f32[64,256]{1,0:T(8,128)S(1)} collective-permute-done((f32[64,256]{1,0:T(8,128)S(1)}, f32[64,256]{1,0:T(8,128)S(1)}, u32[]{:S(2)}, u32[]{:S(2)}) %collective-permute-start.1) | collective-permute-done | bytes 65568 | tf_op jit(solution)/shard_map/ppermute | solution.py:251
  11.7 2.1 %collective-permute-start.2 = (f32[64,256]{1,0:T(8,128)S(1)}, f32[64,256]{1,0:T(8,128)S(1)}, u32[]{:S(2)}, u32[]{:S(2)}) collective-permute-start(f32[64,256]{1,0:T(8,128)S(1)} %add.33), channel_id=1, source_target_pairs={{0,2},{1,3},{2,0},{3,1},{4,6},{5,7},{6,4},{7,5},{8,10},{9,11},{10,... | collective-permute-start | bytes 196616 | tf_op jit(solution)/shard_map/ppermute | solution.py:251
  13.8 2.2 %collective-permute-done.2 = f32[64,256]{1,0:T(8,128)S(1)} collective-permute-done((f32[64,256]{1,0:T(8,128)S(1)}, f32[64,256]{1,0:T(8,128)S(1)}, u32[]{:S(2)}, u32[]{:S(2)}) %collective-permute-start.2) | collective-permute-done | bytes 65568 | tf_op jit(solution)/shard_map/ppermute | solution.py:251
  16.1 3.1 %collective-permute-start.3 = (f32[64,256]{1,0:T(8,128)S(1)}, f32[64,256]{1,0:T(8,128)S(1)}, u32[]{:S(2)}, u32[]{:S(2)}) collective-permute-start(f32[64,256]{1,0:T(8,128)S(1)} %add.34), channel_id=1, source_target_pairs={{0,4},{1,5},{2,6},{3,7},{4,0},{5,1},{6,2},{7,3},{8,12},{9,13},{10,... | collective-permute-start | bytes 196616 | tf_op jit(solution)/shard_map/ppermute | solution.py:251
  19.1 2.2 %collective-permute-done.3 = f32[64,256]{1,0:T(8,128)S(1)} collective-permute-done((f32[64,256]{1,0:T(8,128)S(1)}, f32[64,256]{1,0:T(8,128)S(1)}, u32[]{:S(2)}, u32[]{:S(2)}) %collective-permute-start.3) | collective-permute-done | bytes 65568 | tf_op jit(solution)/shard_map/ppermute | solution.py:251
  21.4 0.1 collective-permute-start.5
  21.5 1.9 %collective-permute-start.4 = (f32[64,256]{1,0:T(8,128)S(1)}, f32[64,256]{1,0:T(8,128)S(1)}, u32[]{:S(2)}, u32[]{:S(2)}) collective-permute-start(f32[64,256]{1,0:T(8,128)S(1)} %add.35.p_ref), channel_id=1, source_target_pairs={{0,8},{8,0},{16,24},{24,16},{1,9},{9,1},{17,25},{25,17},{2,10},{10... | collective-permute-start | bytes 196616 | tf_op jit(solution)/shard_map/ppermute | solution.py:239
  23.4 3.0 %collective-permute-done.5.refs_1_ = f32[64,256]{1,0:T(8,128)S(1)} collective-permute-done((f32[64,256]{1,0:T(8,128)S(1)}, f32[64,256]{1,0:T(8,128)S(1)}, u32[]{:S(2)}, u32[]{:S(2)}) %collective-permute-start.5) | collective-permute-done | bytes 65568 | tf_op jit(solution)/shard_map/ppermute | solution.py:239
  26.4 0.1 collective-permute-start.6
  26.5 0.0 collective-permute-done.4.q_ref
  26.5 1.3 %chip_part.1.t_ref = f32[128,1792]{1,0:T(8,128)S(1)} custom-call(f32[64,256]{1,0:T(8,128)S(1)} %add.35.p_ref, f32[64,256]{1,0:T(8,128)S(1)} %collective-permute-done.4.q_ref, f32[192,3584]{1,0:T(8,128)S(1)} %get-tuple-element.14.s_ref, f32[64,1792]{1,0:T(8,128)S(1)} %get-tuple-element.19.x_ref, f32[64,1792]{1,0:T(8,128)S(1)} %collective-permute-done.y_ref), custom_call_target="tpu_custom_call" | custom-call | tf_op jit(solution)/shard_map/chip_part/pallas_call | solution.py:127
  27.8 0.0 collective-permute-done.7.refs_2_
  27.8 0.0 collective-permute-done.6.refs_0_
  27.8 0.0 collective-permute-done.8.refs_3_
  27.9 1.0 %rest_part.1 = (f32[64,1792]{1,0:T(8,128)S(1)}, f32[64,1792]{1,0:T(8,128)S(1)}, f32[2,64]{1,0:T(2,128)S(1)}) custom-call(f32[128,1792]{1,0:T(8,128)S(1)} %chip_part.1.t_ref, f32[64,256]{1,0:T(8,128)S(1)} %add.35.p_ref, f32[64,256]{1,0:T(8,128)S(1)} %collective-permute-done.4.q_ref, f32[64,256]{1,0:T(8,128)S(1)} %collective-permute-done.6.refs_0_, ...), custom_call_target="tpu_custom_call" | custom-call | tf_op jit(solution)/shard_map/rest_part/pallas_call | solution.py:181
  28.8 0.5 %collective-permute-start.9 = (f32[64,1792]{1,0:T(8,128)S(1)}, f32[64,1792]{1,0:T(8,128)S(1)}, u32[]{:S(2)}, u32[]{:S(2)}) collective-permute-start(f32[64,1792]{1,0:T(8,128)S(1)} %get-tuple-element.17), channel_id=1, source_target_pairs={{0,8},{8,0},{16,24},{24,16},{1,9},{9,1},{17,25},{25,17},{2,10},{10... | collective-permute-start | bytes 1376264 | tf_op jit(solution)/shard_map/ppermute | solution.py:239
  29.3 0.1 collective-permute-start.10
  29.4 1.3 %collective-permute-done.10 = f32[2,64]{1,0:T(2,128)S(1)} collective-permute-done((f32[2,64]{1,0:T(2,128)S(1)}, f32[2,64]{1,0:T(2,128)S(1)}, u32[]{:S(2)}, u32[]{:S(2)}) %collective-permute-start.10) | collective-permute-done | bytes 544 | tf_op jit(solution)/shard_map/ppermute | solution.py:239
  30.7 1.6 %collective-permute-start.11 = (f32[2,64]{1,0:T(2,128)S(1)}, f32[2,64]{1,0:T(2,128)S(1)}, u32[]{:S(2)}, u32[]{:S(2)}) collective-permute-start(f32[2,64]{1,0:T(2,128)S(1)} %add.37), channel_id=1, source_target_pairs={{0,9},{1,8},{2,11},{3,10},{4,13},{5,12},{6,15},{7,14},{8,1},{9,0},... | collective-permute-start | bytes 1544 | tf_op jit(solution)/shard_map/ppermute | solution.py:251
  32.3 1.5 %collective-permute-start.12 = (f32[2,64]{1,0:T(2,128)S(1)}, f32[2,64]{1,0:T(2,128)S(1)}, u32[]{:S(2)}, u32[]{:S(2)}) collective-permute-start(f32[2,64]{1,0:T(2,128)S(1)} %add.37), channel_id=1, source_target_pairs={{0,10},{1,11},{2,8},{3,9},{4,14},{5,15},{6,12},{7,13},{8,2},{9,3},... | collective-permute-start | bytes 1544 | tf_op jit(solution)/shard_map/ppermute | solution.py:251
  33.8 0.2 collective-permute-start.13
  33.9 0.0 collective-permute-done.11
  33.9 1.4 %collective-permute-done.12 = f32[2,64]{1,0:T(2,128)S(1)} collective-permute-done((f32[2,64]{1,0:T(2,128)S(1)}, f32[2,64]{1,0:T(2,128)S(1)}, u32[]{:S(2)}, u32[]{:S(2)}) %collective-permute-start.12) | collective-permute-done | bytes 544 | tf_op jit(solution)/shard_map/ppermute | solution.py:251
  35.3 2.4 %collective-permute-done.13 = f32[2,64]{1,0:T(2,128)S(1)} collective-permute-done((f32[2,64]{1,0:T(2,128)S(1)}, f32[2,64]{1,0:T(2,128)S(1)}, u32[]{:S(2)}, u32[]{:S(2)}) %collective-permute-start.13) | collective-permute-done | bytes 544 | tf_op jit(solution)/shard_map/ppermute | solution.py:251
  37.7 2.8 %collective-permute-start.14 = (f32[2,64]{1,0:T(2,128)S(1)}, f32[2,64]{1,0:T(2,128)S(1)}, u32[]{:S(2)}, u32[]{:S(2)}) collective-permute-start(f32[2,64]{1,0:T(2,128)S(1)} %add_add_fusion.refs_0_), channel_id=1, source_target_pairs={{0,12},{1,13},{2,14},{3,15},{4,8},{5,9},{6,10},{7,11},{8,4},{9,5},... | collective-permute-start | bytes 1544 | tf_op jit(solution)/shard_map/ppermute | solution.py:251
  40.5 1.3 %collective-permute-done.14.refs_1_ = f32[2,64]{1,0:T(2,128)S(1)} collective-permute-done((f32[2,64]{1,0:T(2,128)S(1)}, f32[2,64]{1,0:T(2,128)S(1)}, u32[]{:S(2)}, u32[]{:S(2)}) %collective-permute-start.14) | collective-permute-done | bytes 544 | tf_op jit(solution)/shard_map/ppermute | solution.py:251
  41.8 0.0 collective-permute-done.9.other_ref
  41.8 1.1 %finish.1 = f32[64,3584]{1,0:T(8,128)} custom-call(f32[64,1792]{1,0:T(8,128)S(1)} %get-tuple-element.16.own_ref, f32[64,1792]{1,0:T(8,128)S(1)} %collective-permute-done.9.other_ref, f32[2,64]{1,0:T(2,128)S(1)} %add_add_fusion.refs_0_, f32[2,64]{1,0:T(2,128)S(1)} %collective-permute-done.14.refs_1_), custom_call_target="tpu_custom_call" | custom-call | tf_op jit(solution)/shard_map/finish/pallas_call | solution.py:224
  (5 shorter events, 0.0 us)
Async XLA Ops:
  1.2 6.0 %collective-permute-start = (f32[64,1792]{1,0:T(8,128)S(1)}, f32[64,1792]{1,0:T(8,128)S(1)}, u32[]{:S(2)}, u32[]{:S(2)}) collective-permute-start(f32[64,1792]{1,0:T(8,128)S(1)} %get-tuple-element.20), channel_id=1, source_target_pairs={{0,8},{8,0},{16,24},{24,16},{1,9},{9,1},{17,25},{25,17},{2,10},{10... | collective-permute-start | bytes 1376264 | tf_op jit(solution)/shard_map/ppermute | solution.py:239
  1.7 26.1 %collective-permute-start.7 = (f32[64,1792]{1,0:T(8,128)S(1)}, f32[64,1792]{1,0:T(8,128)S(1)}, u32[]{:S(2)}, u32[]{:S(2)}) collective-permute-start(f32[64,1792]{1,0:T(8,128)S(1)} %get-tuple-element.19.x_ref), channel_id=1, source_target_pairs={{0,16},{8,24},{16,0},{24,8},{1,17},{9,25},{17,1},{25,9},{2,18},{10... | collective-permute-start | bytes 1376264 | tf_op jit(solution)/shard_map/ppermute | solution.py:239
  7.3 20.6 %collective-permute-start.8 = (f32[64,1792]{1,0:T(8,128)S(1)}, f32[64,1792]{1,0:T(8,128)S(1)}, u32[]{:S(2)}, u32[]{:S(2)}) collective-permute-start(f32[64,1792]{1,0:T(8,128)S(1)} %collective-permute-done.y_ref), channel_id=1, source_target_pairs={{0,16},{8,24},{16,0},{24,8},{1,17},{9,25},{17,1},{25,9},{2,18},{10... | collective-permute-start | bytes 1376264 | tf_op jit(solution)/shard_map/ppermute | solution.py:239
  7.4 4.3 %collective-permute-start.1 = (f32[64,256]{1,0:T(8,128)S(1)}, f32[64,256]{1,0:T(8,128)S(1)}, u32[]{:S(2)}, u32[]{:S(2)}) collective-permute-start(f32[64,256]{1,0:T(8,128)S(1)} %get-tuple-element.13), channel_id=1, source_target_pairs={{0,1},{1,0},{2,3},{3,2},{4,5},{5,4},{6,7},{7,6},{8,9},{9,8},{10,11... | collective-permute-start | bytes 196616 | tf_op jit(solution)/shard_map/ppermute | solution.py:251
  11.7 4.3 %collective-permute-start.2 = (f32[64,256]{1,0:T(8,128)S(1)}, f32[64,256]{1,0:T(8,128)S(1)}, u32[]{:S(2)}, u32[]{:S(2)}) collective-permute-start(f32[64,256]{1,0:T(8,128)S(1)} %add.33), channel_id=1, source_target_pairs={{0,2},{1,3},{2,0},{3,1},{4,6},{5,7},{6,4},{7,5},{8,10},{9,11},{10,... | collective-permute-start | bytes 196616 | tf_op jit(solution)/shard_map/ppermute | solution.py:251
  16.1 5.3 %collective-permute-start.3 = (f32[64,256]{1,0:T(8,128)S(1)}, f32[64,256]{1,0:T(8,128)S(1)}, u32[]{:S(2)}, u32[]{:S(2)}) collective-permute-start(f32[64,256]{1,0:T(8,128)S(1)} %add.34), channel_id=1, source_target_pairs={{0,4},{1,5},{2,6},{3,7},{4,0},{5,1},{6,2},{7,3},{8,12},{9,13},{10,... | collective-permute-start | bytes 196616 | tf_op jit(solution)/shard_map/ppermute | solution.py:251
  21.4 5.0 %collective-permute-start.5 = (f32[64,256]{1,0:T(8,128)S(1)}, f32[64,256]{1,0:T(8,128)S(1)}, u32[]{:S(2)}, u32[]{:S(2)}) collective-permute-start(f32[64,256]{1,0:T(8,128)S(1)} %add.35.p_ref), channel_id=1, source_target_pairs={{0,24},{8,16},{16,8},{24,0},{1,25},{9,17},{17,9},{25,1},{2,26},{10... | collective-permute-start | bytes 196616 | tf_op jit(solution)/shard_map/ppermute | solution.py:239
  21.5 5.0 %collective-permute-start.4 = (f32[64,256]{1,0:T(8,128)S(1)}, f32[64,256]{1,0:T(8,128)S(1)}, u32[]{:S(2)}, u32[]{:S(2)}) collective-permute-start(f32[64,256]{1,0:T(8,128)S(1)} %add.35.p_ref), channel_id=1, source_target_pairs={{0,8},{8,0},{16,24},{24,16},{1,9},{9,1},{17,25},{25,17},{2,10},{10... | collective-permute-start | bytes 196616 | tf_op jit(solution)/shard_map/ppermute | solution.py:239
  26.4 1.4 %collective-permute-start.6 = (f32[64,256]{1,0:T(8,128)S(1)}, f32[64,256]{1,0:T(8,128)S(1)}, u32[]{:S(2)}, u32[]{:S(2)}) collective-permute-start(f32[64,256]{1,0:T(8,128)S(1)} %collective-permute-done.5.refs_1_), channel_id=1, source_target_pairs={{0,8},{8,0},{16,24},{24,16},{1,9},{9,1},{17,25},{25,17},{2,10},{10... | collective-permute-start | bytes 196616 | tf_op jit(solution)/shard_map/ppermute | solution.py:239
  28.8 12.9 %collective-permute-start.9 = (f32[64,1792]{1,0:T(8,128)S(1)}, f32[64,1792]{1,0:T(8,128)S(1)}, u32[]{:S(2)}, u32[]{:S(2)}) collective-permute-start(f32[64,1792]{1,0:T(8,128)S(1)} %get-tuple-element.17), channel_id=1, source_target_pairs={{0,8},{8,0},{16,24},{24,16},{1,9},{9,1},{17,25},{25,17},{2,10},{10... | collective-permute-start | bytes 1376264 | tf_op jit(solution)/shard_map/ppermute | solution.py:239
  29.3 1.4 %collective-permute-start.10 = (f32[2,64]{1,0:T(2,128)S(1)}, f32[2,64]{1,0:T(2,128)S(1)}, u32[]{:S(2)}, u32[]{:S(2)}) collective-permute-start(f32[2,64]{1,0:T(2,128)S(1)} %get-tuple-element.18), channel_id=1, source_target_pairs={{0,8},{8,0},{16,24},{24,16},{1,9},{9,1},{17,25},{25,17},{2,10},{10... | collective-permute-start | bytes 1544 | tf_op jit(solution)/shard_map/ppermute | solution.py:239
  30.7 3.2 %collective-permute-start.11 = (f32[2,64]{1,0:T(2,128)S(1)}, f32[2,64]{1,0:T(2,128)S(1)}, u32[]{:S(2)}, u32[]{:S(2)}) collective-permute-start(f32[2,64]{1,0:T(2,128)S(1)} %add.37), channel_id=1, source_target_pairs={{0,9},{1,8},{2,11},{3,10},{4,13},{5,12},{6,15},{7,14},{8,1},{9,0},... | collective-permute-start | bytes 1544 | tf_op jit(solution)/shard_map/ppermute | solution.py:251
  32.3 3.0 %collective-permute-start.12 = (f32[2,64]{1,0:T(2,128)S(1)}, f32[2,64]{1,0:T(2,128)S(1)}, u32[]{:S(2)}, u32[]{:S(2)}) collective-permute-start(f32[2,64]{1,0:T(2,128)S(1)} %add.37), channel_id=1, source_target_pairs={{0,10},{1,11},{2,8},{3,9},{4,14},{5,15},{6,12},{7,13},{8,2},{9,3},... | collective-permute-start | bytes 1544 | tf_op jit(solution)/shard_map/ppermute | solution.py:251
  33.8 3.9 %collective-permute-start.13 = (f32[2,64]{1,0:T(2,128)S(1)}, f32[2,64]{1,0:T(2,128)S(1)}, u32[]{:S(2)}, u32[]{:S(2)}) collective-permute-start(f32[2,64]{1,0:T(2,128)S(1)} %add.37), channel_id=1, source_target_pairs={{0,11},{1,10},{2,9},{3,8},{4,15},{5,14},{6,13},{7,12},{8,3},{9,2},... | collective-permute-start | bytes 1544 | tf_op jit(solution)/shard_map/ppermute | solution.py:251
  37.7 4.1 %collective-permute-start.14 = (f32[2,64]{1,0:T(2,128)S(1)}, f32[2,64]{1,0:T(2,128)S(1)}, u32[]{:S(2)}, u32[]{:S(2)}) collective-permute-start(f32[2,64]{1,0:T(2,128)S(1)} %add_add_fusion.refs_0_), channel_id=1, source_target_pairs={{0,12},{1,13},{2,14},{3,15},{4,8},{5,9},{6,10},{7,11},{8,4},{9,5},... | collective-permute-start | bytes 1544 | tf_op jit(solution)/shard_map/ppermute | solution.py:251

commit v14 on v11

--- a/solution.py
+++ b/solution.py
@@ -147,12 +147,29 @@
     )(projected, sample, x, *others, *blocks)
 
 
-def rest_kernel(features, rows, steps, t_ref, p_ref, *refs):
-    count = len(steps)
-    projected_refs, x_refs, (out_ref, squares_ref) = refs[:count], refs[count : 2 * count], refs[2 * count :]
+def couple_kernel(features, rows, steps, p_ref, *refs):
+    projected_refs, (top_ref, rest_ref) = refs[:-2], refs[-2:]
+    top_ref[...], rest_ref[...] = halves(couplings(images_of(p_ref, rows, features)[0], steps, projected_refs, features))
+
+
+def couple(projected, steps, others, rows, features):
+    per_group = projected.shape[0]
+    return pl.pallas_call(
+        functools.partial(couple_kernel, features, rows, steps),
+        in_specs=[in_vmem] * (1 + len(steps)),
+        out_specs=[in_vmem] * 2,
+        out_shape=[jax.ShapeDtypeStruct((per_group, per_group * len(steps)), jnp.bfloat16)] * 2,
+        compiler_params=params,
+        cost_estimate=pl.CostEstimate(flops=8900000000, bytes_accessed=4 * projected.size, transcendentals=0),
+        name="couple",
+    )(projected, *others)
+
+
+def rest_kernel(count, t_ref, *refs):
+    x_refs, (out_ref, squares_ref) = refs[-2 - count : -2], refs[-2:]
     per_group, columns = t_ref.shape
     if count:
-        weights = halves(couplings(images_of(p_ref, rows, features)[0], steps, projected_refs, features))
+        weights = refs[0][...], refs[1][...]
 
     def body(i, here, squares):
         updated = t_ref[:, here]
@@ -166,10 +183,10 @@
     squares_ref[...] = jnp.sum(jnp.where(diagonal(per_group), spread, 0.0), axis=0, keepdims=True)
 
 
-def rest_part(partly, projected, steps, others, blocks, rows, features):
-    return pl.pallas_call(
-        functools.partial(rest_kernel, features, rows, steps),
-        in_specs=[in_vmem] * (2 + 2 * len(steps)),
+def rest_part(partly, weights, blocks):
+    return pl.pallas_call(
+        functools.partial(rest_kernel, len(blocks)),
+        in_specs=[in_vmem] * (1 + len(weights) + len(blocks)),
         out_specs=[in_vmem, in_vmem],
         out_shape=[
             jax.ShapeDtypeStruct(partly.shape, jnp.float32),
@@ -177,7 +194,7 @@
         ],
         compiler_params=params,
         name="rest_part",
-    )(partly, projected, *others, *blocks)
+    )(partly, *weights, *blocks)
 
 
 def diagonal(count):
@@ -281,11 +298,11 @@
         *(pltpu.with_memory_space_constraint(array, pltpu.HBM) for array in (start_vectors, sample))
     )
     if even and comp > 1:
-        blocks[1] = exchange(vectors, "comp", 1)
+        blocks[1] = exchange(start_vectors, "comp", 1)
     parts = terms(projected, "feat", 1)
     projected = sum(parts[1:], parts[0])
     if even:
-        others = {step: exchange(projected, "comp", step) for step in range(1, comp, 2)}
+        others = {step: exchange(projected, "comp", step) for step in range(1, comp) if step == 1 or step % 2 == 0}
     else:
         others = gather(projected)
     near = [1][: comp - 1]
@@ -297,12 +314,11 @@
     partly = first_part(projected, sample, vectors, near, of(others, near), of(blocks, near), features)
     if even:
         for step in range(2, comp, 2):
-            blocks[step], others[step + 1], others[1] = lax.optimization_barrier(
-                (blocks[step], others[step + 1], others[1])
-            )
+            blocks[step], partly = lax.optimization_barrier((blocks[step], partly))
             blocks[step + 1] = exchange(blocks[step], "comp", 1)
-            others[step] = exchange(others[step + 1], "comp", 1)
-    updated, squares = rest_part(partly, projected, far, of(others, far), of(blocks, far), rows, features)
+            others[step + 1] = exchange(others[step], "comp", 1)
+    weights = couple(projected, far, of(others, far), rows, features) if far else []
+    updated, squares = rest_part(partly, weights, of(blocks, far))
     return finish(updated, flipped_terms(squares), features)
 
 

time: 39.4 us -> 40.4 us (1.025)
  waiting for transfers between devices: 16.7 us -> 18.2 us
  starting transfers between devices: 16.1 us -> 15.5 us
    ppermute x6, waiting for transfers between devices: 4.09 us -> 5.04 us  [flipped_terms(): parts.append(lax.ppermute(array, ('comp', 'feat'), pairs))]
    ppermute x9, starting transfers between devices: 9.91 us -> 9.23 us  [exchange(): lax.ppermute(array, axis, [(i, i ^ step) for i in range(lax.axis_size(axi...]
    ppermute x9, waiting for transfers between devices: 12.6 us -> 13.2 us  [exchange(): lax.ppermute(array, axis, [(i, i ^ step) for i in range(lax.axis_size(axi...]
    pallas_call x1 -> x2, Pallas kernels: 0.9 us -> 0.88 us  [the longest x1 0.61 us: rest_part(): pl.pallas_call(functools.partial(rest_kernel, len(blocks)), in_specs=[in_...]
  transfers between devices with their start and end apart: 15 -> 15, of which waited for: 10 -> 10; matrix products, arithmetic and copies ran while one was open for 0% -> 0% of each run, Pallas kernels for 11% -> 12%
where the time goes in v14:
time: 40.4 us; the launch traced here: 40.2 us
  waiting for transfers between devices  18.2 us (45%)
  starting transfers between devices  15.5 us (38%)
  Pallas kernels  6.37 us (16%)
    ppermute x9, waiting for transfers between devices, exchange(): lax.ppermute(array, axis, [(i, i ^ step) for i in range(lax.axis_size(axi...  13.2 us
    ppermute x9, starting transfers between devices, exchange(): lax.ppermute(array, axis, [(i, i ^ step) for i in range(lax.axis_size(axi...  9.23 us
    ppermute x6, starting transfers between devices, flipped_terms(): parts.append(lax.ppermute(array, ('comp', 'feat'), pairs))  6.26 us
    ppermute x6, waiting for transfers between devices, flipped_terms(): parts.append(lax.ppermute(array, ('comp', 'feat'), pairs))  5.04 us
    pallas_call x1, Pallas kernels, project(): pl.pallas_call(project_kernel, in_specs=[anywhere] * 2, out_specs=[in_vme...  2.94 us
    pallas_call x1, Pallas kernels, first_part(): pl.pallas_call(functools.partial(first_kernel, features, steps), in_specs...  1.47 us
    pallas_call x1, Pallas kernels, finish(): pl.pallas_call(functools.partial(finish_kernel, features, count), in_spec...  1.08 us
  transfers between devices with their start and end apart: 15, of which 10 were waited for; matrix products, arithmetic and copies ran while one was open for 0% of the time, Pallas kernels for 12%

profile of v14, /device:TPU:0, one launch (start us, length us, event | category | flops | bytes accessed | tf_op | source)
XLA Modules:
  0.0 40.2 jit_solution(17708014699685822910)
XLA Ops:
  0.0 0.5 %collective-permute-start.5 = (f32[64,3584]{1,0:T(8,128)}, f32[64,3584]{1,0:T(8,128)S(1)}, u32[]{:S(2)}, u32[]{:S(2)}) collective-permute-start(f32[64,3584]{1,0:T(8,128)} %x_hbm.1), channel_id=1, source_target_pairs={{0,8},{8,0},{16,24},{24,16},{1,9},{9,1},{17,25},{25,17},{2,10},{10... | collective-permute-start | bytes 2752520 | tf_op jit(solution)/shard_map/ppermute | solution.py:242
  0.5 2.5 %collective-permute-start = (f32[64,3584]{1,0:T(8,128)}, f32[64,3584]{1,0:T(8,128)S(1)}, u32[]{:S(2)}, u32[]{:S(2)}) collective-permute-start(f32[64,3584]{1,0:T(8,128)} %x_hbm.1), channel_id=1, source_target_pairs={{0,16},{8,24},{16,0},{24,8},{1,17},{9,25},{17,1},{25,9},{2,18},{10... | collective-permute-start | bytes 2752520 | tf_op jit(solution)/shard_map/ppermute | solution.py:242
  2.9 2.9 %project.1 = (f32[64,256]{1,0:T(8,128)S(1)}, f32[64,3584]{1,0:T(8,128)S(1)}, f32[192,3584]{1,0:T(8,128)S(1)}) custom-call(f32[64,3584]{1,0:T(8,128)} %x_hbm.1, f32[192,3584]{1,0:T(8,128)} %bitcast.1), custom_call_target="tpu_custom_call" | custom-call | tf_op jit(solution)/shard_map/project/pallas_call | solution.py:83
  5.9 1.6 %collective-permute-start.1 = (f32[64,256]{1,0:T(8,128)S(1)}, f32[64,256]{1,0:T(8,128)S(1)}, u32[]{:S(2)}, u32[]{:S(2)}) collective-permute-start(f32[64,256]{1,0:T(8,128)S(1)} %get-tuple-element.14), channel_id=1, source_target_pairs={{0,1},{1,0},{2,3},{3,2},{4,5},{5,4},{6,7},{7,6},{8,9},{9,8},{10,11... | collective-permute-start | bytes 196616 | tf_op jit(solution)/shard_map/ppermute | solution.py:242
  7.5 2.7 %collective-permute-done.1 = f32[64,256]{1,0:T(8,128)S(1)} collective-permute-done((f32[64,256]{1,0:T(8,128)S(1)}, f32[64,256]{1,0:T(8,128)S(1)}, u32[]{:S(2)}, u32[]{:S(2)}) %collective-permute-start.1) | collective-permute-done | bytes 65568 | tf_op jit(solution)/shard_map/ppermute | solution.py:242
  10.2 1.6 %collective-permute-start.2 = (f32[64,256]{1,0:T(8,128)S(1)}, f32[64,256]{1,0:T(8,128)S(1)}, u32[]{:S(2)}, u32[]{:S(2)}) collective-permute-start(f32[64,256]{1,0:T(8,128)S(1)} %add.18), channel_id=1, source_target_pairs={{0,2},{1,3},{2,0},{3,1},{4,6},{5,7},{6,4},{7,5},{8,10},{9,11},{10,... | collective-permute-start | bytes 196616 | tf_op jit(solution)/shard_map/ppermute | solution.py:242
  11.9 2.7 %collective-permute-done.2 = f32[64,256]{1,0:T(8,128)S(1)} collective-permute-done((f32[64,256]{1,0:T(8,128)S(1)}, f32[64,256]{1,0:T(8,128)S(1)}, u32[]{:S(2)}, u32[]{:S(2)}) %collective-permute-start.2) | collective-permute-done | bytes 65568 | tf_op jit(solution)/shard_map/ppermute | solution.py:242
  14.6 2.7 %collective-permute-start.3 = (f32[64,256]{1,0:T(8,128)S(1)}, f32[64,256]{1,0:T(8,128)S(1)}, u32[]{:S(2)}, u32[]{:S(2)}) collective-permute-start(f32[64,256]{1,0:T(8,128)S(1)} %add.19), channel_id=1, source_target_pairs={{0,4},{1,5},{2,6},{3,7},{4,0},{5,1},{6,2},{7,3},{8,12},{9,13},{10,... | collective-permute-start | bytes 196616 | tf_op jit(solution)/shard_map/ppermute | solution.py:242
  17.2 2.6 %collective-permute-done.3 = f32[64,256]{1,0:T(8,128)S(1)} collective-permute-done((f32[64,256]{1,0:T(8,128)S(1)}, f32[64,256]{1,0:T(8,128)S(1)}, u32[]{:S(2)}, u32[]{:S(2)}) %collective-permute-start.3) | collective-permute-done | bytes 65568 | tf_op jit(solution)/shard_map/ppermute | solution.py:242
  19.8 0.1 collective-permute-start.4
  19.9 0.3 collective-permute-start.6
  20.2 0.9 %collective-permute-done.4.refs_0_ = f32[64,256]{1,0:T(8,128)S(1)} collective-permute-done((f32[64,256]{1,0:T(8,128)S(1)}, f32[64,256]{1,0:T(8,128)S(1)}, u32[]{:S(2)}, u32[]{:S(2)}) %collective-permute-start.4) | collective-permute-done | bytes 65568 | tf_op jit(solution)/shard_map/ppermute | solution.py:242
  21.1 0.0 collective-permute-done.5.refs_1_
  21.1 1.5 %first_part.1.t_ref = f32[64,3584]{1,0:T(8,128)S(1)} custom-call(f32[64,256]{1,0:T(8,128)S(1)} %add.20.p_ref, f32[192,3584]{1,0:T(8,128)S(1)} %get-tuple-element.15.s_ref, f32[64,3584]{1,0:T(8,128)S(1)} %get-tuple-element.16.x_ref, f32[64,256]{1,0:T(8,128)S(1)} %collective-permute-done.4.refs_0_, f32[64,3584]{1,0:T(8,128)S(1)} %collective-permute-done.5.refs_1_), custom_call_target="tpu_custom_call" | custom-call | tf_op jit(solution)/shard_map/first_part/pallas_call | solution.py:140
  22.6 1.7 %collective-permute-done.refs_2_ = f32[64,3584]{1,0:T(8,128)S(1)} collective-permute-done((f32[64,3584]{1,0:T(8,128)}, f32[64,3584]{1,0:T(8,128)S(1)}, u32[]{:S(2)}, u32[]{:S(2)}) %collective-permute-start) | collective-permute-done | bytes 917536 | tf_op jit(solution)/shard_map/ppermute | solution.py:242
  24.4 0.0 collective-permute-start.8
  24.4 1.2 %collective-permute-done.6.refs_0_ = f32[64,256]{1,0:T(8,128)S(1)} collective-permute-done((f32[64,256]{1,0:T(8,128)S(1)}, f32[64,256]{1,0:T(8,128)S(1)}, u32[]{:S(2)}, u32[]{:S(2)}) %collective-permute-start.6) | collective-permute-done | bytes 65568 | tf_op jit(solution)/shard_map/ppermute | solution.py:242
  25.6 0.0 collective-permute-start.7
  25.6 1.3 %collective-permute-done.7.refs_1_ = f32[64,256]{1,0:T(8,128)S(1)} collective-permute-done((f32[64,256]{1,0:T(8,128)S(1)}, f32[64,256]{1,0:T(8,128)S(1)}, u32[]{:S(2)}, u32[]{:S(2)}) %collective-permute-start.7) | collective-permute-done | bytes 65568 | tf_op jit(solution)/shard_map/ppermute | solution.py:242
  26.9 0.3 couple.1
  27.2 0.0 collective-permute-done.8.refs_3_
  27.2 0.6 %rest_part.1 = (f32[64,3584]{1,0:T(8,128)S(1)}, f32[1,64]{1,0:T(1,128)S(1)}) custom-call(f32[64,3584]{1,0:T(8,128)S(1)} %first_part.1.t_ref, bf16[64,128]{1,0:T(8,128)(2,1)S(1)} %get-tuple-element.18.refs_0_, bf16[64,128]{1,0:T(8,128)(2,1)S(1)} %get-tuple-element.19.refs_1_, f32[64,3584]{1,0:T(8,128)S(1)} %collective-permute-done.refs_2_, ...), custom_call_target="tpu_custom_call" | custom-call | tf_op jit(solution)/shard_map/rest_part/pallas_call | solution.py:187
  27.8 1.8 %collective-permute-start.10 = (f32[1,64]{1,0:T(1,128)S(1)}, f32[1,64]{1,0:T(1,128)S(1)}, u32[]{:S(2)}, u32[]{:S(2)}) collective-permute-start(f32[1,64]{1,0:T(1,128)S(1)} %get-tuple-element.22), channel_id=1, source_target_pairs={{0,9},{1,8},{2,11},{3,10},{4,13},{5,12},{6,15},{7,14},{8,1},{9,0},... | collective-permute-start | bytes 776 | tf_op jit(solution)/shard_map/ppermute | solution.py:275
  29.6 1.6 %collective-permute-start.11 = (f32[1,64]{1,0:T(1,128)S(1)}, f32[1,64]{1,0:T(1,128)S(1)}, u32[]{:S(2)}, u32[]{:S(2)}) collective-permute-start(f32[1,64]{1,0:T(1,128)S(1)} %get-tuple-element.22), channel_id=1, source_target_pairs={{0,10},{1,11},{2,8},{3,9},{4,14},{5,15},{6,12},{7,13},{8,2},{9,3},... | collective-permute-start | bytes 776 | tf_op jit(solution)/shard_map/ppermute | solution.py:275
  31.2 0.0 collective-permute-start.12
  31.2 0.2 collective-permute-start.9
  31.3 0.0 collective-permute-done.10
  31.3 1.3 %collective-permute-done.11 = f32[1,64]{1,0:T(1,128)S(1)} collective-permute-done((f32[1,64]{1,0:T(1,128)S(1)}, f32[1,64]{1,0:T(1,128)S(1)}, u32[]{:S(2)}, u32[]{:S(2)}) %collective-permute-start.11) | collective-permute-done | bytes 288 | tf_op jit(solution)/shard_map/ppermute | solution.py:275
  32.6 2.4 %collective-permute-done.12 = f32[1,64]{1,0:T(1,128)S(1)} collective-permute-done((f32[1,64]{1,0:T(1,128)S(1)}, f32[1,64]{1,0:T(1,128)S(1)}, u32[]{:S(2)}, u32[]{:S(2)}) %collective-permute-start.12) | collective-permute-done | bytes 288 | tf_op jit(solution)/shard_map/ppermute | solution.py:275
  35.0 0.0 collective-permute-done.9
  35.0 0.2 collective-permute-start.13
  35.3 2.6 %collective-permute-start.14 = (f32[1,64]{1,0:T(1,128)S(1)}, f32[1,64]{1,0:T(1,128)S(1)}, u32[]{:S(2)}, u32[]{:S(2)}) collective-permute-start(f32[1,64]{1,0:T(1,128)S(1)} %add_add_fusion), channel_id=1, source_target_pairs={{0,12},{1,13},{2,14},{3,15},{4,8},{5,9},{6,10},{7,11},{8,4},{9,5},... | collective-permute-start | bytes 776 | tf_op jit(solution)/shard_map/ppermute | solution.py:275
  37.8 0.0 collective-permute-done.13.refs_0_
  37.8 1.3 %collective-permute-done.14.refs_1_ = f32[1,64]{1,0:T(1,128)S(1)} collective-permute-done((f32[1,64]{1,0:T(1,128)S(1)}, f32[1,64]{1,0:T(1,128)S(1)}, u32[]{:S(2)}, u32[]{:S(2)}) %collective-permute-start.14) | collective-permute-done | bytes 288 | tf_op jit(solution)/shard_map/ppermute | solution.py:275
  39.1 1.1 %finish.1 = f32[64,3584]{1,0:T(8,128)} custom-call(f32[64,3584]{1,0:T(8,128)S(1)} %get-tuple-element.21.updated_ref, f32[1,64]{1,0:T(1,128)S(1)} %collective-permute-done.13.refs_0_, f32[1,64]{1,0:T(1,128)S(1)} %collective-permute-done.14.refs_1_), custom_call_target="tpu_custom_call" | custom-call | tf_op jit(solution)/shard_map/finish/pallas_call | solution.py:227
  (4 shorter events, 0.0 us)
Async XLA Ops:
  0.0 21.1 %collective-permute-start.5 = (f32[64,3584]{1,0:T(8,128)}, f32[64,3584]{1,0:T(8,128)S(1)}, u32[]{:S(2)}, u32[]{:S(2)}) collective-permute-start(f32[64,3584]{1,0:T(8,128)} %x_hbm.1), channel_id=1, source_target_pairs={{0,8},{8,0},{16,24},{24,16},{1,9},{9,1},{17,25},{25,17},{2,10},{10... | collective-permute-start | bytes 2752520 | tf_op jit(solution)/shard_map/ppermute | solution.py:242
  0.5 23.9 %collective-permute-start = (f32[64,3584]{1,0:T(8,128)}, f32[64,3584]{1,0:T(8,128)S(1)}, u32[]{:S(2)}, u32[]{:S(2)}) collective-permute-start(f32[64,3584]{1,0:T(8,128)} %x_hbm.1), channel_id=1, source_target_pairs={{0,16},{8,24},{16,0},{24,8},{1,17},{9,25},{17,1},{25,9},{2,18},{10... | collective-permute-start | bytes 2752520 | tf_op jit(solution)/shard_map/ppermute | solution.py:242
  5.9 4.3 %collective-permute-start.1 = (f32[64,256]{1,0:T(8,128)S(1)}, f32[64,256]{1,0:T(8,128)S(1)}, u32[]{:S(2)}, u32[]{:S(2)}) collective-permute-start(f32[64,256]{1,0:T(8,128)S(1)} %get-tuple-element.14), channel_id=1, source_target_pairs={{0,1},{1,0},{2,3},{3,2},{4,5},{5,4},{6,7},{7,6},{8,9},{9,8},{10,11... | collective-permute-start | bytes 196616 | tf_op jit(solution)/shard_map/ppermute | solution.py:242
  10.2 4.3 %collective-permute-start.2 = (f32[64,256]{1,0:T(8,128)S(1)}, f32[64,256]{1,0:T(8,128)S(1)}, u32[]{:S(2)}, u32[]{:S(2)}) collective-permute-start(f32[64,256]{1,0:T(8,128)S(1)} %add.18), channel_id=1, source_target_pairs={{0,2},{1,3},{2,0},{3,1},{4,6},{5,7},{6,4},{7,5},{8,10},{9,11},{10,... | collective-permute-start | bytes 196616 | tf_op jit(solution)/shard_map/ppermute | solution.py:242
  14.6 5.2 %collective-permute-start.3 = (f32[64,256]{1,0:T(8,128)S(1)}, f32[64,256]{1,0:T(8,128)S(1)}, u32[]{:S(2)}, u32[]{:S(2)}) collective-permute-start(f32[64,256]{1,0:T(8,128)S(1)} %add.19), channel_id=1, source_target_pairs={{0,4},{1,5},{2,6},{3,7},{4,0},{5,1},{6,2},{7,3},{8,12},{9,13},{10,... | collective-permute-start | bytes 196616 | tf_op jit(solution)/shard_map/ppermute | solution.py:242
  19.8 1.3 %collective-permute-start.4 = (f32[64,256]{1,0:T(8,128)S(1)}, f32[64,256]{1,0:T(8,128)S(1)}, u32[]{:S(2)}, u32[]{:S(2)}) collective-permute-start(f32[64,256]{1,0:T(8,128)S(1)} %add.20.p_ref), channel_id=1, source_target_pairs={{0,8},{8,0},{16,24},{24,16},{1,9},{9,1},{17,25},{25,17},{2,10},{10... | collective-permute-start | bytes 196616 | tf_op jit(solution)/shard_map/ppermute | solution.py:242
  19.9 5.7 %collective-permute-start.6 = (f32[64,256]{1,0:T(8,128)S(1)}, f32[64,256]{1,0:T(8,128)S(1)}, u32[]{:S(2)}, u32[]{:S(2)}) collective-permute-start(f32[64,256]{1,0:T(8,128)S(1)} %add.20.p_ref), channel_id=1, source_target_pairs={{0,16},{8,24},{16,0},{24,8},{1,17},{9,25},{17,1},{25,9},{2,18},{10... | collective-permute-start | bytes 196616 | tf_op jit(solution)/shard_map/ppermute | solution.py:242
  24.4 2.8 %collective-permute-start.8 = (f32[64,3584]{1,0:T(8,128)S(1)}, f32[64,3584]{1,0:T(8,128)S(1)}, u32[]{:S(2)}, u32[]{:S(2)}) collective-permute-start(f32[64,3584]{1,0:T(8,128)S(1)} %collective-permute-done.refs_2_), channel_id=1, source_target_pairs={{0,8},{8,0},{16,24},{24,16},{1,9},{9,1},{17,25},{25,17},{2,10},{10... | collective-permute-start | bytes 2752520 | tf_op jit(solution)/shard_map/ppermute | solution.py:242
  25.6 1.3 %collective-permute-start.7 = (f32[64,256]{1,0:T(8,128)S(1)}, f32[64,256]{1,0:T(8,128)S(1)}, u32[]{:S(2)}, u32[]{:S(2)}) collective-permute-start(f32[64,256]{1,0:T(8,128)S(1)} %collective-permute-done.6.refs_0_), channel_id=1, source_target_pairs={{0,8},{8,0},{16,24},{24,16},{1,9},{9,1},{17,25},{25,17},{2,10},{10... | collective-permute-start | bytes 196616 | tf_op jit(solution)/shard_map/ppermute | solution.py:242
  27.8 3.5 %collective-permute-start.10 = (f32[1,64]{1,0:T(1,128)S(1)}, f32[1,64]{1,0:T(1,128)S(1)}, u32[]{:S(2)}, u32[]{:S(2)}) collective-permute-start(f32[1,64]{1,0:T(1,128)S(1)} %get-tuple-element.22), channel_id=1, source_target_pairs={{0,9},{1,8},{2,11},{3,10},{4,13},{5,12},{6,15},{7,14},{8,1},{9,0},... | collective-permute-start | bytes 776 | tf_op jit(solution)/shard_map/ppermute | solution.py:275
  29.6 3.0 %collective-permute-start.11 = (f32[1,64]{1,0:T(1,128)S(1)}, f32[1,64]{1,0:T(1,128)S(1)}, u32[]{:S(2)}, u32[]{:S(2)}) collective-permute-start(f32[1,64]{1,0:T(1,128)S(1)} %get-tuple-element.22), channel_id=1, source_target_pairs={{0,10},{1,11},{2,8},{3,9},{4,14},{5,15},{6,12},{7,13},{8,2},{9,3},... | collective-permute-start | bytes 776 | tf_op jit(solution)/shard_map/ppermute | solution.py:275
  31.2 3.9 %collective-permute-start.12 = (f32[1,64]{1,0:T(1,128)S(1)}, f32[1,64]{1,0:T(1,128)S(1)}, u32[]{:S(2)}, u32[]{:S(2)}) collective-permute-start(f32[1,64]{1,0:T(1,128)S(1)} %get-tuple-element.22), channel_id=1, source_target_pairs={{0,11},{1,10},{2,9},{3,8},{4,15},{5,14},{6,13},{7,12},{8,3},{9,2},... | collective-permute-start | bytes 776 | tf_op jit(solution)/shard_map/ppermute | solution.py:275
  31.2 3.9 %collective-permute-start.9 = (f32[1,64]{1,0:T(1,128)S(1)}, f32[1,64]{1,0:T(1,128)S(1)}, u32[]{:S(2)}, u32[]{:S(2)}) collective-permute-start(f32[1,64]{1,0:T(1,128)S(1)} %get-tuple-element.22), channel_id=1, source_target_pairs={{0,8},{1,9},{2,10},{3,11},{4,12},{5,13},{6,14},{7,15},{8,0},{9,1},... | collective-permute-start | bytes 776 | tf_op jit(solution)/shard_map/ppermute | solution.py:275
  35.0 2.8 %collective-permute-start.13 = (f32[1,64]{1,0:T(1,128)S(1)}, f32[1,64]{1,0:T(1,128)S(1)}, u32[]{:S(2)}, u32[]{:S(2)}) collective-permute-start(f32[1,64]{1,0:T(1,128)S(1)} %add_add_fusion), channel_id=1, source_target_pairs={{0,8},{1,9},{2,10},{3,11},{4,12},{5,13},{6,14},{7,15},{8,0},{9,1},... | collective-permute-start | bytes 776 | tf_op jit(solution)/shard_map/ppermute | solution.py:275
  35.3 3.9 %collective-permute-start.14 = (f32[1,64]{1,0:T(1,128)S(1)}, f32[1,64]{1,0:T(1,128)S(1)}, u32[]{:S(2)}, u32[]{:S(2)}) collective-permute-start(f32[1,64]{1,0:T(1,128)S(1)} %add_add_fusion), channel_id=1, source_target_pairs={{0,12},{1,13},{2,14},{3,15},{4,8},{5,9},{6,10},{7,11},{8,4},{9,5},... | collective-permute-start | bytes 776 | tf_op jit(solution)/shard_map/ppermute | solution.py:275

commit v15 on v11

--- a/solution.py
+++ b/solution.py
@@ -276,7 +276,7 @@
     features = sample.shape[1] * feat
     even = comp & (comp - 1) == 0
 
-    blocks = {step: exchange(start_vectors, "comp", step) for step in range(2, comp, 2)} if even else gather(start_vectors)
+    blocks = {step: exchange(start_vectors, "comp", step) for step in range(3, comp, 2)} if even else gather(start_vectors)
     projected, vectors, sample = project(
         *(pltpu.with_memory_space_constraint(array, pltpu.HBM) for array in (start_vectors, sample))
     )
@@ -285,7 +285,7 @@
     parts = terms(projected, "feat", 1)
     projected = sum(parts[1:], parts[0])
     if even:
-        others = {step: exchange(projected, "comp", step) for step in range(1, comp, 2)}
+        others = {step: exchange(projected, "comp", step) for step in range(1, comp) if step == 1 or step % 2 == 0}
     else:
         others = gather(projected)
     near = [1][: comp - 1]
@@ -297,11 +297,11 @@
     partly = first_part(projected, sample, vectors, near, of(others, near), of(blocks, near), features)
     if even:
         for step in range(2, comp, 2):
-            blocks[step], others[step + 1], others[1] = lax.optimization_barrier(
-                (blocks[step], others[step + 1], others[1])
+            blocks[step + 1], others[step], others[1] = lax.optimization_barrier(
+                (blocks[step + 1], others[step], others[1])
             )
-            blocks[step + 1] = exchange(blocks[step], "comp", 1)
-            others[step] = exchange(others[step + 1], "comp", 1)
+            blocks[step] = exchange(blocks[step + 1], "comp", 1)
+            others[step + 1] = exchange(others[step], "comp", 1)
     updated, squares = rest_part(partly, projected, far, of(others, far), of(blocks, far), rows, features)
     return finish(updated, flipped_terms(squares), features)
 

time: 39.4 us -> 40.5 us (1.028)
  waiting for transfers between devices: 16.7 us -> 17.9 us
    ppermute x9, waiting for transfers between devices: 12.6 us -> 13.6 us  [exchange(): lax.ppermute(array, axis, [(i, i ^ step) for i in range(lax.axis_size(axi...]
    ppermute x9, starting transfers between devices: 9.91 us -> 9.38 us  [exchange(): lax.ppermute(array, axis, [(i, i ^ step) for i in range(lax.axis_size(axi...]
where the time goes in v15:
time: 40.5 us; the launch traced here: 40.4 us
  waiting for transfers between devices  17.9 us (44%)
  starting transfers between devices  16 us (40%)
  Pallas kernels  6.39 us (16%)
    ppermute x9, waiting for transfers between devices, exchange(): lax.ppermute(array, axis, [(i, i ^ step) for i in range(lax.axis_size(axi...  13.6 us
    ppermute x9, starting transfers between devices, exchange(): lax.ppermute(array, axis, [(i, i ^ step) for i in range(lax.axis_size(axi...  9.38 us
    ppermute x6, starting transfers between devices, flipped_terms(): parts.append(lax.ppermute(array, ('comp', 'feat'), pairs))  6.61 us
    ppermute x6, waiting for transfers between devices, flipped_terms(): parts.append(lax.ppermute(array, ('comp', 'feat'), pairs))  4.31 us
    pallas_call x1, Pallas kernels, project(): pl.pallas_call(project_kernel, in_specs=[anywhere] * 2, out_specs=[in_vme...  2.94 us
    pallas_call x1, Pallas kernels, first_part(): pl.pallas_call(functools.partial(first_kernel, features, steps), in_specs...  1.47 us
    pallas_call x1, Pallas kernels, finish(): pl.pallas_call(functools.partial(finish_kernel, features, count), in_spec...  1.08 us
    pallas_call x1, Pallas kernels, rest_part(): pl.pallas_call(functools.partial(rest_kernel, features, rows, steps), in_...  0.9 us
  transfers between devices with their start and end apart: 15, of which 10 were waited for; matrix products, arithmetic and copies ran while one was open for 0% of the time, Pallas kernels for 11%

profile of v15, /device:TPU:0, one launch (start us, length us, event | category | flops | bytes accessed | tf_op | source)
XLA Modules:
  0.0 40.4 jit_solution(4957609402396777186)
XLA Ops:
  0.0 2.4 %collective-permute-start.5 = (f32[64,3584]{1,0:T(8,128)}, f32[64,3584]{1,0:T(8,128)S(1)}, u32[]{:S(2)}, u32[]{:S(2)}) collective-permute-start(f32[64,3584]{1,0:T(8,128)} %x_hbm.1), channel_id=1, source_target_pairs={{0,24},{8,16},{16,8},{24,0},{1,25},{9,17},{17,9},{25,1},{2,26},{10... | collective-permute-start | bytes 2752520 | tf_op jit(solution)/shard_map/ppermute | solution.py:225
  2.4 2.9 %project.1 = (f32[64,256]{1,0:T(8,128)S(1)}, f32[64,3584]{1,0:T(8,128)S(1)}, f32[192,3584]{1,0:T(8,128)S(1)}) custom-call(f32[64,3584]{1,0:T(8,128)} %x_hbm.1, f32[192,3584]{1,0:T(8,128)} %bitcast.1), custom_call_target="tpu_custom_call" | custom-call | tf_op jit(solution)/shard_map/project/pallas_call | solution.py:83
  5.3 1.6 %collective-permute-start = (f32[64,256]{1,0:T(8,128)S(1)}, f32[64,256]{1,0:T(8,128)S(1)}, u32[]{:S(2)}, u32[]{:S(2)}) collective-permute-start(f32[64,256]{1,0:T(8,128)S(1)} %get-tuple-element.12), channel_id=1, source_target_pairs={{0,1},{1,0},{2,3},{3,2},{4,5},{5,4},{6,7},{7,6},{8,9},{9,8},{10,11... | collective-permute-start | bytes 196616 | tf_op jit(solution)/shard_map/ppermute | solution.py:225
  6.9 3.2 %collective-permute-done = f32[64,256]{1,0:T(8,128)S(1)} collective-permute-done((f32[64,256]{1,0:T(8,128)S(1)}, f32[64,256]{1,0:T(8,128)S(1)}, u32[]{:S(2)}, u32[]{:S(2)}) %collective-permute-start) | collective-permute-done | bytes 65568 | tf_op jit(solution)/shard_map/ppermute | solution.py:225
  10.1 1.6 %collective-permute-start.1 = (f32[64,256]{1,0:T(8,128)S(1)}, f32[64,256]{1,0:T(8,128)S(1)}, u32[]{:S(2)}, u32[]{:S(2)}) collective-permute-start(f32[64,256]{1,0:T(8,128)S(1)} %add.18), channel_id=1, source_target_pairs={{0,2},{1,3},{2,0},{3,1},{4,6},{5,7},{6,4},{7,5},{8,10},{9,11},{10,... | collective-permute-start | bytes 196616 | tf_op jit(solution)/shard_map/ppermute | solution.py:225
  11.7 2.7 %collective-permute-done.1 = f32[64,256]{1,0:T(8,128)S(1)} collective-permute-done((f32[64,256]{1,0:T(8,128)S(1)}, f32[64,256]{1,0:T(8,128)S(1)}, u32[]{:S(2)}, u32[]{:S(2)}) %collective-permute-start.1) | collective-permute-done | bytes 65568 | tf_op jit(solution)/shard_map/ppermute | solution.py:225
  14.4 2.7 %collective-permute-start.2 = (f32[64,256]{1,0:T(8,128)S(1)}, f32[64,256]{1,0:T(8,128)S(1)}, u32[]{:S(2)}, u32[]{:S(2)}) collective-permute-start(f32[64,256]{1,0:T(8,128)S(1)} %add.19), channel_id=1, source_target_pairs={{0,4},{1,5},{2,6},{3,7},{4,0},{5,1},{6,2},{7,3},{8,12},{9,13},{10,... | collective-permute-start | bytes 196616 | tf_op jit(solution)/shard_map/ppermute | solution.py:225
  17.1 2.6 %collective-permute-done.2 = f32[64,256]{1,0:T(8,128)S(1)} collective-permute-done((f32[64,256]{1,0:T(8,128)S(1)}, f32[64,256]{1,0:T(8,128)S(1)}, u32[]{:S(2)}, u32[]{:S(2)}) %collective-permute-start.2) | collective-permute-done | bytes 65568 | tf_op jit(solution)/shard_map/ppermute | solution.py:225
  19.7 0.1 collective-permute-start.3
  19.7 0.4 collective-permute-start.6
  20.1 0.2 collective-permute-start.4
  20.3 0.7 %collective-permute-done.3.refs_0_ = f32[64,256]{1,0:T(8,128)S(1)} collective-permute-done((f32[64,256]{1,0:T(8,128)S(1)}, f32[64,256]{1,0:T(8,128)S(1)}, u32[]{:S(2)}, u32[]{:S(2)}) %collective-permute-start.3) | collective-permute-done | bytes 65568 | tf_op jit(solution)/shard_map/ppermute | solution.py:225
  21.0 3.9 %collective-permute-done.6.refs_0_ = f32[64,256]{1,0:T(8,128)S(1)} collective-permute-done((f32[64,256]{1,0:T(8,128)S(1)}, f32[64,256]{1,0:T(8,128)S(1)}, u32[]{:S(2)}, u32[]{:S(2)}) %collective-permute-start.6) | collective-permute-done | bytes 65568 | tf_op jit(solution)/shard_map/ppermute | solution.py:225
  24.9 0.0 collective-permute-done.5.refs_3_
  24.9 0.0 collective-permute-start.8
  24.9 0.5 %collective-permute-start.7 = (f32[64,256]{1,0:T(8,128)S(1)}, f32[64,256]{1,0:T(8,128)S(1)}, u32[]{:S(2)}, u32[]{:S(2)}) collective-permute-start(f32[64,256]{1,0:T(8,128)S(1)} %collective-permute-done.6.refs_0_), channel_id=1, source_target_pairs={{0,8},{8,0},{16,24},{24,16},{1,9},{9,1},{17,25},{25,17},{2,10},{10... | collective-permute-start | bytes 196616 | tf_op jit(solution)/shard_map/ppermute | solution.py:225
  25.4 0.0 collective-permute-done.4.refs_1_
  25.4 1.5 %first_part.1.t_ref = f32[64,3584]{1,0:T(8,128)S(1)} custom-call(f32[64,256]{1,0:T(8,128)S(1)} %add.20.p_ref, f32[192,3584]{1,0:T(8,128)S(1)} %get-tuple-element.13.s_ref, f32[64,3584]{1,0:T(8,128)S(1)} %get-tuple-element.14.x_ref, f32[64,256]{1,0:T(8,128)S(1)} %collective-permute-done.3.refs_0_, f32[64,3584]{1,0:T(8,128)S(1)} %collective-permute-done.4.refs_1_), custom_call_target="tpu_custom_call" | custom-call | tf_op jit(solution)/shard_map/first_part/pallas_call | solution.py:140
  26.9 0.6 %collective-permute-done.7.refs_1_ = f32[64,256]{1,0:T(8,128)S(1)} collective-permute-done((f32[64,256]{1,0:T(8,128)S(1)}, f32[64,256]{1,0:T(8,128)S(1)}, u32[]{:S(2)}, u32[]{:S(2)}) %collective-permute-start.7) | collective-permute-done | bytes 65568 | tf_op jit(solution)/shard_map/ppermute | solution.py:225
  27.5 0.0 collective-permute-done.8.refs_2_
  27.5 0.9 %rest_part.1 = (f32[64,3584]{1,0:T(8,128)S(1)}, f32[1,64]{1,0:T(1,128)S(1)}) custom-call(f32[64,3584]{1,0:T(8,128)S(1)} %first_part.1.t_ref, f32[64,256]{1,0:T(8,128)S(1)} %add.20.p_ref, f32[64,256]{1,0:T(8,128)S(1)} %collective-permute-done.6.refs_0_, f32[64,256]{1,0:T(8,128)S(1)} %collective-permute-done.7.refs_1_, ...), custom_call_target="tpu_custom_call" | custom-call | tf_op jit(solution)/shard_map/rest_part/pallas_call | solution.py:170
  28.4 3.2 %collective-permute-start.12 = (f32[1,64]{1,0:T(1,128)S(1)}, f32[1,64]{1,0:T(1,128)S(1)}, u32[]{:S(2)}, u32[]{:S(2)}) collective-permute-start(f32[1,64]{1,0:T(1,128)S(1)} %get-tuple-element.18), channel_id=1, source_target_pairs={{0,11},{1,10},{2,9},{3,8},{4,15},{5,14},{6,13},{7,12},{8,3},{9,2},... | collective-permute-start | bytes 776 | tf_op jit(solution)/shard_map/ppermute | solution.py:258
  31.5 0.4 %collective-permute-start.11 = (f32[1,64]{1,0:T(1,128)S(1)}, f32[1,64]{1,0:T(1,128)S(1)}, u32[]{:S(2)}, u32[]{:S(2)}) collective-permute-start(f32[1,64]{1,0:T(1,128)S(1)} %get-tuple-element.18), channel_id=1, source_target_pairs={{0,10},{1,11},{2,8},{3,9},{4,14},{5,15},{6,12},{7,13},{8,2},{9,3},... | collective-permute-start | bytes 776 | tf_op jit(solution)/shard_map/ppermute | solution.py:258
  32.0 0.1 collective-permute-start.9
  32.1 0.2 collective-permute-start.10
  32.3 0.5 %collective-permute-done.12 = f32[1,64]{1,0:T(1,128)S(1)} collective-permute-done((f32[1,64]{1,0:T(1,128)S(1)}, f32[1,64]{1,0:T(1,128)S(1)}, u32[]{:S(2)}, u32[]{:S(2)}) %collective-permute-start.12) | collective-permute-done | bytes 288 | tf_op jit(solution)/shard_map/ppermute | solution.py:258
  32.8 1.7 %collective-permute-done.11 = f32[1,64]{1,0:T(1,128)S(1)} collective-permute-done((f32[1,64]{1,0:T(1,128)S(1)}, f32[1,64]{1,0:T(1,128)S(1)}, u32[]{:S(2)}, u32[]{:S(2)}) %collective-permute-start.11) | collective-permute-done | bytes 288 | tf_op jit(solution)/shard_map/ppermute | solution.py:258
  34.5 0.0 collective-permute-done.9
  34.5 0.6 %collective-permute-done.10 = f32[1,64]{1,0:T(1,128)S(1)} collective-permute-done((f32[1,64]{1,0:T(1,128)S(1)}, f32[1,64]{1,0:T(1,128)S(1)}, u32[]{:S(2)}, u32[]{:S(2)}) %collective-permute-start.10) | collective-permute-done | bytes 288 | tf_op jit(solution)/shard_map/ppermute | solution.py:258
  35.1 0.3 collective-permute-start.13
  35.4 2.4 %collective-permute-start.14 = (f32[1,64]{1,0:T(1,128)S(1)}, f32[1,64]{1,0:T(1,128)S(1)}, u32[]{:S(2)}, u32[]{:S(2)}) collective-permute-start(f32[1,64]{1,0:T(1,128)S(1)} %add_add_fusion), channel_id=1, source_target_pairs={{0,12},{1,13},{2,14},{3,15},{4,8},{5,9},{6,10},{7,11},{8,4},{9,5},... | collective-permute-start | bytes 776 | tf_op jit(solution)/shard_map/ppermute | solution.py:258
  37.8 0.0 collective-permute-done.13.refs_0_
  37.8 1.5 %collective-permute-done.14.refs_1_ = f32[1,64]{1,0:T(1,128)S(1)} collective-permute-done((f32[1,64]{1,0:T(1,128)S(1)}, f32[1,64]{1,0:T(1,128)S(1)}, u32[]{:S(2)}, u32[]{:S(2)}) %collective-permute-start.14) | collective-permute-done | bytes 288 | tf_op jit(solution)/shard_map/ppermute | solution.py:258
  39.3 1.1 %finish.1 = f32[64,3584]{1,0:T(8,128)} custom-call(f32[64,3584]{1,0:T(8,128)S(1)} %get-tuple-element.17.updated_ref, f32[1,64]{1,0:T(1,128)S(1)} %collective-permute-done.13.refs_0_, f32[1,64]{1,0:T(1,128)S(1)} %collective-permute-done.14.refs_1_), custom_call_target="tpu_custom_call" | custom-call | tf_op jit(solution)/shard_map/finish/pallas_call | solution.py:210
  (4 shorter events, 0.0 us)
Async XLA Ops:
  0.0 24.9 %collective-permute-start.5 = (f32[64,3584]{1,0:T(8,128)}, f32[64,3584]{1,0:T(8,128)S(1)}, u32[]{:S(2)}, u32[]{:S(2)}) collective-permute-start(f32[64,3584]{1,0:T(8,128)} %x_hbm.1), channel_id=1, source_target_pairs={{0,24},{8,16},{16,8},{24,0},{1,25},{9,17},{17,9},{25,1},{2,26},{10... | collective-permute-start | bytes 2752520 | tf_op jit(solution)/shard_map/ppermute | solution.py:225
  5.3 4.7 %collective-permute-start = (f32[64,256]{1,0:T(8,128)S(1)}, f32[64,256]{1,0:T(8,128)S(1)}, u32[]{:S(2)}, u32[]{:S(2)}) collective-permute-start(f32[64,256]{1,0:T(8,128)S(1)} %get-tuple-element.12), channel_id=1, source_target_pairs={{0,1},{1,0},{2,3},{3,2},{4,5},{5,4},{6,7},{7,6},{8,9},{9,8},{10,11... | collective-permute-start | bytes 196616 | tf_op jit(solution)/shard_map/ppermute | solution.py:225
  10.1 4.3 %collective-permute-start.1 = (f32[64,256]{1,0:T(8,128)S(1)}, f32[64,256]{1,0:T(8,128)S(1)}, u32[]{:S(2)}, u32[]{:S(2)}) collective-permute-start(f32[64,256]{1,0:T(8,128)S(1)} %add.18), channel_id=1, source_target_pairs={{0,2},{1,3},{2,0},{3,1},{4,6},{5,7},{6,4},{7,5},{8,10},{9,11},{10,... | collective-permute-start | bytes 196616 | tf_op jit(solution)/shard_map/ppermute | solution.py:225
  14.4 5.2 %collective-permute-start.2 = (f32[64,256]{1,0:T(8,128)S(1)}, f32[64,256]{1,0:T(8,128)S(1)}, u32[]{:S(2)}, u32[]{:S(2)}) collective-permute-start(f32[64,256]{1,0:T(8,128)S(1)} %add.19), channel_id=1, source_target_pairs={{0,4},{1,5},{2,6},{3,7},{4,0},{5,1},{6,2},{7,3},{8,12},{9,13},{10,... | collective-permute-start | bytes 196616 | tf_op jit(solution)/shard_map/ppermute | solution.py:225
  19.7 1.3 %collective-permute-start.3 = (f32[64,256]{1,0:T(8,128)S(1)}, f32[64,256]{1,0:T(8,128)S(1)}, u32[]{:S(2)}, u32[]{:S(2)}) collective-permute-start(f32[64,256]{1,0:T(8,128)S(1)} %add.20.p_ref), channel_id=1, source_target_pairs={{0,8},{8,0},{16,24},{24,16},{1,9},{9,1},{17,25},{25,17},{2,10},{10... | collective-permute-start | bytes 196616 | tf_op jit(solution)/shard_map/ppermute | solution.py:225
  19.7 5.2 %collective-permute-start.6 = (f32[64,256]{1,0:T(8,128)S(1)}, f32[64,256]{1,0:T(8,128)S(1)}, u32[]{:S(2)}, u32[]{:S(2)}) collective-permute-start(f32[64,256]{1,0:T(8,128)S(1)} %add.20.p_ref), channel_id=1, source_target_pairs={{0,16},{8,24},{16,0},{24,8},{1,17},{9,25},{17,1},{25,9},{2,18},{10... | collective-permute-start | bytes 196616 | tf_op jit(solution)/shard_map/ppermute | solution.py:225
  20.1 5.3 %collective-permute-start.4 = (f32[64,3584]{1,0:T(8,128)S(1)}, f32[64,3584]{1,0:T(8,128)S(1)}, u32[]{:S(2)}, u32[]{:S(2)}) collective-permute-start(f32[64,3584]{1,0:T(8,128)S(1)} %get-tuple-element.14.x_ref), channel_id=1, source_target_pairs={{0,8},{8,0},{16,24},{24,16},{1,9},{9,1},{17,25},{25,17},{2,10},{10... | collective-permute-start | bytes 2752520 | tf_op jit(solution)/shard_map/ppermute | solution.py:225
  24.9 2.6 %collective-permute-start.8 = (f32[64,3584]{1,0:T(8,128)S(1)}, f32[64,3584]{1,0:T(8,128)S(1)}, u32[]{:S(2)}, u32[]{:S(2)}) collective-permute-start(f32[64,3584]{1,0:T(8,128)S(1)} %collective-permute-done.5.refs_3_), channel_id=1, source_target_pairs={{0,8},{8,0},{16,24},{24,16},{1,9},{9,1},{17,25},{25,17},{2,10},{10... | collective-permute-start | bytes 2752520 | tf_op jit(solution)/shard_map/ppermute | solution.py:225
  24.9 2.6 %collective-permute-start.7 = (f32[64,256]{1,0:T(8,128)S(1)}, f32[64,256]{1,0:T(8,128)S(1)}, u32[]{:S(2)}, u32[]{:S(2)}) collective-permute-start(f32[64,256]{1,0:T(8,128)S(1)} %collective-permute-done.6.refs_0_), channel_id=1, source_target_pairs={{0,8},{8,0},{16,24},{24,16},{1,9},{9,1},{17,25},{25,17},{2,10},{10... | collective-permute-start | bytes 196616 | tf_op jit(solution)/shard_map/ppermute | solution.py:225
  28.4 4.4 %collective-permute-start.12 = (f32[1,64]{1,0:T(1,128)S(1)}, f32[1,64]{1,0:T(1,128)S(1)}, u32[]{:S(2)}, u32[]{:S(2)}) collective-permute-start(f32[1,64]{1,0:T(1,128)S(1)} %get-tuple-element.18), channel_id=1, source_target_pairs={{0,11},{1,10},{2,9},{3,8},{4,15},{5,14},{6,13},{7,12},{8,3},{9,2},... | collective-permute-start | bytes 776 | tf_op jit(solution)/shard_map/ppermute | solution.py:258
  31.5 3.0 %collective-permute-start.11 = (f32[1,64]{1,0:T(1,128)S(1)}, f32[1,64]{1,0:T(1,128)S(1)}, u32[]{:S(2)}, u32[]{:S(2)}) collective-permute-start(f32[1,64]{1,0:T(1,128)S(1)} %get-tuple-element.18), channel_id=1, source_target_pairs={{0,10},{1,11},{2,8},{3,9},{4,14},{5,15},{6,12},{7,13},{8,2},{9,3},... | collective-permute-start | bytes 776 | tf_op jit(solution)/shard_map/ppermute | solution.py:258
  32.0 2.6 %collective-permute-start.9 = (f32[1,64]{1,0:T(1,128)S(1)}, f32[1,64]{1,0:T(1,128)S(1)}, u32[]{:S(2)}, u32[]{:S(2)}) collective-permute-start(f32[1,64]{1,0:T(1,128)S(1)} %get-tuple-element.18), channel_id=1, source_target_pairs={{0,8},{1,9},{2,10},{3,11},{4,12},{5,13},{6,14},{7,15},{8,0},{9,1},... | collective-permute-start | bytes 776 | tf_op jit(solution)/shard_map/ppermute | solution.py:258
  32.1 3.0 %collective-permute-start.10 = (f32[1,64]{1,0:T(1,128)S(1)}, f32[1,64]{1,0:T(1,128)S(1)}, u32[]{:S(2)}, u32[]{:S(2)}) collective-permute-start(f32[1,64]{1,0:T(1,128)S(1)} %get-tuple-element.18), channel_id=1, source_target_pairs={{0,9},{1,8},{2,11},{3,10},{4,13},{5,12},{6,15},{7,14},{8,1},{9,0},... | collective-permute-start | bytes 776 | tf_op jit(solution)/shard_map/ppermute | solution.py:258
  35.1 2.7 %collective-permute-start.13 = (f32[1,64]{1,0:T(1,128)S(1)}, f32[1,64]{1,0:T(1,128)S(1)}, u32[]{:S(2)}, u32[]{:S(2)}) collective-permute-start(f32[1,64]{1,0:T(1,128)S(1)} %add_add_fusion), channel_id=1, source_target_pairs={{0,8},{1,9},{2,10},{3,11},{4,12},{5,13},{6,14},{7,15},{8,0},{9,1},... | collective-permute-start | bytes 776 | tf_op jit(solution)/shard_map/ppermute | solution.py:258
  35.4 3.9 %collective-permute-start.14 = (f32[1,64]{1,0:T(1,128)S(1)}, f32[1,64]{1,0:T(1,128)S(1)}, u32[]{:S(2)}, u32[]{:S(2)}) collective-permute-start(f32[1,64]{1,0:T(1,128)S(1)} %add_add_fusion), channel_id=1, source_target_pairs={{0,12},{1,13},{2,14},{3,15},{4,8},{5,9},{6,10},{7,11},{8,4},{9,5},... | collective-permute-start | bytes 776 | tf_op jit(solution)/shard_map/ppermute | solution.py:258

commit v16 on v14

--- a/solution.py
+++ b/solution.py
@@ -160,13 +160,13 @@
         out_specs=[in_vmem] * 2,
         out_shape=[jax.ShapeDtypeStruct((per_group, per_group * len(steps)), jnp.bfloat16)] * 2,
         compiler_params=params,
-        cost_estimate=pl.CostEstimate(flops=8900000000, bytes_accessed=4 * projected.size, transcendentals=0),
+        cost_estimate=pl.CostEstimate(flops=9000000000, bytes_accessed=4 * projected.size, transcendentals=0),
         name="couple",
     )(projected, *others)
 
 
 def rest_kernel(count, t_ref, *refs):
-    x_refs, (out_ref, squares_ref) = refs[-2 - count : -2], refs[-2:]
+    x_refs, (out_ref, squares_ref, wide_ref) = refs[-3 - count : -3], refs[-3:]
     per_group, columns = t_ref.shape
     if count:
         weights = refs[0][...], refs[1][...]
@@ -180,17 +180,20 @@
 
     squares = loop(columns, 4, body, jnp.zeros((per_group, 1), jnp.float32))
     spread = jnp.broadcast_to(squares, (per_group, per_group))
-    squares_ref[...] = jnp.sum(jnp.where(diagonal(per_group), spread, 0.0), axis=0, keepdims=True)
+    row = jnp.sum(jnp.where(diagonal(per_group), spread, 0.0), axis=0, keepdims=True)
+    squares_ref[...] = row
+    wide_ref[...] = jnp.broadcast_to(row, wide_ref.shape)
 
 
 def rest_part(partly, weights, blocks):
     return pl.pallas_call(
         functools.partial(rest_kernel, len(blocks)),
         in_specs=[in_vmem] * (1 + len(weights) + len(blocks)),
-        out_specs=[in_vmem, in_vmem],
+        out_specs=[in_vmem] * 3,
         out_shape=[
             jax.ShapeDtypeStruct(partly.shape, jnp.float32),
             jax.ShapeDtypeStruct((1, partly.shape[0]), jnp.float32),
+            jax.ShapeDtypeStruct((8, partly.shape[0]), jnp.float32),
         ],
         compiler_params=params,
         name="rest_part",
@@ -255,7 +258,7 @@
     return parts
 
 
-def flipped_terms(array):
+def flipped_terms(array, wide):
     comp, feat = lax.axis_size("comp"), lax.axis_size("feat")
     if comp % 2 or comp & (comp - 1) or feat & (feat - 1):
         return terms(array, "feat", 2)
@@ -272,7 +275,8 @@
             pairs = [
                 (i * feat + j, (i ^ flip) * feat + (j ^ (k * step))) for i in range(comp) for j in range(feat)
             ]
-            parts.append(lax.ppermute(array, ("comp", "feat"), pairs))
+            farthest = stage == 0 and k == width - 1
+            parts.append(lax.ppermute(wide if farthest else array, ("comp", "feat"), pairs)[:1])
         step *= width
     return parts
 
@@ -298,11 +302,11 @@
         *(pltpu.with_memory_space_constraint(array, pltpu.HBM) for array in (start_vectors, sample))
     )
     if even and comp > 1:
-        blocks[1] = exchange(start_vectors, "comp", 1)
+        blocks[1] = exchange(vectors, "comp", 1)
     parts = terms(projected, "feat", 1)
     projected = sum(parts[1:], parts[0])
     if even:
-        others = {step: exchange(projected, "comp", step) for step in range(1, comp) if step == 1 or step % 2 == 0}
+        others = {step: exchange(projected, "comp", step) for step in range(1, comp, 2)}
     else:
         others = gather(projected)
     near = [1][: comp - 1]
@@ -314,12 +318,13 @@
     partly = first_part(projected, sample, vectors, near, of(others, near), of(blocks, near), features)
     if even:
         for step in range(2, comp, 2):
-            blocks[step], partly = lax.optimization_barrier((blocks[step], partly))
+            blocks[step], others[1] = lax.optimization_barrier((blocks[step], others[1]))
             blocks[step + 1] = exchange(blocks[step], "comp", 1)
-            others[step + 1] = exchange(others[step], "comp", 1)
+            others[step] = exchange(others[step + 1], "comp", 1)
+    projected, partly = lax.optimization_barrier((projected, partly))
     weights = couple(projected, far, of(others, far), rows, features) if far else []
-    updated, squares = rest_part(partly, weights, of(blocks, far))
-    return finish(updated, flipped_terms(squares), features)
+    updated, squares, wide = rest_part(partly, weights, of(blocks, far))
+    return finish(updated, flipped_terms(squares, wide), features)
 
 
 def solution(mesh):

time: 40.4 us -> 38.8 us (0.960)
  waiting for transfers between devices: 18.2 us -> 16.5 us
    ppermute x9, waiting for transfers between devices: 13.2 us -> 12.3 us  [exchange(): lax.ppermute(array, axis, [(i, i ^ step) for i in range(lax.axis_size(axi...]
    ppermute x6, waiting for transfers between devices: 5.04 us -> 4.24 us  [flipped_terms(): lax.ppermute(wide if farthest else array, ('comp', 'feat'), pairs)[:1]]
where the time goes in v16:
time: 38.8 us; the launch traced here: 38.7 us
  waiting for transfers between devices  16.5 us (43%)
  starting transfers between devices  15.7 us (40%)
  Pallas kernels  6.37 us (16%)
    ppermute x9, waiting for transfers between devices, exchange(): lax.ppermute(array, axis, [(i, i ^ step) for i in range(lax.axis_size(axi...  12.3 us
    ppermute x9, starting transfers between devices, exchange(): lax.ppermute(array, axis, [(i, i ^ step) for i in range(lax.axis_size(axi...  9.54 us
    ppermute x6, starting transfers between devices, flipped_terms(): lax.ppermute(wide if farthest else array, ('comp', 'feat'), pairs)[:1]  6.15 us
    ppermute x6, waiting for transfers between devices, flipped_terms(): lax.ppermute(wide if farthest else array, ('comp', 'feat'), pairs)[:1]  4.24 us
    pallas_call x1, Pallas kernels, project(): pl.pallas_call(project_kernel, in_specs=[anywhere] * 2, out_specs=[in_vme...  2.93 us
    pallas_call x1, Pallas kernels, first_part(): pl.pallas_call(functools.partial(first_kernel, features, steps), in_specs...  1.47 us
    pallas_call x1, Pallas kernels, finish(): pl.pallas_call(functools.partial(finish_kernel, features, count), in_spec...  1.08 us
  transfers between devices with their start and end apart: 15, of which 10 were waited for; matrix products, arithmetic and copies ran while one was open for 0% of the time, Pallas kernels for 12%

profile of v16, /device:TPU:0, one launch (start us, length us, event | category | flops | bytes accessed | tf_op | source)
XLA Modules:
  0.0 38.7 jit_solution(17314717386538988615)
XLA Ops:
  0.0 2.9 %collective-permute-start.7 = (f32[64,3584]{1,0:T(8,128)}, f32[64,3584]{1,0:T(8,128)S(1)}, u32[]{:S(2)}, u32[]{:S(2)}) collective-permute-start(f32[64,3584]{1,0:T(8,128)} %x_hbm.1), channel_id=1, source_target_pairs={{0,16},{8,24},{16,0},{24,8},{1,17},{9,25},{17,1},{25,9},{2,18},{10... | collective-permute-start | bytes 2752520 | tf_op jit(solution)/shard_map/ppermute | solution.py:245
  2.9 2.9 %project.1 = (f32[64,256]{1,0:T(8,128)S(1)}, f32[64,3584]{1,0:T(8,128)S(1)}, f32[192,3584]{1,0:T(8,128)S(1)}) custom-call(f32[64,3584]{1,0:T(8,128)} %x_hbm.1, f32[192,3584]{1,0:T(8,128)} %bitcast.1), custom_call_target="tpu_custom_call" | custom-call | tf_op jit(solution)/shard_map/project/pallas_call | solution.py:83
  5.9 0.1 collective-permute-start.4
  6.0 1.6 %collective-permute-start = (f32[64,256]{1,0:T(8,128)S(1)}, f32[64,256]{1,0:T(8,128)S(1)}, u32[]{:S(2)}, u32[]{:S(2)}) collective-permute-start(f32[64,256]{1,0:T(8,128)S(1)} %get-tuple-element.16), channel_id=1, source_target_pairs={{0,1},{1,0},{2,3},{3,2},{4,5},{5,4},{6,7},{7,6},{8,9},{9,8},{10,11... | collective-permute-start | bytes 196616 | tf_op jit(solution)/shard_map/ppermute | solution.py:245
  7.5 2.9 %collective-permute-done = f32[64,256]{1,0:T(8,128)S(1)} collective-permute-done((f32[64,256]{1,0:T(8,128)S(1)}, f32[64,256]{1,0:T(8,128)S(1)}, u32[]{:S(2)}, u32[]{:S(2)}) %collective-permute-start) | collective-permute-done | bytes 65568 | tf_op jit(solution)/shard_map/ppermute | solution.py:245
  10.5 1.6 %collective-permute-start.1 = (f32[64,256]{1,0:T(8,128)S(1)}, f32[64,256]{1,0:T(8,128)S(1)}, u32[]{:S(2)}, u32[]{:S(2)}) collective-permute-start(f32[64,256]{1,0:T(8,128)S(1)} %add.18), channel_id=1, source_target_pairs={{0,2},{1,3},{2,0},{3,1},{4,6},{5,7},{6,4},{7,5},{8,10},{9,11},{10,... | collective-permute-start | bytes 196616 | tf_op jit(solution)/shard_map/ppermute | solution.py:245
  12.1 2.7 %collective-permute-done.1 = f32[64,256]{1,0:T(8,128)S(1)} collective-permute-done((f32[64,256]{1,0:T(8,128)S(1)}, f32[64,256]{1,0:T(8,128)S(1)}, u32[]{:S(2)}, u32[]{:S(2)}) %collective-permute-start.1) | collective-permute-done | bytes 65568 | tf_op jit(solution)/shard_map/ppermute | solution.py:245
  14.8 2.7 %collective-permute-start.2 = (f32[64,256]{1,0:T(8,128)S(1)}, f32[64,256]{1,0:T(8,128)S(1)}, u32[]{:S(2)}, u32[]{:S(2)}) collective-permute-start(f32[64,256]{1,0:T(8,128)S(1)} %add.19), channel_id=1, source_target_pairs={{0,4},{1,5},{2,6},{3,7},{4,0},{5,1},{6,2},{7,3},{8,12},{9,13},{10,... | collective-permute-start | bytes 196616 | tf_op jit(solution)/shard_map/ppermute | solution.py:245
  17.5 2.6 %collective-permute-done.2 = f32[64,256]{1,0:T(8,128)S(1)} collective-permute-done((f32[64,256]{1,0:T(8,128)S(1)}, f32[64,256]{1,0:T(8,128)S(1)}, u32[]{:S(2)}, u32[]{:S(2)}) %collective-permute-start.2) | collective-permute-done | bytes 65568 | tf_op jit(solution)/shard_map/ppermute | solution.py:245
  20.1 0.1 collective-permute-start.3
  20.1 0.4 %collective-permute-start.5 = (f32[64,256]{1,0:T(8,128)S(1)}, f32[64,256]{1,0:T(8,128)S(1)}, u32[]{:S(2)}, u32[]{:S(2)}) collective-permute-start(f32[64,256]{1,0:T(8,128)S(1)} %add.20.p_ref), channel_id=1, source_target_pairs={{0,24},{8,16},{16,8},{24,0},{1,25},{9,17},{17,9},{25,1},{2,26},{10... | collective-permute-start | bytes 196616 | tf_op jit(solution)/shard_map/ppermute | solution.py:245
  20.6 0.8 %collective-permute-done.3.refs_0_ = f32[64,256]{1,0:T(8,128)S(1)} collective-permute-done((f32[64,256]{1,0:T(8,128)S(1)}, f32[64,256]{1,0:T(8,128)S(1)}, u32[]{:S(2)}, u32[]{:S(2)}) %collective-permute-start.3) | collective-permute-done | bytes 65568 | tf_op jit(solution)/shard_map/ppermute | solution.py:245
  21.4 2.3 %collective-permute-done.7.refs_2_ = f32[64,3584]{1,0:T(8,128)S(1)} collective-permute-done((f32[64,3584]{1,0:T(8,128)}, f32[64,3584]{1,0:T(8,128)S(1)}, u32[]{:S(2)}, u32[]{:S(2)}) %collective-permute-start.7) | collective-permute-done | bytes 917536 | tf_op jit(solution)/shard_map/ppermute | solution.py:245
  23.7 0.0 collective-permute-start.8
  23.7 0.8 %collective-permute-done.5.refs_1_ = f32[64,256]{1,0:T(8,128)S(1)} collective-permute-done((f32[64,256]{1,0:T(8,128)S(1)}, f32[64,256]{1,0:T(8,128)S(1)}, u32[]{:S(2)}, u32[]{:S(2)}) %collective-permute-start.5) | collective-permute-done | bytes 65568 | tf_op jit(solution)/shard_map/ppermute | solution.py:245
  24.6 0.2 collective-permute-start.6
  24.7 0.0 collective-permute-done.4.refs_1_
  24.7 1.5 %first_part.1.t_ref = f32[64,3584]{1,0:T(8,128)S(1)} custom-call(f32[64,256]{1,0:T(8,128)S(1)} %add.20.p_ref, f32[192,3584]{1,0:T(8,128)S(1)} %get-tuple-element.17.s_ref, f32[64,3584]{1,0:T(8,128)S(1)} %get-tuple-element.18.x_ref, f32[64,256]{1,0:T(8,128)S(1)} %collective-permute-done.3.refs_0_, f32[64,3584]{1,0:T(8,128)S(1)} %collective-permute-done.4.refs_1_), custom_call_target="tpu_custom_call" | custom-call | tf_op jit(solution)/shard_map/first_part/pallas_call | solution.py:140
  26.2 0.1 collective-permute-done.6.refs_0_
  26.3 0.3 couple.1
  26.6 0.0 collective-permute-done.8.refs_3_
  26.6 0.6 %rest_part.1 = (f32[64,3584]{1,0:T(8,128)S(1)}, f32[1,64]{1,0:T(1,128)S(1)}, f32[8,64]{1,0:T(8,128)S(1)}) custom-call(f32[64,3584]{1,0:T(8,128)S(1)} %first_part.1.t_ref, bf16[64,128]{1,0:T(8,128)(2,1)S(1)} %get-tuple-element.21.refs_0_, bf16[64,128]{1,0:T(8,128)(2,1)S(1)} %get-tuple-element.22.refs_1_, f32[64,3584]{1,0:T(8,128)S(1)} %collective-permute-done.7.refs_2_, ...), custom_call_target="tpu_custom_call" | custom-call | tf_op jit(solution)/shard_map/rest_part/pallas_call | solution.py:189
  27.2 2.8 %collective-permute-start.12 = (f32[8,64]{1,0:T(8,128)S(1)}, f32[8,64]{1,0:T(8,128)S(1)}, u32[]{:S(2)}, u32[]{:S(2)}) collective-permute-start(f32[8,64]{1,0:T(8,128)S(1)} %get-tuple-element.26), channel_id=1, source_target_pairs={{0,11},{1,10},{2,9},{3,8},{4,15},{5,14},{6,13},{7,12},{8,3},{9,2},... | collective-permute-start | bytes 6152 | tf_op jit(solution)/shard_map/ppermute | solution.py:279
  30.0 0.5 %collective-permute-start.10 = (f32[1,64]{1,0:T(1,128)S(1)}, f32[1,64]{1,0:T(1,128)S(1)}, u32[]{:S(2)}, u32[]{:S(2)}) collective-permute-start(f32[1,64]{1,0:T(1,128)S(1)} %get-tuple-element.25), channel_id=1, source_target_pairs={{0,9},{1,8},{2,11},{3,10},{4,13},{5,12},{6,15},{7,14},{8,1},{9,0},... | collective-permute-start | bytes 776 | tf_op jit(solution)/shard_map/ppermute | solution.py:279
  30.5 0.1 collective-permute-start.11
  30.7 0.2 collective-permute-start.9
  30.8 2.2 %collective-permute-done.10 = f32[1,64]{1,0:T(1,128)S(1)} collective-permute-done((f32[1,64]{1,0:T(1,128)S(1)}, f32[1,64]{1,0:T(1,128)S(1)}, u32[]{:S(2)}, u32[]{:S(2)}) %collective-permute-start.10) | collective-permute-done | bytes 288 | tf_op jit(solution)/shard_map/ppermute | solution.py:279
  33.0 0.5 %collective-permute-done.11 = f32[1,64]{1,0:T(1,128)S(1)} collective-permute-done((f32[1,64]{1,0:T(1,128)S(1)}, f32[1,64]{1,0:T(1,128)S(1)}, u32[]{:S(2)}, u32[]{:S(2)}) %collective-permute-start.11) | collective-permute-done | bytes 288 | tf_op jit(solution)/shard_map/ppermute | solution.py:279
  33.5 0.0 collective-permute-done.9
  33.5 0.0 collective-permute-done.12
  33.5 0.2 collective-permute-start.13
  33.7 2.3 %collective-permute-start.14 = (f32[1,64]{1,0:T(1,128)S(1)}, f32[1,64]{1,0:T(1,128)S(1)}, u32[]{:S(2)}, u32[]{:S(2)}) collective-permute-start(f32[1,64]{1,0:T(1,128)S(1)} %slice_add_fusion), channel_id=1, source_target_pairs={{0,12},{1,13},{2,14},{3,15},{4,8},{5,9},{6,10},{7,11},{8,4},{9,5},... | collective-permute-start | bytes 776 | tf_op jit(solution)/shard_map/ppermute | solution.py:279
  36.0 0.0 collective-permute-done.13.refs_0_
  36.0 1.6 %collective-permute-done.14.refs_1_ = f32[1,64]{1,0:T(1,128)S(1)} collective-permute-done((f32[1,64]{1,0:T(1,128)S(1)}, f32[1,64]{1,0:T(1,128)S(1)}, u32[]{:S(2)}, u32[]{:S(2)}) %collective-permute-start.14) | collective-permute-done | bytes 288 | tf_op jit(solution)/shard_map/ppermute | solution.py:279
  37.6 1.1 %finish.1 = f32[64,3584]{1,0:T(8,128)} custom-call(f32[64,3584]{1,0:T(8,128)S(1)} %get-tuple-element.24.updated_ref, f32[1,64]{1,0:T(1,128)S(1)} %collective-permute-done.13.refs_0_, f32[1,64]{1,0:T(1,128)S(1)} %collective-permute-done.14.refs_1_), custom_call_target="tpu_custom_call" | custom-call | tf_op jit(solution)/shard_map/finish/pallas_call | solution.py:230
  (4 shorter events, 0.0 us)
Async XLA Ops:
  0.0 23.7 %collective-permute-start.7 = (f32[64,3584]{1,0:T(8,128)}, f32[64,3584]{1,0:T(8,128)S(1)}, u32[]{:S(2)}, u32[]{:S(2)}) collective-permute-start(f32[64,3584]{1,0:T(8,128)} %x_hbm.1), channel_id=1, source_target_pairs={{0,16},{8,24},{16,0},{24,8},{1,17},{9,25},{17,1},{25,9},{2,18},{10... | collective-permute-start | bytes 2752520 | tf_op jit(solution)/shard_map/ppermute | solution.py:245
  5.9 18.8 %collective-permute-start.4 = (f32[64,3584]{1,0:T(8,128)S(1)}, f32[64,3584]{1,0:T(8,128)S(1)}, u32[]{:S(2)}, u32[]{:S(2)}) collective-permute-start(f32[64,3584]{1,0:T(8,128)S(1)} %get-tuple-element.18.x_ref), channel_id=1, source_target_pairs={{0,8},{8,0},{16,24},{24,16},{1,9},{9,1},{17,25},{25,17},{2,10},{10... | collective-permute-start | bytes 2752520 | tf_op jit(solution)/shard_map/ppermute | solution.py:245
  6.0 4.5 %collective-permute-start = (f32[64,256]{1,0:T(8,128)S(1)}, f32[64,256]{1,0:T(8,128)S(1)}, u32[]{:S(2)}, u32[]{:S(2)}) collective-permute-start(f32[64,256]{1,0:T(8,128)S(1)} %get-tuple-element.16), channel_id=1, source_target_pairs={{0,1},{1,0},{2,3},{3,2},{4,5},{5,4},{6,7},{7,6},{8,9},{9,8},{10,11... | collective-permute-start | bytes 196616 | tf_op jit(solution)/shard_map/ppermute | solution.py:245
  10.5 4.3 %collective-permute-start.1 = (f32[64,256]{1,0:T(8,128)S(1)}, f32[64,256]{1,0:T(8,128)S(1)}, u32[]{:S(2)}, u32[]{:S(2)}) collective-permute-start(f32[64,256]{1,0:T(8,128)S(1)} %add.18), channel_id=1, source_target_pairs={{0,2},{1,3},{2,0},{3,1},{4,6},{5,7},{6,4},{7,5},{8,10},{9,11},{10,... | collective-permute-start | bytes 196616 | tf_op jit(solution)/shard_map/ppermute | solution.py:245
  14.8 5.2 %collective-permute-start.2 = (f32[64,256]{1,0:T(8,128)S(1)}, f32[64,256]{1,0:T(8,128)S(1)}, u32[]{:S(2)}, u32[]{:S(2)}) collective-permute-start(f32[64,256]{1,0:T(8,128)S(1)} %add.19), channel_id=1, source_target_pairs={{0,4},{1,5},{2,6},{3,7},{4,0},{5,1},{6,2},{7,3},{8,12},{9,13},{10,... | collective-permute-start | bytes 196616 | tf_op jit(solution)/shard_map/ppermute | solution.py:245
  20.1 1.3 %collective-permute-start.3 = (f32[64,256]{1,0:T(8,128)S(1)}, f32[64,256]{1,0:T(8,128)S(1)}, u32[]{:S(2)}, u32[]{:S(2)}) collective-permute-start(f32[64,256]{1,0:T(8,128)S(1)} %add.20.p_ref), channel_id=1, source_target_pairs={{0,8},{8,0},{16,24},{24,16},{1,9},{9,1},{17,25},{25,17},{2,10},{10... | collective-permute-start | bytes 196616 | tf_op jit(solution)/shard_map/ppermute | solution.py:245
  20.1 4.4 %collective-permute-start.5 = (f32[64,256]{1,0:T(8,128)S(1)}, f32[64,256]{1,0:T(8,128)S(1)}, u32[]{:S(2)}, u32[]{:S(2)}) collective-permute-start(f32[64,256]{1,0:T(8,128)S(1)} %add.20.p_ref), channel_id=1, source_target_pairs={{0,24},{8,16},{16,8},{24,0},{1,25},{9,17},{17,9},{25,1},{2,26},{10... | collective-permute-start | bytes 196616 | tf_op jit(solution)/shard_map/ppermute | solution.py:245
  23.7 2.8 %collective-permute-start.8 = (f32[64,3584]{1,0:T(8,128)S(1)}, f32[64,3584]{1,0:T(8,128)S(1)}, u32[]{:S(2)}, u32[]{:S(2)}) collective-permute-start(f32[64,3584]{1,0:T(8,128)S(1)} %collective-permute-done.7.refs_2_), channel_id=1, source_target_pairs={{0,8},{8,0},{16,24},{24,16},{1,9},{9,1},{17,25},{25,17},{2,10},{10... | collective-permute-start | bytes 2752520 | tf_op jit(solution)/shard_map/ppermute | solution.py:245
  24.6 1.7 %collective-permute-start.6 = (f32[64,256]{1,0:T(8,128)S(1)}, f32[64,256]{1,0:T(8,128)S(1)}, u32[]{:S(2)}, u32[]{:S(2)}) collective-permute-start(f32[64,256]{1,0:T(8,128)S(1)} %collective-permute-done.5.refs_1_), channel_id=1, source_target_pairs={{0,8},{8,0},{16,24},{24,16},{1,9},{9,1},{17,25},{25,17},{2,10},{10... | collective-permute-start | bytes 196616 | tf_op jit(solution)/shard_map/ppermute | solution.py:245
  27.2 6.3 %collective-permute-start.12 = (f32[8,64]{1,0:T(8,128)S(1)}, f32[8,64]{1,0:T(8,128)S(1)}, u32[]{:S(2)}, u32[]{:S(2)}) collective-permute-start(f32[8,64]{1,0:T(8,128)S(1)} %get-tuple-element.26), channel_id=1, source_target_pairs={{0,11},{1,10},{2,9},{3,8},{4,15},{5,14},{6,13},{7,12},{8,3},{9,2},... | collective-permute-start | bytes 6152 | tf_op jit(solution)/shard_map/ppermute | solution.py:279
  30.0 3.0 %collective-permute-start.10 = (f32[1,64]{1,0:T(1,128)S(1)}, f32[1,64]{1,0:T(1,128)S(1)}, u32[]{:S(2)}, u32[]{:S(2)}) collective-permute-start(f32[1,64]{1,0:T(1,128)S(1)} %get-tuple-element.25), channel_id=1, source_target_pairs={{0,9},{1,8},{2,11},{3,10},{4,13},{5,12},{6,15},{7,14},{8,1},{9,0},... | collective-permute-start | bytes 776 | tf_op jit(solution)/shard_map/ppermute | solution.py:279
  30.5 3.0 %collective-permute-start.11 = (f32[1,64]{1,0:T(1,128)S(1)}, f32[1,64]{1,0:T(1,128)S(1)}, u32[]{:S(2)}, u32[]{:S(2)}) collective-permute-start(f32[1,64]{1,0:T(1,128)S(1)} %get-tuple-element.25), channel_id=1, source_target_pairs={{0,10},{1,11},{2,8},{3,9},{4,14},{5,15},{6,12},{7,13},{8,2},{9,3},... | collective-permute-start | bytes 776 | tf_op jit(solution)/shard_map/ppermute | solution.py:279
  30.7 2.8 %collective-permute-start.9 = (f32[1,64]{1,0:T(1,128)S(1)}, f32[1,64]{1,0:T(1,128)S(1)}, u32[]{:S(2)}, u32[]{:S(2)}) collective-permute-start(f32[1,64]{1,0:T(1,128)S(1)} %get-tuple-element.25), channel_id=1, source_target_pairs={{0,8},{1,9},{2,10},{3,11},{4,12},{5,13},{6,14},{7,15},{8,0},{9,1},... | collective-permute-start | bytes 776 | tf_op jit(solution)/shard_map/ppermute | solution.py:279
  33.5 2.5 %collective-permute-start.13 = (f32[1,64]{1,0:T(1,128)S(1)}, f32[1,64]{1,0:T(1,128)S(1)}, u32[]{:S(2)}, u32[]{:S(2)}) collective-permute-start(f32[1,64]{1,0:T(1,128)S(1)} %slice_add_fusion), channel_id=1, source_target_pairs={{0,8},{1,9},{2,10},{3,11},{4,12},{5,13},{6,14},{7,15},{8,0},{9,1},... | collective-permute-start | bytes 776 | tf_op jit(solution)/shard_map/ppermute | solution.py:279
  33.7 3.9 %collective-permute-start.14 = (f32[1,64]{1,0:T(1,128)S(1)}, f32[1,64]{1,0:T(1,128)S(1)}, u32[]{:S(2)}, u32[]{:S(2)}) collective-permute-start(f32[1,64]{1,0:T(1,128)S(1)} %slice_add_fusion), channel_id=1, source_target_pairs={{0,12},{1,13},{2,14},{3,15},{4,8},{5,9},{6,10},{7,11},{8,4},{9,5},... | collective-permute-start | bytes 776 | tf_op jit(solution)/shard_map/ppermute | solution.py:279

commit v17 on v16

--- a/solution.py
+++ b/solution.py
@@ -209,12 +209,12 @@
 def finish_kernel(features, count, updated_ref, *refs):
     squares_refs, (out_ref, scaled, sems) = refs[:count], refs[count:]
     per_group, columns = updated_ref.shape
-    squares = squares_refs[0][...]
+    squares = squares_refs[0][:1]
     for ref in squares_refs[1:]:
-        squares += ref[...]
+        squares += ref[:1]
     spread = jnp.broadcast_to(scale_of(squares, features), (per_group, per_group))
     scale = jnp.sum(jnp.where(diagonal(per_group), spread, 0.0), axis=1, keepdims=True)
-    tile = tile_of(columns, 7)
+    tile = tile_of(columns, 4)
     copies = []
     for i in range(columns // tile):
         here = pl.ds(i * tile, tile)
@@ -234,7 +234,7 @@
         out_shape=jax.ShapeDtypeStruct(updated.shape, jnp.float32),
         scratch_shapes=[
             pltpu.VMEM(updated.shape, jnp.float32),
-            pltpu.SemaphoreType.DMA((updated.shape[1] // tile_of(updated.shape[1], 7),)),
+            pltpu.SemaphoreType.DMA((updated.shape[1] // tile_of(updated.shape[1], 4),)),
         ],
         compiler_params=params,
         name="finish",
@@ -268,15 +268,16 @@
         step *= widths[-1]
     parts, step = [array], 1
     for stage, width in enumerate(widths):
-        array = sum(parts[1:], parts[0])
+        if stage:
+            array = sum((part[:1] for part in parts[1:]), parts[0][:1])
+            wide = jnp.broadcast_to(array, wide.shape)
         flip = int(stage + 1 < len(widths) or len(widths) % 2 == 0)
         parts = [] if flip else [array]
         for k in range(0 if flip else 1, width):
             pairs = [
                 (i * feat + j, (i ^ flip) * feat + (j ^ (k * step))) for i in range(comp) for j in range(feat)
             ]
-            farthest = stage == 0 and k == width - 1
-            parts.append(lax.ppermute(wide if farthest else array, ("comp", "feat"), pairs)[:1])
+            parts.append(lax.ppermute(wide if k == width - 1 else array, ("comp", "feat"), pairs))
         step *= width
     return parts
 

time: 38.8 us -> 38.8 us (level)
  transfers between devices with their start and end apart: 15 -> 15, of which waited for: 10 -> 11; matrix products, arithmetic and copies ran while one was open for 0% -> 0% of each run, Pallas kernels for 12% -> 12%
where the time goes in v17:
time: 38.8 us; the launch traced here: 38.6 us
  waiting for transfers between devices  16.4 us (42%)
  starting transfers between devices  15.7 us (40%)
  Pallas kernels  6.39 us (16%)
    ppermute x9, waiting for transfers between devices, exchange(): lax.ppermute(array, axis, [(i, i ^ step) for i in range(lax.axis_size(axi...  12.3 us
    ppermute x9, starting transfers between devices, exchange(): lax.ppermute(array, axis, [(i, i ^ step) for i in range(lax.axis_size(axi...  9.54 us
    ppermute x6, starting transfers between devices, flipped_terms(): lax.ppermute(wide if k == width - 1 else array, ('comp', 'feat'), pairs)  6.14 us
    ppermute x6, waiting for transfers between devices, flipped_terms(): lax.ppermute(wide if k == width - 1 else array, ('comp', 'feat'), pairs)  4.16 us
    pallas_call x1, Pallas kernels, project(): pl.pallas_call(project_kernel, in_specs=[anywhere] * 2, out_specs=[in_vme...  2.93 us
    pallas_call x1, Pallas kernels, first_part(): pl.pallas_call(functools.partial(first_kernel, features, steps), in_specs...  1.47 us
    pallas_call x1, Pallas kernels, finish(): pl.pallas_call(functools.partial(finish_kernel, features, count), in_spec...  1.1 us
  transfers between devices with their start and end apart: 15, of which 11 were waited for; matrix products, arithmetic and copies ran while one was open for 0% of the time, Pallas kernels for 12%

profile of v17, /device:TPU:0, one launch (start us, length us, event | category | flops | bytes accessed | tf_op | source)
XLA Modules:
  0.0 38.6 jit_solution(6328265314012662349)
XLA Ops:
  0.0 2.9 %collective-permute-start.7 = (f32[64,3584]{1,0:T(8,128)}, f32[64,3584]{1,0:T(8,128)S(1)}, u32[]{:S(2)}, u32[]{:S(2)}) collective-permute-start(f32[64,3584]{1,0:T(8,128)} %x_hbm.1), channel_id=1, source_target_pairs={{0,16},{8,24},{16,0},{24,8},{1,17},{9,25},{17,1},{25,9},{2,18},{10... | collective-permute-start | bytes 2752520 | tf_op jit(solution)/shard_map/ppermute | solution.py:245
  2.9 2.9 %project.1 = (f32[64,256]{1,0:T(8,128)S(1)}, f32[64,3584]{1,0:T(8,128)S(1)}, f32[192,3584]{1,0:T(8,128)S(1)}) custom-call(f32[64,3584]{1,0:T(8,128)} %x_hbm.1, f32[192,3584]{1,0:T(8,128)} %bitcast.2), custom_call_target="tpu_custom_call" | custom-call | tf_op jit(solution)/shard_map/project/pallas_call | solution.py:83
  5.9 0.1 collective-permute-start.4
  6.0 1.6 %collective-permute-start = (f32[64,256]{1,0:T(8,128)S(1)}, f32[64,256]{1,0:T(8,128)S(1)}, u32[]{:S(2)}, u32[]{:S(2)}) collective-permute-start(f32[64,256]{1,0:T(8,128)S(1)} %get-tuple-element.16), channel_id=1, source_target_pairs={{0,1},{1,0},{2,3},{3,2},{4,5},{5,4},{6,7},{7,6},{8,9},{9,8},{10,11... | collective-permute-start | bytes 196616 | tf_op jit(solution)/shard_map/ppermute | solution.py:245
  7.5 2.9 %collective-permute-done = f32[64,256]{1,0:T(8,128)S(1)} collective-permute-done((f32[64,256]{1,0:T(8,128)S(1)}, f32[64,256]{1,0:T(8,128)S(1)}, u32[]{:S(2)}, u32[]{:S(2)}) %collective-permute-start) | collective-permute-done | bytes 65568 | tf_op jit(solution)/shard_map/ppermute | solution.py:245
  10.5 1.6 %collective-permute-start.1 = (f32[64,256]{1,0:T(8,128)S(1)}, f32[64,256]{1,0:T(8,128)S(1)}, u32[]{:S(2)}, u32[]{:S(2)}) collective-permute-start(f32[64,256]{1,0:T(8,128)S(1)} %add.18), channel_id=1, source_target_pairs={{0,2},{1,3},{2,0},{3,1},{4,6},{5,7},{6,4},{7,5},{8,10},{9,11},{10,... | collective-permute-start | bytes 196616 | tf_op jit(solution)/shard_map/ppermute | solution.py:245
  12.1 2.7 %collective-permute-done.1 = f32[64,256]{1,0:T(8,128)S(1)} collective-permute-done((f32[64,256]{1,0:T(8,128)S(1)}, f32[64,256]{1,0:T(8,128)S(1)}, u32[]{:S(2)}, u32[]{:S(2)}) %collective-permute-start.1) | collective-permute-done | bytes 65568 | tf_op jit(solution)/shard_map/ppermute | solution.py:245
  14.8 2.7 %collective-permute-start.2 = (f32[64,256]{1,0:T(8,128)S(1)}, f32[64,256]{1,0:T(8,128)S(1)}, u32[]{:S(2)}, u32[]{:S(2)}) collective-permute-start(f32[64,256]{1,0:T(8,128)S(1)} %add.19), channel_id=1, source_target_pairs={{0,4},{1,5},{2,6},{3,7},{4,0},{5,1},{6,2},{7,3},{8,12},{9,13},{10,... | collective-permute-start | bytes 196616 | tf_op jit(solution)/shard_map/ppermute | solution.py:245
  17.5 2.6 %collective-permute-done.2 = f32[64,256]{1,0:T(8,128)S(1)} collective-permute-done((f32[64,256]{1,0:T(8,128)S(1)}, f32[64,256]{1,0:T(8,128)S(1)}, u32[]{:S(2)}, u32[]{:S(2)}) %collective-permute-start.2) | collective-permute-done | bytes 65568 | tf_op jit(solution)/shard_map/ppermute | solution.py:245
  20.1 0.1 collective-permute-start.3
  20.1 0.4 %collective-permute-start.5 = (f32[64,256]{1,0:T(8,128)S(1)}, f32[64,256]{1,0:T(8,128)S(1)}, u32[]{:S(2)}, u32[]{:S(2)}) collective-permute-start(f32[64,256]{1,0:T(8,128)S(1)} %add.20.p_ref), channel_id=1, source_target_pairs={{0,24},{8,16},{16,8},{24,0},{1,25},{9,17},{17,9},{25,1},{2,26},{10... | collective-permute-start | bytes 196616 | tf_op jit(solution)/shard_map/ppermute | solution.py:245
  20.6 0.8 %collective-permute-done.3.refs_0_ = f32[64,256]{1,0:T(8,128)S(1)} collective-permute-done((f32[64,256]{1,0:T(8,128)S(1)}, f32[64,256]{1,0:T(8,128)S(1)}, u32[]{:S(2)}, u32[]{:S(2)}) %collective-permute-start.3) | collective-permute-done | bytes 65568 | tf_op jit(solution)/shard_map/ppermute | solution.py:245
  21.4 2.3 %collective-permute-done.7.refs_2_ = f32[64,3584]{1,0:T(8,128)S(1)} collective-permute-done((f32[64,3584]{1,0:T(8,128)}, f32[64,3584]{1,0:T(8,128)S(1)}, u32[]{:S(2)}, u32[]{:S(2)}) %collective-permute-start.7) | collective-permute-done | bytes 917536 | tf_op jit(solution)/shard_map/ppermute | solution.py:245
  23.7 0.0 collective-permute-start.8
  23.7 0.8 %collective-permute-done.5.refs_1_ = f32[64,256]{1,0:T(8,128)S(1)} collective-permute-done((f32[64,256]{1,0:T(8,128)S(1)}, f32[64,256]{1,0:T(8,128)S(1)}, u32[]{:S(2)}, u32[]{:S(2)}) %collective-permute-start.5) | collective-permute-done | bytes 65568 | tf_op jit(solution)/shard_map/ppermute | solution.py:245
  24.6 0.2 collective-permute-start.6
  24.7 0.0 collective-permute-done.4.refs_1_
  24.7 1.5 %first_part.1.t_ref = f32[64,3584]{1,0:T(8,128)S(1)} custom-call(f32[64,256]{1,0:T(8,128)S(1)} %add.20.p_ref, f32[192,3584]{1,0:T(8,128)S(1)} %get-tuple-element.17.s_ref, f32[64,3584]{1,0:T(8,128)S(1)} %get-tuple-element.18.x_ref, f32[64,256]{1,0:T(8,128)S(1)} %collective-permute-done.3.refs_0_, f32[64,3584]{1,0:T(8,128)S(1)} %collective-permute-done.4.refs_1_), custom_call_target="tpu_custom_call" | custom-call | tf_op jit(solution)/shard_map/first_part/pallas_call | solution.py:140
  26.2 0.1 collective-permute-done.6.refs_0_
  26.3 0.3 couple.1
  26.6 0.0 collective-permute-done.8.refs_3_
  26.6 0.6 %rest_part.1 = (f32[64,3584]{1,0:T(8,128)S(1)}, f32[1,64]{1,0:T(1,128)S(1)}, f32[8,64]{1,0:T(8,128)S(1)}) custom-call(f32[64,3584]{1,0:T(8,128)S(1)} %first_part.1.t_ref, bf16[64,128]{1,0:T(8,128)(2,1)S(1)} %get-tuple-element.21.refs_0_, bf16[64,128]{1,0:T(8,128)(2,1)S(1)} %get-tuple-element.22.refs_1_, f32[64,3584]{1,0:T(8,128)S(1)} %collective-permute-done.7.refs_2_, ...), custom_call_target="tpu_custom_call" | custom-call | tf_op jit(solution)/shard_map/rest_part/pallas_call | solution.py:189
  27.2 2.8 %collective-permute-start.12 = (f32[8,64]{1,0:T(8,128)S(1)}, f32[8,64]{1,0:T(8,128)S(1)}, u32[]{:S(2)}, u32[]{:S(2)}) collective-permute-start(f32[8,64]{1,0:T(8,128)S(1)} %get-tuple-element.26), channel_id=1, source_target_pairs={{0,11},{1,10},{2,9},{3,8},{4,15},{5,14},{6,13},{7,12},{8,3},{9,2},... | collective-permute-start | bytes 6152 | tf_op jit(solution)/shard_map/ppermute | solution.py:280
  30.0 0.5 %collective-permute-start.10 = (f32[1,64]{1,0:T(1,128)S(1)}, f32[1,64]{1,0:T(1,128)S(1)}, u32[]{:S(2)}, u32[]{:S(2)}) collective-permute-start(f32[1,64]{1,0:T(1,128)S(1)} %get-tuple-element.25), channel_id=1, source_target_pairs={{0,9},{1,8},{2,11},{3,10},{4,13},{5,12},{6,15},{7,14},{8,1},{9,0},... | collective-permute-start | bytes 776 | tf_op jit(solution)/shard_map/ppermute | solution.py:280
  30.5 0.1 collective-permute-start.11
  30.7 0.2 collective-permute-start.9
  30.8 2.2 %collective-permute-done.10 = f32[1,64]{1,0:T(1,128)S(1)} collective-permute-done((f32[1,64]{1,0:T(1,128)S(1)}, f32[1,64]{1,0:T(1,128)S(1)}, u32[]{:S(2)}, u32[]{:S(2)}) %collective-permute-start.10) | collective-permute-done | bytes 288 | tf_op jit(solution)/shard_map/ppermute | solution.py:280
  33.0 0.5 %collective-permute-done.11 = f32[1,64]{1,0:T(1,128)S(1)} collective-permute-done((f32[1,64]{1,0:T(1,128)S(1)}, f32[1,64]{1,0:T(1,128)S(1)}, u32[]{:S(2)}, u32[]{:S(2)}) %collective-permute-start.11) | collective-permute-done | bytes 288 | tf_op jit(solution)/shard_map/ppermute | solution.py:280
  33.5 0.0 collective-permute-done.9
  33.5 0.0 collective-permute-done.12
  33.5 2.1 %collective-permute-start.14 = (f32[8,64]{1,0:T(8,128)S(1)}, f32[8,64]{1,0:T(8,128)S(1)}, u32[]{:S(2)}, u32[]{:S(2)}) collective-permute-start(f32[8,64]{1,0:T(8,128)S(1)} %broadcast_in_dim.8), channel_id=1, source_target_pairs={{0,12},{1,13},{2,14},{3,15},{4,8},{5,9},{6,10},{7,11},{8,4},{9,5},... | collective-permute-start | bytes 6152 | tf_op jit(solution)/shard_map/ppermute | solution.py:280
  35.6 0.4 %collective-permute-start.13 = (f32[1,64]{1,0:T(1,128)S(1)}, f32[1,64]{1,0:T(1,128)S(1)}, u32[]{:S(2)}, u32[]{:S(2)}) collective-permute-start(f32[1,64]{1,0:T(1,128)S(1)} %slice_add_fusion), channel_id=1, source_target_pairs={{0,8},{1,9},{2,10},{3,11},{4,12},{5,13},{6,14},{7,15},{8,0},{9,1},... | collective-permute-start | bytes 776 | tf_op jit(solution)/shard_map/ppermute | solution.py:280
  36.0 0.8 %collective-permute-done.13.refs_0_ = f32[1,64]{1,0:T(1,128)S(1)} collective-permute-done((f32[1,64]{1,0:T(1,128)S(1)}, f32[1,64]{1,0:T(1,128)S(1)}, u32[]{:S(2)}, u32[]{:S(2)}) %collective-permute-start.13) | collective-permute-done | bytes 288 | tf_op jit(solution)/shard_map/ppermute | solution.py:280
  36.9 0.7 %collective-permute-done.14.refs_1_ = f32[8,64]{1,0:T(8,128)S(1)} collective-permute-done((f32[8,64]{1,0:T(8,128)S(1)}, f32[8,64]{1,0:T(8,128)S(1)}, u32[]{:S(2)}, u32[]{:S(2)}) %collective-permute-start.14) | collective-permute-done | bytes 2080 | tf_op jit(solution)/shard_map/ppermute | solution.py:280
  37.5 1.1 %finish.1 = f32[64,3584]{1,0:T(8,128)} custom-call(f32[64,3584]{1,0:T(8,128)S(1)} %get-tuple-element.24.updated_ref, f32[1,64]{1,0:T(1,128)S(1)} %collective-permute-done.13.refs_0_, f32[8,64]{1,0:T(8,128)S(1)} %collective-permute-done.14.refs_1_), custom_call_target="tpu_custom_call" | custom-call | tf_op jit(solution)/shard_map/finish/pallas_call | solution.py:230
  (5 shorter events, 0.0 us)
Async XLA Ops:
  0.0 23.7 %collective-permute-start.7 = (f32[64,3584]{1,0:T(8,128)}, f32[64,3584]{1,0:T(8,128)S(1)}, u32[]{:S(2)}, u32[]{:S(2)}) collective-permute-start(f32[64,3584]{1,0:T(8,128)} %x_hbm.1), channel_id=1, source_target_pairs={{0,16},{8,24},{16,0},{24,8},{1,17},{9,25},{17,1},{25,9},{2,18},{10... | collective-permute-start | bytes 2752520 | tf_op jit(solution)/shard_map/ppermute | solution.py:245
  5.9 18.8 %collective-permute-start.4 = (f32[64,3584]{1,0:T(8,128)S(1)}, f32[64,3584]{1,0:T(8,128)S(1)}, u32[]{:S(2)}, u32[]{:S(2)}) collective-permute-start(f32[64,3584]{1,0:T(8,128)S(1)} %get-tuple-element.18.x_ref), channel_id=1, source_target_pairs={{0,8},{8,0},{16,24},{24,16},{1,9},{9,1},{17,25},{25,17},{2,10},{10... | collective-permute-start | bytes 2752520 | tf_op jit(solution)/shard_map/ppermute | solution.py:245
  6.0 4.5 %collective-permute-start = (f32[64,256]{1,0:T(8,128)S(1)}, f32[64,256]{1,0:T(8,128)S(1)}, u32[]{:S(2)}, u32[]{:S(2)}) collective-permute-start(f32[64,256]{1,0:T(8,128)S(1)} %get-tuple-element.16), channel_id=1, source_target_pairs={{0,1},{1,0},{2,3},{3,2},{4,5},{5,4},{6,7},{7,6},{8,9},{9,8},{10,11... | collective-permute-start | bytes 196616 | tf_op jit(solution)/shard_map/ppermute | solution.py:245
  10.5 4.3 %collective-permute-start.1 = (f32[64,256]{1,0:T(8,128)S(1)}, f32[64,256]{1,0:T(8,128)S(1)}, u32[]{:S(2)}, u32[]{:S(2)}) collective-permute-start(f32[64,256]{1,0:T(8,128)S(1)} %add.18), channel_id=1, source_target_pairs={{0,2},{1,3},{2,0},{3,1},{4,6},{5,7},{6,4},{7,5},{8,10},{9,11},{10,... | collective-permute-start | bytes 196616 | tf_op jit(solution)/shard_map/ppermute | solution.py:245
  14.8 5.2 %collective-permute-start.2 = (f32[64,256]{1,0:T(8,128)S(1)}, f32[64,256]{1,0:T(8,128)S(1)}, u32[]{:S(2)}, u32[]{:S(2)}) collective-permute-start(f32[64,256]{1,0:T(8,128)S(1)} %add.19), channel_id=1, source_target_pairs={{0,4},{1,5},{2,6},{3,7},{4,0},{5,1},{6,2},{7,3},{8,12},{9,13},{10,... | collective-permute-start | bytes 196616 | tf_op jit(solution)/shard_map/ppermute | solution.py:245
  20.1 1.3 %collective-permute-start.3 = (f32[64,256]{1,0:T(8,128)S(1)}, f32[64,256]{1,0:T(8,128)S(1)}, u32[]{:S(2)}, u32[]{:S(2)}) collective-permute-start(f32[64,256]{1,0:T(8,128)S(1)} %add.20.p_ref), channel_id=1, source_target_pairs={{0,8},{8,0},{16,24},{24,16},{1,9},{9,1},{17,25},{25,17},{2,10},{10... | collective-permute-start | bytes 196616 | tf_op jit(solution)/shard_map/ppermute | solution.py:245
  20.1 4.4 %collective-permute-start.5 = (f32[64,256]{1,0:T(8,128)S(1)}, f32[64,256]{1,0:T(8,128)S(1)}, u32[]{:S(2)}, u32[]{:S(2)}) collective-permute-start(f32[64,256]{1,0:T(8,128)S(1)} %add.20.p_ref), channel_id=1, source_target_pairs={{0,24},{8,16},{16,8},{24,0},{1,25},{9,17},{17,9},{25,1},{2,26},{10... | collective-permute-start | bytes 196616 | tf_op jit(solution)/shard_map/ppermute | solution.py:245
  23.7 2.8 %collective-permute-start.8 = (f32[64,3584]{1,0:T(8,128)S(1)}, f32[64,3584]{1,0:T(8,128)S(1)}, u32[]{:S(2)}, u32[]{:S(2)}) collective-permute-start(f32[64,3584]{1,0:T(8,128)S(1)} %collective-permute-done.7.refs_2_), channel_id=1, source_target_pairs={{0,8},{8,0},{16,24},{24,16},{1,9},{9,1},{17,25},{25,17},{2,10},{10... | collective-permute-start | bytes 2752520 | tf_op jit(solution)/shard_map/ppermute | solution.py:245
  24.6 1.7 %collective-permute-start.6 = (f32[64,256]{1,0:T(8,128)S(1)}, f32[64,256]{1,0:T(8,128)S(1)}, u32[]{:S(2)}, u32[]{:S(2)}) collective-permute-start(f32[64,256]{1,0:T(8,128)S(1)} %collective-permute-done.5.refs_1_), channel_id=1, source_target_pairs={{0,8},{8,0},{16,24},{24,16},{1,9},{9,1},{17,25},{25,17},{2,10},{10... | collective-permute-start | bytes 196616 | tf_op jit(solution)/shard_map/ppermute | solution.py:245
  27.2 6.3 %collective-permute-start.12 = (f32[8,64]{1,0:T(8,128)S(1)}, f32[8,64]{1,0:T(8,128)S(1)}, u32[]{:S(2)}, u32[]{:S(2)}) collective-permute-start(f32[8,64]{1,0:T(8,128)S(1)} %get-tuple-element.26), channel_id=1, source_target_pairs={{0,11},{1,10},{2,9},{3,8},{4,15},{5,14},{6,13},{7,12},{8,3},{9,2},... | collective-permute-start | bytes 6152 | tf_op jit(solution)/shard_map/ppermute | solution.py:280
  30.0 3.0 %collective-permute-start.10 = (f32[1,64]{1,0:T(1,128)S(1)}, f32[1,64]{1,0:T(1,128)S(1)}, u32[]{:S(2)}, u32[]{:S(2)}) collective-permute-start(f32[1,64]{1,0:T(1,128)S(1)} %get-tuple-element.25), channel_id=1, source_target_pairs={{0,9},{1,8},{2,11},{3,10},{4,13},{5,12},{6,15},{7,14},{8,1},{9,0},... | collective-permute-start | bytes 776 | tf_op jit(solution)/shard_map/ppermute | solution.py:280
  30.5 3.0 %collective-permute-start.11 = (f32[1,64]{1,0:T(1,128)S(1)}, f32[1,64]{1,0:T(1,128)S(1)}, u32[]{:S(2)}, u32[]{:S(2)}) collective-permute-start(f32[1,64]{1,0:T(1,128)S(1)} %get-tuple-element.25), channel_id=1, source_target_pairs={{0,10},{1,11},{2,8},{3,9},{4,14},{5,15},{6,12},{7,13},{8,2},{9,3},... | collective-permute-start | bytes 776 | tf_op jit(solution)/shard_map/ppermute | solution.py:280
  30.7 2.8 %collective-permute-start.9 = (f32[1,64]{1,0:T(1,128)S(1)}, f32[1,64]{1,0:T(1,128)S(1)}, u32[]{:S(2)}, u32[]{:S(2)}) collective-permute-start(f32[1,64]{1,0:T(1,128)S(1)} %get-tuple-element.25), channel_id=1, source_target_pairs={{0,8},{1,9},{2,10},{3,11},{4,12},{5,13},{6,14},{7,15},{8,0},{9,1},... | collective-permute-start | bytes 776 | tf_op jit(solution)/shard_map/ppermute | solution.py:280
  33.5 4.0 %collective-permute-start.14 = (f32[8,64]{1,0:T(8,128)S(1)}, f32[8,64]{1,0:T(8,128)S(1)}, u32[]{:S(2)}, u32[]{:S(2)}) collective-permute-start(f32[8,64]{1,0:T(8,128)S(1)} %broadcast_in_dim.8), channel_id=1, source_target_pairs={{0,12},{1,13},{2,14},{3,15},{4,8},{5,9},{6,10},{7,11},{8,4},{9,5},... | collective-permute-start | bytes 6152 | tf_op jit(solution)/shard_map/ppermute | solution.py:280
  35.6 1.2 %collective-permute-start.13 = (f32[1,64]{1,0:T(1,128)S(1)}, f32[1,64]{1,0:T(1,128)S(1)}, u32[]{:S(2)}, u32[]{:S(2)}) collective-permute-start(f32[1,64]{1,0:T(1,128)S(1)} %slice_add_fusion), channel_id=1, source_target_pairs={{0,8},{1,9},{2,10},{3,11},{4,12},{5,13},{6,14},{7,15},{8,0},{9,1},... | collective-permute-start | bytes 776 | tf_op jit(solution)/shard_map/ppermute | solution.py:280

commit v18 on v17

--- a/solution.py
+++ b/solution.py
@@ -43,7 +43,21 @@
 
 def loop(columns, most, body, init):
     tile = tile_of(columns, most)
-    return lax.fori_loop(0, columns // tile, lambda i, c: body(i, pl.ds(pl.multiple_of(i * tile, tile), tile), c), init, unroll=True)
+    for i in range(columns // tile):
+        init = body(i, pl.ds(i * tile, tile), init)
+    return init
+
+
+def squares_by_lane(array):
+    squares = array * array
+    if array.shape[1] % lanes:
+        return jnp.sum(squares, axis=1, keepdims=True)
+    return sum(squares[:, k : k + lanes] for k in range(0, array.shape[1], lanes))
+
+
+def relay_pieces(columns):
+    first = columns // lanes // 2 * lanes + lanes
+    return [(start, stop) for start, stop in ((0, first), (first, columns)) if start < stop <= columns]
 
 
 def project_kernel(x_hbm, s_hbm, out_ref, x_ref, s_ref, sems):
@@ -67,11 +81,11 @@
         x = x_ref[:, here]
         projected, squares = carry
         projected += product(x, s_ref[:, here], transposed=True)
-        return projected, squares + jnp.sum(x * x, axis=1, keepdims=True)
+        return projected, squares + squares_by_lane(x)
 
     loop(columns, 4, begin, 0)
-    zeros = jnp.zeros((per_group, rows), jnp.float32), jnp.zeros((per_group, 1), jnp.float32)
-    projected, squares = loop(columns, 4, body, zeros)
+    projected, squares = loop(columns, 4, body, (0.0, 0.0))
+    squares = jnp.sum(squares, axis=1, keepdims=True)
     out_ref[:, :rows] = projected
     out_ref[:, rows:] = jnp.broadcast_to(squares, (per_group, out_ref.shape[1] - rows))
 
@@ -160,25 +174,34 @@
         out_specs=[in_vmem] * 2,
         out_shape=[jax.ShapeDtypeStruct((per_group, per_group * len(steps)), jnp.bfloat16)] * 2,
         compiler_params=params,
-        cost_estimate=pl.CostEstimate(flops=9000000000, bytes_accessed=4 * projected.size, transcendentals=0),
+        cost_estimate=pl.CostEstimate(flops=4250000000, bytes_accessed=4 * projected.size, transcendentals=0),
         name="couple",
     )(projected, *others)
 
 
-def rest_kernel(count, t_ref, *refs):
-    x_refs, (out_ref, squares_ref, wide_ref) = refs[-3 - count : -3], refs[-3:]
+def rest_kernel(pieces, t_ref, *refs):
+    refs, (out_ref, squares_ref, wide_ref) = list(refs[:-3]), refs[-3:]
     per_group, columns = t_ref.shape
-    if count:
-        weights = refs[0][...], refs[1][...]
+    if pieces:
+        weights = refs.pop(0)[...], refs.pop(0)[...]
+    held = [[(*edges, refs.pop(0)) for edges in ranges] for ranges in pieces]
+
+    def part(ranges, here):
+        columns = []
+        for start, stop, ref in ranges:
+            first, last = max(start, here.start), min(stop, here.start + here.size)
+            if first < last:
+                columns.append(ref[:, first - start : last - start])
+        return columns[0] if len(columns) == 1 else jnp.concatenate(columns, axis=1)
 
     def body(i, here, squares):
         updated = t_ref[:, here]
-        if count:
-            updated += product(weights, jnp.concatenate([ref[:, here] for ref in x_refs], axis=0))
+        if pieces:
+            updated += product(weights, jnp.concatenate([part(ranges, here) for ranges in held], axis=0))
         out_ref[:, here] = updated
-        return squares + jnp.sum(updated * updated, axis=1, keepdims=True)
-
-    squares = loop(columns, 4, body, jnp.zeros((per_group, 1), jnp.float32))
+        return squares + squares_by_lane(updated)
+
+    squares = jnp.sum(loop(columns, 4, body, 0.0), axis=1, keepdims=True)
     spread = jnp.broadcast_to(squares, (per_group, per_group))
     row = jnp.sum(jnp.where(diagonal(per_group), spread, 0.0), axis=0, keepdims=True)
     squares_ref[...] = row
@@ -186,8 +209,13 @@
 
 
 def rest_part(partly, weights, blocks):
-    return pl.pallas_call(
-        functools.partial(rest_kernel, len(blocks)),
+    pieces = []
+    for block in blocks:
+        edges = [sum(piece.shape[1] for piece in block[:k]) for k in range(len(block) + 1)]
+        pieces.append(list(zip(edges[:-1], edges[1:])))
+    blocks = [piece for block in blocks for piece in block]
+    return pl.pallas_call(
+        functools.partial(rest_kernel, pieces),
         in_specs=[in_vmem] * (1 + len(weights) + len(blocks)),
         out_specs=[in_vmem] * 3,
         out_shape=[
@@ -320,11 +348,12 @@
     if even:
         for step in range(2, comp, 2):
             blocks[step], others[1] = lax.optimization_barrier((blocks[step], others[1]))
-            blocks[step + 1] = exchange(blocks[step], "comp", 1)
+            vectors = blocks[step]
+            blocks[step + 1] = [exchange(vectors[:, i:j], "comp", 1) for i, j in relay_pieces(vectors.shape[1])]
             others[step] = exchange(others[step + 1], "comp", 1)
     projected, partly = lax.optimization_barrier((projected, partly))
     weights = couple(projected, far, of(others, far), rows, features) if far else []
-    updated, squares, wide = rest_part(partly, weights, of(blocks, far))
+    updated, squares, wide = rest_part(partly, weights, [b if isinstance(b, list) else [b] for b in of(blocks, far)])
     return finish(updated, flipped_terms(squares, wide), features)
 
 

time: 38.8 us -> 39 us (level)
  starting transfers between devices: 15.7 us -> 16.2 us
    ppermute x9 -> x10, starting transfers between devices: 9.54 us -> 10 us  [exchange(): lax.ppermute(array, axis, [(i, i ^ step) for i in range(lax.axis_size(axi...]
    ppermute x9 -> x10, waiting for transfers between devices: 12.3 us -> 12.1 us  [exchange(): lax.ppermute(array, axis, [(i, i ^ step) for i in range(lax.axis_size(axi...]
  transfers between devices with their start and end apart: 15 -> 16, of which waited for: 11 -> 11; matrix products, arithmetic and copies ran while one was open for 0% -> 0% of each run, Pallas kernels for 12% -> 12%
where the time goes in v18:
time: 39 us; the launch traced here: 38.9 us
  starting transfers between devices  16.2 us (42%)
  waiting for transfers between devices  16.1 us (41%)
  Pallas kernels  6.4 us (16%)
    ppermute x10, waiting for transfers between devices, exchange(): lax.ppermute(array, axis, [(i, i ^ step) for i in range(lax.axis_size(axi...  12.1 us
    ppermute x10, starting transfers between devices, exchange(): lax.ppermute(array, axis, [(i, i ^ step) for i in range(lax.axis_size(axi...  10 us
    ppermute x6, starting transfers between devices, flipped_terms(): lax.ppermute(wide if k == width - 1 else array, ('comp', 'feat'), pairs)  6.21 us
    ppermute x6, waiting for transfers between devices, flipped_terms(): lax.ppermute(wide if k == width - 1 else array, ('comp', 'feat'), pairs)  3.99 us
    pallas_call x1, Pallas kernels, project(): pl.pallas_call(project_kernel, in_specs=[anywhere] * 2, out_specs=[in_vme...  2.94 us
    pallas_call x1, Pallas kernels, first_part(): pl.pallas_call(functools.partial(first_kernel, features, steps), in_specs...  1.47 us
    pallas_call x1, Pallas kernels, finish(): pl.pallas_call(functools.partial(finish_kernel, features, count), in_spec...  1.1 us
  transfers between devices with their start and end apart: 16, of which 11 were waited for; matrix products, arithmetic and copies ran while one was open for 0% of the time, Pallas kernels for 12%

profile of v18, /device:TPU:0, one launch (start us, length us, event | category | flops | bytes accessed | tf_op | source)
XLA Modules:
  0.0 38.9 jit_solution(1485190959337066280)
XLA Ops:
  0.0 2.9 %collective-permute-start.7 = (f32[64,3584]{1,0:T(8,128)}, f32[64,3584]{1,0:T(8,128)S(1)}, u32[]{:S(2)}, u32[]{:S(2)}) collective-permute-start(f32[64,3584]{1,0:T(8,128)} %x_hbm.1), channel_id=1, source_target_pairs={{0,16},{8,24},{16,0},{24,8},{1,17},{9,25},{17,1},{25,9},{2,18},{10... | collective-permute-start | bytes 2752520 | tf_op jit(solution)/shard_map/ppermute | solution.py:273
  2.9 2.9 %project.1 = (f32[64,256]{1,0:T(8,128)S(1)}, f32[64,3584]{1,0:T(8,128)S(1)}, f32[192,3584]{1,0:T(8,128)S(1)}) custom-call(f32[64,3584]{1,0:T(8,128)} %x_hbm.1, f32[192,3584]{1,0:T(8,128)} %bitcast.2), custom_call_target="tpu_custom_call" | custom-call | tf_op jit(solution)/shard_map/project/pallas_call | solution.py:97
  5.9 0.1 collective-permute-start.4
  6.0 1.6 %collective-permute-start = (f32[64,256]{1,0:T(8,128)S(1)}, f32[64,256]{1,0:T(8,128)S(1)}, u32[]{:S(2)}, u32[]{:S(2)}) collective-permute-start(f32[64,256]{1,0:T(8,128)S(1)} %get-tuple-element.16), channel_id=1, source_target_pairs={{0,1},{1,0},{2,3},{3,2},{4,5},{5,4},{6,7},{7,6},{8,9},{9,8},{10,11... | collective-permute-start | bytes 196616 | tf_op jit(solution)/shard_map/ppermute | solution.py:273
  7.6 2.9 %collective-permute-done = f32[64,256]{1,0:T(8,128)S(1)} collective-permute-done((f32[64,256]{1,0:T(8,128)S(1)}, f32[64,256]{1,0:T(8,128)S(1)}, u32[]{:S(2)}, u32[]{:S(2)}) %collective-permute-start) | collective-permute-done | bytes 65568 | tf_op jit(solution)/shard_map/ppermute | solution.py:273
  10.5 1.6 %collective-permute-start.1 = (f32[64,256]{1,0:T(8,128)S(1)}, f32[64,256]{1,0:T(8,128)S(1)}, u32[]{:S(2)}, u32[]{:S(2)}) collective-permute-start(f32[64,256]{1,0:T(8,128)S(1)} %add.18), channel_id=1, source_target_pairs={{0,2},{1,3},{2,0},{3,1},{4,6},{5,7},{6,4},{7,5},{8,10},{9,11},{10,... | collective-permute-start | bytes 196616 | tf_op jit(solution)/shard_map/ppermute | solution.py:273
  12.1 2.7 %collective-permute-done.1 = f32[64,256]{1,0:T(8,128)S(1)} collective-permute-done((f32[64,256]{1,0:T(8,128)S(1)}, f32[64,256]{1,0:T(8,128)S(1)}, u32[]{:S(2)}, u32[]{:S(2)}) %collective-permute-start.1) | collective-permute-done | bytes 65568 | tf_op jit(solution)/shard_map/ppermute | solution.py:273
  14.8 2.7 %collective-permute-start.2 = (f32[64,256]{1,0:T(8,128)S(1)}, f32[64,256]{1,0:T(8,128)S(1)}, u32[]{:S(2)}, u32[]{:S(2)}) collective-permute-start(f32[64,256]{1,0:T(8,128)S(1)} %add.19), channel_id=1, source_target_pairs={{0,4},{1,5},{2,6},{3,7},{4,0},{5,1},{6,2},{7,3},{8,12},{9,13},{10,... | collective-permute-start | bytes 196616 | tf_op jit(solution)/shard_map/ppermute | solution.py:273
  17.5 2.6 %collective-permute-done.2 = f32[64,256]{1,0:T(8,128)S(1)} collective-permute-done((f32[64,256]{1,0:T(8,128)S(1)}, f32[64,256]{1,0:T(8,128)S(1)}, u32[]{:S(2)}, u32[]{:S(2)}) %collective-permute-start.2) | collective-permute-done | bytes 65568 | tf_op jit(solution)/shard_map/ppermute | solution.py:273
  20.1 0.1 collective-permute-start.3
  20.2 0.4 %collective-permute-start.5 = (f32[64,256]{1,0:T(8,128)S(1)}, f32[64,256]{1,0:T(8,128)S(1)}, u32[]{:S(2)}, u32[]{:S(2)}) collective-permute-start(f32[64,256]{1,0:T(8,128)S(1)} %add.20.p_ref), channel_id=1, source_target_pairs={{0,24},{8,16},{16,8},{24,0},{1,25},{9,17},{17,9},{25,1},{2,26},{10... | collective-permute-start | bytes 196616 | tf_op jit(solution)/shard_map/ppermute | solution.py:273
  20.6 0.8 %collective-permute-done.3.refs_0_ = f32[64,256]{1,0:T(8,128)S(1)} collective-permute-done((f32[64,256]{1,0:T(8,128)S(1)}, f32[64,256]{1,0:T(8,128)S(1)}, u32[]{:S(2)}, u32[]{:S(2)}) %collective-permute-start.3) | collective-permute-done | bytes 65568 | tf_op jit(solution)/shard_map/ppermute | solution.py:273
  21.4 2.3 %collective-permute-done.7.refs_2_ = f32[64,3584]{1,0:T(8,128)S(1)} collective-permute-done((f32[64,3584]{1,0:T(8,128)}, f32[64,3584]{1,0:T(8,128)S(1)}, u32[]{:S(2)}, u32[]{:S(2)}) %collective-permute-start.7) | collective-permute-done | bytes 917536 | tf_op jit(solution)/shard_map/ppermute | solution.py:273
  23.7 0.1 collective-permute-start.8
  23.8 0.7 %collective-permute-done.5.refs_1_ = f32[64,256]{1,0:T(8,128)S(1)} collective-permute-done((f32[64,256]{1,0:T(8,128)S(1)}, f32[64,256]{1,0:T(8,128)S(1)}, u32[]{:S(2)}, u32[]{:S(2)}) %collective-permute-start.5) | collective-permute-done | bytes 65568 | tf_op jit(solution)/shard_map/ppermute | solution.py:273
  24.6 0.2 collective-permute-start.6
  24.8 0.4 %collective-permute-start.9 = (f32[64,1664]{1,0:T(8,128)S(1)}, f32[64,1664]{1,0:T(8,128)S(1)}, u32[]{:S(2)}, u32[]{:S(2)}) collective-permute-start(f32[64,1664]{1,0:T(8,128)S(1)} %slice.10), channel_id=1, source_target_pairs={{0,8},{8,0},{16,24},{24,16},{1,9},{9,1},{17,25},{25,17},{2,10},{10... | collective-permute-start | bytes 1277960 | tf_op jit(solution)/shard_map/ppermute | solution.py:273
  25.2 0.0 collective-permute-done.4.refs_1_
  25.2 1.5 %first_part.1.t_ref = f32[64,3584]{1,0:T(8,128)S(1)} custom-call(f32[64,256]{1,0:T(8,128)S(1)} %add.20.p_ref, f32[192,3584]{1,0:T(8,128)S(1)} %get-tuple-element.17.s_ref, f32[64,3584]{1,0:T(8,128)S(1)} %get-tuple-element.18.x_ref, f32[64,256]{1,0:T(8,128)S(1)} %collective-permute-done.3.refs_0_, f32[64,3584]{1,0:T(8,128)S(1)} %collective-permute-done.4.refs_1_), custom_call_target="tpu_custom_call" | custom-call | tf_op jit(solution)/shard_map/first_part/pallas_call | solution.py:154
  26.6 0.0 collective-permute-done.6.refs_0_
  26.7 0.3 couple.1
  26.9 0.0 collective-permute-done.9.refs_4_
  26.9 0.0 collective-permute-done.8.refs_3_
  27.0 0.6 %rest_part.1 = (f32[64,3584]{1,0:T(8,128)S(1)}, f32[1,64]{1,0:T(1,128)S(1)}, f32[8,64]{1,0:T(8,128)S(1)}) custom-call(f32[64,3584]{1,0:T(8,128)S(1)} %first_part.1.t_ref, bf16[64,128]{1,0:T(8,128)(2,1)S(1)} %get-tuple-element.21.refs_0_, bf16[64,128]{1,0:T(8,128)(2,1)S(1)} %get-tuple-element.22.refs_1_, f32[64,3584]{1,0:T(8,128)S(1)} %collective-permute-done.7.refs_2_, ...), custom_call_target="tpu_custom_call" | custom-call | tf_op jit(solution)/shard_map/rest_part/pallas_call | solution.py:217
  27.6 2.6 %collective-permute-start.13 = (f32[8,64]{1,0:T(8,128)S(1)}, f32[8,64]{1,0:T(8,128)S(1)}, u32[]{:S(2)}, u32[]{:S(2)}) collective-permute-start(f32[8,64]{1,0:T(8,128)S(1)} %get-tuple-element.26), channel_id=1, source_target_pairs={{0,11},{1,10},{2,9},{3,8},{4,15},{5,14},{6,13},{7,12},{8,3},{9,2},... | collective-permute-start | bytes 6152 | tf_op jit(solution)/shard_map/ppermute | solution.py:308
  30.2 0.2 collective-permute-start.10
  30.4 0.4 %collective-permute-start.11 = (f32[1,64]{1,0:T(1,128)S(1)}, f32[1,64]{1,0:T(1,128)S(1)}, u32[]{:S(2)}, u32[]{:S(2)}) collective-permute-start(f32[1,64]{1,0:T(1,128)S(1)} %get-tuple-element.25), channel_id=1, source_target_pairs={{0,9},{1,8},{2,11},{3,10},{4,13},{5,12},{6,15},{7,14},{8,1},{9,0},... | collective-permute-start | bytes 776 | tf_op jit(solution)/shard_map/ppermute | solution.py:308
  30.8 0.1 collective-permute-start.12
  31.0 0.4 collective-permute-done.10
  31.3 2.0 %collective-permute-done.11 = f32[1,64]{1,0:T(1,128)S(1)} collective-permute-done((f32[1,64]{1,0:T(1,128)S(1)}, f32[1,64]{1,0:T(1,128)S(1)}, u32[]{:S(2)}, u32[]{:S(2)}) %collective-permute-start.11) | collective-permute-done | bytes 288 | tf_op jit(solution)/shard_map/ppermute | solution.py:308
  33.4 0.4 %collective-permute-done.12 = f32[1,64]{1,0:T(1,128)S(1)} collective-permute-done((f32[1,64]{1,0:T(1,128)S(1)}, f32[1,64]{1,0:T(1,128)S(1)}, u32[]{:S(2)}, u32[]{:S(2)}) %collective-permute-start.12) | collective-permute-done | bytes 288 | tf_op jit(solution)/shard_map/ppermute | solution.py:308
  33.8 0.0 collective-permute-done.13
  33.8 2.5 %collective-permute-start.15 = (f32[8,64]{1,0:T(8,128)S(1)}, f32[8,64]{1,0:T(8,128)S(1)}, u32[]{:S(2)}, u32[]{:S(2)}) collective-permute-start(f32[8,64]{1,0:T(8,128)S(1)} %broadcast_in_dim.8), channel_id=1, source_target_pairs={{0,12},{1,13},{2,14},{3,15},{4,8},{5,9},{6,10},{7,11},{8,4},{9,5},... | collective-permute-start | bytes 6152 | tf_op jit(solution)/shard_map/ppermute | solution.py:308
  36.3 0.3 collective-permute-start.14
  36.6 0.8 %collective-permute-done.14.refs_0_ = f32[1,64]{1,0:T(1,128)S(1)} collective-permute-done((f32[1,64]{1,0:T(1,128)S(1)}, f32[1,64]{1,0:T(1,128)S(1)}, u32[]{:S(2)}, u32[]{:S(2)}) %collective-permute-start.14) | collective-permute-done | bytes 288 | tf_op jit(solution)/shard_map/ppermute | solution.py:308
  37.4 0.4 collective-permute-done.15.refs_1_
  37.8 1.1 %finish.1 = f32[64,3584]{1,0:T(8,128)} custom-call(f32[64,3584]{1,0:T(8,128)S(1)} %get-tuple-element.24.updated_ref, f32[1,64]{1,0:T(1,128)S(1)} %collective-permute-done.14.refs_0_, f32[8,64]{1,0:T(8,128)S(1)} %collective-permute-done.15.refs_1_), custom_call_target="tpu_custom_call" | custom-call | tf_op jit(solution)/shard_map/finish/pallas_call | solution.py:258
  (7 shorter events, 0.1 us)
Async XLA Ops:
  0.0 23.7 %collective-permute-start.7 = (f32[64,3584]{1,0:T(8,128)}, f32[64,3584]{1,0:T(8,128)S(1)}, u32[]{:S(2)}, u32[]{:S(2)}) collective-permute-start(f32[64,3584]{1,0:T(8,128)} %x_hbm.1), channel_id=1, source_target_pairs={{0,16},{8,24},{16,0},{24,8},{1,17},{9,25},{17,1},{25,9},{2,18},{10... | collective-permute-start | bytes 2752520 | tf_op jit(solution)/shard_map/ppermute | solution.py:273
  5.9 19.3 %collective-permute-start.4 = (f32[64,3584]{1,0:T(8,128)S(1)}, f32[64,3584]{1,0:T(8,128)S(1)}, u32[]{:S(2)}, u32[]{:S(2)}) collective-permute-start(f32[64,3584]{1,0:T(8,128)S(1)} %get-tuple-element.18.x_ref), channel_id=1, source_target_pairs={{0,8},{8,0},{16,24},{24,16},{1,9},{9,1},{17,25},{25,17},{2,10},{10... | collective-permute-start | bytes 2752520 | tf_op jit(solution)/shard_map/ppermute | solution.py:273
  6.0 4.5 %collective-permute-start = (f32[64,256]{1,0:T(8,128)S(1)}, f32[64,256]{1,0:T(8,128)S(1)}, u32[]{:S(2)}, u32[]{:S(2)}) collective-permute-start(f32[64,256]{1,0:T(8,128)S(1)} %get-tuple-element.16), channel_id=1, source_target_pairs={{0,1},{1,0},{2,3},{3,2},{4,5},{5,4},{6,7},{7,6},{8,9},{9,8},{10,11... | collective-permute-start | bytes 196616 | tf_op jit(solution)/shard_map/ppermute | solution.py:273
  10.5 4.3 %collective-permute-start.1 = (f32[64,256]{1,0:T(8,128)S(1)}, f32[64,256]{1,0:T(8,128)S(1)}, u32[]{:S(2)}, u32[]{:S(2)}) collective-permute-start(f32[64,256]{1,0:T(8,128)S(1)} %add.18), channel_id=1, source_target_pairs={{0,2},{1,3},{2,0},{3,1},{4,6},{5,7},{6,4},{7,5},{8,10},{9,11},{10,... | collective-permute-start | bytes 196616 | tf_op jit(solution)/shard_map/ppermute | solution.py:273
  14.8 5.2 %collective-permute-start.2 = (f32[64,256]{1,0:T(8,128)S(1)}, f32[64,256]{1,0:T(8,128)S(1)}, u32[]{:S(2)}, u32[]{:S(2)}) collective-permute-start(f32[64,256]{1,0:T(8,128)S(1)} %add.19), channel_id=1, source_target_pairs={{0,4},{1,5},{2,6},{3,7},{4,0},{5,1},{6,2},{7,3},{8,12},{9,13},{10,... | collective-permute-start | bytes 196616 | tf_op jit(solution)/shard_map/ppermute | solution.py:273
  20.1 1.3 %collective-permute-start.3 = (f32[64,256]{1,0:T(8,128)S(1)}, f32[64,256]{1,0:T(8,128)S(1)}, u32[]{:S(2)}, u32[]{:S(2)}) collective-permute-start(f32[64,256]{1,0:T(8,128)S(1)} %add.20.p_ref), channel_id=1, source_target_pairs={{0,8},{8,0},{16,24},{24,16},{1,9},{9,1},{17,25},{25,17},{2,10},{10... | collective-permute-start | bytes 196616 | tf_op jit(solution)/shard_map/ppermute | solution.py:273
  20.2 4.4 %collective-permute-start.5 = (f32[64,256]{1,0:T(8,128)S(1)}, f32[64,256]{1,0:T(8,128)S(1)}, u32[]{:S(2)}, u32[]{:S(2)}) collective-permute-start(f32[64,256]{1,0:T(8,128)S(1)} %add.20.p_ref), channel_id=1, source_target_pairs={{0,24},{8,16},{16,8},{24,0},{1,25},{9,17},{17,9},{25,1},{2,26},{10... | collective-permute-start | bytes 196616 | tf_op jit(solution)/shard_map/ppermute | solution.py:273
  23.7 3.2 %collective-permute-start.8 = (f32[64,1920]{1,0:T(8,128)S(1)}, f32[64,1920]{1,0:T(8,128)S(1)}, u32[]{:S(2)}, u32[]{:S(2)}) collective-permute-start(f32[64,1920]{1,0:T(8,128)S(1)} %slice.9), channel_id=1, source_target_pairs={{0,8},{8,0},{16,24},{24,16},{1,9},{9,1},{17,25},{25,17},{2,10},{10... | collective-permute-start | bytes 1474568 | tf_op jit(solution)/shard_map/ppermute | solution.py:273
  24.6 2.1 %collective-permute-start.6 = (f32[64,256]{1,0:T(8,128)S(1)}, f32[64,256]{1,0:T(8,128)S(1)}, u32[]{:S(2)}, u32[]{:S(2)}) collective-permute-start(f32[64,256]{1,0:T(8,128)S(1)} %collective-permute-done.5.refs_1_), channel_id=1, source_target_pairs={{0,8},{8,0},{16,24},{24,16},{1,9},{9,1},{17,25},{25,17},{2,10},{10... | collective-permute-start | bytes 196616 | tf_op jit(solution)/shard_map/ppermute | solution.py:273
  24.8 2.2 %collective-permute-start.9 = (f32[64,1664]{1,0:T(8,128)S(1)}, f32[64,1664]{1,0:T(8,128)S(1)}, u32[]{:S(2)}, u32[]{:S(2)}) collective-permute-start(f32[64,1664]{1,0:T(8,128)S(1)} %slice.10), channel_id=1, source_target_pairs={{0,8},{8,0},{16,24},{24,16},{1,9},{9,1},{17,25},{25,17},{2,10},{10... | collective-permute-start | bytes 1277960 | tf_op jit(solution)/shard_map/ppermute | solution.py:273
  27.6 6.2 %collective-permute-start.13 = (f32[8,64]{1,0:T(8,128)S(1)}, f32[8,64]{1,0:T(8,128)S(1)}, u32[]{:S(2)}, u32[]{:S(2)}) collective-permute-start(f32[8,64]{1,0:T(8,128)S(1)} %get-tuple-element.26), channel_id=1, source_target_pairs={{0,11},{1,10},{2,9},{3,8},{4,15},{5,14},{6,13},{7,12},{8,3},{9,2},... | collective-permute-start | bytes 6152 | tf_op jit(solution)/shard_map/ppermute | solution.py:308
  30.2 1.1 %collective-permute-start.10 = (f32[1,64]{1,0:T(1,128)S(1)}, f32[1,64]{1,0:T(1,128)S(1)}, u32[]{:S(2)}, u32[]{:S(2)}) collective-permute-start(f32[1,64]{1,0:T(1,128)S(1)} %get-tuple-element.25), channel_id=1, source_target_pairs={{0,8},{1,9},{2,10},{3,11},{4,12},{5,13},{6,14},{7,15},{8,0},{9,1},... | collective-permute-start | bytes 776 | tf_op jit(solution)/shard_map/ppermute | solution.py:308
  30.4 3.0 %collective-permute-start.11 = (f32[1,64]{1,0:T(1,128)S(1)}, f32[1,64]{1,0:T(1,128)S(1)}, u32[]{:S(2)}, u32[]{:S(2)}) collective-permute-start(f32[1,64]{1,0:T(1,128)S(1)} %get-tuple-element.25), channel_id=1, source_target_pairs={{0,9},{1,8},{2,11},{3,10},{4,13},{5,12},{6,15},{7,14},{8,1},{9,0},... | collective-permute-start | bytes 776 | tf_op jit(solution)/shard_map/ppermute | solution.py:308
  30.8 3.0 %collective-permute-start.12 = (f32[1,64]{1,0:T(1,128)S(1)}, f32[1,64]{1,0:T(1,128)S(1)}, u32[]{:S(2)}, u32[]{:S(2)}) collective-permute-start(f32[1,64]{1,0:T(1,128)S(1)} %get-tuple-element.25), channel_id=1, source_target_pairs={{0,10},{1,11},{2,8},{3,9},{4,14},{5,15},{6,12},{7,13},{8,2},{9,3},... | collective-permute-start | bytes 776 | tf_op jit(solution)/shard_map/ppermute | solution.py:308
  33.8 4.0 %collective-permute-start.15 = (f32[8,64]{1,0:T(8,128)S(1)}, f32[8,64]{1,0:T(8,128)S(1)}, u32[]{:S(2)}, u32[]{:S(2)}) collective-permute-start(f32[8,64]{1,0:T(8,128)S(1)} %broadcast_in_dim.8), channel_id=1, source_target_pairs={{0,12},{1,13},{2,14},{3,15},{4,8},{5,9},{6,10},{7,11},{8,4},{9,5},... | collective-permute-start | bytes 6152 | tf_op jit(solution)/shard_map/ppermute | solution.py:308
  36.3 1.2 %collective-permute-start.14 = (f32[1,64]{1,0:T(1,128)S(1)}, f32[1,64]{1,0:T(1,128)S(1)}, u32[]{:S(2)}, u32[]{:S(2)}) collective-permute-start(f32[1,64]{1,0:T(1,128)S(1)} %slice_add_fusion), channel_id=1, source_target_pairs={{0,8},{1,9},{2,10},{3,11},{4,12},{5,13},{6,14},{7,15},{8,0},{9,1},... | collective-permute-start | bytes 776 | tf_op jit(solution)/shard_map/ppermute | solution.py:308

commit v19 on v17

--- a/solution.py
+++ b/solution.py
@@ -160,7 +160,7 @@
         out_specs=[in_vmem] * 2,
         out_shape=[jax.ShapeDtypeStruct((per_group, per_group * len(steps)), jnp.bfloat16)] * 2,
         compiler_params=params,
-        cost_estimate=pl.CostEstimate(flops=9000000000, bytes_accessed=4 * projected.size, transcendentals=0),
+        cost_estimate=pl.CostEstimate(flops=8650000000, bytes_accessed=4 * projected.size, transcendentals=0),
         name="couple",
     )(projected, *others)
 
@@ -306,23 +306,25 @@
         blocks[1] = exchange(vectors, "comp", 1)
     parts = terms(projected, "feat", 1)
     projected = sum(parts[1:], parts[0])
-    if even:
-        others = {step: exchange(projected, "comp", step) for step in range(1, comp, 2)}
-    else:
-        others = gather(projected)
-    near = [1][: comp - 1]
-    far = list(range(2, comp))
+    far = list(range(1, comp))
 
     def of(arrays, steps):
         return [arrays[step] for step in steps]
 
-    partly = first_part(projected, sample, vectors, near, of(others, near), of(blocks, near), features)
+    others = {} if even else gather(projected)
     if even:
+        others = {step: exchange(projected, "comp", step) for step in [1][: comp - 1]}
+        others, projected = lax.optimization_barrier((others, projected))
+    partly = first_part(projected, sample, vectors, [], [], [], features)
+    projected, partly = lax.optimization_barrier((projected, partly))
+    if even:
+        others.update({step: exchange(projected, "comp", step) for step in range(3, comp, 2)})
         for step in range(2, comp, 2):
-            blocks[step], others[1] = lax.optimization_barrier((blocks[step], others[1]))
+            blocks[step], partly = lax.optimization_barrier((blocks[step], partly))
             blocks[step + 1] = exchange(blocks[step], "comp", 1)
             others[step] = exchange(others[step + 1], "comp", 1)
-    projected, partly = lax.optimization_barrier((projected, partly))
+    if even and comp > 1:
+        projected, blocks[1] = lax.optimization_barrier((projected, blocks[1]))
     weights = couple(projected, far, of(others, far), rows, features) if far else []
     updated, squares, wide = rest_part(partly, weights, of(blocks, far))
     return finish(updated, flipped_terms(squares, wide), features)

time: 38.8 us -> 40.4 us (1.041)
  waiting for transfers between devices: 16.4 us -> 17.9 us
    ppermute x9, waiting for transfers between devices: 12.3 us -> 14.5 us  [exchange(): lax.ppermute(array, axis, [(i, i ^ step) for i in range(lax.axis_size(axi...]
    ppermute x6, waiting for transfers between devices: 4.16 us -> 3.38 us  [flipped_terms(): lax.ppermute(wide if k == width - 1 else array, ('comp', 'feat'), pairs)]
    ppermute x6, starting transfers between devices: 6.14 us -> 6.75 us  [flipped_terms(): lax.ppermute(wide if k == width - 1 else array, ('comp', 'feat'), pairs)]
  transfers between devices with their start and end apart: 15 -> 15, of which waited for: 11 -> 11; matrix products, arithmetic and copies ran while one was open for 0% -> 0% of each run, Pallas kernels for 12% -> 11%
where the time goes in v19:
time: 40.4 us; the launch traced here: 40.2 us
  waiting for transfers between devices  17.9 us (44%)
  starting transfers between devices  16 us (40%)
  Pallas kernels  6.22 us (15%)
    ppermute x9, waiting for transfers between devices, exchange(): lax.ppermute(array, axis, [(i, i ^ step) for i in range(lax.axis_size(axi...  14.5 us
    ppermute x9, starting transfers between devices, exchange(): lax.ppermute(array, axis, [(i, i ^ step) for i in range(lax.axis_size(axi...  9.25 us
    ppermute x6, starting transfers between devices, flipped_terms(): lax.ppermute(wide if k == width - 1 else array, ('comp', 'feat'), pairs)  6.75 us
    ppermute x6, waiting for transfers between devices, flipped_terms(): lax.ppermute(wide if k == width - 1 else array, ('comp', 'feat'), pairs)  3.38 us
    pallas_call x1, Pallas kernels, project(): pl.pallas_call(project_kernel, in_specs=[anywhere] * 2, out_specs=[in_vme...  2.94 us
    pallas_call x1, Pallas kernels, first_part(): pl.pallas_call(functools.partial(first_kernel, features, steps), in_specs...  1.14 us
    pallas_call x1, Pallas kernels, finish(): pl.pallas_call(functools.partial(finish_kernel, features, count), in_spec...  1.1 us
  transfers between devices with their start and end apart: 15, of which 11 were waited for; matrix products, arithmetic and copies ran while one was open for 0% of the time, Pallas kernels for 11%

profile of v19, /device:TPU:0, one launch (start us, length us, event | category | flops | bytes accessed | tf_op | source)
XLA Modules:
  0.0 40.2 jit_solution(13798095348398262747)
XLA Ops:
  0.0 2.9 %collective-permute-start = (f32[64,3584]{1,0:T(8,128)}, f32[64,3584]{1,0:T(8,128)S(1)}, u32[]{:S(2)}, u32[]{:S(2)}) collective-permute-start(f32[64,3584]{1,0:T(8,128)} %x_hbm.1), channel_id=1, source_target_pairs={{0,16},{8,24},{16,0},{24,8},{1,17},{9,25},{17,1},{25,9},{2,18},{10... | collective-permute-start | bytes 2752520 | tf_op jit(solution)/shard_map/ppermute | solution.py:245
  2.9 2.9 %project.1 = (f32[64,256]{1,0:T(8,128)S(1)}, f32[64,3584]{1,0:T(8,128)S(1)}, f32[192,3584]{1,0:T(8,128)S(1)}) custom-call(f32[64,3584]{1,0:T(8,128)} %x_hbm.1, f32[192,3584]{1,0:T(8,128)} %bitcast.2), custom_call_target="tpu_custom_call" | custom-call | tf_op jit(solution)/shard_map/project/pallas_call | solution.py:83
  5.9 0.1 collective-permute-start.5
  6.0 1.6 %collective-permute-start.1 = (f32[64,256]{1,0:T(8,128)S(1)}, f32[64,256]{1,0:T(8,128)S(1)}, u32[]{:S(2)}, u32[]{:S(2)}) collective-permute-start(f32[64,256]{1,0:T(8,128)S(1)} %get-tuple-element.21), channel_id=1, source_target_pairs={{0,1},{1,0},{2,3},{3,2},{4,5},{5,4},{6,7},{7,6},{8,9},{9,8},{10,11... | collective-permute-start | bytes 196616 | tf_op jit(solution)/shard_map/ppermute | solution.py:245
  7.6 2.9 %collective-permute-done.1 = f32[64,256]{1,0:T(8,128)S(1)} collective-permute-done((f32[64,256]{1,0:T(8,128)S(1)}, f32[64,256]{1,0:T(8,128)S(1)}, u32[]{:S(2)}, u32[]{:S(2)}) %collective-permute-start.1) | collective-permute-done | bytes 65568 | tf_op jit(solution)/shard_map/ppermute | solution.py:245
  10.5 1.6 %collective-permute-start.2 = (f32[64,256]{1,0:T(8,128)S(1)}, f32[64,256]{1,0:T(8,128)S(1)}, u32[]{:S(2)}, u32[]{:S(2)}) collective-permute-start(f32[64,256]{1,0:T(8,128)S(1)} %add.18), channel_id=1, source_target_pairs={{0,2},{1,3},{2,0},{3,1},{4,6},{5,7},{6,4},{7,5},{8,10},{9,11},{10,... | collective-permute-start | bytes 196616 | tf_op jit(solution)/shard_map/ppermute | solution.py:245
  12.1 2.7 %collective-permute-done.2 = f32[64,256]{1,0:T(8,128)S(1)} collective-permute-done((f32[64,256]{1,0:T(8,128)S(1)}, f32[64,256]{1,0:T(8,128)S(1)}, u32[]{:S(2)}, u32[]{:S(2)}) %collective-permute-start.2) | collective-permute-done | bytes 65568 | tf_op jit(solution)/shard_map/ppermute | solution.py:245
  14.8 2.7 %collective-permute-start.3 = (f32[64,256]{1,0:T(8,128)S(1)}, f32[64,256]{1,0:T(8,128)S(1)}, u32[]{:S(2)}, u32[]{:S(2)}) collective-permute-start(f32[64,256]{1,0:T(8,128)S(1)} %add.19), channel_id=1, source_target_pairs={{0,4},{1,5},{2,6},{3,7},{4,0},{5,1},{6,2},{7,3},{8,12},{9,13},{10,... | collective-permute-start | bytes 196616 | tf_op jit(solution)/shard_map/ppermute | solution.py:245
  17.5 2.6 %collective-permute-done.3 = f32[64,256]{1,0:T(8,128)S(1)} collective-permute-done((f32[64,256]{1,0:T(8,128)S(1)}, f32[64,256]{1,0:T(8,128)S(1)}, u32[]{:S(2)}, u32[]{:S(2)}) %collective-permute-start.3) | collective-permute-done | bytes 65568 | tf_op jit(solution)/shard_map/ppermute | solution.py:245
  20.1 0.1 collective-permute-start.4
  20.2 1.2 %collective-permute-done.4.refs_0_ = f32[64,256]{1,0:T(8,128)S(1)} collective-permute-done((f32[64,256]{1,0:T(8,128)S(1)}, f32[64,256]{1,0:T(8,128)S(1)}, u32[]{:S(2)}, u32[]{:S(2)}) %collective-permute-start.4) | collective-permute-done | bytes 65568 | tf_op jit(solution)/shard_map/ppermute | solution.py:245
  21.4 1.1 %first_part.1.t_ref = f32[64,3584]{1,0:T(8,128)S(1)} custom-call(f32[64,256]{1,0:T(8,128)S(1)} %add.20.p_ref, f32[192,3584]{1,0:T(8,128)S(1)} %get-tuple-element.23.s_ref, f32[64,3584]{1,0:T(8,128)S(1)} %get-tuple-element.24.x_ref), custom_call_target="tpu_custom_call" | custom-call | tf_op jit(solution)/shard_map/first_part/pallas_call | solution.py:140
  22.5 0.1 collective-permute-start.6
  22.7 0.8 %collective-permute-done.refs_3_ = f32[64,3584]{1,0:T(8,128)S(1)} collective-permute-done((f32[64,3584]{1,0:T(8,128)}, f32[64,3584]{1,0:T(8,128)S(1)}, u32[]{:S(2)}, u32[]{:S(2)}) %collective-permute-start) | collective-permute-done | bytes 917536 | tf_op jit(solution)/shard_map/ppermute | solution.py:245
  23.5 0.0 collective-permute-start.8
  23.5 3.2 %collective-permute-done.6.refs_2_ = f32[64,256]{1,0:T(8,128)S(1)} collective-permute-done((f32[64,256]{1,0:T(8,128)S(1)}, f32[64,256]{1,0:T(8,128)S(1)}, u32[]{:S(2)}, u32[]{:S(2)}) %collective-permute-start.6) | collective-permute-done | bytes 65568 | tf_op jit(solution)/shard_map/ppermute | solution.py:245
  26.7 0.2 collective-permute-start.7
  26.8 0.0 collective-permute-done.5.refs_2_
  26.8 1.1 %collective-permute-done.7.refs_1_ = f32[64,256]{1,0:T(8,128)S(1)} collective-permute-done((f32[64,256]{1,0:T(8,128)S(1)}, f32[64,256]{1,0:T(8,128)S(1)}, u32[]{:S(2)}, u32[]{:S(2)}) %collective-permute-start.7) | collective-permute-done | bytes 65568 | tf_op jit(solution)/shard_map/ppermute | solution.py:245
  27.9 0.3 couple.1
  28.2 0.0 collective-permute-done.8.refs_4_
  28.2 0.7 %rest_part.1 = (f32[64,3584]{1,0:T(8,128)S(1)}, f32[1,64]{1,0:T(1,128)S(1)}, f32[8,64]{1,0:T(8,128)S(1)}) custom-call(f32[64,3584]{1,0:T(8,128)S(1)} %first_part.1.t_ref, bf16[64,192]{1,0:T(8,128)(2,1)S(1)} %get-tuple-element.30.refs_0_, bf16[64,192]{1,0:T(8,128)(2,1)S(1)} %get-tuple-element.31.refs_1_, f32[64,3584]{1,0:T(8,128)S(1)} %collective-permute-done.5.refs_2_, ...), custom_call_target="tpu_custom_call" | custom-call | tf_op jit(solution)/shard_map/rest_part/pallas_call | solution.py:189
  29.0 2.4 %collective-permute-start.12 = (f32[8,64]{1,0:T(8,128)S(1)}, f32[8,64]{1,0:T(8,128)S(1)}, u32[]{:S(2)}, u32[]{:S(2)}) collective-permute-start(f32[8,64]{1,0:T(8,128)S(1)} %get-tuple-element.36), channel_id=1, source_target_pairs={{0,11},{1,10},{2,9},{3,8},{4,15},{5,14},{6,13},{7,12},{8,3},{9,2},... | collective-permute-start | bytes 6152 | tf_op jit(solution)/shard_map/ppermute | solution.py:280
  31.3 0.5 %collective-permute-start.10 = (f32[1,64]{1,0:T(1,128)S(1)}, f32[1,64]{1,0:T(1,128)S(1)}, u32[]{:S(2)}, u32[]{:S(2)}) collective-permute-start(f32[1,64]{1,0:T(1,128)S(1)} %get-tuple-element.35), channel_id=1, source_target_pairs={{0,9},{1,8},{2,11},{3,10},{4,13},{5,12},{6,15},{7,14},{8,1},{9,0},... | collective-permute-start | bytes 776 | tf_op jit(solution)/shard_map/ppermute | solution.py:280
  31.8 0.2 collective-permute-start.11
  32.0 0.3 collective-permute-start.9
  32.4 1.9 %collective-permute-done.10 = f32[1,64]{1,0:T(1,128)S(1)} collective-permute-done((f32[1,64]{1,0:T(1,128)S(1)}, f32[1,64]{1,0:T(1,128)S(1)}, u32[]{:S(2)}, u32[]{:S(2)}) %collective-permute-start.10) | collective-permute-done | bytes 288 | tf_op jit(solution)/shard_map/ppermute | solution.py:280
  34.3 0.5 %collective-permute-done.11 = f32[1,64]{1,0:T(1,128)S(1)} collective-permute-done((f32[1,64]{1,0:T(1,128)S(1)}, f32[1,64]{1,0:T(1,128)S(1)}, u32[]{:S(2)}, u32[]{:S(2)}) %collective-permute-start.11) | collective-permute-done | bytes 288 | tf_op jit(solution)/shard_map/ppermute | solution.py:280
  34.8 0.0 collective-permute-done.9
  34.8 0.0 collective-permute-done.12
  34.8 3.0 %collective-permute-start.14 = (f32[8,64]{1,0:T(8,128)S(1)}, f32[8,64]{1,0:T(8,128)S(1)}, u32[]{:S(2)}, u32[]{:S(2)}) collective-permute-start(f32[8,64]{1,0:T(8,128)S(1)} %broadcast_in_dim.8), channel_id=1, source_target_pairs={{0,12},{1,13},{2,14},{3,15},{4,8},{5,9},{6,10},{7,11},{8,4},{9,5},... | collective-permute-start | bytes 6152 | tf_op jit(solution)/shard_map/ppermute | solution.py:280
  37.8 0.4 collective-permute-start.13
  38.2 0.8 %collective-permute-done.13.refs_0_ = f32[1,64]{1,0:T(1,128)S(1)} collective-permute-done((f32[1,64]{1,0:T(1,128)S(1)}, f32[1,64]{1,0:T(1,128)S(1)}, u32[]{:S(2)}, u32[]{:S(2)}) %collective-permute-start.13) | collective-permute-done | bytes 288 | tf_op jit(solution)/shard_map/ppermute | solution.py:280
  39.0 0.2 collective-permute-done.14.refs_1_
  39.1 1.1 %finish.1 = f32[64,3584]{1,0:T(8,128)} custom-call(f32[64,3584]{1,0:T(8,128)S(1)} %get-tuple-element.34.updated_ref, f32[1,64]{1,0:T(1,128)S(1)} %collective-permute-done.13.refs_0_, f32[8,64]{1,0:T(8,128)S(1)} %collective-permute-done.14.refs_1_), custom_call_target="tpu_custom_call" | custom-call | tf_op jit(solution)/shard_map/finish/pallas_call | solution.py:230
  (5 shorter events, 0.0 us)
Async XLA Ops:
  0.0 23.5 %collective-permute-start = (f32[64,3584]{1,0:T(8,128)}, f32[64,3584]{1,0:T(8,128)S(1)}, u32[]{:S(2)}, u32[]{:S(2)}) collective-permute-start(f32[64,3584]{1,0:T(8,128)} %x_hbm.1), channel_id=1, source_target_pairs={{0,16},{8,24},{16,0},{24,8},{1,17},{9,25},{17,1},{25,9},{2,18},{10... | collective-permute-start | bytes 2752520 | tf_op jit(solution)/shard_map/ppermute | solution.py:245
  5.9 20.9 %collective-permute-start.5 = (f32[64,3584]{1,0:T(8,128)S(1)}, f32[64,3584]{1,0:T(8,128)S(1)}, u32[]{:S(2)}, u32[]{:S(2)}) collective-permute-start(f32[64,3584]{1,0:T(8,128)S(1)} %get-tuple-element.24.x_ref), channel_id=1, source_target_pairs={{0,8},{8,0},{16,24},{24,16},{1,9},{9,1},{17,25},{25,17},{2,10},{10... | collective-permute-start | bytes 2752520 | tf_op jit(solution)/shard_map/ppermute | solution.py:245
  6.0 4.5 %collective-permute-start.1 = (f32[64,256]{1,0:T(8,128)S(1)}, f32[64,256]{1,0:T(8,128)S(1)}, u32[]{:S(2)}, u32[]{:S(2)}) collective-permute-start(f32[64,256]{1,0:T(8,128)S(1)} %get-tuple-element.21), channel_id=1, source_target_pairs={{0,1},{1,0},{2,3},{3,2},{4,5},{5,4},{6,7},{7,6},{8,9},{9,8},{10,11... | collective-permute-start | bytes 196616 | tf_op jit(solution)/shard_map/ppermute | solution.py:245
  10.5 4.3 %collective-permute-start.2 = (f32[64,256]{1,0:T(8,128)S(1)}, f32[64,256]{1,0:T(8,128)S(1)}, u32[]{:S(2)}, u32[]{:S(2)}) collective-permute-start(f32[64,256]{1,0:T(8,128)S(1)} %add.18), channel_id=1, source_target_pairs={{0,2},{1,3},{2,0},{3,1},{4,6},{5,7},{6,4},{7,5},{8,10},{9,11},{10,... | collective-permute-start | bytes 196616 | tf_op jit(solution)/shard_map/ppermute | solution.py:245
  14.8 5.2 %collective-permute-start.3 = (f32[64,256]{1,0:T(8,128)S(1)}, f32[64,256]{1,0:T(8,128)S(1)}, u32[]{:S(2)}, u32[]{:S(2)}) collective-permute-start(f32[64,256]{1,0:T(8,128)S(1)} %add.19), channel_id=1, source_target_pairs={{0,4},{1,5},{2,6},{3,7},{4,0},{5,1},{6,2},{7,3},{8,12},{9,13},{10,... | collective-permute-start | bytes 196616 | tf_op jit(solution)/shard_map/ppermute | solution.py:245
  20.1 1.3 %collective-permute-start.4 = (f32[64,256]{1,0:T(8,128)S(1)}, f32[64,256]{1,0:T(8,128)S(1)}, u32[]{:S(2)}, u32[]{:S(2)}) collective-permute-start(f32[64,256]{1,0:T(8,128)S(1)} %add.20.p_ref), channel_id=1, source_target_pairs={{0,8},{8,0},{16,24},{24,16},{1,9},{9,1},{17,25},{25,17},{2,10},{10... | collective-permute-start | bytes 196616 | tf_op jit(solution)/shard_map/ppermute | solution.py:245
  22.5 4.1 %collective-permute-start.6 = (f32[64,256]{1,0:T(8,128)S(1)}, f32[64,256]{1,0:T(8,128)S(1)}, u32[]{:S(2)}, u32[]{:S(2)}) collective-permute-start(f32[64,256]{1,0:T(8,128)S(1)} %add.20.p_ref), channel_id=1, source_target_pairs={{0,24},{8,16},{16,8},{24,0},{1,25},{9,17},{17,9},{25,1},{2,26},{10... | collective-permute-start | bytes 196616 | tf_op jit(solution)/shard_map/ppermute | solution.py:245
  23.5 4.7 %collective-permute-start.8 = (f32[64,3584]{1,0:T(8,128)S(1)}, f32[64,3584]{1,0:T(8,128)S(1)}, u32[]{:S(2)}, u32[]{:S(2)}) collective-permute-start(f32[64,3584]{1,0:T(8,128)S(1)} %collective-permute-done.refs_3_), channel_id=1, source_target_pairs={{0,8},{8,0},{16,24},{24,16},{1,9},{9,1},{17,25},{25,17},{2,10},{10... | collective-permute-start | bytes 2752520 | tf_op jit(solution)/shard_map/ppermute | solution.py:245
  26.7 1.3 %collective-permute-start.7 = (f32[64,256]{1,0:T(8,128)S(1)}, f32[64,256]{1,0:T(8,128)S(1)}, u32[]{:S(2)}, u32[]{:S(2)}) collective-permute-start(f32[64,256]{1,0:T(8,128)S(1)} %collective-permute-done.6.refs_2_), channel_id=1, source_target_pairs={{0,8},{8,0},{16,24},{24,16},{1,9},{9,1},{17,25},{25,17},{2,10},{10... | collective-permute-start | bytes 196616 | tf_op jit(solution)/shard_map/ppermute | solution.py:245
  29.0 5.8 %collective-permute-start.12 = (f32[8,64]{1,0:T(8,128)S(1)}, f32[8,64]{1,0:T(8,128)S(1)}, u32[]{:S(2)}, u32[]{:S(2)}) collective-permute-start(f32[8,64]{1,0:T(8,128)S(1)} %get-tuple-element.36), channel_id=1, source_target_pairs={{0,11},{1,10},{2,9},{3,8},{4,15},{5,14},{6,13},{7,12},{8,3},{9,2},... | collective-permute-start | bytes 6152 | tf_op jit(solution)/shard_map/ppermute | solution.py:280
  31.3 3.0 %collective-permute-start.10 = (f32[1,64]{1,0:T(1,128)S(1)}, f32[1,64]{1,0:T(1,128)S(1)}, u32[]{:S(2)}, u32[]{:S(2)}) collective-permute-start(f32[1,64]{1,0:T(1,128)S(1)} %get-tuple-element.35), channel_id=1, source_target_pairs={{0,9},{1,8},{2,11},{3,10},{4,13},{5,12},{6,15},{7,14},{8,1},{9,0},... | collective-permute-start | bytes 776 | tf_op jit(solution)/shard_map/ppermute | solution.py:280
  31.8 3.0 %collective-permute-start.11 = (f32[1,64]{1,0:T(1,128)S(1)}, f32[1,64]{1,0:T(1,128)S(1)}, u32[]{:S(2)}, u32[]{:S(2)}) collective-permute-start(f32[1,64]{1,0:T(1,128)S(1)} %get-tuple-element.35), channel_id=1, source_target_pairs={{0,10},{1,11},{2,8},{3,9},{4,14},{5,15},{6,12},{7,13},{8,2},{9,3},... | collective-permute-start | bytes 776 | tf_op jit(solution)/shard_map/ppermute | solution.py:280
  32.0 2.8 %collective-permute-start.9 = (f32[1,64]{1,0:T(1,128)S(1)}, f32[1,64]{1,0:T(1,128)S(1)}, u32[]{:S(2)}, u32[]{:S(2)}) collective-permute-start(f32[1,64]{1,0:T(1,128)S(1)} %get-tuple-element.35), channel_id=1, source_target_pairs={{0,8},{1,9},{2,10},{3,11},{4,12},{5,13},{6,14},{7,15},{8,0},{9,1},... | collective-permute-start | bytes 776 | tf_op jit(solution)/shard_map/ppermute | solution.py:280
  34.8 4.3 %collective-permute-start.14 = (f32[8,64]{1,0:T(8,128)S(1)}, f32[8,64]{1,0:T(8,128)S(1)}, u32[]{:S(2)}, u32[]{:S(2)}) collective-permute-start(f32[8,64]{1,0:T(8,128)S(1)} %broadcast_in_dim.8), channel_id=1, source_target_pairs={{0,12},{1,13},{2,14},{3,15},{4,8},{5,9},{6,10},{7,11},{8,4},{9,5},... | collective-permute-start | bytes 6152 | tf_op jit(solution)/shard_map/ppermute | solution.py:280
  37.8 1.2 %collective-permute-start.13 = (f32[1,64]{1,0:T(1,128)S(1)}, f32[1,64]{1,0:T(1,128)S(1)}, u32[]{:S(2)}, u32[]{:S(2)}) collective-permute-start(f32[1,64]{1,0:T(1,128)S(1)} %slice_add_fusion), channel_id=1, source_target_pairs={{0,8},{1,9},{2,10},{3,11},{4,12},{5,13},{6,14},{7,15},{8,0},{9,1},... | collective-permute-start | bytes 776 | tf_op jit(solution)/shard_map/ppermute | solution.py:280

commit v20 on v17

--- a/solution.py
+++ b/solution.py
@@ -262,23 +262,20 @@
     comp, feat = lax.axis_size("comp"), lax.axis_size("feat")
     if comp % 2 or comp & (comp - 1) or feat & (feat - 1):
         return terms(array, "feat", 2)
-    widths, step = [], 1
-    while step < feat:
-        widths.append(min(4, feat // step))
-        step *= widths[-1]
-    parts, step = [array], 1
-    for stage, width in enumerate(widths):
+    bits = [1 << b for b in range(feat.bit_length() - 1)]
+    bits = bits[:1] + bits[2:] + bits[1:2]
+    stages = [bits[k : k + 2] for k in range(0, len(bits), 2)]
+    parts = [array]
+    for stage, own in enumerate(stages):
         if stage:
             array = sum((part[:1] for part in parts[1:]), parts[0][:1])
             wide = jnp.broadcast_to(array, wide.shape)
-        flip = int(stage + 1 < len(widths) or len(widths) % 2 == 0)
+        flip = int(stage + 1 < len(stages) or len(stages) % 2 == 0)
         parts = [] if flip else [array]
-        for k in range(0 if flip else 1, width):
-            pairs = [
-                (i * feat + j, (i ^ flip) * feat + (j ^ (k * step))) for i in range(comp) for j in range(feat)
-            ]
-            parts.append(lax.ppermute(wide if k == width - 1 else array, ("comp", "feat"), pairs))
-        step *= width
+        steps = [0, own[0]] + ([own[1], own[0] ^ own[1]] if len(own) > 1 else [])
+        for step in steps if flip else steps[1:]:
+            pairs = [(i * feat + j, (i ^ flip) * feat + (j ^ step)) for i in range(comp) for j in range(feat)]
+            parts.append(lax.ppermute(wide if step == steps[-1] else array, ("comp", "feat"), pairs))
     return parts
 
 

time: 38.8 us -> 39.7 us (1.023)
  waiting for transfers between devices: 16.4 us -> 17.4 us
    ppermute x6, waiting for transfers between devices: 4.16 us -> 5.11 us  [flipped_terms(): lax.ppermute(wide if step == steps[-1] else array, ('comp', 'feat'), pairs)]
where the time goes in v20:
time: 39.7 us; the launch traced here: 39.6 us
  waiting for transfers between devices  17.4 us (44%)
  starting transfers between devices  15.7 us (40%)
  Pallas kernels  6.39 us (16%)
    ppermute x9, waiting for transfers between devices, exchange(): lax.ppermute(array, axis, [(i, i ^ step) for i in range(lax.axis_size(axi...  12.3 us
    ppermute x9, starting transfers between devices, exchange(): lax.ppermute(array, axis, [(i, i ^ step) for i in range(lax.axis_size(axi...  9.54 us
    ppermute x6, starting transfers between devices, flipped_terms(): lax.ppermute(wide if step == steps[-1] else array, ('comp', 'feat'), pairs)  6.14 us
    ppermute x6, waiting for transfers between devices, flipped_terms(): lax.ppermute(wide if step == steps[-1] else array, ('comp', 'feat'), pairs)  5.11 us
    pallas_call x1, Pallas kernels, project(): pl.pallas_call(project_kernel, in_specs=[anywhere] * 2, out_specs=[in_vme...  2.93 us
    pallas_call x1, Pallas kernels, first_part(): pl.pallas_call(functools.partial(first_kernel, features, steps), in_specs...  1.47 us
    pallas_call x1, Pallas kernels, finish(): pl.pallas_call(functools.partial(finish_kernel, features, count), in_spec...  1.1 us
  transfers between devices with their start and end apart: 15, of which 11 were waited for; matrix products, arithmetic and copies ran while one was open for 0% of the time, Pallas kernels for 12%

profile of v20, /device:TPU:0, one launch (start us, length us, event | category | flops | bytes accessed | tf_op | source)
XLA Modules:
  0.0 39.6 jit_solution(9126906242162346725)
XLA Ops:
  0.0 2.9 %collective-permute-start.7 = (f32[64,3584]{1,0:T(8,128)}, f32[64,3584]{1,0:T(8,128)S(1)}, u32[]{:S(2)}, u32[]{:S(2)}) collective-permute-start(f32[64,3584]{1,0:T(8,128)} %x_hbm.1), channel_id=1, source_target_pairs={{0,16},{8,24},{16,0},{24,8},{1,17},{9,25},{17,1},{25,9},{2,18},{10... | collective-permute-start | bytes 2752520 | tf_op jit(solution)/shard_map/ppermute | solution.py:245
  2.9 2.9 %project.1 = (f32[64,256]{1,0:T(8,128)S(1)}, f32[64,3584]{1,0:T(8,128)S(1)}, f32[192,3584]{1,0:T(8,128)S(1)}) custom-call(f32[64,3584]{1,0:T(8,128)} %x_hbm.1, f32[192,3584]{1,0:T(8,128)} %bitcast.2), custom_call_target="tpu_custom_call" | custom-call | tf_op jit(solution)/shard_map/project/pallas_call | solution.py:83
  5.9 0.1 collective-permute-start.4
  6.0 1.6 %collective-permute-start = (f32[64,256]{1,0:T(8,128)S(1)}, f32[64,256]{1,0:T(8,128)S(1)}, u32[]{:S(2)}, u32[]{:S(2)}) collective-permute-start(f32[64,256]{1,0:T(8,128)S(1)} %get-tuple-element.16), channel_id=1, source_target_pairs={{0,1},{1,0},{2,3},{3,2},{4,5},{5,4},{6,7},{7,6},{8,9},{9,8},{10,11... | collective-permute-start | bytes 196616 | tf_op jit(solution)/shard_map/ppermute | solution.py:245
  7.5 2.9 %collective-permute-done = f32[64,256]{1,0:T(8,128)S(1)} collective-permute-done((f32[64,256]{1,0:T(8,128)S(1)}, f32[64,256]{1,0:T(8,128)S(1)}, u32[]{:S(2)}, u32[]{:S(2)}) %collective-permute-start) | collective-permute-done | bytes 65568 | tf_op jit(solution)/shard_map/ppermute | solution.py:245
  10.5 1.6 %collective-permute-start.1 = (f32[64,256]{1,0:T(8,128)S(1)}, f32[64,256]{1,0:T(8,128)S(1)}, u32[]{:S(2)}, u32[]{:S(2)}) collective-permute-start(f32[64,256]{1,0:T(8,128)S(1)} %add.18), channel_id=1, source_target_pairs={{0,2},{1,3},{2,0},{3,1},{4,6},{5,7},{6,4},{7,5},{8,10},{9,11},{10,... | collective-permute-start | bytes 196616 | tf_op jit(solution)/shard_map/ppermute | solution.py:245
  12.1 2.7 %collective-permute-done.1 = f32[64,256]{1,0:T(8,128)S(1)} collective-permute-done((f32[64,256]{1,0:T(8,128)S(1)}, f32[64,256]{1,0:T(8,128)S(1)}, u32[]{:S(2)}, u32[]{:S(2)}) %collective-permute-start.1) | collective-permute-done | bytes 65568 | tf_op jit(solution)/shard_map/ppermute | solution.py:245
  14.8 2.7 %collective-permute-start.2 = (f32[64,256]{1,0:T(8,128)S(1)}, f32[64,256]{1,0:T(8,128)S(1)}, u32[]{:S(2)}, u32[]{:S(2)}) collective-permute-start(f32[64,256]{1,0:T(8,128)S(1)} %add.19), channel_id=1, source_target_pairs={{0,4},{1,5},{2,6},{3,7},{4,0},{5,1},{6,2},{7,3},{8,12},{9,13},{10,... | collective-permute-start | bytes 196616 | tf_op jit(solution)/shard_map/ppermute | solution.py:245
  17.5 2.6 %collective-permute-done.2 = f32[64,256]{1,0:T(8,128)S(1)} collective-permute-done((f32[64,256]{1,0:T(8,128)S(1)}, f32[64,256]{1,0:T(8,128)S(1)}, u32[]{:S(2)}, u32[]{:S(2)}) %collective-permute-start.2) | collective-permute-done | bytes 65568 | tf_op jit(solution)/shard_map/ppermute | solution.py:245
  20.1 0.1 collective-permute-start.3
  20.1 0.4 %collective-permute-start.5 = (f32[64,256]{1,0:T(8,128)S(1)}, f32[64,256]{1,0:T(8,128)S(1)}, u32[]{:S(2)}, u32[]{:S(2)}) collective-permute-start(f32[64,256]{1,0:T(8,128)S(1)} %add.20.p_ref), channel_id=1, source_target_pairs={{0,24},{8,16},{16,8},{24,0},{1,25},{9,17},{17,9},{25,1},{2,26},{10... | collective-permute-start | bytes 196616 | tf_op jit(solution)/shard_map/ppermute | solution.py:245
  20.6 0.8 %collective-permute-done.3.refs_0_ = f32[64,256]{1,0:T(8,128)S(1)} collective-permute-done((f32[64,256]{1,0:T(8,128)S(1)}, f32[64,256]{1,0:T(8,128)S(1)}, u32[]{:S(2)}, u32[]{:S(2)}) %collective-permute-start.3) | collective-permute-done | bytes 65568 | tf_op jit(solution)/shard_map/ppermute | solution.py:245
  21.4 2.3 %collective-permute-done.7.refs_2_ = f32[64,3584]{1,0:T(8,128)S(1)} collective-permute-done((f32[64,3584]{1,0:T(8,128)}, f32[64,3584]{1,0:T(8,128)S(1)}, u32[]{:S(2)}, u32[]{:S(2)}) %collective-permute-start.7) | collective-permute-done | bytes 917536 | tf_op jit(solution)/shard_map/ppermute | solution.py:245
  23.7 0.0 collective-permute-start.8
  23.7 0.8 %collective-permute-done.5.refs_1_ = f32[64,256]{1,0:T(8,128)S(1)} collective-permute-done((f32[64,256]{1,0:T(8,128)S(1)}, f32[64,256]{1,0:T(8,128)S(1)}, u32[]{:S(2)}, u32[]{:S(2)}) %collective-permute-start.5) | collective-permute-done | bytes 65568 | tf_op jit(solution)/shard_map/ppermute | solution.py:245
  24.6 0.2 collective-permute-start.6
  24.7 0.0 collective-permute-done.4.refs_1_
  24.7 1.5 %first_part.1.t_ref = f32[64,3584]{1,0:T(8,128)S(1)} custom-call(f32[64,256]{1,0:T(8,128)S(1)} %add.20.p_ref, f32[192,3584]{1,0:T(8,128)S(1)} %get-tuple-element.17.s_ref, f32[64,3584]{1,0:T(8,128)S(1)} %get-tuple-element.18.x_ref, f32[64,256]{1,0:T(8,128)S(1)} %collective-permute-done.3.refs_0_, f32[64,3584]{1,0:T(8,128)S(1)} %collective-permute-done.4.refs_1_), custom_call_target="tpu_custom_call" | custom-call | tf_op jit(solution)/shard_map/first_part/pallas_call | solution.py:140
  26.2 0.1 collective-permute-done.6.refs_0_
  26.3 0.3 couple.1
  26.6 0.0 collective-permute-done.8.refs_3_
  26.6 0.6 %rest_part.1 = (f32[64,3584]{1,0:T(8,128)S(1)}, f32[1,64]{1,0:T(1,128)S(1)}, f32[8,64]{1,0:T(8,128)S(1)}) custom-call(f32[64,3584]{1,0:T(8,128)S(1)} %first_part.1.t_ref, bf16[64,128]{1,0:T(8,128)(2,1)S(1)} %get-tuple-element.21.refs_0_, bf16[64,128]{1,0:T(8,128)(2,1)S(1)} %get-tuple-element.22.refs_1_, f32[64,3584]{1,0:T(8,128)S(1)} %collective-permute-done.7.refs_2_, ...), custom_call_target="tpu_custom_call" | custom-call | tf_op jit(solution)/shard_map/rest_part/pallas_call | solution.py:189
  27.2 3.8 %collective-permute-start.12 = (f32[8,64]{1,0:T(8,128)S(1)}, f32[8,64]{1,0:T(8,128)S(1)}, u32[]{:S(2)}, u32[]{:S(2)}) collective-permute-start(f32[8,64]{1,0:T(8,128)S(1)} %get-tuple-element.26), channel_id=1, source_target_pairs={{0,13},{1,12},{2,15},{3,14},{4,9},{5,8},{6,11},{7,10},{8,5},{9,4},... | collective-permute-start | bytes 6152 | tf_op jit(solution)/shard_map/ppermute | solution.py:278
  31.0 0.5 %collective-permute-start.10 = (f32[1,64]{1,0:T(1,128)S(1)}, f32[1,64]{1,0:T(1,128)S(1)}, u32[]{:S(2)}, u32[]{:S(2)}) collective-permute-start(f32[1,64]{1,0:T(1,128)S(1)} %get-tuple-element.25), channel_id=1, source_target_pairs={{0,9},{1,8},{2,11},{3,10},{4,13},{5,12},{6,15},{7,14},{8,1},{9,0},... | collective-permute-start | bytes 776 | tf_op jit(solution)/shard_map/ppermute | solution.py:278
  31.5 0.1 collective-permute-start.11
  31.6 0.1 collective-permute-start.9
  31.8 2.2 %collective-permute-done.10 = f32[1,64]{1,0:T(1,128)S(1)} collective-permute-done((f32[1,64]{1,0:T(1,128)S(1)}, f32[1,64]{1,0:T(1,128)S(1)}, u32[]{:S(2)}, u32[]{:S(2)}) %collective-permute-start.10) | collective-permute-done | bytes 288 | tf_op jit(solution)/shard_map/ppermute | solution.py:278
  34.0 1.4 %collective-permute-done.11 = f32[1,64]{1,0:T(1,128)S(1)} collective-permute-done((f32[1,64]{1,0:T(1,128)S(1)}, f32[1,64]{1,0:T(1,128)S(1)}, u32[]{:S(2)}, u32[]{:S(2)}) %collective-permute-start.11) | collective-permute-done | bytes 288 | tf_op jit(solution)/shard_map/ppermute | solution.py:278
  35.3 0.0 collective-permute-done.9
  35.3 0.0 collective-permute-done.12
  35.4 1.1 %collective-permute-start.14 = (f32[8,64]{1,0:T(8,128)S(1)}, f32[8,64]{1,0:T(8,128)S(1)}, u32[]{:S(2)}, u32[]{:S(2)}) collective-permute-start(f32[8,64]{1,0:T(8,128)S(1)} %broadcast_in_dim.8), channel_id=1, source_target_pairs={{0,10},{1,11},{2,8},{3,9},{4,14},{5,15},{6,12},{7,13},{8,2},{9,3},... | collective-permute-start | bytes 6152 | tf_op jit(solution)/shard_map/ppermute | solution.py:278
  36.5 0.4 %collective-permute-start.13 = (f32[1,64]{1,0:T(1,128)S(1)}, f32[1,64]{1,0:T(1,128)S(1)}, u32[]{:S(2)}, u32[]{:S(2)}) collective-permute-start(f32[1,64]{1,0:T(1,128)S(1)} %slice_add_fusion), channel_id=1, source_target_pairs={{0,8},{1,9},{2,10},{3,11},{4,12},{5,13},{6,14},{7,15},{8,0},{9,1},... | collective-permute-start | bytes 776 | tf_op jit(solution)/shard_map/ppermute | solution.py:278
  36.9 0.8 %collective-permute-done.13.refs_0_ = f32[1,64]{1,0:T(1,128)S(1)} collective-permute-done((f32[1,64]{1,0:T(1,128)S(1)}, f32[1,64]{1,0:T(1,128)S(1)}, u32[]{:S(2)}, u32[]{:S(2)}) %collective-permute-start.13) | collective-permute-done | bytes 288 | tf_op jit(solution)/shard_map/ppermute | solution.py:278
  37.8 0.7 %collective-permute-done.14.refs_1_ = f32[8,64]{1,0:T(8,128)S(1)} collective-permute-done((f32[8,64]{1,0:T(8,128)S(1)}, f32[8,64]{1,0:T(8,128)S(1)}, u32[]{:S(2)}, u32[]{:S(2)}) %collective-permute-start.14) | collective-permute-done | bytes 2080 | tf_op jit(solution)/shard_map/ppermute | solution.py:278
  38.5 1.1 %finish.1 = f32[64,3584]{1,0:T(8,128)} custom-call(f32[64,3584]{1,0:T(8,128)S(1)} %get-tuple-element.24.updated_ref, f32[1,64]{1,0:T(1,128)S(1)} %collective-permute-done.13.refs_0_, f32[8,64]{1,0:T(8,128)S(1)} %collective-permute-done.14.refs_1_), custom_call_target="tpu_custom_call" | custom-call | tf_op jit(solution)/shard_map/finish/pallas_call | solution.py:230
  (5 shorter events, 0.0 us)
Async XLA Ops:
  0.0 23.7 %collective-permute-start.7 = (f32[64,3584]{1,0:T(8,128)}, f32[64,3584]{1,0:T(8,128)S(1)}, u32[]{:S(2)}, u32[]{:S(2)}) collective-permute-start(f32[64,3584]{1,0:T(8,128)} %x_hbm.1), channel_id=1, source_target_pairs={{0,16},{8,24},{16,0},{24,8},{1,17},{9,25},{17,1},{25,9},{2,18},{10... | collective-permute-start | bytes 2752520 | tf_op jit(solution)/shard_map/ppermute | solution.py:245
  5.9 18.8 %collective-permute-start.4 = (f32[64,3584]{1,0:T(8,128)S(1)}, f32[64,3584]{1,0:T(8,128)S(1)}, u32[]{:S(2)}, u32[]{:S(2)}) collective-permute-start(f32[64,3584]{1,0:T(8,128)S(1)} %get-tuple-element.18.x_ref), channel_id=1, source_target_pairs={{0,8},{8,0},{16,24},{24,16},{1,9},{9,1},{17,25},{25,17},{2,10},{10... | collective-permute-start | bytes 2752520 | tf_op jit(solution)/shard_map/ppermute | solution.py:245
  6.0 4.5 %collective-permute-start = (f32[64,256]{1,0:T(8,128)S(1)}, f32[64,256]{1,0:T(8,128)S(1)}, u32[]{:S(2)}, u32[]{:S(2)}) collective-permute-start(f32[64,256]{1,0:T(8,128)S(1)} %get-tuple-element.16), channel_id=1, source_target_pairs={{0,1},{1,0},{2,3},{3,2},{4,5},{5,4},{6,7},{7,6},{8,9},{9,8},{10,11... | collective-permute-start | bytes 196616 | tf_op jit(solution)/shard_map/ppermute | solution.py:245
  10.5 4.3 %collective-permute-start.1 = (f32[64,256]{1,0:T(8,128)S(1)}, f32[64,256]{1,0:T(8,128)S(1)}, u32[]{:S(2)}, u32[]{:S(2)}) collective-permute-start(f32[64,256]{1,0:T(8,128)S(1)} %add.18), channel_id=1, source_target_pairs={{0,2},{1,3},{2,0},{3,1},{4,6},{5,7},{6,4},{7,5},{8,10},{9,11},{10,... | collective-permute-start | bytes 196616 | tf_op jit(solution)/shard_map/ppermute | solution.py:245
  14.8 5.2 %collective-permute-start.2 = (f32[64,256]{1,0:T(8,128)S(1)}, f32[64,256]{1,0:T(8,128)S(1)}, u32[]{:S(2)}, u32[]{:S(2)}) collective-permute-start(f32[64,256]{1,0:T(8,128)S(1)} %add.19), channel_id=1, source_target_pairs={{0,4},{1,5},{2,6},{3,7},{4,0},{5,1},{6,2},{7,3},{8,12},{9,13},{10,... | collective-permute-start | bytes 196616 | tf_op jit(solution)/shard_map/ppermute | solution.py:245
  20.1 1.3 %collective-permute-start.3 = (f32[64,256]{1,0:T(8,128)S(1)}, f32[64,256]{1,0:T(8,128)S(1)}, u32[]{:S(2)}, u32[]{:S(2)}) collective-permute-start(f32[64,256]{1,0:T(8,128)S(1)} %add.20.p_ref), channel_id=1, source_target_pairs={{0,8},{8,0},{16,24},{24,16},{1,9},{9,1},{17,25},{25,17},{2,10},{10... | collective-permute-start | bytes 196616 | tf_op jit(solution)/shard_map/ppermute | solution.py:245
  20.1 4.4 %collective-permute-start.5 = (f32[64,256]{1,0:T(8,128)S(1)}, f32[64,256]{1,0:T(8,128)S(1)}, u32[]{:S(2)}, u32[]{:S(2)}) collective-permute-start(f32[64,256]{1,0:T(8,128)S(1)} %add.20.p_ref), channel_id=1, source_target_pairs={{0,24},{8,16},{16,8},{24,0},{1,25},{9,17},{17,9},{25,1},{2,26},{10... | collective-permute-start | bytes 196616 | tf_op jit(solution)/shard_map/ppermute | solution.py:245
  23.7 2.8 %collective-permute-start.8 = (f32[64,3584]{1,0:T(8,128)S(1)}, f32[64,3584]{1,0:T(8,128)S(1)}, u32[]{:S(2)}, u32[]{:S(2)}) collective-permute-start(f32[64,3584]{1,0:T(8,128)S(1)} %collective-permute-done.7.refs_2_), channel_id=1, source_target_pairs={{0,8},{8,0},{16,24},{24,16},{1,9},{9,1},{17,25},{25,17},{2,10},{10... | collective-permute-start | bytes 2752520 | tf_op jit(solution)/shard_map/ppermute | solution.py:245
  24.6 1.7 %collective-permute-start.6 = (f32[64,256]{1,0:T(8,128)S(1)}, f32[64,256]{1,0:T(8,128)S(1)}, u32[]{:S(2)}, u32[]{:S(2)}) collective-permute-start(f32[64,256]{1,0:T(8,128)S(1)} %collective-permute-done.5.refs_1_), channel_id=1, source_target_pairs={{0,8},{8,0},{16,24},{24,16},{1,9},{9,1},{17,25},{25,17},{2,10},{10... | collective-permute-start | bytes 196616 | tf_op jit(solution)/shard_map/ppermute | solution.py:245
  27.2 8.2 %collective-permute-start.12 = (f32[8,64]{1,0:T(8,128)S(1)}, f32[8,64]{1,0:T(8,128)S(1)}, u32[]{:S(2)}, u32[]{:S(2)}) collective-permute-start(f32[8,64]{1,0:T(8,128)S(1)} %get-tuple-element.26), channel_id=1, source_target_pairs={{0,13},{1,12},{2,15},{3,14},{4,9},{5,8},{6,11},{7,10},{8,5},{9,4},... | collective-permute-start | bytes 6152 | tf_op jit(solution)/shard_map/ppermute | solution.py:278
  31.0 3.0 %collective-permute-start.10 = (f32[1,64]{1,0:T(1,128)S(1)}, f32[1,64]{1,0:T(1,128)S(1)}, u32[]{:S(2)}, u32[]{:S(2)}) collective-permute-start(f32[1,64]{1,0:T(1,128)S(1)} %get-tuple-element.25), channel_id=1, source_target_pairs={{0,9},{1,8},{2,11},{3,10},{4,13},{5,12},{6,15},{7,14},{8,1},{9,0},... | collective-permute-start | bytes 776 | tf_op jit(solution)/shard_map/ppermute | solution.py:278
  31.5 3.9 %collective-permute-start.11 = (f32[1,64]{1,0:T(1,128)S(1)}, f32[1,64]{1,0:T(1,128)S(1)}, u32[]{:S(2)}, u32[]{:S(2)}) collective-permute-start(f32[1,64]{1,0:T(1,128)S(1)} %get-tuple-element.25), channel_id=1, source_target_pairs={{0,12},{1,13},{2,14},{3,15},{4,8},{5,9},{6,10},{7,11},{8,4},{9,5},... | collective-permute-start | bytes 776 | tf_op jit(solution)/shard_map/ppermute | solution.py:278
  31.6 3.7 %collective-permute-start.9 = (f32[1,64]{1,0:T(1,128)S(1)}, f32[1,64]{1,0:T(1,128)S(1)}, u32[]{:S(2)}, u32[]{:S(2)}) collective-permute-start(f32[1,64]{1,0:T(1,128)S(1)} %get-tuple-element.25), channel_id=1, source_target_pairs={{0,8},{1,9},{2,10},{3,11},{4,12},{5,13},{6,14},{7,15},{8,0},{9,1},... | collective-permute-start | bytes 776 | tf_op jit(solution)/shard_map/ppermute | solution.py:278
  35.4 3.1 %collective-permute-start.14 = (f32[8,64]{1,0:T(8,128)S(1)}, f32[8,64]{1,0:T(8,128)S(1)}, u32[]{:S(2)}, u32[]{:S(2)}) collective-permute-start(f32[8,64]{1,0:T(8,128)S(1)} %broadcast_in_dim.8), channel_id=1, source_target_pairs={{0,10},{1,11},{2,8},{3,9},{4,14},{5,15},{6,12},{7,13},{8,2},{9,3},... | collective-permute-start | bytes 6152 | tf_op jit(solution)/shard_map/ppermute | solution.py:278
  36.5 1.2 %collective-permute-start.13 = (f32[1,64]{1,0:T(1,128)S(1)}, f32[1,64]{1,0:T(1,128)S(1)}, u32[]{:S(2)}, u32[]{:S(2)}) collective-permute-start(f32[1,64]{1,0:T(1,128)S(1)} %slice_add_fusion), channel_id=1, source_target_pairs={{0,8},{1,9},{2,10},{3,11},{4,12},{5,13},{6,14},{7,15},{8,0},{9,1},... | collective-permute-start | bytes 776 | tf_op jit(solution)/shard_map/ppermute | solution.py:278

commit v21 on v17

--- a/solution.py
+++ b/solution.py
@@ -10,6 +10,7 @@
 step_rate = 0.1
 epsilon = 1e-06
 lanes = 128
+block_rows = 16
 in_vmem = pl.BlockSpec(memory_space=pltpu.VMEM)
 anywhere = pl.BlockSpec(memory_space=pl.ANY)
 params = pltpu.CompilerParams(vmem_limit_bytes=16 << 20)
@@ -214,12 +215,11 @@
         squares += ref[:1]
     spread = jnp.broadcast_to(scale_of(squares, features), (per_group, per_group))
     scale = jnp.sum(jnp.where(diagonal(per_group), spread, 0.0), axis=1, keepdims=True)
-    tile = tile_of(columns, 4)
     copies = []
-    for i in range(columns // tile):
-        here = pl.ds(i * tile, tile)
-        scaled[:, here] = updated_ref[:, here] * scale
-        copies.append(pltpu.make_async_copy(scaled.at[:, here], out_ref.at[:, here], sems.at[i]))
+    for i, first in enumerate(range(0, per_group, block_rows)):
+        here = pl.ds(first, min(block_rows, per_group - first))
+        scaled[here, :] = updated_ref[here, :] * scale[first : first + block_rows]
+        copies.append(pltpu.make_async_copy(scaled.at[here, :], out_ref.at[here, :], sems.at[i]))
         copies[-1].start()
     for copy in copies:
         copy.wait()
@@ -234,7 +234,7 @@
         out_shape=jax.ShapeDtypeStruct(updated.shape, jnp.float32),
         scratch_shapes=[
             pltpu.VMEM(updated.shape, jnp.float32),
-            pltpu.SemaphoreType.DMA((updated.shape[1] // tile_of(updated.shape[1], 4),)),
+            pltpu.SemaphoreType.DMA((-(-updated.shape[0] // block_rows),)),
         ],
         compiler_params=params,
         name="finish",

time: 38.8 us -> 38.7 us (level)
  no operation moved by 1% of the time
where the time goes in v21:
time: 38.7 us; the launch traced here: 38.6 us
  waiting for transfers between devices  16.4 us (42%)
  starting transfers between devices  15.7 us (41%)
  Pallas kernels  6.35 us (16%)
    ppermute x9, waiting for transfers between devices, exchange(): lax.ppermute(array, axis, [(i, i ^ step) for i in range(lax.axis_size(axi...  12.3 us
    ppermute x9, starting transfers between devices, exchange(): lax.ppermute(array, axis, [(i, i ^ step) for i in range(lax.axis_size(axi...  9.54 us
    ppermute x6, starting transfers between devices, flipped_terms(): lax.ppermute(wide if k == width - 1 else array, ('comp', 'feat'), pairs)  6.14 us
    ppermute x6, waiting for transfers between devices, flipped_terms(): lax.ppermute(wide if k == width - 1 else array, ('comp', 'feat'), pairs)  4.16 us
    pallas_call x1, Pallas kernels, project(): pl.pallas_call(project_kernel, in_specs=[anywhere] * 2, out_specs=[in_vme...  2.93 us
    pallas_call x1, Pallas kernels, first_part(): pl.pallas_call(functools.partial(first_kernel, features, steps), in_specs...  1.47 us
    pallas_call x1, Pallas kernels, finish(): pl.pallas_call(functools.partial(finish_kernel, features, count), in_spec...  1.06 us
  transfers between devices with their start and end apart: 15, of which 11 were waited for; matrix products, arithmetic and copies ran while one was open for 0% of the time, Pallas kernels for 12%

profile of v21, /device:TPU:0, one launch (start us, length us, event | category | flops | bytes accessed | tf_op | source)
XLA Modules:
  0.0 38.6 jit_solution(14785748377304988742)
XLA Ops:
  0.0 2.9 %collective-permute-start.7 = (f32[64,3584]{1,0:T(8,128)}, f32[64,3584]{1,0:T(8,128)S(1)}, u32[]{:S(2)}, u32[]{:S(2)}) collective-permute-start(f32[64,3584]{1,0:T(8,128)} %x_hbm.1), channel_id=1, source_target_pairs={{0,16},{8,24},{16,0},{24,8},{1,17},{9,25},{17,1},{25,9},{2,18},{10... | collective-permute-start | bytes 2752520 | tf_op jit(solution)/shard_map/ppermute | solution.py:245
  2.9 2.9 %project.1 = (f32[64,256]{1,0:T(8,128)S(1)}, f32[64,3584]{1,0:T(8,128)S(1)}, f32[192,3584]{1,0:T(8,128)S(1)}) custom-call(f32[64,3584]{1,0:T(8,128)} %x_hbm.1, f32[192,3584]{1,0:T(8,128)} %bitcast.2), custom_call_target="tpu_custom_call" | custom-call | tf_op jit(solution)/shard_map/project/pallas_call | solution.py:84
  5.9 0.1 collective-permute-start.4
  6.0 1.6 %collective-permute-start = (f32[64,256]{1,0:T(8,128)S(1)}, f32[64,256]{1,0:T(8,128)S(1)}, u32[]{:S(2)}, u32[]{:S(2)}) collective-permute-start(f32[64,256]{1,0:T(8,128)S(1)} %get-tuple-element.16), channel_id=1, source_target_pairs={{0,1},{1,0},{2,3},{3,2},{4,5},{5,4},{6,7},{7,6},{8,9},{9,8},{10,11... | collective-permute-start | bytes 196616 | tf_op jit(solution)/shard_map/ppermute | solution.py:245
  7.5 2.9 %collective-permute-done = f32[64,256]{1,0:T(8,128)S(1)} collective-permute-done((f32[64,256]{1,0:T(8,128)S(1)}, f32[64,256]{1,0:T(8,128)S(1)}, u32[]{:S(2)}, u32[]{:S(2)}) %collective-permute-start) | collective-permute-done | bytes 65568 | tf_op jit(solution)/shard_map/ppermute | solution.py:245
  10.5 1.6 %collective-permute-start.1 = (f32[64,256]{1,0:T(8,128)S(1)}, f32[64,256]{1,0:T(8,128)S(1)}, u32[]{:S(2)}, u32[]{:S(2)}) collective-permute-start(f32[64,256]{1,0:T(8,128)S(1)} %add.18), channel_id=1, source_target_pairs={{0,2},{1,3},{2,0},{3,1},{4,6},{5,7},{6,4},{7,5},{8,10},{9,11},{10,... | collective-permute-start | bytes 196616 | tf_op jit(solution)/shard_map/ppermute | solution.py:245
  12.1 2.7 %collective-permute-done.1 = f32[64,256]{1,0:T(8,128)S(1)} collective-permute-done((f32[64,256]{1,0:T(8,128)S(1)}, f32[64,256]{1,0:T(8,128)S(1)}, u32[]{:S(2)}, u32[]{:S(2)}) %collective-permute-start.1) | collective-permute-done | bytes 65568 | tf_op jit(solution)/shard_map/ppermute | solution.py:245
  14.8 2.7 %collective-permute-start.2 = (f32[64,256]{1,0:T(8,128)S(1)}, f32[64,256]{1,0:T(8,128)S(1)}, u32[]{:S(2)}, u32[]{:S(2)}) collective-permute-start(f32[64,256]{1,0:T(8,128)S(1)} %add.19), channel_id=1, source_target_pairs={{0,4},{1,5},{2,6},{3,7},{4,0},{5,1},{6,2},{7,3},{8,12},{9,13},{10,... | collective-permute-start | bytes 196616 | tf_op jit(solution)/shard_map/ppermute | solution.py:245
  17.5 2.6 %collective-permute-done.2 = f32[64,256]{1,0:T(8,128)S(1)} collective-permute-done((f32[64,256]{1,0:T(8,128)S(1)}, f32[64,256]{1,0:T(8,128)S(1)}, u32[]{:S(2)}, u32[]{:S(2)}) %collective-permute-start.2) | collective-permute-done | bytes 65568 | tf_op jit(solution)/shard_map/ppermute | solution.py:245
  20.1 0.1 collective-permute-start.3
  20.1 0.4 %collective-permute-start.5 = (f32[64,256]{1,0:T(8,128)S(1)}, f32[64,256]{1,0:T(8,128)S(1)}, u32[]{:S(2)}, u32[]{:S(2)}) collective-permute-start(f32[64,256]{1,0:T(8,128)S(1)} %add.20.p_ref), channel_id=1, source_target_pairs={{0,24},{8,16},{16,8},{24,0},{1,25},{9,17},{17,9},{25,1},{2,26},{10... | collective-permute-start | bytes 196616 | tf_op jit(solution)/shard_map/ppermute | solution.py:245
  20.6 0.8 %collective-permute-done.3.refs_0_ = f32[64,256]{1,0:T(8,128)S(1)} collective-permute-done((f32[64,256]{1,0:T(8,128)S(1)}, f32[64,256]{1,0:T(8,128)S(1)}, u32[]{:S(2)}, u32[]{:S(2)}) %collective-permute-start.3) | collective-permute-done | bytes 65568 | tf_op jit(solution)/shard_map/ppermute | solution.py:245
  21.4 2.3 %collective-permute-done.7.refs_2_ = f32[64,3584]{1,0:T(8,128)S(1)} collective-permute-done((f32[64,3584]{1,0:T(8,128)}, f32[64,3584]{1,0:T(8,128)S(1)}, u32[]{:S(2)}, u32[]{:S(2)}) %collective-permute-start.7) | collective-permute-done | bytes 917536 | tf_op jit(solution)/shard_map/ppermute | solution.py:245
  23.7 0.0 collective-permute-start.8
  23.7 0.8 %collective-permute-done.5.refs_1_ = f32[64,256]{1,0:T(8,128)S(1)} collective-permute-done((f32[64,256]{1,0:T(8,128)S(1)}, f32[64,256]{1,0:T(8,128)S(1)}, u32[]{:S(2)}, u32[]{:S(2)}) %collective-permute-start.5) | collective-permute-done | bytes 65568 | tf_op jit(solution)/shard_map/ppermute | solution.py:245
  24.6 0.2 collective-permute-start.6
  24.7 0.0 collective-permute-done.4.refs_1_
  24.7 1.5 %first_part.1.t_ref = f32[64,3584]{1,0:T(8,128)S(1)} custom-call(f32[64,256]{1,0:T(8,128)S(1)} %add.20.p_ref, f32[192,3584]{1,0:T(8,128)S(1)} %get-tuple-element.17.s_ref, f32[64,3584]{1,0:T(8,128)S(1)} %get-tuple-element.18.x_ref, f32[64,256]{1,0:T(8,128)S(1)} %collective-permute-done.3.refs_0_, f32[64,3584]{1,0:T(8,128)S(1)} %collective-permute-done.4.refs_1_), custom_call_target="tpu_custom_call" | custom-call | tf_op jit(solution)/shard_map/first_part/pallas_call | solution.py:141
  26.2 0.1 collective-permute-done.6.refs_0_
  26.3 0.3 couple.1
  26.6 0.0 collective-permute-done.8.refs_3_
  26.6 0.6 %rest_part.1 = (f32[64,3584]{1,0:T(8,128)S(1)}, f32[1,64]{1,0:T(1,128)S(1)}, f32[8,64]{1,0:T(8,128)S(1)}) custom-call(f32[64,3584]{1,0:T(8,128)S(1)} %first_part.1.t_ref, bf16[64,128]{1,0:T(8,128)(2,1)S(1)} %get-tuple-element.21.refs_0_, bf16[64,128]{1,0:T(8,128)(2,1)S(1)} %get-tuple-element.22.refs_1_, f32[64,3584]{1,0:T(8,128)S(1)} %collective-permute-done.7.refs_2_, ...), custom_call_target="tpu_custom_call" | custom-call | tf_op jit(solution)/shard_map/rest_part/pallas_call | solution.py:190
  27.2 2.8 %collective-permute-start.12 = (f32[8,64]{1,0:T(8,128)S(1)}, f32[8,64]{1,0:T(8,128)S(1)}, u32[]{:S(2)}, u32[]{:S(2)}) collective-permute-start(f32[8,64]{1,0:T(8,128)S(1)} %get-tuple-element.26), channel_id=1, source_target_pairs={{0,11},{1,10},{2,9},{3,8},{4,15},{5,14},{6,13},{7,12},{8,3},{9,2},... | collective-permute-start | bytes 6152 | tf_op jit(solution)/shard_map/ppermute | solution.py:280
  30.0 0.5 %collective-permute-start.10 = (f32[1,64]{1,0:T(1,128)S(1)}, f32[1,64]{1,0:T(1,128)S(1)}, u32[]{:S(2)}, u32[]{:S(2)}) collective-permute-start(f32[1,64]{1,0:T(1,128)S(1)} %get-tuple-element.25), channel_id=1, source_target_pairs={{0,9},{1,8},{2,11},{3,10},{4,13},{5,12},{6,15},{7,14},{8,1},{9,0},... | collective-permute-start | bytes 776 | tf_op jit(solution)/shard_map/ppermute | solution.py:280
  30.5 0.1 collective-permute-start.11
  30.7 0.2 collective-permute-start.9
  30.8 2.2 %collective-permute-done.10 = f32[1,64]{1,0:T(1,128)S(1)} collective-permute-done((f32[1,64]{1,0:T(1,128)S(1)}, f32[1,64]{1,0:T(1,128)S(1)}, u32[]{:S(2)}, u32[]{:S(2)}) %collective-permute-start.10) | collective-permute-done | bytes 288 | tf_op jit(solution)/shard_map/ppermute | solution.py:280
  33.0 0.5 %collective-permute-done.11 = f32[1,64]{1,0:T(1,128)S(1)} collective-permute-done((f32[1,64]{1,0:T(1,128)S(1)}, f32[1,64]{1,0:T(1,128)S(1)}, u32[]{:S(2)}, u32[]{:S(2)}) %collective-permute-start.11) | collective-permute-done | bytes 288 | tf_op jit(solution)/shard_map/ppermute | solution.py:280
  33.5 0.0 collective-permute-done.9
  33.5 0.0 collective-permute-done.12
  33.5 2.1 %collective-permute-start.14 = (f32[8,64]{1,0:T(8,128)S(1)}, f32[8,64]{1,0:T(8,128)S(1)}, u32[]{:S(2)}, u32[]{:S(2)}) collective-permute-start(f32[8,64]{1,0:T(8,128)S(1)} %broadcast_in_dim.8), channel_id=1, source_target_pairs={{0,12},{1,13},{2,14},{3,15},{4,8},{5,9},{6,10},{7,11},{8,4},{9,5},... | collective-permute-start | bytes 6152 | tf_op jit(solution)/shard_map/ppermute | solution.py:280
  35.6 0.4 %collective-permute-start.13 = (f32[1,64]{1,0:T(1,128)S(1)}, f32[1,64]{1,0:T(1,128)S(1)}, u32[]{:S(2)}, u32[]{:S(2)}) collective-permute-start(f32[1,64]{1,0:T(1,128)S(1)} %slice_add_fusion), channel_id=1, source_target_pairs={{0,8},{1,9},{2,10},{3,11},{4,12},{5,13},{6,14},{7,15},{8,0},{9,1},... | collective-permute-start | bytes 776 | tf_op jit(solution)/shard_map/ppermute | solution.py:280
  36.0 0.8 %collective-permute-done.13.refs_0_ = f32[1,64]{1,0:T(1,128)S(1)} collective-permute-done((f32[1,64]{1,0:T(1,128)S(1)}, f32[1,64]{1,0:T(1,128)S(1)}, u32[]{:S(2)}, u32[]{:S(2)}) %collective-permute-start.13) | collective-permute-done | bytes 288 | tf_op jit(solution)/shard_map/ppermute | solution.py:280
  36.9 0.7 %collective-permute-done.14.refs_1_ = f32[8,64]{1,0:T(8,128)S(1)} collective-permute-done((f32[8,64]{1,0:T(8,128)S(1)}, f32[8,64]{1,0:T(8,128)S(1)}, u32[]{:S(2)}, u32[]{:S(2)}) %collective-permute-start.14) | collective-permute-done | bytes 2080 | tf_op jit(solution)/shard_map/ppermute | solution.py:280
  37.5 1.1 %finish.1 = f32[64,3584]{1,0:T(8,128)} custom-call(f32[64,3584]{1,0:T(8,128)S(1)} %get-tuple-element.24.updated_ref, f32[1,64]{1,0:T(1,128)S(1)} %collective-permute-done.13.refs_0_, f32[8,64]{1,0:T(8,128)S(1)} %collective-permute-done.14.refs_1_), custom_call_target="tpu_custom_call" | custom-call | tf_op jit(solution)/shard_map/finish/pallas_call | solution.py:230
  (5 shorter events, 0.0 us)
Async XLA Ops:
  0.0 23.7 %collective-permute-start.7 = (f32[64,3584]{1,0:T(8,128)}, f32[64,3584]{1,0:T(8,128)S(1)}, u32[]{:S(2)}, u32[]{:S(2)}) collective-permute-start(f32[64,3584]{1,0:T(8,128)} %x_hbm.1), channel_id=1, source_target_pairs={{0,16},{8,24},{16,0},{24,8},{1,17},{9,25},{17,1},{25,9},{2,18},{10... | collective-permute-start | bytes 2752520 | tf_op jit(solution)/shard_map/ppermute | solution.py:245
  5.9 18.8 %collective-permute-start.4 = (f32[64,3584]{1,0:T(8,128)S(1)}, f32[64,3584]{1,0:T(8,128)S(1)}, u32[]{:S(2)}, u32[]{:S(2)}) collective-permute-start(f32[64,3584]{1,0:T(8,128)S(1)} %get-tuple-element.18.x_ref), channel_id=1, source_target_pairs={{0,8},{8,0},{16,24},{24,16},{1,9},{9,1},{17,25},{25,17},{2,10},{10... | collective-permute-start | bytes 2752520 | tf_op jit(solution)/shard_map/ppermute | solution.py:245
  6.0 4.5 %collective-permute-start = (f32[64,256]{1,0:T(8,128)S(1)}, f32[64,256]{1,0:T(8,128)S(1)}, u32[]{:S(2)}, u32[]{:S(2)}) collective-permute-start(f32[64,256]{1,0:T(8,128)S(1)} %get-tuple-element.16), channel_id=1, source_target_pairs={{0,1},{1,0},{2,3},{3,2},{4,5},{5,4},{6,7},{7,6},{8,9},{9,8},{10,11... | collective-permute-start | bytes 196616 | tf_op jit(solution)/shard_map/ppermute | solution.py:245
  10.5 4.3 %collective-permute-start.1 = (f32[64,256]{1,0:T(8,128)S(1)}, f32[64,256]{1,0:T(8,128)S(1)}, u32[]{:S(2)}, u32[]{:S(2)}) collective-permute-start(f32[64,256]{1,0:T(8,128)S(1)} %add.18), channel_id=1, source_target_pairs={{0,2},{1,3},{2,0},{3,1},{4,6},{5,7},{6,4},{7,5},{8,10},{9,11},{10,... | collective-permute-start | bytes 196616 | tf_op jit(solution)/shard_map/ppermute | solution.py:245
  14.8 5.2 %collective-permute-start.2 = (f32[64,256]{1,0:T(8,128)S(1)}, f32[64,256]{1,0:T(8,128)S(1)}, u32[]{:S(2)}, u32[]{:S(2)}) collective-permute-start(f32[64,256]{1,0:T(8,128)S(1)} %add.19), channel_id=1, source_target_pairs={{0,4},{1,5},{2,6},{3,7},{4,0},{5,1},{6,2},{7,3},{8,12},{9,13},{10,... | collective-permute-start | bytes 196616 | tf_op jit(solution)/shard_map/ppermute | solution.py:245
  20.1 1.3 %collective-permute-start.3 = (f32[64,256]{1,0:T(8,128)S(1)}, f32[64,256]{1,0:T(8,128)S(1)}, u32[]{:S(2)}, u32[]{:S(2)}) collective-permute-start(f32[64,256]{1,0:T(8,128)S(1)} %add.20.p_ref), channel_id=1, source_target_pairs={{0,8},{8,0},{16,24},{24,16},{1,9},{9,1},{17,25},{25,17},{2,10},{10... | collective-permute-start | bytes 196616 | tf_op jit(solution)/shard_map/ppermute | solution.py:245
  20.1 4.4 %collective-permute-start.5 = (f32[64,256]{1,0:T(8,128)S(1)}, f32[64,256]{1,0:T(8,128)S(1)}, u32[]{:S(2)}, u32[]{:S(2)}) collective-permute-start(f32[64,256]{1,0:T(8,128)S(1)} %add.20.p_ref), channel_id=1, source_target_pairs={{0,24},{8,16},{16,8},{24,0},{1,25},{9,17},{17,9},{25,1},{2,26},{10... | collective-permute-start | bytes 196616 | tf_op jit(solution)/shard_map/ppermute | solution.py:245
  23.7 2.8 %collective-permute-start.8 = (f32[64,3584]{1,0:T(8,128)S(1)}, f32[64,3584]{1,0:T(8,128)S(1)}, u32[]{:S(2)}, u32[]{:S(2)}) collective-permute-start(f32[64,3584]{1,0:T(8,128)S(1)} %collective-permute-done.7.refs_2_), channel_id=1, source_target_pairs={{0,8},{8,0},{16,24},{24,16},{1,9},{9,1},{17,25},{25,17},{2,10},{10... | collective-permute-start | bytes 2752520 | tf_op jit(solution)/shard_map/ppermute | solution.py:245
  24.6 1.7 %collective-permute-start.6 = (f32[64,256]{1,0:T(8,128)S(1)}, f32[64,256]{1,0:T(8,128)S(1)}, u32[]{:S(2)}, u32[]{:S(2)}) collective-permute-start(f32[64,256]{1,0:T(8,128)S(1)} %collective-permute-done.5.refs_1_), channel_id=1, source_target_pairs={{0,8},{8,0},{16,24},{24,16},{1,9},{9,1},{17,25},{25,17},{2,10},{10... | collective-permute-start | bytes 196616 | tf_op jit(solution)/shard_map/ppermute | solution.py:245
  27.2 6.3 %collective-permute-start.12 = (f32[8,64]{1,0:T(8,128)S(1)}, f32[8,64]{1,0:T(8,128)S(1)}, u32[]{:S(2)}, u32[]{:S(2)}) collective-permute-start(f32[8,64]{1,0:T(8,128)S(1)} %get-tuple-element.26), channel_id=1, source_target_pairs={{0,11},{1,10},{2,9},{3,8},{4,15},{5,14},{6,13},{7,12},{8,3},{9,2},... | collective-permute-start | bytes 6152 | tf_op jit(solution)/shard_map/ppermute | solution.py:280
  30.0 3.0 %collective-permute-start.10 = (f32[1,64]{1,0:T(1,128)S(1)}, f32[1,64]{1,0:T(1,128)S(1)}, u32[]{:S(2)}, u32[]{:S(2)}) collective-permute-start(f32[1,64]{1,0:T(1,128)S(1)} %get-tuple-element.25), channel_id=1, source_target_pairs={{0,9},{1,8},{2,11},{3,10},{4,13},{5,12},{6,15},{7,14},{8,1},{9,0},... | collective-permute-start | bytes 776 | tf_op jit(solution)/shard_map/ppermute | solution.py:280
  30.5 3.0 %collective-permute-start.11 = (f32[1,64]{1,0:T(1,128)S(1)}, f32[1,64]{1,0:T(1,128)S(1)}, u32[]{:S(2)}, u32[]{:S(2)}) collective-permute-start(f32[1,64]{1,0:T(1,128)S(1)} %get-tuple-element.25), channel_id=1, source_target_pairs={{0,10},{1,11},{2,8},{3,9},{4,14},{5,15},{6,12},{7,13},{8,2},{9,3},... | collective-permute-start | bytes 776 | tf_op jit(solution)/shard_map/ppermute | solution.py:280
  30.7 2.8 %collective-permute-start.9 = (f32[1,64]{1,0:T(1,128)S(1)}, f32[1,64]{1,0:T(1,128)S(1)}, u32[]{:S(2)}, u32[]{:S(2)}) collective-permute-start(f32[1,64]{1,0:T(1,128)S(1)} %get-tuple-element.25), channel_id=1, source_target_pairs={{0,8},{1,9},{2,10},{3,11},{4,12},{5,13},{6,14},{7,15},{8,0},{9,1},... | collective-permute-start | bytes 776 | tf_op jit(solution)/shard_map/ppermute | solution.py:280
  33.5 4.0 %collective-permute-start.14 = (f32[8,64]{1,0:T(8,128)S(1)}, f32[8,64]{1,0:T(8,128)S(1)}, u32[]{:S(2)}, u32[]{:S(2)}) collective-permute-start(f32[8,64]{1,0:T(8,128)S(1)} %broadcast_in_dim.8), channel_id=1, source_target_pairs={{0,12},{1,13},{2,14},{3,15},{4,8},{5,9},{6,10},{7,11},{8,4},{9,5},... | collective-permute-start | bytes 6152 | tf_op jit(solution)/shard_map/ppermute | solution.py:280
  35.6 1.2 %collective-permute-start.13 = (f32[1,64]{1,0:T(1,128)S(1)}, f32[1,64]{1,0:T(1,128)S(1)}, u32[]{:S(2)}, u32[]{:S(2)}) collective-permute-start(f32[1,64]{1,0:T(1,128)S(1)} %slice_add_fusion), channel_id=1, source_target_pairs={{0,8},{1,9},{2,10},{3,11},{4,12},{5,13},{6,14},{7,15},{8,0},{9,1},... | collective-permute-start | bytes 776 | tf_op jit(solution)/shard_map/ppermute | solution.py:280

commit v22 on v18

--- a/solution.py
+++ b/solution.py
@@ -174,7 +174,7 @@
         out_specs=[in_vmem] * 2,
         out_shape=[jax.ShapeDtypeStruct((per_group, per_group * len(steps)), jnp.bfloat16)] * 2,
         compiler_params=params,
-        cost_estimate=pl.CostEstimate(flops=4250000000, bytes_accessed=4 * projected.size, transcendentals=0),
+        cost_estimate=pl.CostEstimate(flops=4150000000, bytes_accessed=4 * projected.size, transcendentals=0),
         name="couple",
     )(projected, *others)
 
@@ -338,20 +338,21 @@
         others = {step: exchange(projected, "comp", step) for step in range(1, comp, 2)}
     else:
         others = gather(projected)
-    near = [1][: comp - 1]
-    far = list(range(2, comp))
+    far = list(range(1, comp))
 
     def of(arrays, steps):
         return [arrays[step] for step in steps]
 
-    partly = first_part(projected, sample, vectors, near, of(others, near), of(blocks, near), features)
+    partly = first_part(projected, sample, vectors, [], [], [], features)
     if even:
         for step in range(2, comp, 2):
-            blocks[step], others[1] = lax.optimization_barrier((blocks[step], others[1]))
+            blocks[step], partly = lax.optimization_barrier((blocks[step], partly))
             vectors = blocks[step]
             blocks[step + 1] = [exchange(vectors[:, i:j], "comp", 1) for i, j in relay_pieces(vectors.shape[1])]
             others[step] = exchange(others[step + 1], "comp", 1)
     projected, partly = lax.optimization_barrier((projected, partly))
+    if even and comp > 1:
+        projected, blocks[1] = lax.optimization_barrier((projected, blocks[1]))
     weights = couple(projected, far, of(others, far), rows, features) if far else []
     updated, squares, wide = rest_part(partly, weights, [b if isinstance(b, list) else [b] for b in of(blocks, far)])
     return finish(updated, flipped_terms(squares, wide), features)

time: 39 us -> 39.1 us (level)
  starting transfers between devices: 16.2 us -> 16.7 us
    ppermute x6, starting transfers between devices: 6.21 us -> 6.65 us  [flipped_terms(): lax.ppermute(wide if k == width - 1 else array, ('comp', 'feat'), pairs)]
  transfers between devices with their start and end apart: 16 -> 16, of which waited for: 11 -> 13; matrix products, arithmetic and copies ran while one was open for 0% -> 0% of each run, Pallas kernels for 12% -> 11%
where the time goes in v22:
time: 39.1 us; the launch traced here: 39 us
  starting transfers between devices  16.7 us (43%)
  waiting for transfers between devices  15.8 us (40%)
  Pallas kernels  6.27 us (16%)
    ppermute x10, waiting for transfers between devices, exchange(): lax.ppermute(array, axis, [(i, i ^ step) for i in range(lax.axis_size(axi...  12 us
    ppermute x10, starting transfers between devices, exchange(): lax.ppermute(array, axis, [(i, i ^ step) for i in range(lax.axis_size(axi...  10.1 us
    ppermute x6, starting transfers between devices, flipped_terms(): lax.ppermute(wide if k == width - 1 else array, ('comp', 'feat'), pairs)  6.65 us
    ppermute x6, waiting for transfers between devices, flipped_terms(): lax.ppermute(wide if k == width - 1 else array, ('comp', 'feat'), pairs)  3.82 us
    pallas_call x1, Pallas kernels, project(): pl.pallas_call(project_kernel, in_specs=[anywhere] * 2, out_specs=[in_vme...  2.95 us
    pallas_call x1, Pallas kernels, first_part(): pl.pallas_call(functools.partial(first_kernel, features, steps), in_specs...  1.15 us
    pallas_call x1, Pallas kernels, finish(): pl.pallas_call(functools.partial(finish_kernel, features, count), in_spec...  1.1 us
  transfers between devices with their start and end apart: 16, of which 13 were waited for; matrix products, arithmetic and copies ran while one was open for 0% of the time, Pallas kernels for 11%

profile of v22, /device:TPU:0, one launch (start us, length us, event | category | flops | bytes accessed | tf_op | source)
XLA Modules:
  0.0 39.0 jit_solution(12980917544426028034)
XLA Ops:
  0.0 2.9 %collective-permute-start.3 = (f32[64,3584]{1,0:T(8,128)}, f32[64,3584]{1,0:T(8,128)S(1)}, u32[]{:S(2)}, u32[]{:S(2)}) collective-permute-start(f32[64,3584]{1,0:T(8,128)} %x_hbm.1), channel_id=1, source_target_pairs={{0,16},{8,24},{16,0},{24,8},{1,17},{9,25},{17,1},{25,9},{2,18},{10... | collective-permute-start | bytes 2752520 | tf_op jit(solution)/shard_map/ppermute | solution.py:273
  2.9 3.0 %project.1 = (f32[64,256]{1,0:T(8,128)S(1)}, f32[64,3584]{1,0:T(8,128)S(1)}, f32[192,3584]{1,0:T(8,128)S(1)}) custom-call(f32[64,3584]{1,0:T(8,128)} %x_hbm.1, f32[192,3584]{1,0:T(8,128)} %bitcast.2), custom_call_target="tpu_custom_call" | custom-call | tf_op jit(solution)/shard_map/project/pallas_call | solution.py:97
  5.9 0.1 collective-permute-start.4
  6.0 1.6 %collective-permute-start = (f32[64,256]{1,0:T(8,128)S(1)}, f32[64,256]{1,0:T(8,128)S(1)}, u32[]{:S(2)}, u32[]{:S(2)}) collective-permute-start(f32[64,256]{1,0:T(8,128)S(1)} %get-tuple-element.19), channel_id=1, source_target_pairs={{0,1},{1,0},{2,3},{3,2},{4,5},{5,4},{6,7},{7,6},{8,9},{9,8},{10,11... | collective-permute-start | bytes 196616 | tf_op jit(solution)/shard_map/ppermute | solution.py:273
  7.6 2.9 %collective-permute-done = f32[64,256]{1,0:T(8,128)S(1)} collective-permute-done((f32[64,256]{1,0:T(8,128)S(1)}, f32[64,256]{1,0:T(8,128)S(1)}, u32[]{:S(2)}, u32[]{:S(2)}) %collective-permute-start) | collective-permute-done | bytes 65568 | tf_op jit(solution)/shard_map/ppermute | solution.py:273
  10.5 1.6 %collective-permute-start.1 = (f32[64,256]{1,0:T(8,128)S(1)}, f32[64,256]{1,0:T(8,128)S(1)}, u32[]{:S(2)}, u32[]{:S(2)}) collective-permute-start(f32[64,256]{1,0:T(8,128)S(1)} %add.18), channel_id=1, source_target_pairs={{0,2},{1,3},{2,0},{3,1},{4,6},{5,7},{6,4},{7,5},{8,10},{9,11},{10,... | collective-permute-start | bytes 196616 | tf_op jit(solution)/shard_map/ppermute | solution.py:273
  12.1 2.7 %collective-permute-done.1 = f32[64,256]{1,0:T(8,128)S(1)} collective-permute-done((f32[64,256]{1,0:T(8,128)S(1)}, f32[64,256]{1,0:T(8,128)S(1)}, u32[]{:S(2)}, u32[]{:S(2)}) %collective-permute-start.1) | collective-permute-done | bytes 65568 | tf_op jit(solution)/shard_map/ppermute | solution.py:273
  14.8 2.7 %collective-permute-start.2 = (f32[64,256]{1,0:T(8,128)S(1)}, f32[64,256]{1,0:T(8,128)S(1)}, u32[]{:S(2)}, u32[]{:S(2)}) collective-permute-start(f32[64,256]{1,0:T(8,128)S(1)} %add.19), channel_id=1, source_target_pairs={{0,4},{1,5},{2,6},{3,7},{4,0},{5,1},{6,2},{7,3},{8,12},{9,13},{10,... | collective-permute-start | bytes 196616 | tf_op jit(solution)/shard_map/ppermute | solution.py:273
  17.5 2.6 %collective-permute-done.2 = f32[64,256]{1,0:T(8,128)S(1)} collective-permute-done((f32[64,256]{1,0:T(8,128)S(1)}, f32[64,256]{1,0:T(8,128)S(1)}, u32[]{:S(2)}, u32[]{:S(2)}) %collective-permute-start.2) | collective-permute-done | bytes 65568 | tf_op jit(solution)/shard_map/ppermute | solution.py:273
  20.1 0.1 collective-permute-start.6
  20.2 1.1 %first_part.1.t_ref = f32[64,3584]{1,0:T(8,128)S(1)} custom-call(f32[64,256]{1,0:T(8,128)S(1)} %add.20.p_ref, f32[192,3584]{1,0:T(8,128)S(1)} %get-tuple-element.20.s_ref, f32[64,3584]{1,0:T(8,128)S(1)} %get-tuple-element.21.x_ref), custom_call_target="tpu_custom_call" | custom-call | tf_op jit(solution)/shard_map/first_part/pallas_call | solution.py:154
  21.3 2.5 %collective-permute-done.3.refs_3_ = f32[64,3584]{1,0:T(8,128)S(1)} collective-permute-done((f32[64,3584]{1,0:T(8,128)}, f32[64,3584]{1,0:T(8,128)S(1)}, u32[]{:S(2)}, u32[]{:S(2)}) %collective-permute-start.3) | collective-permute-done | bytes 917536 | tf_op jit(solution)/shard_map/ppermute | solution.py:273
  23.8 0.1 collective-permute-start.8
  23.9 0.5 %collective-permute-start.5 = (f32[64,256]{1,0:T(8,128)S(1)}, f32[64,256]{1,0:T(8,128)S(1)}, u32[]{:S(2)}, u32[]{:S(2)}) collective-permute-start(f32[64,256]{1,0:T(8,128)S(1)} %add.20.p_ref), channel_id=1, source_target_pairs={{0,8},{8,0},{16,24},{24,16},{1,9},{9,1},{17,25},{25,17},{2,10},{10... | collective-permute-start | bytes 196616 | tf_op jit(solution)/shard_map/ppermute | solution.py:273
  24.4 0.2 collective-permute-done.6.refs_2_
  24.6 0.1 collective-permute-start.7
  24.8 0.5 %collective-permute-start.9 = (f32[64,1664]{1,0:T(8,128)S(1)}, f32[64,1664]{1,0:T(8,128)S(1)}, u32[]{:S(2)}, u32[]{:S(2)}) collective-permute-start(f32[64,1664]{1,0:T(8,128)S(1)} %slice.10), channel_id=1, source_target_pairs={{0,8},{8,0},{16,24},{24,16},{1,9},{9,1},{17,25},{25,17},{2,10},{10... | collective-permute-start | bytes 1277960 | tf_op jit(solution)/shard_map/ppermute | solution.py:273
  25.2 0.0 collective-permute-done.4.refs_2_
  25.2 0.6 %collective-permute-done.5.refs_0_ = f32[64,256]{1,0:T(8,128)S(1)} collective-permute-done((f32[64,256]{1,0:T(8,128)S(1)}, f32[64,256]{1,0:T(8,128)S(1)}, u32[]{:S(2)}, u32[]{:S(2)}) %collective-permute-start.5) | collective-permute-done | bytes 65568 | tf_op jit(solution)/shard_map/ppermute | solution.py:273
  25.8 0.1 collective-permute-done.7.refs_1_
  25.9 0.3 couple.1
  26.2 0.4 collective-permute-done.9.refs_5_
  26.6 0.0 collective-permute-done.8.refs_4_
  26.6 0.8 %rest_part.1 = (f32[64,3584]{1,0:T(8,128)S(1)}, f32[1,64]{1,0:T(1,128)S(1)}, f32[8,64]{1,0:T(8,128)S(1)}) custom-call(f32[64,3584]{1,0:T(8,128)S(1)} %first_part.1.t_ref, bf16[64,192]{1,0:T(8,128)(2,1)S(1)} %get-tuple-element.26.refs_0_, bf16[64,192]{1,0:T(8,128)(2,1)S(1)} %get-tuple-element.27.refs_1_, f32[64,3584]{1,0:T(8,128)S(1)} %collective-permute-done.4.refs_2_, ...), custom_call_target="tpu_custom_call" | custom-call | tf_op jit(solution)/shard_map/rest_part/pallas_call | solution.py:217
  27.4 2.9 %collective-permute-start.13 = (f32[8,64]{1,0:T(8,128)S(1)}, f32[8,64]{1,0:T(8,128)S(1)}, u32[]{:S(2)}, u32[]{:S(2)}) collective-permute-start(f32[8,64]{1,0:T(8,128)S(1)} %get-tuple-element.32), channel_id=1, source_target_pairs={{0,11},{1,10},{2,9},{3,8},{4,15},{5,14},{6,13},{7,12},{8,3},{9,2},... | collective-permute-start | bytes 6152 | tf_op jit(solution)/shard_map/ppermute | solution.py:308
  30.3 0.3 collective-permute-start.10
  30.5 0.3 collective-permute-start.11
  30.9 0.1 collective-permute-start.12
  31.0 0.4 collective-permute-done.10
  31.4 2.1 %collective-permute-done.11 = f32[1,64]{1,0:T(1,128)S(1)} collective-permute-done((f32[1,64]{1,0:T(1,128)S(1)}, f32[1,64]{1,0:T(1,128)S(1)}, u32[]{:S(2)}, u32[]{:S(2)}) %collective-permute-start.11) | collective-permute-done | bytes 288 | tf_op jit(solution)/shard_map/ppermute | solution.py:308
  33.5 0.3 collective-permute-done.12
  33.9 0.0 collective-permute-done.13
  33.9 2.7 %collective-permute-start.15 = (f32[8,64]{1,0:T(8,128)S(1)}, f32[8,64]{1,0:T(8,128)S(1)}, u32[]{:S(2)}, u32[]{:S(2)}) collective-permute-start(f32[8,64]{1,0:T(8,128)S(1)} %broadcast_in_dim.8), channel_id=1, source_target_pairs={{0,12},{1,13},{2,14},{3,15},{4,8},{5,9},{6,10},{7,11},{8,4},{9,5},... | collective-permute-start | bytes 6152 | tf_op jit(solution)/shard_map/ppermute | solution.py:308
  36.6 0.3 collective-permute-start.14
  36.9 0.8 %collective-permute-done.14.refs_0_ = f32[1,64]{1,0:T(1,128)S(1)} collective-permute-done((f32[1,64]{1,0:T(1,128)S(1)}, f32[1,64]{1,0:T(1,128)S(1)}, u32[]{:S(2)}, u32[]{:S(2)}) %collective-permute-start.14) | collective-permute-done | bytes 288 | tf_op jit(solution)/shard_map/ppermute | solution.py:308
  37.7 0.2 collective-permute-done.15.refs_1_
  37.9 1.1 %finish.1 = f32[64,3584]{1,0:T(8,128)} custom-call(f32[64,3584]{1,0:T(8,128)S(1)} %get-tuple-element.30.updated_ref, f32[1,64]{1,0:T(1,128)S(1)} %collective-permute-done.14.refs_0_, f32[8,64]{1,0:T(8,128)S(1)} %collective-permute-done.15.refs_1_), custom_call_target="tpu_custom_call" | custom-call | tf_op jit(solution)/shard_map/finish/pallas_call | solution.py:258
  (7 shorter events, 0.1 us)
Async XLA Ops:
  0.0 23.8 %collective-permute-start.3 = (f32[64,3584]{1,0:T(8,128)}, f32[64,3584]{1,0:T(8,128)S(1)}, u32[]{:S(2)}, u32[]{:S(2)}) collective-permute-start(f32[64,3584]{1,0:T(8,128)} %x_hbm.1), channel_id=1, source_target_pairs={{0,16},{8,24},{16,0},{24,8},{1,17},{9,25},{17,1},{25,9},{2,18},{10... | collective-permute-start | bytes 2752520 | tf_op jit(solution)/shard_map/ppermute | solution.py:273
  5.9 19.3 %collective-permute-start.4 = (f32[64,3584]{1,0:T(8,128)S(1)}, f32[64,3584]{1,0:T(8,128)S(1)}, u32[]{:S(2)}, u32[]{:S(2)}) collective-permute-start(f32[64,3584]{1,0:T(8,128)S(1)} %get-tuple-element.21.x_ref), channel_id=1, source_target_pairs={{0,8},{8,0},{16,24},{24,16},{1,9},{9,1},{17,25},{25,17},{2,10},{10... | collective-permute-start | bytes 2752520 | tf_op jit(solution)/shard_map/ppermute | solution.py:273
  6.0 4.5 %collective-permute-start = (f32[64,256]{1,0:T(8,128)S(1)}, f32[64,256]{1,0:T(8,128)S(1)}, u32[]{:S(2)}, u32[]{:S(2)}) collective-permute-start(f32[64,256]{1,0:T(8,128)S(1)} %get-tuple-element.19), channel_id=1, source_target_pairs={{0,1},{1,0},{2,3},{3,2},{4,5},{5,4},{6,7},{7,6},{8,9},{9,8},{10,11... | collective-permute-start | bytes 196616 | tf_op jit(solution)/shard_map/ppermute | solution.py:273
  10.5 4.3 %collective-permute-start.1 = (f32[64,256]{1,0:T(8,128)S(1)}, f32[64,256]{1,0:T(8,128)S(1)}, u32[]{:S(2)}, u32[]{:S(2)}) collective-permute-start(f32[64,256]{1,0:T(8,128)S(1)} %add.18), channel_id=1, source_target_pairs={{0,2},{1,3},{2,0},{3,1},{4,6},{5,7},{6,4},{7,5},{8,10},{9,11},{10,... | collective-permute-start | bytes 196616 | tf_op jit(solution)/shard_map/ppermute | solution.py:273
  14.8 5.2 %collective-permute-start.2 = (f32[64,256]{1,0:T(8,128)S(1)}, f32[64,256]{1,0:T(8,128)S(1)}, u32[]{:S(2)}, u32[]{:S(2)}) collective-permute-start(f32[64,256]{1,0:T(8,128)S(1)} %add.19), channel_id=1, source_target_pairs={{0,4},{1,5},{2,6},{3,7},{4,0},{5,1},{6,2},{7,3},{8,12},{9,13},{10,... | collective-permute-start | bytes 196616 | tf_op jit(solution)/shard_map/ppermute | solution.py:273
  20.1 4.5 %collective-permute-start.6 = (f32[64,256]{1,0:T(8,128)S(1)}, f32[64,256]{1,0:T(8,128)S(1)}, u32[]{:S(2)}, u32[]{:S(2)}) collective-permute-start(f32[64,256]{1,0:T(8,128)S(1)} %add.20.p_ref), channel_id=1, source_target_pairs={{0,24},{8,16},{16,8},{24,0},{1,25},{9,17},{17,9},{25,1},{2,26},{10... | collective-permute-start | bytes 196616 | tf_op jit(solution)/shard_map/ppermute | solution.py:273
  23.8 2.8 %collective-permute-start.8 = (f32[64,1920]{1,0:T(8,128)S(1)}, f32[64,1920]{1,0:T(8,128)S(1)}, u32[]{:S(2)}, u32[]{:S(2)}) collective-permute-start(f32[64,1920]{1,0:T(8,128)S(1)} %slice.9), channel_id=1, source_target_pairs={{0,8},{8,0},{16,24},{24,16},{1,9},{9,1},{17,25},{25,17},{2,10},{10... | collective-permute-start | bytes 1474568 | tf_op jit(solution)/shard_map/ppermute | solution.py:273
  23.9 1.9 %collective-permute-start.5 = (f32[64,256]{1,0:T(8,128)S(1)}, f32[64,256]{1,0:T(8,128)S(1)}, u32[]{:S(2)}, u32[]{:S(2)}) collective-permute-start(f32[64,256]{1,0:T(8,128)S(1)} %add.20.p_ref), channel_id=1, source_target_pairs={{0,8},{8,0},{16,24},{24,16},{1,9},{9,1},{17,25},{25,17},{2,10},{10... | collective-permute-start | bytes 196616 | tf_op jit(solution)/shard_map/ppermute | solution.py:273
  24.6 1.3 %collective-permute-start.7 = (f32[64,256]{1,0:T(8,128)S(1)}, f32[64,256]{1,0:T(8,128)S(1)}, u32[]{:S(2)}, u32[]{:S(2)}) collective-permute-start(f32[64,256]{1,0:T(8,128)S(1)} %collective-permute-done.6.refs_2_), channel_id=1, source_target_pairs={{0,8},{8,0},{16,24},{24,16},{1,9},{9,1},{17,25},{25,17},{2,10},{10... | collective-permute-start | bytes 196616 | tf_op jit(solution)/shard_map/ppermute | solution.py:273
  24.8 1.9 %collective-permute-start.9 = (f32[64,1664]{1,0:T(8,128)S(1)}, f32[64,1664]{1,0:T(8,128)S(1)}, u32[]{:S(2)}, u32[]{:S(2)}) collective-permute-start(f32[64,1664]{1,0:T(8,128)S(1)} %slice.10), channel_id=1, source_target_pairs={{0,8},{8,0},{16,24},{24,16},{1,9},{9,1},{17,25},{25,17},{2,10},{10... | collective-permute-start | bytes 1277960 | tf_op jit(solution)/shard_map/ppermute | solution.py:273
  27.4 6.5 %collective-permute-start.13 = (f32[8,64]{1,0:T(8,128)S(1)}, f32[8,64]{1,0:T(8,128)S(1)}, u32[]{:S(2)}, u32[]{:S(2)}) collective-permute-start(f32[8,64]{1,0:T(8,128)S(1)} %get-tuple-element.32), channel_id=1, source_target_pairs={{0,11},{1,10},{2,9},{3,8},{4,15},{5,14},{6,13},{7,12},{8,3},{9,2},... | collective-permute-start | bytes 6152 | tf_op jit(solution)/shard_map/ppermute | solution.py:308
  30.3 1.1 %collective-permute-start.10 = (f32[1,64]{1,0:T(1,128)S(1)}, f32[1,64]{1,0:T(1,128)S(1)}, u32[]{:S(2)}, u32[]{:S(2)}) collective-permute-start(f32[1,64]{1,0:T(1,128)S(1)} %get-tuple-element.31), channel_id=1, source_target_pairs={{0,8},{1,9},{2,10},{3,11},{4,12},{5,13},{6,14},{7,15},{8,0},{9,1},... | collective-permute-start | bytes 776 | tf_op jit(solution)/shard_map/ppermute | solution.py:308
  30.5 3.0 %collective-permute-start.11 = (f32[1,64]{1,0:T(1,128)S(1)}, f32[1,64]{1,0:T(1,128)S(1)}, u32[]{:S(2)}, u32[]{:S(2)}) collective-permute-start(f32[1,64]{1,0:T(1,128)S(1)} %get-tuple-element.31), channel_id=1, source_target_pairs={{0,9},{1,8},{2,11},{3,10},{4,13},{5,12},{6,15},{7,14},{8,1},{9,0},... | collective-permute-start | bytes 776 | tf_op jit(solution)/shard_map/ppermute | solution.py:308
  30.9 3.0 %collective-permute-start.12 = (f32[1,64]{1,0:T(1,128)S(1)}, f32[1,64]{1,0:T(1,128)S(1)}, u32[]{:S(2)}, u32[]{:S(2)}) collective-permute-start(f32[1,64]{1,0:T(1,128)S(1)} %get-tuple-element.31), channel_id=1, source_target_pairs={{0,10},{1,11},{2,8},{3,9},{4,14},{5,15},{6,12},{7,13},{8,2},{9,3},... | collective-permute-start | bytes 776 | tf_op jit(solution)/shard_map/ppermute | solution.py:308
  33.9 4.0 %collective-permute-start.15 = (f32[8,64]{1,0:T(8,128)S(1)}, f32[8,64]{1,0:T(8,128)S(1)}, u32[]{:S(2)}, u32[]{:S(2)}) collective-permute-start(f32[8,64]{1,0:T(8,128)S(1)} %broadcast_in_dim.8), channel_id=1, source_target_pairs={{0,12},{1,13},{2,14},{3,15},{4,8},{5,9},{6,10},{7,11},{8,4},{9,5},... | collective-permute-start | bytes 6152 | tf_op jit(solution)/shard_map/ppermute | solution.py:308
  36.6 1.2 %collective-permute-start.14 = (f32[1,64]{1,0:T(1,128)S(1)}, f32[1,64]{1,0:T(1,128)S(1)}, u32[]{:S(2)}, u32[]{:S(2)}) collective-permute-start(f32[1,64]{1,0:T(1,128)S(1)} %slice_add_fusion), channel_id=1, source_target_pairs={{0,8},{1,9},{2,10},{3,11},{4,12},{5,13},{6,14},{7,15},{8,0},{9,1},... | collective-permute-start | bytes 776 | tf_op jit(solution)/shard_map/ppermute | solution.py:308

commit v23 on v17

--- a/solution.py
+++ b/solution.py
@@ -133,7 +133,7 @@
         out_ref[:, here] = scale * x + product(weights, jnp.concatenate([s_ref[:, here], x, *others], axis=0))
         return carry
 
-    loop(x_ref.shape[1], 4, body, 0)
+    loop(x_ref.shape[1], 7, body, 0)
 
 
 def first_part(projected, sample, x, steps, others, blocks, features):
@@ -178,7 +178,7 @@
         out_ref[:, here] = updated
         return squares + jnp.sum(updated * updated, axis=1, keepdims=True)
 
-    squares = loop(columns, 4, body, jnp.zeros((per_group, 1), jnp.float32))
+    squares = loop(columns, 7, body, jnp.zeros((per_group, 1), jnp.float32))
     spread = jnp.broadcast_to(squares, (per_group, per_group))
     row = jnp.sum(jnp.where(diagonal(per_group), spread, 0.0), axis=0, keepdims=True)
     squares_ref[...] = row

time: 38.8 us -> 38.8 us (level)
  no operation moved by 1% of the time
where the time goes in v23:
time: 38.8 us; the launch traced here: 38.6 us
  waiting for transfers between devices  16.6 us (43%)
  starting transfers between devices  15.6 us (40%)
  Pallas kernels  6.36 us (16%)
    ppermute x9, waiting for transfers between devices, exchange(): lax.ppermute(array, axis, [(i, i ^ step) for i in range(lax.axis_size(axi...  12.3 us
    ppermute x9, starting transfers between devices, exchange(): lax.ppermute(array, axis, [(i, i ^ step) for i in range(lax.axis_size(axi...  9.54 us
    ppermute x6, starting transfers between devices, flipped_terms(): lax.ppermute(wide if k == width - 1 else array, ('comp', 'feat'), pairs)  6.05 us
    ppermute x6, waiting for transfers between devices, flipped_terms(): lax.ppermute(wide if k == width - 1 else array, ('comp', 'feat'), pairs)  4.25 us
    pallas_call x1, Pallas kernels, project(): pl.pallas_call(project_kernel, in_specs=[anywhere] * 2, out_specs=[in_vme...  2.93 us
    pallas_call x1, Pallas kernels, first_part(): pl.pallas_call(functools.partial(first_kernel, features, steps), in_specs...  1.42 us
    pallas_call x1, Pallas kernels, finish(): pl.pallas_call(functools.partial(finish_kernel, features, count), in_spec...  1.1 us
  transfers between devices with their start and end apart: 15, of which 11 were waited for; matrix products, arithmetic and copies ran while one was open for 0% of the time, Pallas kernels for 12%

profile of v23, /device:TPU:0, one launch (start us, length us, event | category | flops | bytes accessed | tf_op | source)
XLA Modules:
  0.0 38.6 jit_solution(17803295862191699277)
XLA Ops:
  0.0 2.9 %collective-permute-start.7 = (f32[64,3584]{1,0:T(8,128)}, f32[64,3584]{1,0:T(8,128)S(1)}, u32[]{:S(2)}, u32[]{:S(2)}) collective-permute-start(f32[64,3584]{1,0:T(8,128)} %x_hbm.1), channel_id=1, source_target_pairs={{0,16},{8,24},{16,0},{24,8},{1,17},{9,25},{17,1},{25,9},{2,18},{10... | collective-permute-start | bytes 2752520 | tf_op jit(solution)/shard_map/ppermute | solution.py:245
  2.9 2.9 %project.1 = (f32[64,256]{1,0:T(8,128)S(1)}, f32[64,3584]{1,0:T(8,128)S(1)}, f32[192,3584]{1,0:T(8,128)S(1)}) custom-call(f32[64,3584]{1,0:T(8,128)} %x_hbm.1, f32[192,3584]{1,0:T(8,128)} %bitcast.2), custom_call_target="tpu_custom_call" | custom-call | tf_op jit(solution)/shard_map/project/pallas_call | solution.py:83
  5.9 0.1 collective-permute-start.4
  6.0 1.6 %collective-permute-start = (f32[64,256]{1,0:T(8,128)S(1)}, f32[64,256]{1,0:T(8,128)S(1)}, u32[]{:S(2)}, u32[]{:S(2)}) collective-permute-start(f32[64,256]{1,0:T(8,128)S(1)} %get-tuple-element.16), channel_id=1, source_target_pairs={{0,1},{1,0},{2,3},{3,2},{4,5},{5,4},{6,7},{7,6},{8,9},{9,8},{10,11... | collective-permute-start | bytes 196616 | tf_op jit(solution)/shard_map/ppermute | solution.py:245
  7.5 2.9 %collective-permute-done = f32[64,256]{1,0:T(8,128)S(1)} collective-permute-done((f32[64,256]{1,0:T(8,128)S(1)}, f32[64,256]{1,0:T(8,128)S(1)}, u32[]{:S(2)}, u32[]{:S(2)}) %collective-permute-start) | collective-permute-done | bytes 65568 | tf_op jit(solution)/shard_map/ppermute | solution.py:245
  10.5 1.6 %collective-permute-start.1 = (f32[64,256]{1,0:T(8,128)S(1)}, f32[64,256]{1,0:T(8,128)S(1)}, u32[]{:S(2)}, u32[]{:S(2)}) collective-permute-start(f32[64,256]{1,0:T(8,128)S(1)} %add.18), channel_id=1, source_target_pairs={{0,2},{1,3},{2,0},{3,1},{4,6},{5,7},{6,4},{7,5},{8,10},{9,11},{10,... | collective-permute-start | bytes 196616 | tf_op jit(solution)/shard_map/ppermute | solution.py:245
  12.1 2.7 %collective-permute-done.1 = f32[64,256]{1,0:T(8,128)S(1)} collective-permute-done((f32[64,256]{1,0:T(8,128)S(1)}, f32[64,256]{1,0:T(8,128)S(1)}, u32[]{:S(2)}, u32[]{:S(2)}) %collective-permute-start.1) | collective-permute-done | bytes 65568 | tf_op jit(solution)/shard_map/ppermute | solution.py:245
  14.8 2.7 %collective-permute-start.2 = (f32[64,256]{1,0:T(8,128)S(1)}, f32[64,256]{1,0:T(8,128)S(1)}, u32[]{:S(2)}, u32[]{:S(2)}) collective-permute-start(f32[64,256]{1,0:T(8,128)S(1)} %add.19), channel_id=1, source_target_pairs={{0,4},{1,5},{2,6},{3,7},{4,0},{5,1},{6,2},{7,3},{8,12},{9,13},{10,... | collective-permute-start | bytes 196616 | tf_op jit(solution)/shard_map/ppermute | solution.py:245
  17.5 2.6 %collective-permute-done.2 = f32[64,256]{1,0:T(8,128)S(1)} collective-permute-done((f32[64,256]{1,0:T(8,128)S(1)}, f32[64,256]{1,0:T(8,128)S(1)}, u32[]{:S(2)}, u32[]{:S(2)}) %collective-permute-start.2) | collective-permute-done | bytes 65568 | tf_op jit(solution)/shard_map/ppermute | solution.py:245
  20.1 0.1 collective-permute-start.3
  20.1 0.4 %collective-permute-start.5 = (f32[64,256]{1,0:T(8,128)S(1)}, f32[64,256]{1,0:T(8,128)S(1)}, u32[]{:S(2)}, u32[]{:S(2)}) collective-permute-start(f32[64,256]{1,0:T(8,128)S(1)} %add.20.p_ref), channel_id=1, source_target_pairs={{0,24},{8,16},{16,8},{24,0},{1,25},{9,17},{17,9},{25,1},{2,26},{10... | collective-permute-start | bytes 196616 | tf_op jit(solution)/shard_map/ppermute | solution.py:245
  20.6 0.8 %collective-permute-done.3.refs_0_ = f32[64,256]{1,0:T(8,128)S(1)} collective-permute-done((f32[64,256]{1,0:T(8,128)S(1)}, f32[64,256]{1,0:T(8,128)S(1)}, u32[]{:S(2)}, u32[]{:S(2)}) %collective-permute-start.3) | collective-permute-done | bytes 65568 | tf_op jit(solution)/shard_map/ppermute | solution.py:245
  21.4 2.3 %collective-permute-done.7.refs_2_ = f32[64,3584]{1,0:T(8,128)S(1)} collective-permute-done((f32[64,3584]{1,0:T(8,128)}, f32[64,3584]{1,0:T(8,128)S(1)}, u32[]{:S(2)}, u32[]{:S(2)}) %collective-permute-start.7) | collective-permute-done | bytes 917536 | tf_op jit(solution)/shard_map/ppermute | solution.py:245
  23.7 0.0 collective-permute-start.8
  23.7 0.8 %collective-permute-done.5.refs_1_ = f32[64,256]{1,0:T(8,128)S(1)} collective-permute-done((f32[64,256]{1,0:T(8,128)S(1)}, f32[64,256]{1,0:T(8,128)S(1)}, u32[]{:S(2)}, u32[]{:S(2)}) %collective-permute-start.5) | collective-permute-done | bytes 65568 | tf_op jit(solution)/shard_map/ppermute | solution.py:245
  24.6 0.2 collective-permute-start.6
  24.7 0.0 collective-permute-done.4.refs_1_
  24.7 1.4 %first_part.1.t_ref = f32[64,3584]{1,0:T(8,128)S(1)} custom-call(f32[64,256]{1,0:T(8,128)S(1)} %add.20.p_ref, f32[192,3584]{1,0:T(8,128)S(1)} %get-tuple-element.17.s_ref, f32[64,3584]{1,0:T(8,128)S(1)} %get-tuple-element.18.x_ref, f32[64,256]{1,0:T(8,128)S(1)} %collective-permute-done.3.refs_0_, f32[64,3584]{1,0:T(8,128)S(1)} %collective-permute-done.4.refs_1_), custom_call_target="tpu_custom_call" | custom-call | tf_op jit(solution)/shard_map/first_part/pallas_call | solution.py:140
  26.2 0.1 collective-permute-done.6.refs_0_
  26.3 0.3 couple.1
  26.6 0.0 collective-permute-done.8.refs_3_
  26.6 0.6 %rest_part.1 = (f32[64,3584]{1,0:T(8,128)S(1)}, f32[1,64]{1,0:T(1,128)S(1)}, f32[8,64]{1,0:T(8,128)S(1)}) custom-call(f32[64,3584]{1,0:T(8,128)S(1)} %first_part.1.t_ref, bf16[64,128]{1,0:T(8,128)(2,1)S(1)} %get-tuple-element.21.refs_0_, bf16[64,128]{1,0:T(8,128)(2,1)S(1)} %get-tuple-element.22.refs_1_, f32[64,3584]{1,0:T(8,128)S(1)} %collective-permute-done.7.refs_2_, ...), custom_call_target="tpu_custom_call" | custom-call | tf_op jit(solution)/shard_map/rest_part/pallas_call | solution.py:189
  27.2 2.8 %collective-permute-start.12 = (f32[8,64]{1,0:T(8,128)S(1)}, f32[8,64]{1,0:T(8,128)S(1)}, u32[]{:S(2)}, u32[]{:S(2)}) collective-permute-start(f32[8,64]{1,0:T(8,128)S(1)} %get-tuple-element.26), channel_id=1, source_target_pairs={{0,11},{1,10},{2,9},{3,8},{4,15},{5,14},{6,13},{7,12},{8,3},{9,2},... | collective-permute-start | bytes 6152 | tf_op jit(solution)/shard_map/ppermute | solution.py:280
  30.1 0.5 %collective-permute-start.10 = (f32[1,64]{1,0:T(1,128)S(1)}, f32[1,64]{1,0:T(1,128)S(1)}, u32[]{:S(2)}, u32[]{:S(2)}) collective-permute-start(f32[1,64]{1,0:T(1,128)S(1)} %get-tuple-element.25), channel_id=1, source_target_pairs={{0,9},{1,8},{2,11},{3,10},{4,13},{5,12},{6,15},{7,14},{8,1},{9,0},... | collective-permute-start | bytes 776 | tf_op jit(solution)/shard_map/ppermute | solution.py:280
  30.5 0.1 collective-permute-start.11
  30.7 0.1 collective-permute-start.9
  30.8 2.2 %collective-permute-done.10 = f32[1,64]{1,0:T(1,128)S(1)} collective-permute-done((f32[1,64]{1,0:T(1,128)S(1)}, f32[1,64]{1,0:T(1,128)S(1)}, u32[]{:S(2)}, u32[]{:S(2)}) %collective-permute-start.10) | collective-permute-done | bytes 288 | tf_op jit(solution)/shard_map/ppermute | solution.py:280
  33.0 0.5 %collective-permute-done.11 = f32[1,64]{1,0:T(1,128)S(1)} collective-permute-done((f32[1,64]{1,0:T(1,128)S(1)}, f32[1,64]{1,0:T(1,128)S(1)}, u32[]{:S(2)}, u32[]{:S(2)}) %collective-permute-start.11) | collective-permute-done | bytes 288 | tf_op jit(solution)/shard_map/ppermute | solution.py:280
  33.5 0.0 collective-permute-done.9
  33.5 0.0 collective-permute-done.12
  33.5 2.1 %collective-permute-start.14 = (f32[8,64]{1,0:T(8,128)S(1)}, f32[8,64]{1,0:T(8,128)S(1)}, u32[]{:S(2)}, u32[]{:S(2)}) collective-permute-start(f32[8,64]{1,0:T(8,128)S(1)} %broadcast_in_dim.8), channel_id=1, source_target_pairs={{0,12},{1,13},{2,14},{3,15},{4,8},{5,9},{6,10},{7,11},{8,4},{9,5},... | collective-permute-start | bytes 6152 | tf_op jit(solution)/shard_map/ppermute | solution.py:280
  35.6 0.4 collective-permute-start.13
  36.0 0.8 %collective-permute-done.13.refs_0_ = f32[1,64]{1,0:T(1,128)S(1)} collective-permute-done((f32[1,64]{1,0:T(1,128)S(1)}, f32[1,64]{1,0:T(1,128)S(1)}, u32[]{:S(2)}, u32[]{:S(2)}) %collective-permute-start.13) | collective-permute-done | bytes 288 | tf_op jit(solution)/shard_map/ppermute | solution.py:280
  36.8 0.7 %collective-permute-done.14.refs_1_ = f32[8,64]{1,0:T(8,128)S(1)} collective-permute-done((f32[8,64]{1,0:T(8,128)S(1)}, f32[8,64]{1,0:T(8,128)S(1)}, u32[]{:S(2)}, u32[]{:S(2)}) %collective-permute-start.14) | collective-permute-done | bytes 2080 | tf_op jit(solution)/shard_map/ppermute | solution.py:280
  37.5 1.1 %finish.1 = f32[64,3584]{1,0:T(8,128)} custom-call(f32[64,3584]{1,0:T(8,128)S(1)} %get-tuple-element.24.updated_ref, f32[1,64]{1,0:T(1,128)S(1)} %collective-permute-done.13.refs_0_, f32[8,64]{1,0:T(8,128)S(1)} %collective-permute-done.14.refs_1_), custom_call_target="tpu_custom_call" | custom-call | tf_op jit(solution)/shard_map/finish/pallas_call | solution.py:230
  (5 shorter events, 0.0 us)
Async XLA Ops:
  0.0 23.7 %collective-permute-start.7 = (f32[64,3584]{1,0:T(8,128)}, f32[64,3584]{1,0:T(8,128)S(1)}, u32[]{:S(2)}, u32[]{:S(2)}) collective-permute-start(f32[64,3584]{1,0:T(8,128)} %x_hbm.1), channel_id=1, source_target_pairs={{0,16},{8,24},{16,0},{24,8},{1,17},{9,25},{17,1},{25,9},{2,18},{10... | collective-permute-start | bytes 2752520 | tf_op jit(solution)/shard_map/ppermute | solution.py:245
  5.9 18.8 %collective-permute-start.4 = (f32[64,3584]{1,0:T(8,128)S(1)}, f32[64,3584]{1,0:T(8,128)S(1)}, u32[]{:S(2)}, u32[]{:S(2)}) collective-permute-start(f32[64,3584]{1,0:T(8,128)S(1)} %get-tuple-element.18.x_ref), channel_id=1, source_target_pairs={{0,8},{8,0},{16,24},{24,16},{1,9},{9,1},{17,25},{25,17},{2,10},{10... | collective-permute-start | bytes 2752520 | tf_op jit(solution)/shard_map/ppermute | solution.py:245
  6.0 4.5 %collective-permute-start = (f32[64,256]{1,0:T(8,128)S(1)}, f32[64,256]{1,0:T(8,128)S(1)}, u32[]{:S(2)}, u32[]{:S(2)}) collective-permute-start(f32[64,256]{1,0:T(8,128)S(1)} %get-tuple-element.16), channel_id=1, source_target_pairs={{0,1},{1,0},{2,3},{3,2},{4,5},{5,4},{6,7},{7,6},{8,9},{9,8},{10,11... | collective-permute-start | bytes 196616 | tf_op jit(solution)/shard_map/ppermute | solution.py:245
  10.5 4.3 %collective-permute-start.1 = (f32[64,256]{1,0:T(8,128)S(1)}, f32[64,256]{1,0:T(8,128)S(1)}, u32[]{:S(2)}, u32[]{:S(2)}) collective-permute-start(f32[64,256]{1,0:T(8,128)S(1)} %add.18), channel_id=1, source_target_pairs={{0,2},{1,3},{2,0},{3,1},{4,6},{5,7},{6,4},{7,5},{8,10},{9,11},{10,... | collective-permute-start | bytes 196616 | tf_op jit(solution)/shard_map/ppermute | solution.py:245
  14.8 5.2 %collective-permute-start.2 = (f32[64,256]{1,0:T(8,128)S(1)}, f32[64,256]{1,0:T(8,128)S(1)}, u32[]{:S(2)}, u32[]{:S(2)}) collective-permute-start(f32[64,256]{1,0:T(8,128)S(1)} %add.19), channel_id=1, source_target_pairs={{0,4},{1,5},{2,6},{3,7},{4,0},{5,1},{6,2},{7,3},{8,12},{9,13},{10,... | collective-permute-start | bytes 196616 | tf_op jit(solution)/shard_map/ppermute | solution.py:245
  20.1 1.3 %collective-permute-start.3 = (f32[64,256]{1,0:T(8,128)S(1)}, f32[64,256]{1,0:T(8,128)S(1)}, u32[]{:S(2)}, u32[]{:S(2)}) collective-permute-start(f32[64,256]{1,0:T(8,128)S(1)} %add.20.p_ref), channel_id=1, source_target_pairs={{0,8},{8,0},{16,24},{24,16},{1,9},{9,1},{17,25},{25,17},{2,10},{10... | collective-permute-start | bytes 196616 | tf_op jit(solution)/shard_map/ppermute | solution.py:245
  20.1 4.4 %collective-permute-start.5 = (f32[64,256]{1,0:T(8,128)S(1)}, f32[64,256]{1,0:T(8,128)S(1)}, u32[]{:S(2)}, u32[]{:S(2)}) collective-permute-start(f32[64,256]{1,0:T(8,128)S(1)} %add.20.p_ref), channel_id=1, source_target_pairs={{0,24},{8,16},{16,8},{24,0},{1,25},{9,17},{17,9},{25,1},{2,26},{10... | collective-permute-start | bytes 196616 | tf_op jit(solution)/shard_map/ppermute | solution.py:245
  23.7 2.8 %collective-permute-start.8 = (f32[64,3584]{1,0:T(8,128)S(1)}, f32[64,3584]{1,0:T(8,128)S(1)}, u32[]{:S(2)}, u32[]{:S(2)}) collective-permute-start(f32[64,3584]{1,0:T(8,128)S(1)} %collective-permute-done.7.refs_2_), channel_id=1, source_target_pairs={{0,8},{8,0},{16,24},{24,16},{1,9},{9,1},{17,25},{25,17},{2,10},{10... | collective-permute-start | bytes 2752520 | tf_op jit(solution)/shard_map/ppermute | solution.py:245
  24.6 1.7 %collective-permute-start.6 = (f32[64,256]{1,0:T(8,128)S(1)}, f32[64,256]{1,0:T(8,128)S(1)}, u32[]{:S(2)}, u32[]{:S(2)}) collective-permute-start(f32[64,256]{1,0:T(8,128)S(1)} %collective-permute-done.5.refs_1_), channel_id=1, source_target_pairs={{0,8},{8,0},{16,24},{24,16},{1,9},{9,1},{17,25},{25,17},{2,10},{10... | collective-permute-start | bytes 196616 | tf_op jit(solution)/shard_map/ppermute | solution.py:245
  27.2 6.3 %collective-permute-start.12 = (f32[8,64]{1,0:T(8,128)S(1)}, f32[8,64]{1,0:T(8,128)S(1)}, u32[]{:S(2)}, u32[]{:S(2)}) collective-permute-start(f32[8,64]{1,0:T(8,128)S(1)} %get-tuple-element.26), channel_id=1, source_target_pairs={{0,11},{1,10},{2,9},{3,8},{4,15},{5,14},{6,13},{7,12},{8,3},{9,2},... | collective-permute-start | bytes 6152 | tf_op jit(solution)/shard_map/ppermute | solution.py:280
  30.1 3.0 %collective-permute-start.10 = (f32[1,64]{1,0:T(1,128)S(1)}, f32[1,64]{1,0:T(1,128)S(1)}, u32[]{:S(2)}, u32[]{:S(2)}) collective-permute-start(f32[1,64]{1,0:T(1,128)S(1)} %get-tuple-element.25), channel_id=1, source_target_pairs={{0,9},{1,8},{2,11},{3,10},{4,13},{5,12},{6,15},{7,14},{8,1},{9,0},... | collective-permute-start | bytes 776 | tf_op jit(solution)/shard_map/ppermute | solution.py:280
  30.5 3.0 %collective-permute-start.11 = (f32[1,64]{1,0:T(1,128)S(1)}, f32[1,64]{1,0:T(1,128)S(1)}, u32[]{:S(2)}, u32[]{:S(2)}) collective-permute-start(f32[1,64]{1,0:T(1,128)S(1)} %get-tuple-element.25), channel_id=1, source_target_pairs={{0,10},{1,11},{2,8},{3,9},{4,14},{5,15},{6,12},{7,13},{8,2},{9,3},... | collective-permute-start | bytes 776 | tf_op jit(solution)/shard_map/ppermute | solution.py:280
  30.7 2.8 %collective-permute-start.9 = (f32[1,64]{1,0:T(1,128)S(1)}, f32[1,64]{1,0:T(1,128)S(1)}, u32[]{:S(2)}, u32[]{:S(2)}) collective-permute-start(f32[1,64]{1,0:T(1,128)S(1)} %get-tuple-element.25), channel_id=1, source_target_pairs={{0,8},{1,9},{2,10},{3,11},{4,12},{5,13},{6,14},{7,15},{8,0},{9,1},... | collective-permute-start | bytes 776 | tf_op jit(solution)/shard_map/ppermute | solution.py:280
  33.5 4.0 %collective-permute-start.14 = (f32[8,64]{1,0:T(8,128)S(1)}, f32[8,64]{1,0:T(8,128)S(1)}, u32[]{:S(2)}, u32[]{:S(2)}) collective-permute-start(f32[8,64]{1,0:T(8,128)S(1)} %broadcast_in_dim.8), channel_id=1, source_target_pairs={{0,12},{1,13},{2,14},{3,15},{4,8},{5,9},{6,10},{7,11},{8,4},{9,5},... | collective-permute-start | bytes 6152 | tf_op jit(solution)/shard_map/ppermute | solution.py:280
  35.6 1.2 %collective-permute-start.13 = (f32[1,64]{1,0:T(1,128)S(1)}, f32[1,64]{1,0:T(1,128)S(1)}, u32[]{:S(2)}, u32[]{:S(2)}) collective-permute-start(f32[1,64]{1,0:T(1,128)S(1)} %slice_add_fusion), channel_id=1, source_target_pairs={{0,8},{1,9},{2,10},{3,11},{4,12},{5,13},{6,14},{7,15},{8,0},{9,1},... | collective-permute-start | bytes 776 | tf_op jit(solution)/shard_map/ppermute | solution.py:280

commit v24 on v21

--- a/solution.py
+++ b/solution.py
@@ -134,7 +134,7 @@
         out_ref[:, here] = scale * x + product(weights, jnp.concatenate([s_ref[:, here], x, *others], axis=0))
         return carry
 
-    loop(x_ref.shape[1], 4, body, 0)
+    loop(x_ref.shape[1], 2, body, 0)
 
 
 def first_part(projected, sample, x, steps, others, blocks, features):
@@ -179,7 +179,7 @@
         out_ref[:, here] = updated
         return squares + jnp.sum(updated * updated, axis=1, keepdims=True)
 
-    squares = loop(columns, 4, body, jnp.zeros((per_group, 1), jnp.float32))
+    squares = loop(columns, 2, body, jnp.zeros((per_group, 1), jnp.float32))
     spread = jnp.broadcast_to(squares, (per_group, per_group))
     row = jnp.sum(jnp.where(diagonal(per_group), spread, 0.0), axis=0, keepdims=True)
     squares_ref[...] = row

time: 38.7 us -> 38.7 us (level)
  no operation moved by 1% of the time
where the time goes in v24:
time: 38.7 us; the launch traced here: 38.6 us
  waiting for transfers between devices  16.4 us (42%)
  starting transfers between devices  15.7 us (41%)
  Pallas kernels  6.34 us (16%)
    ppermute x9, waiting for transfers between devices, exchange(): lax.ppermute(array, axis, [(i, i ^ step) for i in range(lax.axis_size(axi...  12.3 us
    ppermute x9, starting transfers between devices, exchange(): lax.ppermute(array, axis, [(i, i ^ step) for i in range(lax.axis_size(axi...  9.54 us
    ppermute x6, starting transfers between devices, flipped_terms(): lax.ppermute(wide if k == width - 1 else array, ('comp', 'feat'), pairs)  6.13 us
    ppermute x6, waiting for transfers between devices, flipped_terms(): lax.ppermute(wide if k == width - 1 else array, ('comp', 'feat'), pairs)  4.16 us
    pallas_call x1, Pallas kernels, project(): pl.pallas_call(project_kernel, in_specs=[anywhere] * 2, out_specs=[in_vme...  2.93 us
    pallas_call x1, Pallas kernels, first_part(): pl.pallas_call(functools.partial(first_kernel, features, steps), in_specs...  1.46 us
    pallas_call x1, Pallas kernels, finish(): pl.pallas_call(functools.partial(finish_kernel, features, count), in_spec...  1.06 us
  transfers between devices with their start and end apart: 15, of which 11 were waited for; matrix products, arithmetic and copies ran while one was open for 0% of the time, Pallas kernels for 12%

profile of v24, /device:TPU:0, one launch (start us, length us, event | category | flops | bytes accessed | tf_op | source)
XLA Modules:
  0.0 38.6 jit_solution(15046040189779817905)
XLA Ops:
  0.0 2.9 %collective-permute-start.7 = (f32[64,3584]{1,0:T(8,128)}, f32[64,3584]{1,0:T(8,128)S(1)}, u32[]{:S(2)}, u32[]{:S(2)}) collective-permute-start(f32[64,3584]{1,0:T(8,128)} %x_hbm.1), channel_id=1, source_target_pairs={{0,16},{8,24},{16,0},{24,8},{1,17},{9,25},{17,1},{25,9},{2,18},{10... | collective-permute-start | bytes 2752520 | tf_op jit(solution)/shard_map/ppermute | solution.py:245
  2.9 2.9 %project.1 = (f32[64,256]{1,0:T(8,128)S(1)}, f32[64,3584]{1,0:T(8,128)S(1)}, f32[192,3584]{1,0:T(8,128)S(1)}) custom-call(f32[64,3584]{1,0:T(8,128)} %x_hbm.1, f32[192,3584]{1,0:T(8,128)} %bitcast.2), custom_call_target="tpu_custom_call" | custom-call | tf_op jit(solution)/shard_map/project/pallas_call | solution.py:84
  5.9 0.1 collective-permute-start.4
  6.0 1.6 %collective-permute-start = (f32[64,256]{1,0:T(8,128)S(1)}, f32[64,256]{1,0:T(8,128)S(1)}, u32[]{:S(2)}, u32[]{:S(2)}) collective-permute-start(f32[64,256]{1,0:T(8,128)S(1)} %get-tuple-element.16), channel_id=1, source_target_pairs={{0,1},{1,0},{2,3},{3,2},{4,5},{5,4},{6,7},{7,6},{8,9},{9,8},{10,11... | collective-permute-start | bytes 196616 | tf_op jit(solution)/shard_map/ppermute | solution.py:245
  7.5 2.9 %collective-permute-done = f32[64,256]{1,0:T(8,128)S(1)} collective-permute-done((f32[64,256]{1,0:T(8,128)S(1)}, f32[64,256]{1,0:T(8,128)S(1)}, u32[]{:S(2)}, u32[]{:S(2)}) %collective-permute-start) | collective-permute-done | bytes 65568 | tf_op jit(solution)/shard_map/ppermute | solution.py:245
  10.5 1.6 %collective-permute-start.1 = (f32[64,256]{1,0:T(8,128)S(1)}, f32[64,256]{1,0:T(8,128)S(1)}, u32[]{:S(2)}, u32[]{:S(2)}) collective-permute-start(f32[64,256]{1,0:T(8,128)S(1)} %add.18), channel_id=1, source_target_pairs={{0,2},{1,3},{2,0},{3,1},{4,6},{5,7},{6,4},{7,5},{8,10},{9,11},{10,... | collective-permute-start | bytes 196616 | tf_op jit(solution)/shard_map/ppermute | solution.py:245
  12.1 2.7 %collective-permute-done.1 = f32[64,256]{1,0:T(8,128)S(1)} collective-permute-done((f32[64,256]{1,0:T(8,128)S(1)}, f32[64,256]{1,0:T(8,128)S(1)}, u32[]{:S(2)}, u32[]{:S(2)}) %collective-permute-start.1) | collective-permute-done | bytes 65568 | tf_op jit(solution)/shard_map/ppermute | solution.py:245
  14.8 2.7 %collective-permute-start.2 = (f32[64,256]{1,0:T(8,128)S(1)}, f32[64,256]{1,0:T(8,128)S(1)}, u32[]{:S(2)}, u32[]{:S(2)}) collective-permute-start(f32[64,256]{1,0:T(8,128)S(1)} %add.19), channel_id=1, source_target_pairs={{0,4},{1,5},{2,6},{3,7},{4,0},{5,1},{6,2},{7,3},{8,12},{9,13},{10,... | collective-permute-start | bytes 196616 | tf_op jit(solution)/shard_map/ppermute | solution.py:245
  17.5 2.6 %collective-permute-done.2 = f32[64,256]{1,0:T(8,128)S(1)} collective-permute-done((f32[64,256]{1,0:T(8,128)S(1)}, f32[64,256]{1,0:T(8,128)S(1)}, u32[]{:S(2)}, u32[]{:S(2)}) %collective-permute-start.2) | collective-permute-done | bytes 65568 | tf_op jit(solution)/shard_map/ppermute | solution.py:245
  20.1 0.1 collective-permute-start.3
  20.1 0.4 %collective-permute-start.5 = (f32[64,256]{1,0:T(8,128)S(1)}, f32[64,256]{1,0:T(8,128)S(1)}, u32[]{:S(2)}, u32[]{:S(2)}) collective-permute-start(f32[64,256]{1,0:T(8,128)S(1)} %add.20.p_ref), channel_id=1, source_target_pairs={{0,24},{8,16},{16,8},{24,0},{1,25},{9,17},{17,9},{25,1},{2,26},{10... | collective-permute-start | bytes 196616 | tf_op jit(solution)/shard_map/ppermute | solution.py:245
  20.6 0.8 %collective-permute-done.3.refs_0_ = f32[64,256]{1,0:T(8,128)S(1)} collective-permute-done((f32[64,256]{1,0:T(8,128)S(1)}, f32[64,256]{1,0:T(8,128)S(1)}, u32[]{:S(2)}, u32[]{:S(2)}) %collective-permute-start.3) | collective-permute-done | bytes 65568 | tf_op jit(solution)/shard_map/ppermute | solution.py:245
  21.4 2.3 %collective-permute-done.7.refs_2_ = f32[64,3584]{1,0:T(8,128)S(1)} collective-permute-done((f32[64,3584]{1,0:T(8,128)}, f32[64,3584]{1,0:T(8,128)S(1)}, u32[]{:S(2)}, u32[]{:S(2)}) %collective-permute-start.7) | collective-permute-done | bytes 917536 | tf_op jit(solution)/shard_map/ppermute | solution.py:245
  23.7 0.0 collective-permute-start.8
  23.7 0.8 %collective-permute-done.5.refs_1_ = f32[64,256]{1,0:T(8,128)S(1)} collective-permute-done((f32[64,256]{1,0:T(8,128)S(1)}, f32[64,256]{1,0:T(8,128)S(1)}, u32[]{:S(2)}, u32[]{:S(2)}) %collective-permute-start.5) | collective-permute-done | bytes 65568 | tf_op jit(solution)/shard_map/ppermute | solution.py:245
  24.6 0.2 collective-permute-start.6
  24.7 0.0 collective-permute-done.4.refs_1_
  24.7 1.5 %first_part.1.t_ref = f32[64,3584]{1,0:T(8,128)S(1)} custom-call(f32[64,256]{1,0:T(8,128)S(1)} %add.20.p_ref, f32[192,3584]{1,0:T(8,128)S(1)} %get-tuple-element.17.s_ref, f32[64,3584]{1,0:T(8,128)S(1)} %get-tuple-element.18.x_ref, f32[64,256]{1,0:T(8,128)S(1)} %collective-permute-done.3.refs_0_, f32[64,3584]{1,0:T(8,128)S(1)} %collective-permute-done.4.refs_1_), custom_call_target="tpu_custom_call" | custom-call | tf_op jit(solution)/shard_map/first_part/pallas_call | solution.py:141
  26.2 0.1 collective-permute-done.6.refs_0_
  26.3 0.3 couple.1
  26.6 0.0 collective-permute-done.8.refs_3_
  26.6 0.6 %rest_part.1 = (f32[64,3584]{1,0:T(8,128)S(1)}, f32[1,64]{1,0:T(1,128)S(1)}, f32[8,64]{1,0:T(8,128)S(1)}) custom-call(f32[64,3584]{1,0:T(8,128)S(1)} %first_part.1.t_ref, bf16[64,128]{1,0:T(8,128)(2,1)S(1)} %get-tuple-element.21.refs_0_, bf16[64,128]{1,0:T(8,128)(2,1)S(1)} %get-tuple-element.22.refs_1_, f32[64,3584]{1,0:T(8,128)S(1)} %collective-permute-done.7.refs_2_, ...), custom_call_target="tpu_custom_call" | custom-call | tf_op jit(solution)/shard_map/rest_part/pallas_call | solution.py:190
  27.2 2.8 %collective-permute-start.12 = (f32[8,64]{1,0:T(8,128)S(1)}, f32[8,64]{1,0:T(8,128)S(1)}, u32[]{:S(2)}, u32[]{:S(2)}) collective-permute-start(f32[8,64]{1,0:T(8,128)S(1)} %get-tuple-element.26), channel_id=1, source_target_pairs={{0,11},{1,10},{2,9},{3,8},{4,15},{5,14},{6,13},{7,12},{8,3},{9,2},... | collective-permute-start | bytes 6152 | tf_op jit(solution)/shard_map/ppermute | solution.py:280
  30.0 0.5 %collective-permute-start.10 = (f32[1,64]{1,0:T(1,128)S(1)}, f32[1,64]{1,0:T(1,128)S(1)}, u32[]{:S(2)}, u32[]{:S(2)}) collective-permute-start(f32[1,64]{1,0:T(1,128)S(1)} %get-tuple-element.25), channel_id=1, source_target_pairs={{0,9},{1,8},{2,11},{3,10},{4,13},{5,12},{6,15},{7,14},{8,1},{9,0},... | collective-permute-start | bytes 776 | tf_op jit(solution)/shard_map/ppermute | solution.py:280
  30.5 0.1 collective-permute-start.11
  30.7 0.2 collective-permute-start.9
  30.8 2.2 %collective-permute-done.10 = f32[1,64]{1,0:T(1,128)S(1)} collective-permute-done((f32[1,64]{1,0:T(1,128)S(1)}, f32[1,64]{1,0:T(1,128)S(1)}, u32[]{:S(2)}, u32[]{:S(2)}) %collective-permute-start.10) | collective-permute-done | bytes 288 | tf_op jit(solution)/shard_map/ppermute | solution.py:280
  33.0 0.5 %collective-permute-done.11 = f32[1,64]{1,0:T(1,128)S(1)} collective-permute-done((f32[1,64]{1,0:T(1,128)S(1)}, f32[1,64]{1,0:T(1,128)S(1)}, u32[]{:S(2)}, u32[]{:S(2)}) %collective-permute-start.11) | collective-permute-done | bytes 288 | tf_op jit(solution)/shard_map/ppermute | solution.py:280
  33.5 0.0 collective-permute-done.9
  33.5 0.0 collective-permute-done.12
  33.5 2.1 %collective-permute-start.14 = (f32[8,64]{1,0:T(8,128)S(1)}, f32[8,64]{1,0:T(8,128)S(1)}, u32[]{:S(2)}, u32[]{:S(2)}) collective-permute-start(f32[8,64]{1,0:T(8,128)S(1)} %broadcast_in_dim.8), channel_id=1, source_target_pairs={{0,12},{1,13},{2,14},{3,15},{4,8},{5,9},{6,10},{7,11},{8,4},{9,5},... | collective-permute-start | bytes 6152 | tf_op jit(solution)/shard_map/ppermute | solution.py:280
  35.6 0.4 %collective-permute-start.13 = (f32[1,64]{1,0:T(1,128)S(1)}, f32[1,64]{1,0:T(1,128)S(1)}, u32[]{:S(2)}, u32[]{:S(2)}) collective-permute-start(f32[1,64]{1,0:T(1,128)S(1)} %slice_add_fusion), channel_id=1, source_target_pairs={{0,8},{1,9},{2,10},{3,11},{4,12},{5,13},{6,14},{7,15},{8,0},{9,1},... | collective-permute-start | bytes 776 | tf_op jit(solution)/shard_map/ppermute | solution.py:280
  36.0 0.8 %collective-permute-done.13.refs_0_ = f32[1,64]{1,0:T(1,128)S(1)} collective-permute-done((f32[1,64]{1,0:T(1,128)S(1)}, f32[1,64]{1,0:T(1,128)S(1)}, u32[]{:S(2)}, u32[]{:S(2)}) %collective-permute-start.13) | collective-permute-done | bytes 288 | tf_op jit(solution)/shard_map/ppermute | solution.py:280
  36.9 0.7 %collective-permute-done.14.refs_1_ = f32[8,64]{1,0:T(8,128)S(1)} collective-permute-done((f32[8,64]{1,0:T(8,128)S(1)}, f32[8,64]{1,0:T(8,128)S(1)}, u32[]{:S(2)}, u32[]{:S(2)}) %collective-permute-start.14) | collective-permute-done | bytes 2080 | tf_op jit(solution)/shard_map/ppermute | solution.py:280
  37.5 1.1 %finish.1 = f32[64,3584]{1,0:T(8,128)} custom-call(f32[64,3584]{1,0:T(8,128)S(1)} %get-tuple-element.24.updated_ref, f32[1,64]{1,0:T(1,128)S(1)} %collective-permute-done.13.refs_0_, f32[8,64]{1,0:T(8,128)S(1)} %collective-permute-done.14.refs_1_), custom_call_target="tpu_custom_call" | custom-call | tf_op jit(solution)/shard_map/finish/pallas_call | solution.py:230
  (5 shorter events, 0.0 us)
Async XLA Ops:
  0.0 23.7 %collective-permute-start.7 = (f32[64,3584]{1,0:T(8,128)}, f32[64,3584]{1,0:T(8,128)S(1)}, u32[]{:S(2)}, u32[]{:S(2)}) collective-permute-start(f32[64,3584]{1,0:T(8,128)} %x_hbm.1), channel_id=1, source_target_pairs={{0,16},{8,24},{16,0},{24,8},{1,17},{9,25},{17,1},{25,9},{2,18},{10... | collective-permute-start | bytes 2752520 | tf_op jit(solution)/shard_map/ppermute | solution.py:245
  5.9 18.8 %collective-permute-start.4 = (f32[64,3584]{1,0:T(8,128)S(1)}, f32[64,3584]{1,0:T(8,128)S(1)}, u32[]{:S(2)}, u32[]{:S(2)}) collective-permute-start(f32[64,3584]{1,0:T(8,128)S(1)} %get-tuple-element.18.x_ref), channel_id=1, source_target_pairs={{0,8},{8,0},{16,24},{24,16},{1,9},{9,1},{17,25},{25,17},{2,10},{10... | collective-permute-start | bytes 2752520 | tf_op jit(solution)/shard_map/ppermute | solution.py:245
  6.0 4.5 %collective-permute-start = (f32[64,256]{1,0:T(8,128)S(1)}, f32[64,256]{1,0:T(8,128)S(1)}, u32[]{:S(2)}, u32[]{:S(2)}) collective-permute-start(f32[64,256]{1,0:T(8,128)S(1)} %get-tuple-element.16), channel_id=1, source_target_pairs={{0,1},{1,0},{2,3},{3,2},{4,5},{5,4},{6,7},{7,6},{8,9},{9,8},{10,11... | collective-permute-start | bytes 196616 | tf_op jit(solution)/shard_map/ppermute | solution.py:245
  10.5 4.3 %collective-permute-start.1 = (f32[64,256]{1,0:T(8,128)S(1)}, f32[64,256]{1,0:T(8,128)S(1)}, u32[]{:S(2)}, u32[]{:S(2)}) collective-permute-start(f32[64,256]{1,0:T(8,128)S(1)} %add.18), channel_id=1, source_target_pairs={{0,2},{1,3},{2,0},{3,1},{4,6},{5,7},{6,4},{7,5},{8,10},{9,11},{10,... | collective-permute-start | bytes 196616 | tf_op jit(solution)/shard_map/ppermute | solution.py:245
  14.8 5.2 %collective-permute-start.2 = (f32[64,256]{1,0:T(8,128)S(1)}, f32[64,256]{1,0:T(8,128)S(1)}, u32[]{:S(2)}, u32[]{:S(2)}) collective-permute-start(f32[64,256]{1,0:T(8,128)S(1)} %add.19), channel_id=1, source_target_pairs={{0,4},{1,5},{2,6},{3,7},{4,0},{5,1},{6,2},{7,3},{8,12},{9,13},{10,... | collective-permute-start | bytes 196616 | tf_op jit(solution)/shard_map/ppermute | solution.py:245
  20.1 1.3 %collective-permute-start.3 = (f32[64,256]{1,0:T(8,128)S(1)}, f32[64,256]{1,0:T(8,128)S(1)}, u32[]{:S(2)}, u32[]{:S(2)}) collective-permute-start(f32[64,256]{1,0:T(8,128)S(1)} %add.20.p_ref), channel_id=1, source_target_pairs={{0,8},{8,0},{16,24},{24,16},{1,9},{9,1},{17,25},{25,17},{2,10},{10... | collective-permute-start | bytes 196616 | tf_op jit(solution)/shard_map/ppermute | solution.py:245
  20.1 4.4 %collective-permute-start.5 = (f32[64,256]{1,0:T(8,128)S(1)}, f32[64,256]{1,0:T(8,128)S(1)}, u32[]{:S(2)}, u32[]{:S(2)}) collective-permute-start(f32[64,256]{1,0:T(8,128)S(1)} %add.20.p_ref), channel_id=1, source_target_pairs={{0,24},{8,16},{16,8},{24,0},{1,25},{9,17},{17,9},{25,1},{2,26},{10... | collective-permute-start | bytes 196616 | tf_op jit(solution)/shard_map/ppermute | solution.py:245
  23.7 2.8 %collective-permute-start.8 = (f32[64,3584]{1,0:T(8,128)S(1)}, f32[64,3584]{1,0:T(8,128)S(1)}, u32[]{:S(2)}, u32[]{:S(2)}) collective-permute-start(f32[64,3584]{1,0:T(8,128)S(1)} %collective-permute-done.7.refs_2_), channel_id=1, source_target_pairs={{0,8},{8,0},{16,24},{24,16},{1,9},{9,1},{17,25},{25,17},{2,10},{10... | collective-permute-start | bytes 2752520 | tf_op jit(solution)/shard_map/ppermute | solution.py:245
  24.6 1.7 %collective-permute-start.6 = (f32[64,256]{1,0:T(8,128)S(1)}, f32[64,256]{1,0:T(8,128)S(1)}, u32[]{:S(2)}, u32[]{:S(2)}) collective-permute-start(f32[64,256]{1,0:T(8,128)S(1)} %collective-permute-done.5.refs_1_), channel_id=1, source_target_pairs={{0,8},{8,0},{16,24},{24,16},{1,9},{9,1},{17,25},{25,17},{2,10},{10... | collective-permute-start | bytes 196616 | tf_op jit(solution)/shard_map/ppermute | solution.py:245
  27.2 6.3 %collective-permute-start.12 = (f32[8,64]{1,0:T(8,128)S(1)}, f32[8,64]{1,0:T(8,128)S(1)}, u32[]{:S(2)}, u32[]{:S(2)}) collective-permute-start(f32[8,64]{1,0:T(8,128)S(1)} %get-tuple-element.26), channel_id=1, source_target_pairs={{0,11},{1,10},{2,9},{3,8},{4,15},{5,14},{6,13},{7,12},{8,3},{9,2},... | collective-permute-start | bytes 6152 | tf_op jit(solution)/shard_map/ppermute | solution.py:280
  30.0 3.0 %collective-permute-start.10 = (f32[1,64]{1,0:T(1,128)S(1)}, f32[1,64]{1,0:T(1,128)S(1)}, u32[]{:S(2)}, u32[]{:S(2)}) collective-permute-start(f32[1,64]{1,0:T(1,128)S(1)} %get-tuple-element.25), channel_id=1, source_target_pairs={{0,9},{1,8},{2,11},{3,10},{4,13},{5,12},{6,15},{7,14},{8,1},{9,0},... | collective-permute-start | bytes 776 | tf_op jit(solution)/shard_map/ppermute | solution.py:280
  30.5 3.0 %collective-permute-start.11 = (f32[1,64]{1,0:T(1,128)S(1)}, f32[1,64]{1,0:T(1,128)S(1)}, u32[]{:S(2)}, u32[]{:S(2)}) collective-permute-start(f32[1,64]{1,0:T(1,128)S(1)} %get-tuple-element.25), channel_id=1, source_target_pairs={{0,10},{1,11},{2,8},{3,9},{4,14},{5,15},{6,12},{7,13},{8,2},{9,3},... | collective-permute-start | bytes 776 | tf_op jit(solution)/shard_map/ppermute | solution.py:280
  30.7 2.8 %collective-permute-start.9 = (f32[1,64]{1,0:T(1,128)S(1)}, f32[1,64]{1,0:T(1,128)S(1)}, u32[]{:S(2)}, u32[]{:S(2)}) collective-permute-start(f32[1,64]{1,0:T(1,128)S(1)} %get-tuple-element.25), channel_id=1, source_target_pairs={{0,8},{1,9},{2,10},{3,11},{4,12},{5,13},{6,14},{7,15},{8,0},{9,1},... | collective-permute-start | bytes 776 | tf_op jit(solution)/shard_map/ppermute | solution.py:280
  33.5 4.0 %collective-permute-start.14 = (f32[8,64]{1,0:T(8,128)S(1)}, f32[8,64]{1,0:T(8,128)S(1)}, u32[]{:S(2)}, u32[]{:S(2)}) collective-permute-start(f32[8,64]{1,0:T(8,128)S(1)} %broadcast_in_dim.8), channel_id=1, source_target_pairs={{0,12},{1,13},{2,14},{3,15},{4,8},{5,9},{6,10},{7,11},{8,4},{9,5},... | collective-permute-start | bytes 6152 | tf_op jit(solution)/shard_map/ppermute | solution.py:280
  35.6 1.2 %collective-permute-start.13 = (f32[1,64]{1,0:T(1,128)S(1)}, f32[1,64]{1,0:T(1,128)S(1)}, u32[]{:S(2)}, u32[]{:S(2)}) collective-permute-start(f32[1,64]{1,0:T(1,128)S(1)} %slice_add_fusion), channel_id=1, source_target_pairs={{0,8},{1,9},{2,10},{3,11},{4,12},{5,13},{6,14},{7,15},{8,0},{9,1},... | collective-permute-start | bytes 776 | tf_op jit(solution)/shard_map/ppermute | solution.py:280

commit v25 on v21

--- a/solution.py
+++ b/solution.py
@@ -10,7 +10,7 @@
 step_rate = 0.1
 epsilon = 1e-06
 lanes = 128
-block_rows = 16
+block_rows = 8
 in_vmem = pl.BlockSpec(memory_space=pltpu.VMEM)
 anywhere = pl.BlockSpec(memory_space=pl.ANY)
 params = pltpu.CompilerParams(vmem_limit_bytes=16 << 20)

time: 38.7 us -> 38.7 us (level)
  no operation moved by 1% of the time
where the time goes in v25:
time: 38.7 us; the launch traced here: 38.6 us
  waiting for transfers between devices  16.4 us (42%)
  starting transfers between devices  15.7 us (41%)
  Pallas kernels  6.36 us (16%)
    ppermute x9, waiting for transfers between devices, exchange(): lax.ppermute(array, axis, [(i, i ^ step) for i in range(lax.axis_size(axi...  12.3 us
    ppermute x9, starting transfers between devices, exchange(): lax.ppermute(array, axis, [(i, i ^ step) for i in range(lax.axis_size(axi...  9.54 us
    ppermute x6, starting transfers between devices, flipped_terms(): lax.ppermute(wide if k == width - 1 else array, ('comp', 'feat'), pairs)  6.14 us
    ppermute x6, waiting for transfers between devices, flipped_terms(): lax.ppermute(wide if k == width - 1 else array, ('comp', 'feat'), pairs)  4.16 us
    pallas_call x1, Pallas kernels, project(): pl.pallas_call(project_kernel, in_specs=[anywhere] * 2, out_specs=[in_vme...  2.93 us
    pallas_call x1, Pallas kernels, first_part(): pl.pallas_call(functools.partial(first_kernel, features, steps), in_specs...  1.47 us
    pallas_call x1, Pallas kernels, finish(): pl.pallas_call(functools.partial(finish_kernel, features, count), in_spec...  1.07 us
  transfers between devices with their start and end apart: 15, of which 11 were waited for; matrix products, arithmetic and copies ran while one was open for 0% of the time, Pallas kernels for 12%

profile of v25, /device:TPU:0, one launch (start us, length us, event | category | flops | bytes accessed | tf_op | source)
XLA Modules:
  0.0 38.6 jit_solution(9121613818013541334)
XLA Ops:
  0.0 2.9 %collective-permute-start.7 = (f32[64,3584]{1,0:T(8,128)}, f32[64,3584]{1,0:T(8,128)S(1)}, u32[]{:S(2)}, u32[]{:S(2)}) collective-permute-start(f32[64,3584]{1,0:T(8,128)} %x_hbm.1), channel_id=1, source_target_pairs={{0,16},{8,24},{16,0},{24,8},{1,17},{9,25},{17,1},{25,9},{2,18},{10... | collective-permute-start | bytes 2752520 | tf_op jit(solution)/shard_map/ppermute | solution.py:245
  2.9 2.9 %project.1 = (f32[64,256]{1,0:T(8,128)S(1)}, f32[64,3584]{1,0:T(8,128)S(1)}, f32[192,3584]{1,0:T(8,128)S(1)}) custom-call(f32[64,3584]{1,0:T(8,128)} %x_hbm.1, f32[192,3584]{1,0:T(8,128)} %bitcast.2), custom_call_target="tpu_custom_call" | custom-call | tf_op jit(solution)/shard_map/project/pallas_call | solution.py:84
  5.9 0.1 collective-permute-start.4
  6.0 1.6 %collective-permute-start = (f32[64,256]{1,0:T(8,128)S(1)}, f32[64,256]{1,0:T(8,128)S(1)}, u32[]{:S(2)}, u32[]{:S(2)}) collective-permute-start(f32[64,256]{1,0:T(8,128)S(1)} %get-tuple-element.16), channel_id=1, source_target_pairs={{0,1},{1,0},{2,3},{3,2},{4,5},{5,4},{6,7},{7,6},{8,9},{9,8},{10,11... | collective-permute-start | bytes 196616 | tf_op jit(solution)/shard_map/ppermute | solution.py:245
  7.5 2.9 %collective-permute-done = f32[64,256]{1,0:T(8,128)S(1)} collective-permute-done((f32[64,256]{1,0:T(8,128)S(1)}, f32[64,256]{1,0:T(8,128)S(1)}, u32[]{:S(2)}, u32[]{:S(2)}) %collective-permute-start) | collective-permute-done | bytes 65568 | tf_op jit(solution)/shard_map/ppermute | solution.py:245
  10.5 1.6 %collective-permute-start.1 = (f32[64,256]{1,0:T(8,128)S(1)}, f32[64,256]{1,0:T(8,128)S(1)}, u32[]{:S(2)}, u32[]{:S(2)}) collective-permute-start(f32[64,256]{1,0:T(8,128)S(1)} %add.18), channel_id=1, source_target_pairs={{0,2},{1,3},{2,0},{3,1},{4,6},{5,7},{6,4},{7,5},{8,10},{9,11},{10,... | collective-permute-start | bytes 196616 | tf_op jit(solution)/shard_map/ppermute | solution.py:245
  12.1 2.7 %collective-permute-done.1 = f32[64,256]{1,0:T(8,128)S(1)} collective-permute-done((f32[64,256]{1,0:T(8,128)S(1)}, f32[64,256]{1,0:T(8,128)S(1)}, u32[]{:S(2)}, u32[]{:S(2)}) %collective-permute-start.1) | collective-permute-done | bytes 65568 | tf_op jit(solution)/shard_map/ppermute | solution.py:245
  14.8 2.7 %collective-permute-start.2 = (f32[64,256]{1,0:T(8,128)S(1)}, f32[64,256]{1,0:T(8,128)S(1)}, u32[]{:S(2)}, u32[]{:S(2)}) collective-permute-start(f32[64,256]{1,0:T(8,128)S(1)} %add.19), channel_id=1, source_target_pairs={{0,4},{1,5},{2,6},{3,7},{4,0},{5,1},{6,2},{7,3},{8,12},{9,13},{10,... | collective-permute-start | bytes 196616 | tf_op jit(solution)/shard_map/ppermute | solution.py:245
  17.5 2.6 %collective-permute-done.2 = f32[64,256]{1,0:T(8,128)S(1)} collective-permute-done((f32[64,256]{1,0:T(8,128)S(1)}, f32[64,256]{1,0:T(8,128)S(1)}, u32[]{:S(2)}, u32[]{:S(2)}) %collective-permute-start.2) | collective-permute-done | bytes 65568 | tf_op jit(solution)/shard_map/ppermute | solution.py:245
  20.1 0.1 collective-permute-start.3
  20.1 0.4 %collective-permute-start.5 = (f32[64,256]{1,0:T(8,128)S(1)}, f32[64,256]{1,0:T(8,128)S(1)}, u32[]{:S(2)}, u32[]{:S(2)}) collective-permute-start(f32[64,256]{1,0:T(8,128)S(1)} %add.20.p_ref), channel_id=1, source_target_pairs={{0,24},{8,16},{16,8},{24,0},{1,25},{9,17},{17,9},{25,1},{2,26},{10... | collective-permute-start | bytes 196616 | tf_op jit(solution)/shard_map/ppermute | solution.py:245
  20.6 0.8 %collective-permute-done.3.refs_0_ = f32[64,256]{1,0:T(8,128)S(1)} collective-permute-done((f32[64,256]{1,0:T(8,128)S(1)}, f32[64,256]{1,0:T(8,128)S(1)}, u32[]{:S(2)}, u32[]{:S(2)}) %collective-permute-start.3) | collective-permute-done | bytes 65568 | tf_op jit(solution)/shard_map/ppermute | solution.py:245
  21.4 2.3 %collective-permute-done.7.refs_2_ = f32[64,3584]{1,0:T(8,128)S(1)} collective-permute-done((f32[64,3584]{1,0:T(8,128)}, f32[64,3584]{1,0:T(8,128)S(1)}, u32[]{:S(2)}, u32[]{:S(2)}) %collective-permute-start.7) | collective-permute-done | bytes 917536 | tf_op jit(solution)/shard_map/ppermute | solution.py:245
  23.7 0.0 collective-permute-start.8
  23.7 0.8 %collective-permute-done.5.refs_1_ = f32[64,256]{1,0:T(8,128)S(1)} collective-permute-done((f32[64,256]{1,0:T(8,128)S(1)}, f32[64,256]{1,0:T(8,128)S(1)}, u32[]{:S(2)}, u32[]{:S(2)}) %collective-permute-start.5) | collective-permute-done | bytes 65568 | tf_op jit(solution)/shard_map/ppermute | solution.py:245
  24.6 0.2 collective-permute-start.6
  24.7 0.0 collective-permute-done.4.refs_1_
  24.7 1.5 %first_part.1.t_ref = f32[64,3584]{1,0:T(8,128)S(1)} custom-call(f32[64,256]{1,0:T(8,128)S(1)} %add.20.p_ref, f32[192,3584]{1,0:T(8,128)S(1)} %get-tuple-element.17.s_ref, f32[64,3584]{1,0:T(8,128)S(1)} %get-tuple-element.18.x_ref, f32[64,256]{1,0:T(8,128)S(1)} %collective-permute-done.3.refs_0_, f32[64,3584]{1,0:T(8,128)S(1)} %collective-permute-done.4.refs_1_), custom_call_target="tpu_custom_call" | custom-call | tf_op jit(solution)/shard_map/first_part/pallas_call | solution.py:141
  26.2 0.1 collective-permute-done.6.refs_0_
  26.3 0.3 couple.1
  26.6 0.0 collective-permute-done.8.refs_3_
  26.6 0.6 %rest_part.1 = (f32[64,3584]{1,0:T(8,128)S(1)}, f32[1,64]{1,0:T(1,128)S(1)}, f32[8,64]{1,0:T(8,128)S(1)}) custom-call(f32[64,3584]{1,0:T(8,128)S(1)} %first_part.1.t_ref, bf16[64,128]{1,0:T(8,128)(2,1)S(1)} %get-tuple-element.21.refs_0_, bf16[64,128]{1,0:T(8,128)(2,1)S(1)} %get-tuple-element.22.refs_1_, f32[64,3584]{1,0:T(8,128)S(1)} %collective-permute-done.7.refs_2_, ...), custom_call_target="tpu_custom_call" | custom-call | tf_op jit(solution)/shard_map/rest_part/pallas_call | solution.py:190
  27.2 2.8 %collective-permute-start.12 = (f32[8,64]{1,0:T(8,128)S(1)}, f32[8,64]{1,0:T(8,128)S(1)}, u32[]{:S(2)}, u32[]{:S(2)}) collective-permute-start(f32[8,64]{1,0:T(8,128)S(1)} %get-tuple-element.26), channel_id=1, source_target_pairs={{0,11},{1,10},{2,9},{3,8},{4,15},{5,14},{6,13},{7,12},{8,3},{9,2},... | collective-permute-start | bytes 6152 | tf_op jit(solution)/shard_map/ppermute | solution.py:280
  30.0 0.5 %collective-permute-start.10 = (f32[1,64]{1,0:T(1,128)S(1)}, f32[1,64]{1,0:T(1,128)S(1)}, u32[]{:S(2)}, u32[]{:S(2)}) collective-permute-start(f32[1,64]{1,0:T(1,128)S(1)} %get-tuple-element.25), channel_id=1, source_target_pairs={{0,9},{1,8},{2,11},{3,10},{4,13},{5,12},{6,15},{7,14},{8,1},{9,0},... | collective-permute-start | bytes 776 | tf_op jit(solution)/shard_map/ppermute | solution.py:280
  30.5 0.1 collective-permute-start.11
  30.7 0.2 collective-permute-start.9
  30.8 2.2 %collective-permute-done.10 = f32[1,64]{1,0:T(1,128)S(1)} collective-permute-done((f32[1,64]{1,0:T(1,128)S(1)}, f32[1,64]{1,0:T(1,128)S(1)}, u32[]{:S(2)}, u32[]{:S(2)}) %collective-permute-start.10) | collective-permute-done | bytes 288 | tf_op jit(solution)/shard_map/ppermute | solution.py:280
  33.0 0.5 %collective-permute-done.11 = f32[1,64]{1,0:T(1,128)S(1)} collective-permute-done((f32[1,64]{1,0:T(1,128)S(1)}, f32[1,64]{1,0:T(1,128)S(1)}, u32[]{:S(2)}, u32[]{:S(2)}) %collective-permute-start.11) | collective-permute-done | bytes 288 | tf_op jit(solution)/shard_map/ppermute | solution.py:280
  33.5 0.0 collective-permute-done.9
  33.5 0.0 collective-permute-done.12
  33.5 2.1 %collective-permute-start.14 = (f32[8,64]{1,0:T(8,128)S(1)}, f32[8,64]{1,0:T(8,128)S(1)}, u32[]{:S(2)}, u32[]{:S(2)}) collective-permute-start(f32[8,64]{1,0:T(8,128)S(1)} %broadcast_in_dim.8), channel_id=1, source_target_pairs={{0,12},{1,13},{2,14},{3,15},{4,8},{5,9},{6,10},{7,11},{8,4},{9,5},... | collective-permute-start | bytes 6152 | tf_op jit(solution)/shard_map/ppermute | solution.py:280
  35.6 0.4 %collective-permute-start.13 = (f32[1,64]{1,0:T(1,128)S(1)}, f32[1,64]{1,0:T(1,128)S(1)}, u32[]{:S(2)}, u32[]{:S(2)}) collective-permute-start(f32[1,64]{1,0:T(1,128)S(1)} %slice_add_fusion), channel_id=1, source_target_pairs={{0,8},{1,9},{2,10},{3,11},{4,12},{5,13},{6,14},{7,15},{8,0},{9,1},... | collective-permute-start | bytes 776 | tf_op jit(solution)/shard_map/ppermute | solution.py:280
  36.0 0.8 %collective-permute-done.13.refs_0_ = f32[1,64]{1,0:T(1,128)S(1)} collective-permute-done((f32[1,64]{1,0:T(1,128)S(1)}, f32[1,64]{1,0:T(1,128)S(1)}, u32[]{:S(2)}, u32[]{:S(2)}) %collective-permute-start.13) | collective-permute-done | bytes 288 | tf_op jit(solution)/shard_map/ppermute | solution.py:280
  36.9 0.7 %collective-permute-done.14.refs_1_ = f32[8,64]{1,0:T(8,128)S(1)} collective-permute-done((f32[8,64]{1,0:T(8,128)S(1)}, f32[8,64]{1,0:T(8,128)S(1)}, u32[]{:S(2)}, u32[]{:S(2)}) %collective-permute-start.14) | collective-permute-done | bytes 2080 | tf_op jit(solution)/shard_map/ppermute | solution.py:280
  37.5 1.1 %finish.1 = f32[64,3584]{1,0:T(8,128)} custom-call(f32[64,3584]{1,0:T(8,128)S(1)} %get-tuple-element.24.updated_ref, f32[1,64]{1,0:T(1,128)S(1)} %collective-permute-done.13.refs_0_, f32[8,64]{1,0:T(8,128)S(1)} %collective-permute-done.14.refs_1_), custom_call_target="tpu_custom_call" | custom-call | tf_op jit(solution)/shard_map/finish/pallas_call | solution.py:230
  (5 shorter events, 0.0 us)
Async XLA Ops:
  0.0 23.7 %collective-permute-start.7 = (f32[64,3584]{1,0:T(8,128)}, f32[64,3584]{1,0:T(8,128)S(1)}, u32[]{:S(2)}, u32[]{:S(2)}) collective-permute-start(f32[64,3584]{1,0:T(8,128)} %x_hbm.1), channel_id=1, source_target_pairs={{0,16},{8,24},{16,0},{24,8},{1,17},{9,25},{17,1},{25,9},{2,18},{10... | collective-permute-start | bytes 2752520 | tf_op jit(solution)/shard_map/ppermute | solution.py:245
  5.9 18.8 %collective-permute-start.4 = (f32[64,3584]{1,0:T(8,128)S(1)}, f32[64,3584]{1,0:T(8,128)S(1)}, u32[]{:S(2)}, u32[]{:S(2)}) collective-permute-start(f32[64,3584]{1,0:T(8,128)S(1)} %get-tuple-element.18.x_ref), channel_id=1, source_target_pairs={{0,8},{8,0},{16,24},{24,16},{1,9},{9,1},{17,25},{25,17},{2,10},{10... | collective-permute-start | bytes 2752520 | tf_op jit(solution)/shard_map/ppermute | solution.py:245
  6.0 4.5 %collective-permute-start = (f32[64,256]{1,0:T(8,128)S(1)}, f32[64,256]{1,0:T(8,128)S(1)}, u32[]{:S(2)}, u32[]{:S(2)}) collective-permute-start(f32[64,256]{1,0:T(8,128)S(1)} %get-tuple-element.16), channel_id=1, source_target_pairs={{0,1},{1,0},{2,3},{3,2},{4,5},{5,4},{6,7},{7,6},{8,9},{9,8},{10,11... | collective-permute-start | bytes 196616 | tf_op jit(solution)/shard_map/ppermute | solution.py:245
  10.5 4.3 %collective-permute-start.1 = (f32[64,256]{1,0:T(8,128)S(1)}, f32[64,256]{1,0:T(8,128)S(1)}, u32[]{:S(2)}, u32[]{:S(2)}) collective-permute-start(f32[64,256]{1,0:T(8,128)S(1)} %add.18), channel_id=1, source_target_pairs={{0,2},{1,3},{2,0},{3,1},{4,6},{5,7},{6,4},{7,5},{8,10},{9,11},{10,... | collective-permute-start | bytes 196616 | tf_op jit(solution)/shard_map/ppermute | solution.py:245
  14.8 5.2 %collective-permute-start.2 = (f32[64,256]{1,0:T(8,128)S(1)}, f32[64,256]{1,0:T(8,128)S(1)}, u32[]{:S(2)}, u32[]{:S(2)}) collective-permute-start(f32[64,256]{1,0:T(8,128)S(1)} %add.19), channel_id=1, source_target_pairs={{0,4},{1,5},{2,6},{3,7},{4,0},{5,1},{6,2},{7,3},{8,12},{9,13},{10,... | collective-permute-start | bytes 196616 | tf_op jit(solution)/shard_map/ppermute | solution.py:245
  20.1 1.3 %collective-permute-start.3 = (f32[64,256]{1,0:T(8,128)S(1)}, f32[64,256]{1,0:T(8,128)S(1)}, u32[]{:S(2)}, u32[]{:S(2)}) collective-permute-start(f32[64,256]{1,0:T(8,128)S(1)} %add.20.p_ref), channel_id=1, source_target_pairs={{0,8},{8,0},{16,24},{24,16},{1,9},{9,1},{17,25},{25,17},{2,10},{10... | collective-permute-start | bytes 196616 | tf_op jit(solution)/shard_map/ppermute | solution.py:245
  20.1 4.4 %collective-permute-start.5 = (f32[64,256]{1,0:T(8,128)S(1)}, f32[64,256]{1,0:T(8,128)S(1)}, u32[]{:S(2)}, u32[]{:S(2)}) collective-permute-start(f32[64,256]{1,0:T(8,128)S(1)} %add.20.p_ref), channel_id=1, source_target_pairs={{0,24},{8,16},{16,8},{24,0},{1,25},{9,17},{17,9},{25,1},{2,26},{10... | collective-permute-start | bytes 196616 | tf_op jit(solution)/shard_map/ppermute | solution.py:245
  23.7 2.8 %collective-permute-start.8 = (f32[64,3584]{1,0:T(8,128)S(1)}, f32[64,3584]{1,0:T(8,128)S(1)}, u32[]{:S(2)}, u32[]{:S(2)}) collective-permute-start(f32[64,3584]{1,0:T(8,128)S(1)} %collective-permute-done.7.refs_2_), channel_id=1, source_target_pairs={{0,8},{8,0},{16,24},{24,16},{1,9},{9,1},{17,25},{25,17},{2,10},{10... | collective-permute-start | bytes 2752520 | tf_op jit(solution)/shard_map/ppermute | solution.py:245
  24.6 1.7 %collective-permute-start.6 = (f32[64,256]{1,0:T(8,128)S(1)}, f32[64,256]{1,0:T(8,128)S(1)}, u32[]{:S(2)}, u32[]{:S(2)}) collective-permute-start(f32[64,256]{1,0:T(8,128)S(1)} %collective-permute-done.5.refs_1_), channel_id=1, source_target_pairs={{0,8},{8,0},{16,24},{24,16},{1,9},{9,1},{17,25},{25,17},{2,10},{10... | collective-permute-start | bytes 196616 | tf_op jit(solution)/shard_map/ppermute | solution.py:245
  27.2 6.3 %collective-permute-start.12 = (f32[8,64]{1,0:T(8,128)S(1)}, f32[8,64]{1,0:T(8,128)S(1)}, u32[]{:S(2)}, u32[]{:S(2)}) collective-permute-start(f32[8,64]{1,0:T(8,128)S(1)} %get-tuple-element.26), channel_id=1, source_target_pairs={{0,11},{1,10},{2,9},{3,8},{4,15},{5,14},{6,13},{7,12},{8,3},{9,2},... | collective-permute-start | bytes 6152 | tf_op jit(solution)/shard_map/ppermute | solution.py:280
  30.0 3.0 %collective-permute-start.10 = (f32[1,64]{1,0:T(1,128)S(1)}, f32[1,64]{1,0:T(1,128)S(1)}, u32[]{:S(2)}, u32[]{:S(2)}) collective-permute-start(f32[1,64]{1,0:T(1,128)S(1)} %get-tuple-element.25), channel_id=1, source_target_pairs={{0,9},{1,8},{2,11},{3,10},{4,13},{5,12},{6,15},{7,14},{8,1},{9,0},... | collective-permute-start | bytes 776 | tf_op jit(solution)/shard_map/ppermute | solution.py:280
  30.5 3.0 %collective-permute-start.11 = (f32[1,64]{1,0:T(1,128)S(1)}, f32[1,64]{1,0:T(1,128)S(1)}, u32[]{:S(2)}, u32[]{:S(2)}) collective-permute-start(f32[1,64]{1,0:T(1,128)S(1)} %get-tuple-element.25), channel_id=1, source_target_pairs={{0,10},{1,11},{2,8},{3,9},{4,14},{5,15},{6,12},{7,13},{8,2},{9,3},... | collective-permute-start | bytes 776 | tf_op jit(solution)/shard_map/ppermute | solution.py:280
  30.7 2.8 %collective-permute-start.9 = (f32[1,64]{1,0:T(1,128)S(1)}, f32[1,64]{1,0:T(1,128)S(1)}, u32[]{:S(2)}, u32[]{:S(2)}) collective-permute-start(f32[1,64]{1,0:T(1,128)S(1)} %get-tuple-element.25), channel_id=1, source_target_pairs={{0,8},{1,9},{2,10},{3,11},{4,12},{5,13},{6,14},{7,15},{8,0},{9,1},... | collective-permute-start | bytes 776 | tf_op jit(solution)/shard_map/ppermute | solution.py:280
  33.5 4.0 %collective-permute-start.14 = (f32[8,64]{1,0:T(8,128)S(1)}, f32[8,64]{1,0:T(8,128)S(1)}, u32[]{:S(2)}, u32[]{:S(2)}) collective-permute-start(f32[8,64]{1,0:T(8,128)S(1)} %broadcast_in_dim.8), channel_id=1, source_target_pairs={{0,12},{1,13},{2,14},{3,15},{4,8},{5,9},{6,10},{7,11},{8,4},{9,5},... | collective-permute-start | bytes 6152 | tf_op jit(solution)/shard_map/ppermute | solution.py:280
  35.6 1.2 %collective-permute-start.13 = (f32[1,64]{1,0:T(1,128)S(1)}, f32[1,64]{1,0:T(1,128)S(1)}, u32[]{:S(2)}, u32[]{:S(2)}) collective-permute-start(f32[1,64]{1,0:T(1,128)S(1)} %slice_add_fusion), channel_id=1, source_target_pairs={{0,8},{1,9},{2,10},{3,11},{4,12},{5,13},{6,14},{7,15},{8,0},{9,1},... | collective-permute-start | bytes 776 | tf_op jit(solution)/shard_map/ppermute | solution.py:280
